TPU v7x, 256 devices: a whole 4x4x8 slice. The times are simulated.
256 devices in a mesh: shot: 32 (over x, z_lo, core), dom: 8 (over z_hi, y).
Axes of the slice: x: 4, y: 4, z: 8 (z_hi: 2, z_lo: 4; z = z_hi * 4 + z_lo), core: 2. Of those that a mesh axis runs over, the one named last changes fastest.
Arguments:
- velocity: bfloat16 [192, 320, 128], P('shot', 'dom'), may hold values from 0.19921875 to 0.43945312
- anchors: int32 [32, 2], P('shot'), may hold values from 0 to 128, as said below
- start_step: int32 [32], P('shot'), may hold values from 0 to 62
- source: int32 [32, 3], P('shot'), may hold values from 0 to 255, as said below
- receivers: int32 [32, 3, 512], P('shot'), may hold values from 0 to 255, as said below
- traces: float32 [32, 64, 512], P('shot'), may hold values from -6 to 6
- wavelet: float32 [64], replicated, may hold values from -6 to 6
- fwd_prev: float32 [32, 64, 256, 128], P('shot', 'dom'), may hold values from -6 to 6
- fwd_now: float32 [32, 64, 256, 128], P('shot', 'dom'), may hold values from -6 to 6
- adj_prev: float32 [32, 64, 256, 128], P('shot', 'dom'), may hold values from -6 to 6
- adj_now: float32 [32, 64, 256, 128], P('shot', 'dom'), may hold values from -6 to 6
Outputs:
- forward_field: float32 [32, 64, 256, 128], P('shot', 'dom')
- adjoint_field: float32 [32, 64, 256, 128], P('shot', 'dom')
- gradient: float32 [192, 320, 128], P('shot', 'dom')
Inputs may be any that keep to these rules, and one draw needn't show every extreme that they name: `anchors`: column 0 runs from 0 to 128, column 1 from 0 to 64; both ends of both columns occur in every draw. `source`: columns are the cell along the first, second and third aperture dimension, below 64, 256 and 128; some shot sits at the last cell of all three, some at the first. `receivers`: components 0, 1, 2 are below 64, 256 and 128; cells may repeat; some receiver sits at the last cell of all three, some at the first.
All inputs are finite; a program needn't handle non-finite values.
Results may differ from a plain program's by a relative error of at most 0.00055.
Values may be sent and summed in bfloat16 or wider, within the bound.
No kernel may reach another device: no remote copies, remote signals or barrier semaphores. Data moves between devices by JAX's collectives and lax.ppermute only.
A program may use at most 128 MiB of HBM per device.

v0:
```python
import jax
import jax.numpy as jnp
from jax import lax
from jax.sharding import PartitionSpec as P

STEPS = 2


CENTER = -205.0 / 72.0
COEFFS = (8.0 / 5.0, -1.0 / 5.0, 8.0 / 315.0, -1.0 / 560.0)


def with_halo(block, sides, width):
    for axis, dim in sides:
        count = lax.axis_size(axis)
        forward = [(i, i + 1) for i in range(count - 1)]
        backward = [(target, source) for source, target in forward]
        low = lax.ppermute(
            lax.slice_in_dim(block, block.shape[dim] - width, None, axis=dim), axis, forward
        )
        high = lax.ppermute(lax.slice_in_dim(block, 0, width, axis=dim), axis, backward)
        block = jnp.concatenate([low, block, high], axis=dim)
    return block


def laplace_rows(extended):
    row_count = extended.shape[0] - 8
    count_y = extended.shape[1]
    count_z = extended.shape[2]
    middle = extended[4 : 4 + row_count]
    padded = jnp.pad(middle, ((0, 0), (4, 4), (4, 4)))
    summed = 3.0 * CENTER * middle
    for k in range(1, 5):
        weight = COEFFS[k - 1]
        summed = summed + weight * (
            extended[4 + k : 4 + k + row_count] + extended[4 - k : 4 - k + row_count]
        )
        summed = summed + weight * (
            padded[:, 4 + k : 4 + k + count_y, 4 : 4 + count_z]
            + padded[:, 4 - k : 4 - k + count_y, 4 : 4 + count_z]
        )
        summed = summed + weight * (
            padded[:, 4 : 4 + count_y, 4 + k : 4 + k + count_z]
            + padded[:, 4 : 4 + count_y, 4 - k : 4 - k + count_z]
        )
    return summed


def source_term(x_start, row_count, count_y, count_z, shot_source, amplitude):
    grid_shape = (row_count, count_y, count_z)
    cell_x = x_start + lax.broadcasted_iota(jnp.int32, grid_shape, 0)
    cell_y = lax.broadcasted_iota(jnp.int32, grid_shape, 1)
    cell_z = lax.broadcasted_iota(jnp.int32, grid_shape, 2)
    is_hit = (cell_x == shot_source[0]) & (cell_y == shot_source[1]) & (cell_z == shot_source[2])
    return jnp.where(is_hit, amplitude, jnp.zeros((), amplitude.dtype))


def receiver_term(x_start, row_count, count_y, count_z, shot_receivers, amplitudes):
    local_x = shot_receivers[0] - x_start
    valid = (local_x >= 0) & (local_x < row_count)
    local_x = jnp.where(valid, local_x, row_count)
    grid = jnp.zeros((row_count, count_y, count_z), amplitudes.dtype)
    return grid.at[local_x, shot_receivers[1], shot_receivers[2]].add(amplitudes, mode="drop")


def advance(prev_middle, extended, factor, injected):
    return 2.0 * extended[4:-4] - prev_middle + factor * laplace_rows(extended) + injected


def window_rows(table, offset, count):
    padded = jnp.pad(table, ((count, count), (0, 0)))
    limit = table.shape[0] + count
    begin = jnp.clip(offset + count, 0, limit)
    return lax.dynamic_slice_in_dim(padded, begin, count, 0)


def body(
    velocity,
    anchors,
    start_step,
    source,
    receivers,
    traces,
    wavelet,
    fwd_prev,
    fwd_now,
    adj_prev,
    adj_now,
):
    row_count = fwd_now.shape[1]
    count_y = fwd_now.shape[2]
    count_z = fwd_now.shape[3]
    groups = lax.axis_size("dom")
    span_x = row_count * groups
    own_rows = velocity.shape[0]
    band_y = velocity.shape[1]
    anchor_x = anchors[0, 0]
    anchor_y = anchors[0, 1]
    first_step = start_step[0]
    shot_source = source[0]
    shot_receivers = receivers[0]
    shot_traces = traces[0]
    x_base = lax.axis_index("dom") * row_count
    flat_slab = velocity.reshape(own_rows, band_y * count_z)
    placed = window_rows(lax.all_gather(flat_slab, "shot", axis=0, tiled=True), anchor_x, span_x)
    picked = placed.astype(jnp.float32)
    picked = picked.astype(jnp.bfloat16).reshape(span_x, band_y, count_z)
    columns = lax.all_to_all(picked, "dom", split_axis=0, concat_axis=1, tiled=True)
    local_speed = lax.dynamic_slice_in_dim(columns, anchor_y, count_y, 1)
    courant = jnp.square(local_speed.astype(jnp.float32))
    forward = [fwd_prev[0], fwd_now[0]]
    adjoint = [adj_prev[0], adj_now[0]]
    for k in range(STEPS):
        extended = with_halo(forward[-1], (("dom", 0),), 4)
        amplitude = lax.dynamic_index_in_dim(wavelet, first_step + k, 0, keepdims=False)
        forward.append(
            advance(
                forward[-2],
                extended,
                courant,
                source_term(x_base, row_count, count_y, count_z, shot_source, amplitude),
            )
        )
    for k in range(STEPS):
        extended = with_halo(adjoint[-1], (("dom", 0),), 4)
        amplitudes = lax.dynamic_index_in_dim(
            shot_traces, first_step + STEPS - 1 - k, 0, keepdims=False
        )
        adjoint.append(
            advance(
                adjoint[-2],
                extended,
                courant,
                receiver_term(x_base, row_count, count_y, count_z, shot_receivers, amplitudes),
            )
        )
    imaged = jnp.zeros_like(forward[1])
    for k in range(1, STEPS + 1):
        imaged = imaged + adjoint[k + 1] * (
            forward[STEPS - k + 2] - 2.0 * forward[STEPS - k + 1] + forward[STEPS - k]
        )
    frame = jnp.zeros((row_count, band_y * groups, count_z), jnp.float32)
    frame = lax.dynamic_update_slice_in_dim(frame, imaged, anchor_y, 1)
    bands = lax.all_to_all(frame, "dom", split_axis=1, concat_axis=0, tiled=True)
    flat_image = bands.reshape(span_x, band_y * count_z)
    summed = lax.psum_scatter(
        window_rows(flat_image, jnp.int32(0) - anchor_x, own_rows * lax.axis_size("shot")),
        "shot",
        scatter_dimension=0,
        tiled=True,
    )
    gradient = summed.reshape(own_rows, band_y, count_z)
    return (forward[-1][None], adjoint[-1][None], gradient)


def solution(mesh):
    placed = (
        P("shot", "dom", None),
        P("shot", None),
        P("shot"),
        P("shot", None),
        P("shot", None, None),
        P("shot", None, None),
        P(),
        P("shot", "dom", None, None),
        P("shot", "dom", None, None),
        P("shot", "dom", None, None),
        P("shot", "dom", None, None),
    )
    return jax.shard_map(
        body,
        mesh=mesh,
        in_specs=placed,
        out_specs=(
            P("shot", "dom", None, None),
            P("shot", "dom", None, None),
            P("shot", "dom", None),
        ),
        check_vma=False,
    )
```

profile of v0, /device:TPU:6, one launch (start us, length us, event | category | flops | bytes accessed | tf_op | source)
XLA Modules:
  0.0 417.0 jit_solution(424696927417511912)
XLA Ops:
  7.2 1.6 reshape.156
  8.8 1.4 fusion.179
  10.8 62.6 %all-gather.3.cloned.1.call-done = bf16[32,6,5120]{2,1,0:T(8,128)(2,1)} async-done(((bf16[1,6,5120]{2,1,0:T(8,128)(2,1)}), bf16[32,6,5120]{2,1,0:T(8,128)(2,1)}) %all-gather.3.cloned.1.call-update) | async-done | bytes 1966096 | tf_op jit(solution)/shard_map/all_gather | solution.py:105
  73.4 2.8 reshape.157
  76.5 0.9 copy.22
  77.4 7.9 %all-to-all-start = ((bf16[64,40,128]{2,1,0:T(8,128)(2,1)}), bf16[64,40,128]{2,1,0:T(8,128)(2,1)S(1)}, u32[]{:S(2)}, u32[]{:S(2)}) async-start(bf16[64,40,128]{2,1,0:T(8,128)(2,1)} %bitcast.38), calls=%async_computation | async-start | bytes 1310720 | tf_op jit(solution)/shard_map/all_to_all | solution.py:108
  85.3 1.0 slice_bitcast_fusion.1
  86.4 4.9 %collective-permute-start.5 = (f32[4,256,128]{2,1,0:T(8,128)}, f32[4,256,128]{2,1,0:T(8,128)}, u32[]{:S(2)}, u32[]{:S(2)}) collective-permute-start(f32[4,256,128]{2,1,0:T(8,128)} %get-tuple-element.14), channel_id=1, source_target_pairs={{0,1},{1,2},{2,3},{3,4},{4,5},{5,6},{6,7},{8,9},{9,10},{10,11},{11... | collective-permute-start | bytes 1572872 | tf_op jit(solution)/shard_map/ppermute | solution.py:18
  91.2 1.3 collective-permute-start.4
  92.5 1.1 slice_bitcast_fusion.3
  93.6 4.6 %collective-permute-start.1 = (f32[4,256,128]{2,1,0:T(8,128)}, f32[4,256,128]{2,1,0:T(8,128)S(1)}, u32[]{:S(2)}, u32[]{:S(2)}) collective-permute-start(f32[4,256,128]{2,1,0:T(8,128)} %get-tuple-element.8), channel_id=1, source_target_pairs={{0,1},{1,2},{2,3},{3,4},{4,5},{5,6},{6,7},{8,9},{9,10},{10,11},{11... | collective-permute-start | bytes 1572872 | tf_op jit(solution)/shard_map/ppermute | solution.py:18
  98.2 1.3 collective-permute-start
  102.2 0.7 fusion.177
  102.9 0.6 fusion.178
  105.3 0.8 constant_dynamic-slice_fusion
  106.6 2.0 collective-permute-done.4
  108.5 4.3 %fusion.11 = f32[8,256,128]{2,1,0:T(8,128)S(1)} fusion(f32[8,256,128]{2,1,0:T(8,128)S(1)} %bitcast.79, f32[4,256,128]{2,1,0:T(8,128)} %collective-permute-done.5, f32[4,256,128]{2,1,0:T(8,128)} %collective-permute-done.4, f32[1,8,256,128]{3,2,1,0:T(8,128)} %param.20, bf16[8,320,128]{2,1,0:T(8,128)(2,1)S(1)} %bitcast.75, s32[]{:T(128)S(6)} %select_n.68), kind=kLoop, calls=%fused_computation.114 | loop fusion | flops 13369344 | bytes 4718596 | tf_op jit(solution)/shard_map/add | solution.py:67
  112.9 30.8 %scatter_fusion = f32[8,256,128]{2,1,0:T(8,128)S(1)} fusion(f32[8,256,128]{2,1,0:T(8,128)S(1)} %fusion.11, s32[512]{0:T(512)S(1)} %bitcast.72, f32[512]{0:T(512)S(1)} %bitcast.86), kind=kCustom, calls=%fused_computation | custom fusion | flops 512 | bytes 12288 | tf_op jit(solution)/shard_map/scatter-add | solution.py:63
  143.8 3.3 collective-permute-start.7
  147.1 1.3 collective-permute-start.6
  148.4 4.9 %fusion.65 = f32[8,256,128]{2,1,0:T(8,128)S(1)} fusion(f32[8,256,128]{2,1,0:T(8,128)S(1)} %bitcast.80, f32[4,256,128]{2,1,0:T(8,128)S(1)} %collective-permute-done.1, f32[4,256,128]{2,1,0:T(8,128)} %collective-permute-done, f32[1,8,256,128]{3,2,1,0:T(8,128)S(1)} %copy-done.6, f32[]{:T(128)} %bitcast.13, pred[128]{0:T(512)(128)(4,1)S(1)} %iota_compare_fusion.1, ...), kind=kLoop, calls=%fused_computation.168 | loop fusion | flops 14417920 | bytes 4718992 | tf_op jit(solution)/shard_map/add | solution.py:67
  153.4 1.2 fusion.175
  154.5 5.0 %collective-permute-start.3 = (f32[4,256,128]{2,1,0:T(8,128)}, f32[4,256,128]{2,1,0:T(8,128)S(1)}, u32[]{:S(2)}, u32[]{:S(2)}) collective-permute-start(f32[4,256,128]{2,1,0:T(8,128)} %get-tuple-element.6), channel_id=1, source_target_pairs={{0,1},{1,2},{2,3},{3,4},{4,5},{5,6},{6,7},{8,9},{9,10},{10,11},{11... | collective-permute-start | bytes 1572872 | tf_op jit(solution)/shard_map/ppermute | solution.py:18
  159.5 1.3 collective-permute-start.2
  161.1 1.2 collective-permute-done.6
  162.4 2.7 fusion.143
  165.0 30.8 %scatter_fusion.1 = f32[8,256,128]{2,1,0:T(8,128)S(1)} fusion(f32[8,256,128]{2,1,0:T(8,128)S(1)} %fusion.143, s32[512]{0:T(512)S(1)} %bitcast.73, f32[512]{0:T(512)S(1)} %bitcast.85), kind=kCustom, calls=%fused_computation.1 | custom fusion | flops 512 | bytes 12288 | tf_op jit(solution)/shard_map/scatter-add | solution.py:63
  195.9 17.7 %fusion.170 = (f32[8,256,128]{2,1,0:T(8,128)S(1)}, f32[8,256,128]{2,1,0:T(8,128)}) fusion(f32[8,256,128]{2,1,0:T(8,128)S(1)} %scatter_fusion.1, f32[1,8,256,128]{3,2,1,0:T(8,128)} %param.18, f32[8,256,128]{2,1,0:T(8,128)} %copy-done.5, f32[8,256,128]{2,1,0:T(8,128)S(1)} %scatter_fusion, f32[1,8,256,128]{3,2,1,0:T(8,128)} %param.19, f32[]{:T(128)} %bitcast.14, ...), kind=kLoop, calls=%fused_computation.286 | loop fusion | flops 16515072 | bytes 8913296 | tf_op jit(solution)/shard_map/add | solution.py:139
  213.7 1.2 broadcast_in_dim.35
  214.8 1.6 copy_dynamic-update-slice_fusion
  216.4 29.4 %all-to-all-start.1 = ((f32[8,320,128]{2,0,1:T(8,128)}), f32[8,320,128]{2,0,1:T(8,128)S(1)}, u32[]{:S(2)}, u32[]{:S(2)}) async-start(f32[8,320,128]{2,0,1:T(8,128)} %copy_dynamic-update-slice_fusion), calls=%async_computation.1 | async-start | bytes 2621440 | tf_op jit(solution)/shard_map/all_to_all | solution.py:144
  246.5 17.9 %all-to-all-done.1 = f32[8,320,128]{2,0,1:T(8,128)S(1)} async-done(((f32[8,320,128]{2,0,1:T(8,128)}), f32[8,320,128]{2,0,1:T(8,128)S(1)}, u32[]{:S(2)}, u32[]{:S(2)}) %all-to-all-start.1) | async-done | bytes 1310752 | tf_op jit(solution)/shard_map/all_to_all | solution.py:144
  264.4 2.4 pad_dynamic-slice_fusion
  266.8 100.2 %fusion = f32[8,5120]{1,0:T(8,128)S(1)} fusion(f32[192,5120]{1,0:T(8,128)} %pad_dynamic-slice_fusion), kind=kCustom, calls=%all-reduce-scatter | all-reduce-scatter fusion | flops 1310721 | bytes 4097024
  367.0 8.5 %collective-permute-start.14 = (f32[8,5120]{1,0:T(8,128)S(1)}, f32[8,5120]{1,0:T(8,128)S(1)}, u32[]{:S(2)}, u32[]{:S(2)}) collective-permute-start(f32[8,5120]{1,0:T(8,128)S(1)} %fusion), channel_id=1, source_target_pairs={{0,56},{8,64},{16,72},{24,80},{32,88},{40,96},{48,104},{56,112},{6... | collective-permute-start | bytes 491528
  375.5 1.9 collective-permute-start.13
  377.5 1.3 collective-permute-start.15
  378.8 1.9 collective-permute-start.12
  380.7 1.9 collective-permute-start.11
  382.6 11.1 %collective-permute-done.15 = f32[6,5120]{1,0:T(8,128)S(1)} collective-permute-done((f32[6,5120]{1,0:T(8,128)S(1)}, f32[6,5120]{1,0:T(8,128)S(1)}, u32[]{:S(2)}, u32[]{:S(2)}) %collective-permute-start.15) | collective-permute-done | bytes 122912
  393.7 1.9 collective-permute-start.10
  395.7 1.9 collective-permute-start.9
  397.6 1.9 collective-permute-start.8
  400.8 2.0 collective-permute-done.10
  402.8 3.1 collective-permute-done.9
  405.9 1.4 collective-permute-done.8
  407.3 2.1 concatenate.69
  409.5 0.7 copy.26
  (48 shorter events, 3.5 us)
Async XLA Ops:
  7.2 66.3 %all-gather.3.cloned.1.call-start = ((), (), s32[]{:S(2)}) async-start(), calls=%async_computation.2 | async-start | bytes 2703360 | tf_op jit(solution)/shard_map/all_gather | solution.py:105
  76.5 8.8 %copy-start.1 = (f32[1,8,256,128]{3,2,1,0:T(8,128)S(1)}, f32[1,8,256,128]{3,2,1,0:T(8,128)}, u32[]{:S(2)}) copy-start(f32[1,8,256,128]{3,2,1,0:T(8,128)} %param.21) | copy-start | bytes 3145732
  77.4 15.1 %copy-start.3 = (f32[1,8,256,128]{3,2,1,0:T(8,128)S(1)}, f32[1,8,256,128]{3,2,1,0:T(8,128)}, u32[]{:S(2)}) copy-start(f32[1,8,256,128]{3,2,1,0:T(8,128)} %param.19) | copy-start | bytes 3145732
  77.4 28.7 %all-to-all-start = ((bf16[64,40,128]{2,1,0:T(8,128)(2,1)}), bf16[64,40,128]{2,1,0:T(8,128)(2,1)S(1)}, u32[]{:S(2)}, u32[]{:S(2)}) async-start(bf16[64,40,128]{2,1,0:T(8,128)(2,1)} %bitcast.38), calls=%async_computation | async-start | bytes 1310720 | tf_op jit(solution)/shard_map/all_to_all | solution.py:108
  86.3 15.8 %copy-start.9 = (f32[64]{0:T(128)S(1)}, f32[64]{0:T(128)}, u32[]{:S(2)}) copy-start(f32[64]{0:T(128)} %param.17) | copy-start | bytes 772
  86.4 16.5 %copy-start.8 = (s32[1,3]{1,0:T(1,128)S(1)}, s32[1,3]{1,0:T(1,128)}, u32[]{:S(2)}) copy-start(s32[1,3]{1,0:T(1,128)} %param.14) | copy-start | bytes 40
  86.4 19.7 %copy-start.7 = (s32[1,3,512]{2,0,1:T(1,128)S(1)}, s32[1,3,512]{2,0,1:T(1,128)}, u32[]{:S(2)}) copy-start(s32[1,3,512]{2,0,1:T(1,128)} %param.15) | copy-start | bytes 18436
  86.4 20.2 %collective-permute-start.5 = (f32[4,256,128]{2,1,0:T(8,128)}, f32[4,256,128]{2,1,0:T(8,128)}, u32[]{:S(2)}, u32[]{:S(2)}) collective-permute-start(f32[4,256,128]{2,1,0:T(8,128)} %get-tuple-element.14), channel_id=1, source_target_pairs={{0,1},{1,2},{2,3},{3,4},{4,5},{5,6},{6,7},{8,9},{9,10},{10,11},{11... | collective-permute-start | bytes 1572872 | tf_op jit(solution)/shard_map/ppermute | solution.py:18
  91.2 17.3 %collective-permute-start.4 = (f32[4,256,128]{2,1,0:T(8,128)}, f32[4,256,128]{2,1,0:T(8,128)}, u32[]{:S(2)}, u32[]{:S(2)}) collective-permute-start(f32[4,256,128]{2,1,0:T(8,128)} %get-tuple-element.13), channel_id=1, source_target_pairs={{1,0},{2,1},{3,2},{4,3},{5,4},{6,5},{7,6},{9,8},{10,9},{11,10},{12... | collective-permute-start | bytes 1572872 | tf_op jit(solution)/shard_map/ppermute | solution.py:21
  93.6 54.8 %collective-permute-start.1 = (f32[4,256,128]{2,1,0:T(8,128)}, f32[4,256,128]{2,1,0:T(8,128)S(1)}, u32[]{:S(2)}, u32[]{:S(2)}) collective-permute-start(f32[4,256,128]{2,1,0:T(8,128)} %get-tuple-element.8), channel_id=1, source_target_pairs={{0,1},{1,2},{2,3},{3,4},{4,5},{5,6},{6,7},{8,9},{9,10},{10,11},{11... | collective-permute-start | bytes 1572872 | tf_op jit(solution)/shard_map/ppermute | solution.py:18
  98.2 50.3 %collective-permute-start = (f32[4,256,128]{2,1,0:T(8,128)}, f32[4,256,128]{2,1,0:T(8,128)}, u32[]{:S(2)}, u32[]{:S(2)}) collective-permute-start(f32[4,256,128]{2,1,0:T(8,128)} %get-tuple-element.7), channel_id=1, source_target_pairs={{1,0},{2,1},{3,2},{4,3},{5,4},{6,5},{7,6},{9,8},{10,9},{11,10},{12... | collective-permute-start | bytes 1572872 | tf_op jit(solution)/shard_map/ppermute | solution.py:21
  143.7 4.7 %copy-start.4 = (f32[1,8,256,128]{3,2,1,0:T(8,128)S(1)}, f32[1,8,256,128]{3,2,1,0:T(8,128)}, u32[]{:S(2)}) copy-start(f32[1,8,256,128]{3,2,1,0:T(8,128)} %param.19) | copy-start | bytes 3145732
  143.7 4.7 %copy-start.6 = (f32[1,8,256,128]{3,2,1,0:T(8,128)S(1)}, f32[1,8,256,128]{3,2,1,0:T(8,128)}, u32[]{:S(2)}) copy-start(f32[1,8,256,128]{3,2,1,0:T(8,128)} %param.18) | copy-start | bytes 3145732
  143.8 17.0 %collective-permute-start.7 = (f32[4,256,128]{2,1,0:T(8,128)S(1)}, f32[4,256,128]{2,1,0:T(8,128)S(1)}, u32[]{:S(2)}, u32[]{:S(2)}) collective-permute-start(f32[4,256,128]{2,1,0:T(8,128)S(1)} %get-tuple-element.10), channel_id=1, source_target_pairs={{0,1},{1,2},{2,3},{3,4},{4,5},{5,6},{6,7},{8,9},{9,10},{10,11},{11... | collective-permute-start | bytes 1572872 | tf_op jit(solution)/shard_map/ppermute | solution.py:18
  147.1 15.2 %collective-permute-start.6 = (f32[4,256,128]{2,1,0:T(8,128)S(1)}, f32[4,256,128]{2,1,0:T(8,128)S(1)}, u32[]{:S(2)}, u32[]{:S(2)}) collective-permute-start(f32[4,256,128]{2,1,0:T(8,128)S(1)} %get-tuple-element.9), channel_id=1, source_target_pairs={{1,0},{2,1},{3,2},{4,3},{5,4},{6,5},{7,6},{9,8},{10,9},{11,10},{12... | collective-permute-start | bytes 1572872 | tf_op jit(solution)/shard_map/ppermute | solution.py:21
  153.4 7.5 %copy-start.5 = (f32[8,256,128]{2,1,0:T(8,128)}, f32[8,256,128]{2,1,0:T(8,128)S(1)}, u32[]{:S(2)}) copy-start(f32[8,256,128]{2,1,0:T(8,128)S(1)} %fusion.65) | copy-start | bytes 3145732
  154.5 41.4 %collective-permute-start.3 = (f32[4,256,128]{2,1,0:T(8,128)}, f32[4,256,128]{2,1,0:T(8,128)S(1)}, u32[]{:S(2)}, u32[]{:S(2)}) collective-permute-start(f32[4,256,128]{2,1,0:T(8,128)} %get-tuple-element.6), channel_id=1, source_target_pairs={{0,1},{1,2},{2,3},{3,4},{4,5},{5,6},{6,7},{8,9},{9,10},{10,11},{11... | collective-permute-start | bytes 1572872 | tf_op jit(solution)/shard_map/ppermute | solution.py:18
  159.5 36.4 %collective-permute-start.2 = (f32[4,256,128]{2,1,0:T(8,128)}, f32[4,256,128]{2,1,0:T(8,128)}, u32[]{:S(2)}, u32[]{:S(2)}) collective-permute-start(f32[4,256,128]{2,1,0:T(8,128)} %get-tuple-element.5), channel_id=1, source_target_pairs={{1,0},{2,1},{3,2},{4,3},{5,4},{6,5},{7,6},{9,8},{10,9},{11,10},{12... | collective-permute-start | bytes 1572872 | tf_op jit(solution)/shard_map/ppermute | solution.py:21
  160.9 1.5 copy-start.2
  195.9 17.8 %copy-start = (f32[8,256,128]{2,1,0:T(8,128)}, f32[8,256,128]{2,1,0:T(8,128)S(1)}, u32[]{:S(2)}) copy-start(f32[8,256,128]{2,1,0:T(8,128)S(1)} %scatter_fusion.1) | copy-start | bytes 3145732
  216.4 48.0 %all-to-all-start.1 = ((f32[8,320,128]{2,0,1:T(8,128)}), f32[8,320,128]{2,0,1:T(8,128)S(1)}, u32[]{:S(2)}, u32[]{:S(2)}) async-start(f32[8,320,128]{2,0,1:T(8,128)} %copy_dynamic-update-slice_fusion), calls=%async_computation.1 | async-start | bytes 2621440 | tf_op jit(solution)/shard_map/all_to_all | solution.py:144
  266.8 132.7 %copy-start.10 = (u32[256]{0:T(256)S(1)}, u32[256]{0:T(256)}, u32[]{:S(2)}) copy-start(u32[256]{0:T(256)} %constant.146) | copy-start | bytes 3076
  367.0 28.6 %collective-permute-start.14 = (f32[8,5120]{1,0:T(8,128)S(1)}, f32[8,5120]{1,0:T(8,128)S(1)}, u32[]{:S(2)}, u32[]{:S(2)}) collective-permute-start(f32[8,5120]{1,0:T(8,128)S(1)} %fusion), channel_id=1, source_target_pairs={{0,56},{8,64},{16,72},{24,80},{32,88},{40,96},{48,104},{56,112},{6... | collective-permute-start | bytes 491528
  375.5 22.1 %collective-permute-start.13 = (f32[8,5120]{1,0:T(8,128)S(1)}, f32[8,5120]{1,0:T(8,128)S(1)}, u32[]{:S(2)}, u32[]{:S(2)}) collective-permute-start(f32[8,5120]{1,0:T(8,128)S(1)} %fusion), channel_id=1, source_target_pairs={{0,48},{8,56},{16,64},{24,72},{32,80},{40,88},{48,96},{56,104},{64... | collective-permute-start | bytes 491528
  377.5 16.3 %collective-permute-start.15 = (f32[6,5120]{1,0:T(8,128)S(1)}, f32[6,5120]{1,0:T(8,128)S(1)}, u32[]{:S(2)}, u32[]{:S(2)}) collective-permute-start(f32[6,5120]{1,0:T(8,128)S(1)} %slice.562), channel_id=1, source_target_pairs={{0,64},{8,72},{16,80},{24,88},{32,96},{40,104},{48,112},{56,120},{... | collective-permute-start | bytes 368648
  378.8 22.0 %collective-permute-start.12 = (f32[8,5120]{1,0:T(8,128)S(1)}, f32[8,5120]{1,0:T(8,128)S(1)}, u32[]{:S(2)}, u32[]{:S(2)}) collective-permute-start(f32[8,5120]{1,0:T(8,128)S(1)} %fusion), channel_id=1, source_target_pairs={{0,40},{8,48},{16,56},{24,64},{32,72},{40,80},{48,88},{56,96},{64,... | collective-permute-start | bytes 491528
  380.7 20.1 %collective-permute-start.11 = (f32[8,5120]{1,0:T(8,128)S(1)}, f32[8,5120]{1,0:T(8,128)S(1)}, u32[]{:S(2)}, u32[]{:S(2)}) collective-permute-start(f32[8,5120]{1,0:T(8,128)S(1)} %fusion), channel_id=1, source_target_pairs={{0,32},{8,40},{16,48},{24,56},{32,64},{40,72},{48,80},{56,88},{64,... | collective-permute-start | bytes 491528
  393.7 9.1 %collective-permute-start.10 = (f32[8,5120]{1,0:T(8,128)S(1)}, f32[8,5120]{1,0:T(8,128)S(1)}, u32[]{:S(2)}, u32[]{:S(2)}) collective-permute-start(f32[8,5120]{1,0:T(8,128)S(1)} %fusion), channel_id=1, source_target_pairs={{0,24},{8,32},{16,40},{24,48},{32,56},{40,64},{48,72},{56,80},{64,... | collective-permute-start | bytes 491528
  395.7 10.2 %collective-permute-start.9 = (f32[8,5120]{1,0:T(8,128)S(1)}, f32[8,5120]{1,0:T(8,128)S(1)}, u32[]{:S(2)}, u32[]{:S(2)}) collective-permute-start(f32[8,5120]{1,0:T(8,128)S(1)} %fusion), channel_id=1, source_target_pairs={{0,16},{8,24},{16,32},{24,40},{32,48},{40,56},{48,64},{56,72},{64,... | collective-permute-start | bytes 491528
  397.6 9.7 %collective-permute-start.8 = (f32[8,5120]{1,0:T(8,128)S(1)}, f32[8,5120]{1,0:T(8,128)S(1)}, u32[]{:S(2)}, u32[]{:S(2)}) collective-permute-start(f32[8,5120]{1,0:T(8,128)S(1)} %fusion), channel_id=1, source_target_pairs={{0,8},{8,16},{16,24},{24,32},{32,40},{40,48},{48,56},{56,64},{64,7... | collective-permute-start | bytes 491528
Sparse Core Ops, SparseCore 0:
  10.4 62.9 all-gather.2
where the time goes:
time: 418 us; the launch traced here: 417 us
  waiting for transfers between devices  102 us (24%)
  blocking collectives  100 us (24%)
  other arithmetic  93.1 us (22%)
  starting transfers between devices  81.5 us (19%)
  local copies, waits for them, and re-layouts  21.3 us (5%)
  between operations  19.1 us (5%)
    unnamed x1, blocking collectives  100 us
    all_gather x1, waiting for transfers between devices, body(): lax.all_gather(flat_slab, 'shot', axis=0, tiled=True)  62.6 us
    scatter-add x2, other arithmetic, receiver_term(): grid.at[local_x, shot_receivers[1], shot_receivers[2]]  61.7 us
    all_to_all x1, starting transfers between devices, body(): lax.all_to_all(frame, 'dom', split_axis=1, concat_axis=0, tiled=True)  29.4 us
    unnamed x8, starting transfers between devices  21.3 us
    all_to_all x1, waiting for transfers between devices, body(): lax.all_to_all(frame, 'dom', split_axis=1, concat_axis=0, tiled=True)  17.9 us
    add x1, other arithmetic, body(): imaged + adjoint[k + 1] * (forward[STEPS - k + 2] - 2.0 * forward[STEPS -...  17.7 us
    ppermute x4, starting transfers between devices, with_halo(): lax.ppermute(lax.slice_in_dim(block, block.shape[dim] - width, None, axis...  17.7 us
  transfers between devices with their start and end apart: 19, of which 9 were waited for; matrix products, arithmetic and copies ran while one was open for 20% of the time, Pallas kernels for 0%

commit v1 on v0

v1 whole, which is shorter than its diff:
```python
import functools

import jax
import jax.numpy as jnp
from jax import lax
from jax.experimental import pallas as pl
from jax.experimental.pallas import tpu as pltpu
from jax.sharding import PartitionSpec as P

STEPS = 2
CENTER = -205.0 / 72.0
COEFFS = (8.0 / 5.0, -1.0 / 5.0, 8.0 / 315.0, -1.0 / 560.0)

F32 = jnp.float32
BF16 = jnp.bfloat16
I16 = jnp.int16
I32 = jnp.int32

VMEM_LIMIT = 56 * 1024 * 1024
FLOOR = 1e-33
TOP = 32700.0
HALO = 4
GROUP = 32


def vmem():
    return pl.BlockSpec(memory_space=pltpu.VMEM)


def smem():
    return pl.BlockSpec(memory_space=pltpu.SMEM)


def call(kernel, outs, args, spaces, scratch=(), cost=1_000_000):
    moved = sum(a.size * a.dtype.itemsize for a in (*outs, *args))
    return pl.pallas_call(
        kernel,
        out_shape=list(outs),
        in_specs=[smem() if s == "s" else vmem() for s in spaces],
        out_specs=[vmem()] * len(outs),
        scratch_shapes=list(scratch),
        compiler_params=pltpu.CompilerParams(vmem_limit_bytes=VMEM_LIMIT),
        cost_estimate=pl.CostEstimate(flops=cost, bytes_accessed=moved, transcendentals=0),
    )(*args)


def struct(shape, dtype):
    return jax.ShapeDtypeStruct(shape, dtype)


def code_group(values):
    top = jnp.max(jnp.abs(values), axis=0, keepdims=True)
    level = jnp.ceil(jnp.log2(jnp.maximum(top, FLOOR)) * 256.0) + 1.0
    scaled = values * (TOP * jnp.exp2(level * (-1.0 / 256.0)))
    return jnp.round(scaled).astype(I32), level.astype(I32)


def code_rows(values, out_ref, base):
    band = values[0].shape[0]
    levels = []
    for n in range(0, len(values), 2):
        codes = []
        for value in values[n : n + 2]:
            code, level = code_group(value)
            codes.append(code)
            levels.append(level)
        out_ref[pl.ds(base + n * band, 2 * band), :] = jnp.concatenate(codes, axis=0).astype(I16)
    levels += [jnp.zeros((-len(levels) % 16, values[0].shape[1]), I32)]
    spot = pl.ds(base + len(values) * band, code_rows_of(len(values), band) - len(values) * band)
    out_ref[spot, :] = jnp.concatenate(levels, axis=0).astype(I16)


def code_rows_of(groups, band):
    return groups * band + groups + -groups % 16


def decode_rows(in_ref, groups, band):
    scales = decode_scale(in_ref[pl.ds(groups * band, groups + -groups % 16), :])
    for n in range(0, groups, 2):
        pair = in_ref[pl.ds(n * band, 2 * band), :].astype(I32).astype(F32)
        yield pair[:band] * scales[n : n + 1]
        yield pair[band:] * scales[n + 1 : n + 2]


def decode_scale(levels):
    return jnp.exp2(levels.astype(I32).astype(F32) * (1.0 / 256.0)) * (1.0 / TOP)


def code_halos(field, rows, out_ref, level_ref, base):
    for n, layer in enumerate(rows):
        value = field(layer)
        count = value.shape[0] // GROUP
        for g in range(count):
            code, level = code_group(value[g * GROUP : (g + 1) * GROUP])
            spot = base + n * count + g
            out_ref[pl.ds(spot * GROUP, GROUP), :] = code.astype(I16)
            level_ref[pl.ds(spot, 1), :] = level


def halo_rows(layers, count_y):
    groups = layers * count_y // GROUP
    return groups * GROUP + groups


def encode_kernel(now_f, now_a, low_ref, high_ref, level_ref):
    count_y = now_f.shape[1]
    per = HALO * count_y // GROUP
    for out_ref, first in ((low_ref, 0), (high_ref, now_f.shape[0] - HALO)):
        for f, ref in enumerate((now_f, now_a)):
            code_halos(lambda x: ref[x], range(first, first + HALO), out_ref, level_ref, f * per)
        out_ref[2 * per * GROUP :, :] = level_ref[...].astype(I16)


def decode_halo(in_ref, scale_ref, pad_ref, f, first, count_y):
    per = count_y // GROUP
    for layer in range(HALO):
        for g in range(per):
            spot = (f * HALO + layer) * per + g
            code = in_ref[pl.ds(spot * GROUP, GROUP), :].astype(I32).astype(F32)
            pad_ref[first + layer, pl.ds(PAD + g * GROUP, GROUP), :] = code * scale_ref[pl.ds(spot, 1), :]


PAD = 8


def laplace_tile(pad_ref, layer, y, rows, masks):
    middle = pad_ref[layer, pl.ds(PAD + y, rows), :]
    summed = (3.0 * CENTER) * middle
    for k in range(1, HALO + 1):
        up, down = masks[k - 1]
        count = middle.shape[1]
        part = pad_ref[layer + k, pl.ds(PAD + y, rows), :] + pad_ref[layer - k, pl.ds(PAD + y, rows), :]
        part += pad_ref[layer, pl.ds(PAD + y + k, rows), :] + pad_ref[layer, pl.ds(PAD + y - k, rows), :]
        part += jnp.where(up, pltpu.roll(middle, k, 1), 0.0)
        part += jnp.where(down, pltpu.roll(middle, count - k, 1), 0.0)
        summed += COEFFS[k - 1] * part
    return middle, summed


TILE = 32


def lane_masks(rows, count):
    lane = lax.broadcasted_iota(I32, (rows, count), 1)
    return [(lane >= k, lane < count - k) for k in range(1, HALO + 1)]


def fill(pad_ref, field_ref, low_ref, high_ref, scales, f):
    row_count, count_y = field_ref.shape[0], field_ref.shape[1]
    pad_ref[:, 0:PAD, :] = jnp.zeros((pad_ref.shape[0], PAD, pad_ref.shape[2]), F32)
    pad_ref[:, PAD + count_y :, :] = jnp.zeros((pad_ref.shape[0], PAD, pad_ref.shape[2]), F32)
    for x in range(row_count):
        pad_ref[HALO + x, PAD : PAD + count_y, :] = field_ref[x]
    decode_halo(low_ref, scales[0], pad_ref, f, 0, count_y)
    decode_halo(high_ref, scales[1], pad_ref, f, HALO + row_count, count_y)


def load_scales(in_ref, scale_ref):
    groups = scale_ref.shape[0]
    scale_ref[...] = decode_scale(in_ref[groups * GROUP :, :])


def add_source(source, start, wave, ref, k):
    x = source[0, 0] - lax.axis_index("dom") * ref.shape[0]
    lane = lax.broadcasted_iota(I32, (1, ref.shape[2]), 1)

    @pl.when((x >= 0) & (x < ref.shape[0]))
    def _():
        y = source[0, 1]
        row = ref[x, pl.ds(y, 1), :]
        ref[x, pl.ds(y, 1), :] = row + jnp.where(lane == source[0, 2], wave[start[0] + k], 0.0)


def first_kernel(groups, anchors, source, begin, wave, now_f, now_a, prev_f, prev_a, low, high, hit, *rest):
    pieces, rest = rest[:groups], rest[groups:]
    next_f, next_a, courant, send_low, send_high, slab, pad, scale_low, scale_high, level = rest
    row_count, count_y, count_z = now_f.shape
    band = pieces[0].shape[0] // row_count
    me = lax.axis_index("dom")
    for k in range(groups):
        start = pl.multiple_of(lax.rem(me + groups - k, groups) * band, 8)
        for x in range(0, row_count, 2):
            speed = pieces[k][pl.ds(x * band, 2 * band), :].astype(F32)
            slab[x, pl.ds(start, band), :] = jnp.square(speed[:band])
            slab[x + 1, pl.ds(start, band), :] = jnp.square(speed[band:])
    masks = lane_masks(TILE, count_z)
    load_scales(low, scale_low)
    load_scales(high, scale_high)
    for f, (now, prev, out) in enumerate(((now_f, prev_f, next_f), (now_a, prev_a, next_a))):
        fill(pad, now, low, high, (scale_low, scale_high), f)

        @pl.loop(0, row_count)
        def _(x):
            for y in range(0, count_y, TILE):
                if f == 0:
                    factor = slab[x, pl.ds(anchors[0, 1] + y, TILE), :]
                    courant[x, pl.ds(y, TILE), :] = factor
                else:
                    factor = courant[x, pl.ds(y, TILE), :]
                middle, summed = laplace_tile(pad, HALO + x, y, TILE, masks)
                value = 2.0 * middle - prev[x, pl.ds(y, TILE), :] + factor * summed
                if f == 1:
                    value += hit[x, pl.ds(y, TILE), :]
                out[x, pl.ds(y, TILE), :] = value

        if f == 0:
            add_source(source, begin, wave, out, 0)
    per = HALO * count_y // GROUP
    for out_ref, first in ((send_low, 0), (send_high, row_count - HALO)):
        for f, ref in enumerate((next_f, next_a)):
            code_halos(lambda x: ref[x], range(first, first + HALO), out_ref, level, f * per)
        out_ref[2 * per * GROUP :, :] = level[...].astype(I16)


def second_kernel(groups, anchors, source, begin, wave, p1, q1, p0, q0, prev_f, courant, low, high, hit, *rest):
    next_f, next_a, own = rest[:3]
    sends = rest[3 : 2 + groups]
    frame, pad, pad_a, scale_low, scale_high = rest[2 + groups :]
    row_count, count_y, count_z = p1.shape
    band = own.shape[0] // row_count
    masks = lane_masks(TILE, count_z)
    load_scales(low, scale_low)
    load_scales(high, scale_high)
    fill(pad, p1, low, high, (scale_low, scale_high), 0)
    fill(pad_a, q1, low, high, (scale_low, scale_high), 1)
    edge = (frame.shape[1] - count_y) // 2
    frame[:, 0:edge, :] = jnp.zeros((row_count, edge, count_z), F32)
    frame[:, edge + count_y :, :] = jnp.zeros((row_count, edge, count_z), F32)

    @pl.loop(0, row_count)
    def _(x):
        for y in range(0, count_y, TILE):
            spot = pl.ds(y, TILE)
            middle, summed = laplace_tile(pad, HALO + x, y, TILE, masks)
            before = p0[x, spot, :]
            next_f[x, spot, :] = 2.0 * middle - before + courant[x, spot, :] * summed
            middle_a, summed = laplace_tile(pad_a, HALO + x, y, TILE, masks)
            last = 2.0 * middle_a - q0[x, spot, :] + courant[x, spot, :] * summed + hit[x, spot, :]
            next_a[x, spot, :] = last

    add_source(source, begin, wave, next_f, 1)

    @pl.loop(0, row_count)
    def _(x):
        for y in range(0, count_y, TILE):
            spot = pl.ds(y, TILE)
            before, middle = p0[x, spot, :], p1[x, spot, :]
            image = q1[x, spot, :] * (next_f[x, spot, :] - 2.0 * middle + before)
            image += next_a[x, spot, :] * (middle - 2.0 * before + prev_f[x, spot, :])
            frame[x, pl.ds(edge + y, TILE), :] = image

    me = lax.axis_index("dom")
    for k in range(groups):
        target = lax.rem(me + k, groups)
        start = edge - anchors[0, 1] + target * band
        values = [frame[x, pl.ds(start, band), :] for x in range(row_count)]
        if k == 0:
            for x in range(row_count):
                own[pl.ds(x * band, band), :] = values[x]
        else:
            code_rows(values, sends[k - 1], 0)


def hit_kernel(begin, cells, traces, first, second):
    row_count, count_y, count_z = first.shape
    x = cells[0:1, :] - lax.axis_index("dom") * row_count
    inside = (x >= 0) & (x < row_count)
    row = jnp.where(inside, x * count_y + cells[1:2, :], -1)
    depth = lax.broadcasted_iota(I32, (count_z, row.shape[1]), 0)
    at_depth = depth == cells[2:3, :]
    parts = []
    for k in range(STEPS):
        left = traces[pl.ds(begin[0] + (STEPS - 1 - k), 1), :]
        for _ in range(3):
            part = left.astype(BF16).astype(F32)
            parts.append(jnp.where(at_depth, part, 0.0).astype(BF16))
            left = left - part
    right = jnp.concatenate(parts, axis=0)

    @pl.loop(0, row_count)
    def _(i):
        cell = i * count_y + lax.broadcasted_iota(I32, (count_y, row.shape[1]), 0)
        left = jnp.where(cell == row, 1.0, 0.0).astype(BF16)
        got = lax.dot_general(left, right, (((1,), (1,)), ((), ())), preferred_element_type=F32)
        for k, out in enumerate((first, second)):
            base = 3 * k * count_z
            high = got[:, base : base + count_z]
            middle = got[:, base + count_z : base + 2 * count_z]
            low = got[:, base + 2 * count_z : base + 3 * count_z]
            out[i] = high + (middle + low)


SIZE_X, SIZE_Z, SIZE_C = 4, 4, 2


def place_of(shot):
    return shot // (SIZE_Z * SIZE_C), lax.rem(shot // SIZE_C, SIZE_Z), lax.rem(shot, SIZE_C)


def turn(axis, k):
    pairs = []
    for shot in range(SIZE_X * SIZE_Z * SIZE_C):
        x, z, c = shot // (SIZE_Z * SIZE_C), shot // SIZE_C % SIZE_Z, shot % SIZE_C
        x = (x + k) % SIZE_X if axis == "x" else x
        z = (z + k) % SIZE_Z if axis == "z" else z
        c = (c + k) % SIZE_C if axis == "c" else c
        pairs.append((shot, (x * SIZE_Z + z) * SIZE_C + c))
    return pairs


def pick_kernel(layout, row_count, anchors, *refs):
    count = len(layout)
    ins, outs, table = refs[:count], refs[count:-1], refs[-1]
    groups = len(outs)
    per = outs[0].shape[0] // row_count
    block = ins[0].shape[0] // len(layout[0])
    own = block // per
    x, z, c = place_of(lax.axis_index("shot"))
    me = lax.axis_index("dom")
    anchor = anchors[0, 0]
    first = anchor // own
    span = table.shape[0] // block
    for ref, owners in zip(ins, layout):
        for n, (dx, dz, dc) in enumerate(owners):
            owner = lax.rem(x + dx, SIZE_X) * SIZE_Z + lax.rem(z + dz, SIZE_Z)
            place = owner * SIZE_C + lax.rem(c + dc, SIZE_C) - first

            @pl.when((place >= 0) & (place < span))
            def _():
                start = pl.multiple_of(place * block, 8)
                table[pl.ds(start, block), :] = ref[pl.ds(n * block, block), :].astype(F32)

    offset = (anchor - first * own) * per
    for k in range(groups):
        start = pl.multiple_of(offset + lax.rem(me + k, groups) * (row_count * per), 8)
        outs[k][...] = table[pl.ds(start, row_count * per), :].astype(BF16)


def band_kernel(groups, row_count, block, anchors, own, *refs):
    got, (keep, send, table) = refs[: groups - 1], refs[groups - 1 :]
    per = own.shape[0] // row_count
    c = lax.rem(lax.axis_index("shot"), SIZE_C)
    me = lax.axis_index("dom")
    anchor = anchors[0, 0]
    first = anchor // (block // per)
    table[...] = jnp.zeros(table.shape, F32)
    offset = (anchor - first * (block // per)) * per
    for k in range(groups):
        base = offset + lax.rem(me + groups - k, groups) * (row_count * per)
        if k == 0:
            table[pl.ds(pl.multiple_of(base, 8), row_count * per), :] = own[...]
        else:
            for n, value in enumerate(decode_rows(got[k - 1], row_count, per)):
                table[pl.ds(pl.multiple_of(base + n * per, 8), per), :] = value
    mine = lax.rem(c + first, SIZE_C)
    for i in range(keep.shape[0] // block):
        for out, parity in ((keep, mine), (send, 1 - mine)):
            start = pl.multiple_of((SIZE_C * i + parity) * block, 8)
            out[pl.ds(i * block, block), :] = table[pl.ds(start, block), :]


def core_kernel(block, per, anchors, other, keep, got, own, *refs):
    sends, total = refs[:-1], refs[-1]
    x, _, c = place_of(lax.axis_index("shot"))
    total[...] = jnp.zeros(total.shape, F32)
    for ref, place in ((keep, anchors), (got, other)):
        first = place[0, 0] // (block // per)
        low = (first + lax.rem(c + first, SIZE_C)) // SIZE_C
        for i in range(ref.shape[0] // block):
            spot = pl.ds(pl.multiple_of((low + i) * block, 8), block)
            total[spot, :] += ref[pl.ds(i * block, block), :]
    size = own.shape[0]
    own[...] = total[pl.ds(pl.multiple_of(x * size, 8), size), :]
    for k, send in enumerate(sends, 1):
        start = lax.rem(x + k, SIZE_X) * size
        values = [total[pl.ds(pl.multiple_of(start + n * per, 8), per), :] for n in range(size // per)]
        code_rows(values, send, 0)


def along_x_kernel(per, mine, *refs):
    got, rest = refs[: SIZE_X - 1], refs[SIZE_X - 1 :]
    own, sends, total = rest[0], rest[1:-1], rest[-1]
    total[...] = mine[...]
    for ref in got:
        for n, value in enumerate(decode_rows(ref, total.shape[0] // per, per)):
            total[pl.ds(n * per, per), :] += value
    _, z, _ = place_of(lax.axis_index("shot"))
    size = own.shape[0]
    own[...] = total[pl.ds(pl.multiple_of(z * size, 8), size), :]
    for k, send in enumerate(sends, 1):
        start = lax.rem(z + k, SIZE_Z) * size
        values = [total[pl.ds(pl.multiple_of(start + n * per, 8), per), :] for n in range(size // per)]
        code_rows(values, send, 0)


def along_z_kernel(per, mine, *refs):
    got, out = refs[:-1], refs[-1]
    for parts in zip(range(mine.shape[0] // per), *[decode_rows(r, mine.shape[0] // per, per) for r in got]):
        n, values = parts[0], parts[1:]
        total = mine[pl.ds(n * per, per), :]
        for value in values:
            total += value
        out[pl.ds(n * per, per), :] = total


def around(groups, k):
    return [(i, (i + k) % groups) for i in range(groups)]


def body(
    velocity,
    anchors,
    start_step,
    source,
    receivers,
    traces,
    wavelet,
    fwd_prev,
    fwd_now,
    adj_prev,
    adj_now,
):
    row_count, count_y, count_z = fwd_now.shape[1:]
    groups = lax.axis_size("dom")
    own_rows, band = velocity.shape[:2]
    block = own_rows * band
    piece = row_count * band
    p0, q0, p_prev, q_prev = fwd_now[0], adj_now[0], fwd_prev[0], adj_prev[0]
    scalars = (anchors, source, start_step, wavelet)
    up = [(i, i + 1) for i in range(groups - 1)]
    down = [(b, a) for a, b in up]

    local = velocity.reshape(block, count_z)
    near = [local] + [lax.ppermute(local, "shot", turn("z", k)) for k in range(1, SIZE_Z)]
    other = lax.ppermute(anchors, "shot", turn("c", 1))

    half = halo_rows(2 * HALO, count_y)
    code = struct((half, count_z), I16)
    levels = pltpu.VMEM((2 * HALO * count_y // GROUP, count_z), I32)
    low, high = call(encode_kernel, (code, code), (p0, q0), "vv", (levels,))
    from_low = lax.ppermute(high, "dom", up)
    from_high = lax.ppermute(low, "dom", down)

    field = struct((row_count, count_y, count_z), F32)
    hits = call(hit_kernel, (field, field), (start_step, receivers[0], traces[0]), "svv")

    line = jnp.concatenate(near, axis=0)
    plane = [line] + [lax.ppermute(line, "shot", turn("x", k)) for k in range(1, SIZE_X)]
    plane += [lax.ppermute(part, "shot", turn("c", 1)) for part in plane]
    layout = [
        [(-dx % SIZE_X, -dz % SIZE_Z, dc) for dz in range(SIZE_Z)]
        for dc in range(SIZE_C)
        for dx in range(SIZE_X)
    ]
    span = -(-(row_count * groups + own_rows - 1) // own_rows)
    span += span % SIZE_C
    table = pltpu.VMEM((span * block, count_z), F32)
    pieces = call(
        functools.partial(pick_kernel, layout, row_count),
        [struct((piece, count_z), BF16)] * groups,
        (anchors, *plane),
        "s" + "v" * len(plane),
        (table,),
    )
    pieces = [pieces[0]] + [lax.ppermute(pieces[k], "dom", around(groups, k)) for k in range(1, groups)]

    padded = pltpu.VMEM((row_count + 2 * HALO, count_y + 2 * PAD, count_z), F32)
    scale = pltpu.VMEM((2 * HALO * count_y // GROUP, count_z), F32)
    slab = pltpu.VMEM((row_count, groups * band, count_z), F32)
    p1, q1, courant, low, high = call(
        functools.partial(first_kernel, groups),
        (field, field, field, code, code),
        (*scalars, p0, q0, p_prev, q_prev, from_low, from_high, hits[0], *pieces),
        "ssss" + "v" * (7 + groups),
        (slab, padded, scale, scale, levels),
    )
    from_low = lax.ppermute(high, "dom", up)
    from_high = lax.ppermute(low, "dom", down)

    edge = groups * band - count_y
    coded = struct((code_rows_of(row_count, band), count_z), I16)
    frame = pltpu.VMEM((row_count, count_y + 2 * edge, count_z), F32)
    p2, q2, own, *sends = call(
        functools.partial(second_kernel, groups),
        (field, field, struct((piece, count_z), F32), *[coded] * (groups - 1)),
        (*scalars, p1, q1, p0, q0, p_prev, courant, from_low, from_high, hits[1]),
        "ssss" + "v" * 9,
        (frame, padded, padded, scale, scale),
    )
    got = [lax.ppermute(send, "dom", around(groups, k)) for k, send in enumerate(sends, 1)]

    part = struct((span // SIZE_C * block, count_z), F32)
    keep, send = call(
        functools.partial(band_kernel, groups, row_count, block),
        (part, part),
        (anchors, own, *got),
        "s" + "v" * groups,
        (table,),
    )
    got = lax.ppermute(send, "shot", turn("c", 1))

    size = SIZE_Z * block
    coded = struct((code_rows_of(size // band, band), count_z), I16)
    total = pltpu.VMEM(((SIZE_X * SIZE_Z + 1) * block, count_z), F32)
    own, *sends = call(
        functools.partial(core_kernel, block, band),
        (struct((size, count_z), F32), *[coded] * (SIZE_X - 1)),
        (anchors, other, keep, got),
        "ssvv",
        (total,),
    )
    got = [lax.ppermute(send, "shot", turn("x", k)) for k, send in enumerate(sends, 1)]

    coded = struct((code_rows_of(own_rows, band), count_z), I16)
    own, *sends = call(
        functools.partial(along_x_kernel, band),
        (struct((block, count_z), F32), *[coded] * (SIZE_Z - 1)),
        (own, *got),
        "v" * SIZE_X,
        (pltpu.VMEM((size, count_z), F32),),
    )
    got = [lax.ppermute(send, "shot", turn("z", k)) for k, send in enumerate(sends, 1)]

    (gradient,) = call(
        functools.partial(along_z_kernel, band),
        (struct((block, count_z), F32),),
        (own, *got),
        "v" * SIZE_Z,
    )
    return (p2[None], q2[None], gradient.reshape(own_rows, band, count_z))


def solution(mesh):
    placed = (
        P("shot", "dom", None),
        P("shot", None),
        P("shot"),
        P("shot", None),
        P("shot", None, None),
        P("shot", None, None),
        P(),
        P("shot", "dom", None, None),
        P("shot", "dom", None, None),
        P("shot", "dom", None, None),
        P("shot", "dom", None, None),
    )
    return jax.shard_map(
        body,
        mesh=mesh,
        in_specs=placed,
        out_specs=(
            P("shot", "dom", None, None),
            P("shot", "dom", None, None),
            P("shot", "dom", None),
        ),
        check_vma=False,
    )
```

time: 418 us -> 192 us (0.46)
  blocking collectives: 100 us -> 0 us
  other arithmetic: 93.1 us -> 0.85 us
  waiting for transfers between devices: 102 us -> 42.7 us
  Pallas kernels: 0 us -> 43.1 us
  between operations: 19.1 us -> 1.58 us
  local copies, waits for them, and re-layouts: 21.3 us -> 6.56 us
  starting transfers between devices: 81.5 us -> 95.1 us
    unnamed x1 -> x0, blocking collectives: 100 us -> none
    ppermute x8 -> x36, starting transfers between devices: 22.8 us -> 95.1 us  [the longest x7 29.7 us: body(): lax.ppermute(pieces[k], 'dom', around(groups, k))]
    all_gather x1 -> x0, waiting for transfers between devices: 62.6 us -> none  [body(): lax.all_gather(flat_slab, 'shot', axis=0, tiled=True)]
    scatter-add x2 -> x0, other arithmetic: 61.7 us -> none  [receiver_term(): grid.at[local_x, shot_receivers[1], shot_receivers[2]]]
    pallas_call x0 -> x9, Pallas kernels: none -> 43.1 us  [call(): pl.pallas_call(kernel, out_shape=list(outs), in_specs=[smem() if s == 's'...]
    ppermute x8 -> x36, waiting for transfers between devices: 3.57 us -> 42.7 us  [the longest x3 13.6 us: body(): lax.ppermute(send, 'shot', turn('x', k))]
    all_to_all x2 -> x0, starting transfers between devices: 37.3 us -> none  [the longest x1 29.4 us: body(): lax.all_to_all(frame, 'dom', split_axis=1, concat_axis=0, tiled=True)]
    add x4 -> x0, other arithmetic: 29.6 us -> none  [the longest x1 17.7 us: body(): imaged + adjoint[k + 1] * (forward[STEPS - k + 2] - 2.0 * forward[STEPS -...]
  transfers between devices with their start and end apart: 19 -> 36, of which waited for: 9 -> 19; matrix products, arithmetic and copies ran while one was open for 20% -> 0% of each run, Pallas kernels for 0% -> 6%
where the time goes in v1:
time: 192 us; the launch traced here: 190 us
  starting transfers between devices  95.1 us (50%)
  Pallas kernels  43.1 us (22%)
  waiting for transfers between devices  42.7 us (22%)
  local copies, waits for them, and re-layouts  6.56 us (3%)
    pallas_call x9, Pallas kernels, call(): pl.pallas_call(kernel, out_shape=list(outs), in_specs=[smem() if s == 's'...  43.1 us
    ppermute x7, starting transfers between devices, body(): lax.ppermute(pieces[k], 'dom', around(groups, k))  29.7 us
    ppermute x7, starting transfers between devices, body(): lax.ppermute(send, 'dom', around(groups, k))  25.2 us
    ppermute x3, starting transfers between devices, body(): lax.ppermute(send, 'shot', turn('z', k))  18.8 us
    ppermute x3, waiting for transfers between devices, body(): lax.ppermute(send, 'shot', turn('x', k))  13.6 us
    ppermute x2, waiting for transfers between devices, body(): from_low = lax.ppermute(high, 'dom', up)  8.28 us
    unnamed x73, local copies, waits for them, and re-layouts  6.56 us
    ppermute x3, starting transfers between devices, body(): lax.ppermute(local, 'shot', turn('z', k))  6.27 us
  transfers between devices with their start and end apart: 36, of which 19 were waited for; matrix products, arithmetic and copies ran while one was open for 0% of the time, Pallas kernels for 6%

profile of v1, /device:TPU:6, one launch (start us, length us, event | category | flops | bytes accessed | tf_op | source)
XLA Modules:
  0.0 189.9 jit_solution(7920494489695286630)
XLA Ops:
  0.6 2.0 %collective-permute-start.2 = (bf16[240,128]{1,0:T(8,128)(2,1)}, bf16[240,128]{1,0:T(8,128)(2,1)S(1)}, u32[]{:S(2)}, u32[]{:S(2)}) collective-permute-start(bf16[240,128]{1,0:T(8,128)(2,1)} %bitcast.23), channel_id=1, source_target_pairs={{0,16},{8,24},{16,32},{24,40},{32,48},{40,56},{48,0},{56,8},{64,80... | collective-permute-start | bytes 184328 | tf_op jit(solution)/shard_map/ppermute | solution.py:434
  2.6 3.3 %collective-permute-start.3 = (bf16[240,128]{1,0:T(8,128)(2,1)}, bf16[240,128]{1,0:T(8,128)(2,1)S(1)}, u32[]{:S(2)}, u32[]{:S(2)}) collective-permute-start(bf16[240,128]{1,0:T(8,128)(2,1)} %bitcast.24), channel_id=1, source_target_pairs={{0,32},{8,40},{16,48},{24,56},{32,0},{40,8},{48,16},{56,24},{64,96... | collective-permute-start | bytes 184328 | tf_op jit(solution)/shard_map/ppermute | solution.py:434
  5.9 1.0 collective-permute-start.4
  6.9 1.3 collective-permute-done.2
  8.2 2.1 %collective-permute-done.3 = bf16[240,128]{1,0:T(8,128)(2,1)S(1)} collective-permute-done((bf16[240,128]{1,0:T(8,128)(2,1)}, bf16[240,128]{1,0:T(8,128)(2,1)S(1)}, u32[]{:S(2)}, u32[]{:S(2)}) %collective-permute-start.3) | collective-permute-done | bytes 61472 | tf_op jit(solution)/shard_map/ppermute | solution.py:434
  10.8 0.8 pad_maximum_fusion.refs_0_
  11.6 1.5 collective-permute-start.6
  13.1 3.2 %collective-permute-start.5 = (bf16[960,128]{1,0:T(8,128)(2,1)S(1)}, bf16[960,128]{1,0:T(8,128)(2,1)S(1)}, u32[]{:S(2)}, u32[]{:S(2)}) collective-permute-start(bf16[960,128]{1,0:T(8,128)(2,1)S(1)} %pad_maximum_fusion.refs_0_), channel_id=1, source_target_pairs={{0,64},{8,72},{16,80},{24,88},{32,96},{40,104},{48,112},{56,120},{... | collective-permute-start | bytes 737288 | tf_op jit(solution)/shard_map/ppermute | solution.py:448
  16.4 3.0 %shard_map.130 = (s16[2112,128]{1,0:T(8,128)(2,1)}, s16[2112,128]{1,0:T(8,128)(2,1)}) custom-call(f32[8,256,128]{2,1,0:T(8,128)} %bitcast.12, f32[8,256,128]{2,1,0:T(8,128)} %bitcast.15), custom_call_target="tpu_custom_call" | custom-call | flops 1000000 | bytes 3178496 | tf_op jit(solution)/shard_map/pallas_call | solution.py:36
  19.4 3.5 %collective-permute-start = (s16[2112,128]{1,0:T(8,128)(2,1)}, s16[2112,128]{1,0:T(8,128)(2,1)S(1)}, u32[]{:S(2)}, u32[]{:S(2)}) collective-permute-start(s16[2112,128]{1,0:T(8,128)(2,1)} %get-tuple-element.40), channel_id=1, source_target_pairs={{0,1},{1,2},{2,3},{3,4},{4,5},{5,6},{6,7},{8,9},{9,10},{10,11},{11... | collective-permute-start | bytes 1622024 | tf_op jit(solution)/shard_map/ppermute | solution.py:441
  22.9 1.3 collective-permute-start.1
  24.2 1.5 collective-permute-done.7.refs_3_
  26.3 0.9 collective-permute-done.10.refs_6_
  28.9 2.9 %shard_map.132 = (bf16[320,128]{1,0:T(8,128)(2,1)}, bf16[320,128]{1,0:T(8,128)(2,1)}, bf16[320,128]{1,0:T(8,128)(2,1)}, bf16[320,128]{1,0:T(8,128)(2,1)}, bf16[3...) custom-call(s32[1,2]{1,0:T(1,128)} %anchors.9, ...), custom_call_target="tpu_custom_call" | custom-call | flops 1000000 | bytes 2621448 | tf_op jit(solution)/shard_map/pallas_call | solution.py:36
  31.8 1.6 collective-permute-start.12
  33.4 5.8 %collective-permute-start.13 = (bf16[320,128]{1,0:T(8,128)(2,1)}, bf16[320,128]{1,0:T(8,128)(2,1)S(1)}, u32[]{:S(2)}, u32[]{:S(2)}) collective-permute-start(bf16[320,128]{1,0:T(8,128)(2,1)} %get-tuple-element.45), channel_id=1, source_target_pairs={{0,2},{1,3},{2,4},{3,5},{4,6},{5,7},{6,0},{7,1},{8,10},{9,11},{10,... | collective-permute-start | bytes 245768 | tf_op jit(solution)/shard_map/ppermute | solution.py:465
  39.2 6.6 %collective-permute-start.14 = (bf16[320,128]{1,0:T(8,128)(2,1)}, bf16[320,128]{1,0:T(8,128)(2,1)S(1)}, u32[]{:S(2)}, u32[]{:S(2)}) collective-permute-start(bf16[320,128]{1,0:T(8,128)(2,1)} %get-tuple-element.46), channel_id=1, source_target_pairs={{0,3},{1,4},{2,5},{3,6},{4,7},{5,0},{6,1},{7,2},{8,11},{9,12},{10,... | collective-permute-start | bytes 245768 | tf_op jit(solution)/shard_map/ppermute | solution.py:465
  45.8 3.6 %collective-permute-start.15 = (bf16[320,128]{1,0:T(8,128)(2,1)}, bf16[320,128]{1,0:T(8,128)(2,1)S(1)}, u32[]{:S(2)}, u32[]{:S(2)}) collective-permute-start(bf16[320,128]{1,0:T(8,128)(2,1)} %get-tuple-element.47), channel_id=1, source_target_pairs={{0,4},{1,5},{2,6},{3,7},{4,0},{5,1},{6,2},{7,3},{8,12},{9,13},{10,... | collective-permute-start | bytes 245768 | tf_op jit(solution)/shard_map/ppermute | solution.py:465
  49.4 2.7 %collective-permute-start.16 = (bf16[320,128]{1,0:T(8,128)(2,1)}, bf16[320,128]{1,0:T(8,128)(2,1)S(1)}, u32[]{:S(2)}, u32[]{:S(2)}) collective-permute-start(bf16[320,128]{1,0:T(8,128)(2,1)} %get-tuple-element.48), channel_id=1, source_target_pairs={{0,5},{1,6},{2,7},{3,0},{4,1},{5,2},{6,3},{7,4},{8,13},{9,14},{10,... | collective-permute-start | bytes 245768 | tf_op jit(solution)/shard_map/ppermute | solution.py:465
  52.1 7.6 %collective-permute-start.17 = (bf16[320,128]{1,0:T(8,128)(2,1)}, bf16[320,128]{1,0:T(8,128)(2,1)S(1)}, u32[]{:S(2)}, u32[]{:S(2)}) collective-permute-start(bf16[320,128]{1,0:T(8,128)(2,1)} %get-tuple-element.49), channel_id=1, source_target_pairs={{0,6},{1,7},{2,0},{3,1},{4,2},{5,3},{6,4},{7,5},{8,14},{9,15},{10,... | collective-permute-start | bytes 245768 | tf_op jit(solution)/shard_map/ppermute | solution.py:465
  59.7 1.8 collective-permute-start.18
  62.8 5.6 %shard_map.131 = (f32[8,256,128]{2,1,0:T(8,128)}, f32[8,256,128]{2,1,0:T(8,128)}) custom-call(s32[1]{0:T(128)S(6)} %copy.17.begin, s32[3,512]{1,0:T(4,128)} %bitcast.27, f32[64,512]{1,0:T(8,128)} %bitcast.21), custom_call_target="tpu_custom_call" | custom-call | flops 1000000 | bytes 2234372 | tf_op jit(solution)/shard_map/pallas_call | solution.py:36
  68.5 1.0 collective-permute-done.18.rest_7_
  70.1 10.8 %shard_map.133 = (f32[8,256,128]{2,1,0:T(8,128)}, f32[8,256,128]{2,1,0:T(8,128)}, f32[8,256,128]{2,1,0:T(8,128)}, s16[2112,128]{1,0:T(8,128)(2,1)}, s16[2112,128]{1,0:T(8,128)(2,1)}) custom-call(s32[1,2]{1,0:T(1,128)} %anchors.9, s32[1,3]{1,0:T(1,128)} %source.3, s32[1]{0:T(128)S(6)} %copy.17.begin, f32[64]{0:T(128)} %wave.3, f32[8,256,128]{2,1,0:T(8,128)} %bitcast.13, ...), custom_call_target="tpu_custom_call" | custom-call | flops 1000000 | bytes 11206936 | tf_op jit(solution)/shard_map/pallas_call | solution.py:36
  81.0 1.3 collective-permute-start.19
  82.3 1.3 collective-permute-start.20
  83.6 8.3 %collective-permute-done.19.low = s16[2112,128]{1,0:T(8,128)(2,1)S(1)} collective-permute-done((s16[2112,128]{1,0:T(8,128)(2,1)}, s16[2112,128]{1,0:T(8,128)(2,1)S(1)}, u32[]{:S(2)}, u32[]{:S(2)}) %collective-permute-start.19) | collective-permute-done | bytes 540704 | tf_op jit(solution)/shard_map/ppermute | solution.py:477
  91.9 4.0 %collective-permute-done.20.high = s16[2112,128]{1,0:T(8,128)(2,1)S(1)} collective-permute-done((s16[2112,128]{1,0:T(8,128)(2,1)}, s16[2112,128]{1,0:T(8,128)(2,1)S(1)}, u32[]{:S(2)}, u32[]{:S(2)}) %collective-permute-start.20) | collective-permute-done | bytes 540704 | tf_op jit(solution)/shard_map/ppermute | solution.py:478
  95.9 0.8 copy-done.5
  96.7 11.2 %shard_map.134 = (f32[8,256,128]{2,1,0:T(8,128)}, f32[8,256,128]{2,1,0:T(8,128)}, f32[320,128]{1,0:T(8,128)}, s16[336,128]{1,0:T(8,128)(2,1)}, s16[336,128]{1,0:...) custom-call(s32[1,2]{1,0:T(1,128)} %anchors.9, ...), custom_call_target="tpu_custom_call" | custom-call | flops 1000000 | bytes 11284760 | tf_op jit(solution)/shard_map/pallas_call | solution.py:36
  108.1 10.7 %collective-permute-start.23 = (s16[336,128]{1,0:T(8,128)(2,1)}, s16[336,128]{1,0:T(8,128)(2,1)S(1)}, u32[]{:S(2)}, u32[]{:S(2)}) collective-permute-start(s16[336,128]{1,0:T(8,128)(2,1)} %get-tuple-element.61), channel_id=1, source_target_pairs={{0,2},{1,3},{2,4},{3,5},{4,6},{5,7},{6,0},{7,1},{8,10},{9,11},{10,... | collective-permute-start | bytes 258056 | tf_op jit(solution)/shard_map/ppermute | solution.py:490
  119.1 6.6 %collective-permute-start.26 = (s16[336,128]{1,0:T(8,128)(2,1)}, s16[336,128]{1,0:T(8,128)(2,1)S(1)}, u32[]{:S(2)}, u32[]{:S(2)}) collective-permute-start(s16[336,128]{1,0:T(8,128)(2,1)} %get-tuple-element.64), channel_id=1, source_target_pairs={{0,5},{1,6},{2,7},{3,0},{4,1},{5,2},{6,3},{7,4},{8,13},{9,14},{10,... | collective-permute-start | bytes 258056 | tf_op jit(solution)/shard_map/ppermute | solution.py:490
  125.6 5.4 %collective-permute-start.27 = (s16[336,128]{1,0:T(8,128)(2,1)}, s16[336,128]{1,0:T(8,128)(2,1)S(1)}, u32[]{:S(2)}, u32[]{:S(2)}) collective-permute-start(s16[336,128]{1,0:T(8,128)(2,1)} %get-tuple-element.65), channel_id=1, source_target_pairs={{0,6},{1,7},{2,0},{3,1},{4,2},{5,3},{6,4},{7,5},{8,14},{9,15},{10,... | collective-permute-start | bytes 258056 | tf_op jit(solution)/shard_map/ppermute | solution.py:490
  131.0 2.2 %collective-permute-start.28 = (s16[336,128]{1,0:T(8,128)(2,1)}, s16[336,128]{1,0:T(8,128)(2,1)S(1)}, u32[]{:S(2)}, u32[]{:S(2)}) collective-permute-start(s16[336,128]{1,0:T(8,128)(2,1)} %get-tuple-element.66), channel_id=1, source_target_pairs={{0,7},{1,0},{2,1},{3,2},{4,3},{5,4},{6,5},{7,6},{8,15},{9,8},{10,9... | collective-permute-start | bytes 258056 | tf_op jit(solution)/shard_map/ppermute | solution.py:490
  133.4 3.0 %collective-permute-done.28.refs_6_ = s16[336,128]{1,0:T(8,128)(2,1)S(1)} collective-permute-done((s16[336,128]{1,0:T(8,128)(2,1)}, s16[336,128]{1,0:T(8,128)(2,1)S(1)}, u32[]{:S(2)}, u32[]{:S(2)}) %collective-permute-start.28) | collective-permute-done | bytes 86048 | tf_op jit(solution)/shard_map/ppermute | solution.py:490
  137.1 2.7 %shard_map.135 = (f32[1440,128]{1,0:T(8,128)}, f32[1440,128]{1,0:T(8,128)}) custom-call(s32[1,2]{1,0:T(1,128)} %anchors.9, f32[320,128]{1,0:T(8,128)} %get-tuple-element.59.own, s16[336,128]{1,0:T(8,128)(2,1)} %copy-done.16, s16[336,128]{1,0:T(8,128)(2,1)} %copy-done.17, s16[336,128]{1,0:T(8,128)(2,1)} %copy-done.18, s16[336,128]{1,0:T(8,128)(2,1)} %copy-done.19, ...), custom_call_target="tpu_custom_call" | custom-call | flops 1000000 | bytes 2240520 | tf_op jit(solution)/shard_map/pallas_call | solution.py:36
  140.4 1.5 collective-permute-done.21.other
  143.1 3.0 %shard_map.136 = (f32[960,128]{1,0:T(8,128)}, s16[992,128]{1,0:T(8,128)(2,1)}, s16[992,128]{1,0:T(8,128)(2,1)}, s16[992,128]{1,0:T(8,128)(2,1)}) custom-call(s32[1,2]{1,0:T(1,128)} %anchors.9, s32[1,2]{1,0:T(1,128)} %copy-done.35, f32[1440,128]{1,0:T(8,128)} %get-tuple-element.67.keep, f32[1440,128]{1,0:T(8,128)} %copy-done.1), custom_call_target="tpu_custom_call" | custom-call | flops 1000000 | bytes 2727952 | tf_op jit(solution)/shard_map/pallas_call | solution.py:36
  146.0 0.9 collective-permute-start.30
  147.0 1.4 collective-permute-start.32
  148.3 6.9 %collective-permute-done.30.refs_0_ = s16[992,128]{1,0:T(8,128)(2,1)S(1)} collective-permute-done((s16[992,128]{1,0:T(8,128)(2,1)}, s16[992,128]{1,0:T(8,128)(2,1)S(1)}, u32[]{:S(2)}, u32[]{:S(2)}) %collective-permute-start.30) | collective-permute-done | bytes 253984 | tf_op jit(solution)/shard_map/ppermute | solution.py:512
  155.2 2.5 %collective-permute-done.31.refs_1_ = s16[992,128]{1,0:T(8,128)(2,1)S(1)} collective-permute-done((s16[992,128]{1,0:T(8,128)(2,1)}, s16[992,128]{1,0:T(8,128)(2,1)S(1)}, u32[]{:S(2)}, u32[]{:S(2)}) %collective-permute-start.31) | collective-permute-done | bytes 253984 | tf_op jit(solution)/shard_map/ppermute | solution.py:512
  157.7 4.2 %collective-permute-done.32.refs_2_ = s16[992,128]{1,0:T(8,128)(2,1)S(1)} collective-permute-done((s16[992,128]{1,0:T(8,128)(2,1)}, s16[992,128]{1,0:T(8,128)(2,1)S(1)}, u32[]{:S(2)}, u32[]{:S(2)}) %collective-permute-start.32) | collective-permute-done | bytes 253984 | tf_op jit(solution)/shard_map/ppermute | solution.py:512
  162.6 2.3 %shard_map.137 = (f32[240,128]{1,0:T(8,128)}, s16[256,128]{1,0:T(8,128)(2,1)}, s16[256,128]{1,0:T(8,128)(2,1)}, s16[256,128]{1,0:T(8,128)(2,1)}) custom-call(f32[960,128]{1,0:T(8,128)} %get-tuple-element.69.mine, s16[992,128]{1,0:T(8,128)(2,1)} %copy-done.6, s16[992,128]{1,0:T(8,128)(2,1)} %copy-done.7, s16[992,128]{1,0:T(8,128)(2,1)} %copy-done.8), custom_call_target="tpu_custom_call" | custom-call | flops 1000000 | bytes 1572864 | tf_op jit(solution)/shard_map/pallas_call | solution.py:36
  164.9 16.4 %collective-permute-start.33 = (s16[256,128]{1,0:T(8,128)(2,1)}, s16[256,128]{1,0:T(8,128)(2,1)S(1)}, u32[]{:S(2)}, u32[]{:S(2)}) collective-permute-start(s16[256,128]{1,0:T(8,128)(2,1)} %get-tuple-element.74), channel_id=1, source_target_pairs={{0,16},{8,24},{16,32},{24,40},{32,48},{40,56},{48,0},{56,8},{64,80... | collective-permute-start | bytes 196616 | tf_op jit(solution)/shard_map/ppermute | solution.py:522
  181.3 2.4 %collective-permute-start.35 = (s16[256,128]{1,0:T(8,128)(2,1)}, s16[256,128]{1,0:T(8,128)(2,1)S(1)}, u32[]{:S(2)}, u32[]{:S(2)}) collective-permute-start(s16[256,128]{1,0:T(8,128)(2,1)} %get-tuple-element.76), channel_id=1, source_target_pairs={{0,48},{8,56},{16,0},{24,8},{32,16},{40,24},{48,32},{56,40},{64,11... | collective-permute-start | bytes 196616 | tf_op jit(solution)/shard_map/ppermute | solution.py:522
  183.8 3.8 %collective-permute-done.34.refs_1_ = s16[256,128]{1,0:T(8,128)(2,1)S(1)} collective-permute-done((s16[256,128]{1,0:T(8,128)(2,1)}, s16[256,128]{1,0:T(8,128)(2,1)S(1)}, u32[]{:S(2)}, u32[]{:S(2)}) %collective-permute-start.34) | collective-permute-done | bytes 65568 | tf_op jit(solution)/shard_map/ppermute | solution.py:522
  188.3 1.7 shard_map.138
  (107 shorter events, 8.6 us)
Async XLA Ops:
  0.6 7.6 %collective-permute-start.2 = (bf16[240,128]{1,0:T(8,128)(2,1)}, bf16[240,128]{1,0:T(8,128)(2,1)S(1)}, u32[]{:S(2)}, u32[]{:S(2)}) collective-permute-start(bf16[240,128]{1,0:T(8,128)(2,1)} %bitcast.23), channel_id=1, source_target_pairs={{0,16},{8,24},{16,32},{24,40},{32,48},{40,56},{48,0},{56,8},{64,80... | collective-permute-start | bytes 184328 | tf_op jit(solution)/shard_map/ppermute | solution.py:434
  2.6 7.7 %collective-permute-start.3 = (bf16[240,128]{1,0:T(8,128)(2,1)}, bf16[240,128]{1,0:T(8,128)(2,1)S(1)}, u32[]{:S(2)}, u32[]{:S(2)}) collective-permute-start(bf16[240,128]{1,0:T(8,128)(2,1)} %bitcast.24), channel_id=1, source_target_pairs={{0,32},{8,40},{16,48},{24,56},{32,0},{40,8},{48,16},{56,24},{64,96... | collective-permute-start | bytes 184328 | tf_op jit(solution)/shard_map/ppermute | solution.py:434
  5.9 4.9 %collective-permute-start.4 = (bf16[240,128]{1,0:T(8,128)(2,1)}, bf16[240,128]{1,0:T(8,128)(2,1)S(1)}, u32[]{:S(2)}, u32[]{:S(2)}) collective-permute-start(bf16[240,128]{1,0:T(8,128)(2,1)} %bitcast.25), channel_id=1, source_target_pairs={{0,48},{8,56},{16,0},{24,8},{32,16},{40,24},{48,32},{56,40},{64,11... | collective-permute-start | bytes 184328 | tf_op jit(solution)/shard_map/ppermute | solution.py:434
  11.6 7.8 %copy-start = (bf16[960,128]{1,0:T(8,128)(2,1)}, bf16[960,128]{1,0:T(8,128)(2,1)S(1)}, u32[]{:S(2)}) copy-start(bf16[960,128]{1,0:T(8,128)(2,1)S(1)} %pad_maximum_fusion.refs_0_) | copy-start | bytes 737284
  11.6 11.3 %collective-permute-start.6 = (bf16[960,128]{1,0:T(8,128)(2,1)S(1)}, bf16[960,128]{1,0:T(8,128)(2,1)S(1)}, u32[]{:S(2)}, u32[]{:S(2)}) collective-permute-start(bf16[960,128]{1,0:T(8,128)(2,1)S(1)} %pad_maximum_fusion.refs_0_), channel_id=1, source_target_pairs={{0,128},{8,136},{16,144},{24,152},{32,160},{40,168},{48,176},{56,1... | collective-permute-start | bytes 737288 | tf_op jit(solution)/shard_map/ppermute | solution.py:448
  13.1 12.5 %collective-permute-start.7 = (bf16[960,128]{1,0:T(8,128)(2,1)S(1)}, bf16[960,128]{1,0:T(8,128)(2,1)S(1)}, u32[]{:S(2)}, u32[]{:S(2)}) collective-permute-start(bf16[960,128]{1,0:T(8,128)(2,1)S(1)} %pad_maximum_fusion.refs_0_), channel_id=1, source_target_pairs={{0,192},{8,200},{16,208},{24,216},{32,224},{40,232},{48,240},{56,2... | collective-permute-start | bytes 737288 | tf_op jit(solution)/shard_map/ppermute | solution.py:448
  13.1 12.6 %collective-permute-start.5 = (bf16[960,128]{1,0:T(8,128)(2,1)S(1)}, bf16[960,128]{1,0:T(8,128)(2,1)S(1)}, u32[]{:S(2)}, u32[]{:S(2)}) collective-permute-start(bf16[960,128]{1,0:T(8,128)(2,1)S(1)} %pad_maximum_fusion.refs_0_), channel_id=1, source_target_pairs={{0,64},{8,72},{16,80},{24,88},{32,96},{40,104},{48,112},{56,120},{... | collective-permute-start | bytes 737288 | tf_op jit(solution)/shard_map/ppermute | solution.py:448
  16.4 9.8 %collective-permute-start.8 = (bf16[960,128]{1,0:T(8,128)(2,1)S(1)}, bf16[960,128]{1,0:T(8,128)(2,1)S(1)}, u32[]{:S(2)}, u32[]{:S(2)}) collective-permute-start(bf16[960,128]{1,0:T(8,128)(2,1)S(1)} %pad_maximum_fusion.refs_0_), channel_id=1, source_target_pairs={{0,8},{8,0},{16,24},{24,16},{32,40},{40,32},{48,56},{56,48},{64,72... | collective-permute-start | bytes 737288 | tf_op jit(solution)/shard_map/ppermute | solution.py:449
  19.4 26.4 %collective-permute-start = (s16[2112,128]{1,0:T(8,128)(2,1)}, s16[2112,128]{1,0:T(8,128)(2,1)S(1)}, u32[]{:S(2)}, u32[]{:S(2)}) collective-permute-start(s16[2112,128]{1,0:T(8,128)(2,1)} %get-tuple-element.40), channel_id=1, source_target_pairs={{0,1},{1,2},{2,3},{3,4},{4,5},{5,6},{6,7},{8,9},{9,10},{10,11},{11... | collective-permute-start | bytes 1622024 | tf_op jit(solution)/shard_map/ppermute | solution.py:441
  22.9 5.0 %copy-start.9 = (bf16[960,128]{1,0:T(8,128)(2,1)}, bf16[960,128]{1,0:T(8,128)(2,1)S(1)}, u32[]{:S(2)}) copy-start(bf16[960,128]{1,0:T(8,128)(2,1)S(1)} %collective-permute-done.6.refs_2_) | copy-start | bytes 737284
  22.9 26.5 %collective-permute-start.1 = (s16[2112,128]{1,0:T(8,128)(2,1)}, s16[2112,128]{1,0:T(8,128)(2,1)S(1)}, u32[]{:S(2)}, u32[]{:S(2)}) collective-permute-start(s16[2112,128]{1,0:T(8,128)(2,1)} %get-tuple-element.41), channel_id=1, source_target_pairs={{1,0},{2,1},{3,2},{4,3},{5,4},{6,5},{7,6},{9,8},{10,9},{11,10},{12... | collective-permute-start | bytes 1622024 | tf_op jit(solution)/shard_map/ppermute | solution.py:442
  25.7 1.5 collective-permute-start.10
  25.7 1.8 collective-permute-start.11
  26.2 1.7 collective-permute-start.9
  31.8 20.3 %collective-permute-start.12 = (bf16[320,128]{1,0:T(8,128)(2,1)}, bf16[320,128]{1,0:T(8,128)(2,1)S(1)}, u32[]{:S(2)}, u32[]{:S(2)}) collective-permute-start(bf16[320,128]{1,0:T(8,128)(2,1)} %get-tuple-element.44), channel_id=1, source_target_pairs={{0,1},{1,2},{2,3},{3,4},{4,5},{5,6},{6,7},{7,0},{8,9},{9,10},{10,1... | collective-permute-start | bytes 245768 | tf_op jit(solution)/shard_map/ppermute | solution.py:465
  33.4 28.8 %copy-start.34 = (s32[1,3,512]{2,0,1:T(1,128)S(1)}, s32[1,3,512]{2,0,1:T(1,128)}, u32[]{:S(2)}) copy-start(s32[1,3,512]{2,0,1:T(1,128)} %param.15) | copy-start | bytes 18436
  33.4 26.3 %collective-permute-start.13 = (bf16[320,128]{1,0:T(8,128)(2,1)}, bf16[320,128]{1,0:T(8,128)(2,1)S(1)}, u32[]{:S(2)}, u32[]{:S(2)}) collective-permute-start(bf16[320,128]{1,0:T(8,128)(2,1)} %get-tuple-element.45), channel_id=1, source_target_pairs={{0,2},{1,3},{2,4},{3,5},{4,6},{5,7},{6,0},{7,1},{8,10},{9,11},{10,... | collective-permute-start | bytes 245768 | tf_op jit(solution)/shard_map/ppermute | solution.py:465
  39.2 29.2 %collective-permute-start.14 = (bf16[320,128]{1,0:T(8,128)(2,1)}, bf16[320,128]{1,0:T(8,128)(2,1)S(1)}, u32[]{:S(2)}, u32[]{:S(2)}) collective-permute-start(bf16[320,128]{1,0:T(8,128)(2,1)} %get-tuple-element.46), channel_id=1, source_target_pairs={{0,3},{1,4},{2,5},{3,6},{4,7},{5,0},{6,1},{7,2},{8,11},{9,12},{10,... | collective-permute-start | bytes 245768 | tf_op jit(solution)/shard_map/ppermute | solution.py:465
  45.8 23.7 %copy-start.2 = (s16[2112,128]{1,0:T(8,128)(2,1)}, s16[2112,128]{1,0:T(8,128)(2,1)S(1)}, u32[]{:S(2)}) copy-start(s16[2112,128]{1,0:T(8,128)(2,1)S(1)} %collective-permute-done.low) | copy-start | bytes 1622020
  45.8 22.6 %collective-permute-start.15 = (bf16[320,128]{1,0:T(8,128)(2,1)}, bf16[320,128]{1,0:T(8,128)(2,1)S(1)}, u32[]{:S(2)}, u32[]{:S(2)}) collective-permute-start(bf16[320,128]{1,0:T(8,128)(2,1)} %get-tuple-element.47), channel_id=1, source_target_pairs={{0,4},{1,5},{2,6},{3,7},{4,0},{5,1},{6,2},{7,3},{8,12},{9,13},{10,... | collective-permute-start | bytes 245768 | tf_op jit(solution)/shard_map/ppermute | solution.py:465
  49.4 20.1 %copy-start.3 = (s16[2112,128]{1,0:T(8,128)(2,1)}, s16[2112,128]{1,0:T(8,128)(2,1)S(1)}, u32[]{:S(2)}) copy-start(s16[2112,128]{1,0:T(8,128)(2,1)S(1)} %collective-permute-done.1.high) | copy-start | bytes 1622020
  49.4 19.0 %collective-permute-start.16 = (bf16[320,128]{1,0:T(8,128)(2,1)}, bf16[320,128]{1,0:T(8,128)(2,1)S(1)}, u32[]{:S(2)}, u32[]{:S(2)}) collective-permute-start(bf16[320,128]{1,0:T(8,128)(2,1)} %get-tuple-element.48), channel_id=1, source_target_pairs={{0,5},{1,6},{2,7},{3,0},{4,1},{5,2},{6,3},{7,4},{8,13},{9,14},{10,... | collective-permute-start | bytes 245768 | tf_op jit(solution)/shard_map/ppermute | solution.py:465
  52.1 17.3 %copy-start.23 = (bf16[320,128]{1,0:T(8,128)(2,1)}, bf16[320,128]{1,0:T(8,128)(2,1)S(1)}, u32[]{:S(2)}) copy-start(bf16[320,128]{1,0:T(8,128)(2,1)S(1)} %collective-permute-done.12.rest_1_) | copy-start | bytes 245764
  52.1 16.3 %collective-permute-start.17 = (bf16[320,128]{1,0:T(8,128)(2,1)}, bf16[320,128]{1,0:T(8,128)(2,1)S(1)}, u32[]{:S(2)}, u32[]{:S(2)}) collective-permute-start(bf16[320,128]{1,0:T(8,128)(2,1)} %get-tuple-element.49), channel_id=1, source_target_pairs={{0,6},{1,7},{2,0},{3,1},{4,2},{5,3},{6,4},{7,5},{8,14},{9,15},{10,... | collective-permute-start | bytes 245768 | tf_op jit(solution)/shard_map/ppermute | solution.py:465
  59.7 9.8 %copy-start.24 = (bf16[320,128]{1,0:T(8,128)(2,1)}, bf16[320,128]{1,0:T(8,128)(2,1)S(1)}, u32[]{:S(2)}) copy-start(bf16[320,128]{1,0:T(8,128)(2,1)S(1)} %collective-permute-done.13.rest_2_) | copy-start | bytes 245764
  59.7 9.8 %collective-permute-start.18 = (bf16[320,128]{1,0:T(8,128)(2,1)}, bf16[320,128]{1,0:T(8,128)(2,1)S(1)}, u32[]{:S(2)}, u32[]{:S(2)}) collective-permute-start(bf16[320,128]{1,0:T(8,128)(2,1)} %get-tuple-element.50), channel_id=1, source_target_pairs={{0,7},{1,0},{2,1},{3,2},{4,3},{5,4},{6,5},{7,6},{8,15},{9,8},{10,9... | collective-permute-start | bytes 245768 | tf_op jit(solution)/shard_map/ppermute | solution.py:465
  81.0 10.9 %collective-permute-start.19 = (s16[2112,128]{1,0:T(8,128)(2,1)}, s16[2112,128]{1,0:T(8,128)(2,1)S(1)}, u32[]{:S(2)}, u32[]{:S(2)}) collective-permute-start(s16[2112,128]{1,0:T(8,128)(2,1)} %get-tuple-element.54), channel_id=1, source_target_pairs={{0,1},{1,2},{2,3},{3,4},{4,5},{5,6},{6,7},{8,9},{9,10},{10,11},{11... | collective-permute-start | bytes 1622024 | tf_op jit(solution)/shard_map/ppermute | solution.py:477
  82.3 13.6 %collective-permute-start.20 = (s16[2112,128]{1,0:T(8,128)(2,1)}, s16[2112,128]{1,0:T(8,128)(2,1)S(1)}, u32[]{:S(2)}, u32[]{:S(2)}) collective-permute-start(s16[2112,128]{1,0:T(8,128)(2,1)} %get-tuple-element.55), channel_id=1, source_target_pairs={{1,0},{2,1},{3,2},{4,3},{5,4},{6,5},{7,6},{9,8},{10,9},{11,10},{12... | collective-permute-start | bytes 1622024 | tf_op jit(solution)/shard_map/ppermute | solution.py:478
  91.9 4.0 %copy-start.4 = (s16[2112,128]{1,0:T(8,128)(2,1)}, s16[2112,128]{1,0:T(8,128)(2,1)S(1)}, u32[]{:S(2)}) copy-start(s16[2112,128]{1,0:T(8,128)(2,1)S(1)} %collective-permute-done.19.low) | copy-start | bytes 1622020
  107.9 17.7 %collective-permute-start.22 = (s16[336,128]{1,0:T(8,128)(2,1)}, s16[336,128]{1,0:T(8,128)(2,1)S(1)}, u32[]{:S(2)}, u32[]{:S(2)}) collective-permute-start(s16[336,128]{1,0:T(8,128)(2,1)} %get-tuple-element.60), channel_id=1, source_target_pairs={{0,1},{1,2},{2,3},{3,4},{4,5},{5,6},{6,7},{7,0},{8,9},{9,10},{10,1... | collective-permute-start | bytes 258056 | tf_op jit(solution)/shard_map/ppermute | solution.py:490
  108.1 22.9 %collective-permute-start.23 = (s16[336,128]{1,0:T(8,128)(2,1)}, s16[336,128]{1,0:T(8,128)(2,1)S(1)}, u32[]{:S(2)}, u32[]{:S(2)}) collective-permute-start(s16[336,128]{1,0:T(8,128)(2,1)} %get-tuple-element.61), channel_id=1, source_target_pairs={{0,2},{1,3},{2,4},{3,5},{4,6},{5,7},{6,0},{7,1},{8,10},{9,11},{10,... | collective-permute-start | bytes 258056 | tf_op jit(solution)/shard_map/ppermute | solution.py:490
  118.8 14.4 %collective-permute-start.24 = (s16[336,128]{1,0:T(8,128)(2,1)}, s16[336,128]{1,0:T(8,128)(2,1)S(1)}, u32[]{:S(2)}, u32[]{:S(2)}) collective-permute-start(s16[336,128]{1,0:T(8,128)(2,1)} %get-tuple-element.62), channel_id=1, source_target_pairs={{0,3},{1,4},{2,5},{3,6},{4,7},{5,0},{6,1},{7,2},{8,11},{9,12},{10,... | collective-permute-start | bytes 258056 | tf_op jit(solution)/shard_map/ppermute | solution.py:490
  118.9 14.3 %collective-permute-start.25 = (s16[336,128]{1,0:T(8,128)(2,1)}, s16[336,128]{1,0:T(8,128)(2,1)S(1)}, u32[]{:S(2)}, u32[]{:S(2)}) collective-permute-start(s16[336,128]{1,0:T(8,128)(2,1)} %get-tuple-element.63), channel_id=1, source_target_pairs={{0,4},{1,5},{2,6},{3,7},{4,0},{5,1},{6,2},{7,3},{8,12},{9,13},{10,... | collective-permute-start | bytes 258056 | tf_op jit(solution)/shard_map/ppermute | solution.py:490
  119.1 14.1 %collective-permute-start.26 = (s16[336,128]{1,0:T(8,128)(2,1)}, s16[336,128]{1,0:T(8,128)(2,1)S(1)}, u32[]{:S(2)}, u32[]{:S(2)}) collective-permute-start(s16[336,128]{1,0:T(8,128)(2,1)} %get-tuple-element.64), channel_id=1, source_target_pairs={{0,5},{1,6},{2,7},{3,0},{4,1},{5,2},{6,3},{7,4},{8,13},{9,14},{10,... | collective-permute-start | bytes 258056 | tf_op jit(solution)/shard_map/ppermute | solution.py:490
  125.6 10.8 %copy-start.16 = (s16[336,128]{1,0:T(8,128)(2,1)}, s16[336,128]{1,0:T(8,128)(2,1)S(1)}, u32[]{:S(2)}) copy-start(s16[336,128]{1,0:T(8,128)(2,1)S(1)} %collective-permute-done.22.refs_0_) | copy-start | bytes 258052
  125.6 7.8 %collective-permute-start.27 = (s16[336,128]{1,0:T(8,128)(2,1)}, s16[336,128]{1,0:T(8,128)(2,1)S(1)}, u32[]{:S(2)}, u32[]{:S(2)}) collective-permute-start(s16[336,128]{1,0:T(8,128)(2,1)} %get-tuple-element.65), channel_id=1, source_target_pairs={{0,6},{1,7},{2,0},{3,1},{4,2},{5,3},{6,4},{7,5},{8,14},{9,15},{10,... | collective-permute-start | bytes 258056 | tf_op jit(solution)/shard_map/ppermute | solution.py:490
  131.0 5.4 %copy-start.17 = (s16[336,128]{1,0:T(8,128)(2,1)}, s16[336,128]{1,0:T(8,128)(2,1)S(1)}, u32[]{:S(2)}) copy-start(s16[336,128]{1,0:T(8,128)(2,1)S(1)} %collective-permute-done.23.refs_1_) | copy-start | bytes 258052
  131.0 5.4 %collective-permute-start.28 = (s16[336,128]{1,0:T(8,128)(2,1)}, s16[336,128]{1,0:T(8,128)(2,1)S(1)}, u32[]{:S(2)}, u32[]{:S(2)}) collective-permute-start(s16[336,128]{1,0:T(8,128)(2,1)} %get-tuple-element.66), channel_id=1, source_target_pairs={{0,7},{1,0},{2,1},{3,2},{4,3},{5,4},{6,5},{7,6},{8,15},{9,8},{10,9... | collective-permute-start | bytes 258056 | tf_op jit(solution)/shard_map/ppermute | solution.py:490
  139.8 2.4 %collective-permute-start.29 = (f32[1440,128]{1,0:T(8,128)}, f32[1440,128]{1,0:T(8,128)S(1)}, u32[]{:S(2)}, u32[]{:S(2)}) collective-permute-start(f32[1440,128]{1,0:T(8,128)} %get-tuple-element.68), channel_id=1, source_target_pairs={{0,8},{8,0},{16,24},{24,16},{32,40},{40,32},{48,56},{56,48},{64,72... | collective-permute-start | bytes 2211848 | tf_op jit(solution)/shard_map/ppermute | solution.py:500
  140.4 1.5 collective-permute-start.21
  146.0 9.2 %collective-permute-start.30 = (s16[992,128]{1,0:T(8,128)(2,1)}, s16[992,128]{1,0:T(8,128)(2,1)S(1)}, u32[]{:S(2)}, u32[]{:S(2)}) collective-permute-start(s16[992,128]{1,0:T(8,128)(2,1)} %get-tuple-element.70), channel_id=1, source_target_pairs={{0,64},{8,72},{16,80},{24,88},{32,96},{40,104},{48,112},{56,120},{... | collective-permute-start | bytes 761864 | tf_op jit(solution)/shard_map/ppermute | solution.py:512
  146.9 10.8 %collective-permute-start.31 = (s16[992,128]{1,0:T(8,128)(2,1)}, s16[992,128]{1,0:T(8,128)(2,1)S(1)}, u32[]{:S(2)}, u32[]{:S(2)}) collective-permute-start(s16[992,128]{1,0:T(8,128)(2,1)} %get-tuple-element.71), channel_id=1, source_target_pairs={{0,128},{8,136},{16,144},{24,152},{32,160},{40,168},{48,176},{56,1... | collective-permute-start | bytes 761864 | tf_op jit(solution)/shard_map/ppermute | solution.py:512
  147.0 15.0 %collective-permute-start.32 = (s16[992,128]{1,0:T(8,128)(2,1)}, s16[992,128]{1,0:T(8,128)(2,1)S(1)}, u32[]{:S(2)}, u32[]{:S(2)}) collective-permute-start(s16[992,128]{1,0:T(8,128)(2,1)} %get-tuple-element.72), channel_id=1, source_target_pairs={{0,192},{8,200},{16,208},{24,216},{32,224},{40,232},{48,240},{56,2... | collective-permute-start | bytes 761864 | tf_op jit(solution)/shard_map/ppermute | solution.py:512
  155.2 6.7 %copy-start.6 = (s16[992,128]{1,0:T(8,128)(2,1)}, s16[992,128]{1,0:T(8,128)(2,1)S(1)}, u32[]{:S(2)}) copy-start(s16[992,128]{1,0:T(8,128)(2,1)S(1)} %collective-permute-done.30.refs_0_) | copy-start | bytes 761860
  157.7 4.3 %copy-start.7 = (s16[992,128]{1,0:T(8,128)(2,1)}, s16[992,128]{1,0:T(8,128)(2,1)S(1)}, u32[]{:S(2)}) copy-start(s16[992,128]{1,0:T(8,128)(2,1)S(1)} %collective-permute-done.31.refs_1_) | copy-start | bytes 761860
  164.9 18.9 %collective-permute-start.33 = (s16[256,128]{1,0:T(8,128)(2,1)}, s16[256,128]{1,0:T(8,128)(2,1)S(1)}, u32[]{:S(2)}, u32[]{:S(2)}) collective-permute-start(s16[256,128]{1,0:T(8,128)(2,1)} %get-tuple-element.74), channel_id=1, source_target_pairs={{0,16},{8,24},{16,32},{24,40},{32,48},{40,56},{48,0},{56,8},{64,80... | collective-permute-start | bytes 196616 | tf_op jit(solution)/shard_map/ppermute | solution.py:522
  181.3 6.3 %collective-permute-start.34 = (s16[256,128]{1,0:T(8,128)(2,1)}, s16[256,128]{1,0:T(8,128)(2,1)S(1)}, u32[]{:S(2)}, u32[]{:S(2)}) collective-permute-start(s16[256,128]{1,0:T(8,128)(2,1)} %get-tuple-element.75), channel_id=1, source_target_pairs={{0,32},{8,40},{16,48},{24,56},{32,0},{40,8},{48,16},{56,24},{64,96... | collective-permute-start | bytes 196616 | tf_op jit(solution)/shard_map/ppermute | solution.py:522
  181.3 6.3 %collective-permute-start.35 = (s16[256,128]{1,0:T(8,128)(2,1)}, s16[256,128]{1,0:T(8,128)(2,1)S(1)}, u32[]{:S(2)}, u32[]{:S(2)}) collective-permute-start(s16[256,128]{1,0:T(8,128)(2,1)} %get-tuple-element.76), channel_id=1, source_target_pairs={{0,48},{8,56},{16,0},{24,8},{32,16},{40,24},{48,32},{56,40},{64,11... | collective-permute-start | bytes 196616 | tf_op jit(solution)/shard_map/ppermute | solution.py:522
  (24 other events, 35.2 us)

commit v2 on v1

--- a/solution.py
+++ b/solution.py
@@ -16,7 +16,7 @@
 I16 = jnp.int16
 I32 = jnp.int32
 
-VMEM_LIMIT = 56 * 1024 * 1024
+VMEM_LIMIT = 32 * 1024 * 1024
 FLOOR = 1e-33
 TOP = 32700.0
 HALO = 4
@@ -40,7 +40,7 @@
         out_specs=[vmem()] * len(outs),
         scratch_shapes=list(scratch),
         compiler_params=pltpu.CompilerParams(vmem_limit_bytes=VMEM_LIMIT),
-        cost_estimate=pl.CostEstimate(flops=cost, bytes_accessed=moved, transcendentals=0),
+        cost_estimate=pl.CostEstimate(flops=0, bytes_accessed=0, transcendentals=0),
     )(*args)
 
 
@@ -145,14 +145,13 @@
     return [(lane >= k, lane < count - k) for k in range(1, HALO + 1)]
 
 
-def fill(pad_ref, field_ref, low_ref, high_ref, scales, f):
-    row_count, count_y = field_ref.shape[0], field_ref.shape[1]
-    pad_ref[:, 0:PAD, :] = jnp.zeros((pad_ref.shape[0], PAD, pad_ref.shape[2]), F32)
-    pad_ref[:, PAD + count_y :, :] = jnp.zeros((pad_ref.shape[0], PAD, pad_ref.shape[2]), F32)
+def fill(pad_ref, field_ref):
+    row_count, count_y, count_z = field_ref.shape
+    edge = jnp.zeros((pad_ref.shape[0], PAD, count_z), F32)
+    pad_ref[:, 0:PAD, :] = edge
+    pad_ref[:, PAD + count_y :, :] = edge
     for x in range(row_count):
         pad_ref[HALO + x, PAD : PAD + count_y, :] = field_ref[x]
-    decode_halo(low_ref, scales[0], pad_ref, f, 0, count_y)
-    decode_halo(high_ref, scales[1], pad_ref, f, HALO + row_count, count_y)
 
 
 def load_scales(in_ref, scale_ref):
@@ -160,51 +159,62 @@
     scale_ref[...] = decode_scale(in_ref[groups * GROUP :, :])
 
 
-def add_source(source, start, wave, ref, k):
+def add_source(source, start, wave, ref, k, edge=0):
     x = source[0, 0] - lax.axis_index("dom") * ref.shape[0]
     lane = lax.broadcasted_iota(I32, (1, ref.shape[2]), 1)
 
     @pl.when((x >= 0) & (x < ref.shape[0]))
     def _():
-        y = source[0, 1]
+        y = source[0, 1] + edge
         row = ref[x, pl.ds(y, 1), :]
         ref[x, pl.ds(y, 1), :] = row + jnp.where(lane == source[0, 2], wave[start[0] + k], 0.0)
 
 
-def first_kernel(groups, anchors, source, begin, wave, now_f, now_a, prev_f, prev_a, low, high, hit, *rest):
+def before_kernel(now_f, now_a, prev_f, prev_a, low, high, hit, *rest):
+    sum_f, sum_a, base_f, base_a, pad, scale_low, scale_high = rest
+    row_count, count_y, count_z = now_f.shape
+    masks = lane_masks(TILE, count_z)
+    load_scales(low, scale_low)
+    load_scales(high, scale_high)
+    fields = ((now_f, prev_f, sum_f, base_f), (now_a, prev_a, sum_a, base_a))
+    for f, (now, prev, total, base) in enumerate(fields):
+        fill(pad, now)
+        decode_halo(low, scale_low, pad, f, 0, count_y)
+        decode_halo(high, scale_high, pad, f, HALO + row_count, count_y)
+
+        @pl.loop(0, row_count)
+        def _(x):
+            for y in range(0, count_y, TILE):
+                spot = pl.ds(y, TILE)
+                middle, summed = laplace_tile(pad, HALO + x, y, TILE, masks)
+                total[x, spot, :] = summed
+                value = 2.0 * middle - prev[x, spot, :]
+                base[x, spot, :] = value + hit[x, spot, :] if f else value
+
+
+def first_kernel(groups, anchors, source, begin, wave, sum_f, sum_a, base_f, base_a, *rest):
     pieces, rest = rest[:groups], rest[groups:]
-    next_f, next_a, courant, send_low, send_high, slab, pad, scale_low, scale_high, level = rest
-    row_count, count_y, count_z = now_f.shape
+    next_f, next_a, courant, send_low, send_high, slab, level = rest
+    row_count, count_y, _ = sum_f.shape
     band = pieces[0].shape[0] // row_count
     me = lax.axis_index("dom")
     for k in range(groups):
-        start = pl.multiple_of(lax.rem(me + groups - k, groups) * band, 8)
+        start = pl.multiple_of((me ^ k) * band, 8)
         for x in range(0, row_count, 2):
-            speed = pieces[k][pl.ds(x * band, 2 * band), :].astype(F32)
+            speed = pieces[-k][pl.ds(x * band, 2 * band), :].astype(F32)
             slab[x, pl.ds(start, band), :] = jnp.square(speed[:band])
             slab[x + 1, pl.ds(start, band), :] = jnp.square(speed[band:])
-    masks = lane_masks(TILE, count_z)
-    load_scales(low, scale_low)
-    load_scales(high, scale_high)
-    for f, (now, prev, out) in enumerate(((now_f, prev_f, next_f), (now_a, prev_a, next_a))):
-        fill(pad, now, low, high, (scale_low, scale_high), f)
-
-        @pl.loop(0, row_count)
-        def _(x):
-            for y in range(0, count_y, TILE):
-                if f == 0:
-                    factor = slab[x, pl.ds(anchors[0, 1] + y, TILE), :]
-                    courant[x, pl.ds(y, TILE), :] = factor
-                else:
-                    factor = courant[x, pl.ds(y, TILE), :]
-                middle, summed = laplace_tile(pad, HALO + x, y, TILE, masks)
-                value = 2.0 * middle - prev[x, pl.ds(y, TILE), :] + factor * summed
-                if f == 1:
-                    value += hit[x, pl.ds(y, TILE), :]
-                out[x, pl.ds(y, TILE), :] = value
-
-        if f == 0:
-            add_source(source, begin, wave, out, 0)
+
+    @pl.loop(0, row_count)
+    def _(x):
+        for y in range(0, count_y, TILE):
+            spot = pl.ds(y, TILE)
+            factor = slab[x, pl.ds(anchors[0, 1] + y, TILE), :]
+            courant[x, spot, :] = factor
+            next_f[x, spot, :] = base_f[x, spot, :] + factor * sum_f[x, spot, :]
+            next_a[x, spot, :] = base_a[x, spot, :] + factor * sum_a[x, spot, :]
+
+    add_source(source, begin, wave, next_f, 0)
     per = HALO * count_y // GROUP
     for out_ref, first in ((send_low, 0), (send_high, row_count - HALO)):
         for f, ref in enumerate((next_f, next_a)):
@@ -212,47 +222,77 @@
         out_ref[2 * per * GROUP :, :] = level[...].astype(I16)
 
 
-def second_kernel(groups, anchors, source, begin, wave, p1, q1, p0, q0, prev_f, courant, low, high, hit, *rest):
+def between_kernel(p1, q1, p0, q0, prev_f, courant, hit, part_f, part_a, bend, pad):
+    row_count, count_y, count_z = p1.shape
+    masks = lane_masks(TILE, count_z)
+    outer = jnp.zeros((HALO, pad.shape[1], count_z), F32)
+    pad[0:HALO] = outer
+    pad[HALO + row_count :] = outer
+    for f, (now, out) in enumerate(((p1, part_f), (q1, part_a))):
+        fill(pad, now)
+
+        @pl.loop(0, row_count)
+        def _(x):
+            for y in range(0, count_y, TILE):
+                spot = pl.ds(y, TILE)
+                middle, summed = laplace_tile(pad, HALO + x, y, TILE, masks)
+                value = courant[x, spot, :] * summed
+                if f == 0:
+                    bend[x, spot, :] = middle - 2.0 * p0[x, spot, :] + prev_f[x, spot, :]
+                else:
+                    value += hit[x, spot, :] + (2.0 * middle - q0[x, spot, :])
+                out[x, spot, :] = value
+
+
+def halo_terms(in_ref, scale_ref, f, spot_y, count_y, low):
+    per = count_y // GROUP
+    rows = []
+    for layer in range(HALO):
+        spot = (f * HALO + layer) * per + spot_y // GROUP
+        code = in_ref[pl.ds(spot * GROUP, GROUP), :].astype(I32).astype(F32)
+        rows.append(code * scale_ref[pl.ds(spot, 1), :])
+    if low:
+        rows = rows[::-1]
+    return [sum(COEFFS[r + j] * rows[j] for j in range(HALO - r)) for r in range(HALO)]
+
+
+def second_kernel(groups, anchors, source, begin, wave, p1, q1, p0, courant, part_f, part_a, bend, low, high, *rest):
     next_f, next_a, own = rest[:3]
     sends = rest[3 : 2 + groups]
-    frame, pad, pad_a, scale_low, scale_high = rest[2 + groups :]
+    frame, scale_low, scale_high = rest[2 + groups :]
     row_count, count_y, count_z = p1.shape
     band = own.shape[0] // row_count
-    masks = lane_masks(TILE, count_z)
     load_scales(low, scale_low)
     load_scales(high, scale_high)
-    fill(pad, p1, low, high, (scale_low, scale_high), 0)
-    fill(pad_a, q1, low, high, (scale_low, scale_high), 1)
     edge = (frame.shape[1] - count_y) // 2
     frame[:, 0:edge, :] = jnp.zeros((row_count, edge, count_z), F32)
     frame[:, edge + count_y :, :] = jnp.zeros((row_count, edge, count_z), F32)
+    for y in range(0, count_y, GROUP):
+        spot = pl.ds(y, GROUP)
+        for ref, scale, side in ((low, scale_low, True), (high, scale_high, False)):
+            for f in range(2):
+                for r, term in enumerate(halo_terms(ref, scale, f, y, count_y, side)):
+                    x = r if side else row_count - 1 - r
+                    term = courant[x, spot, :] * term
+                    if f == 0:
+                        frame[x, pl.ds(edge + y, GROUP), :] = part_f[x, spot, :] + term
+                    else:
+                        next_a[x, spot, :] = part_a[x, spot, :] + term
+
+    add_source(source, begin, wave, frame, 1, edge)
 
     @pl.loop(0, row_count)
     def _(x):
         for y in range(0, count_y, TILE):
             spot = pl.ds(y, TILE)
-            middle, summed = laplace_tile(pad, HALO + x, y, TILE, masks)
-            before = p0[x, spot, :]
-            next_f[x, spot, :] = 2.0 * middle - before + courant[x, spot, :] * summed
-            middle_a, summed = laplace_tile(pad_a, HALO + x, y, TILE, masks)
-            last = 2.0 * middle_a - q0[x, spot, :] + courant[x, spot, :] * summed + hit[x, spot, :]
-            next_a[x, spot, :] = last
-
-    add_source(source, begin, wave, next_f, 1)
-
-    @pl.loop(0, row_count)
-    def _(x):
-        for y in range(0, count_y, TILE):
-            spot = pl.ds(y, TILE)
-            before, middle = p0[x, spot, :], p1[x, spot, :]
-            image = q1[x, spot, :] * (next_f[x, spot, :] - 2.0 * middle + before)
-            image += next_a[x, spot, :] * (middle - 2.0 * before + prev_f[x, spot, :])
+            change = frame[x, pl.ds(edge + y, TILE), :]
+            next_f[x, spot, :] = 2.0 * p1[x, spot, :] - p0[x, spot, :] + change
+            image = q1[x, spot, :] * change + next_a[x, spot, :] * bend[x, spot, :]
             frame[x, pl.ds(edge + y, TILE), :] = image
 
     me = lax.axis_index("dom")
     for k in range(groups):
-        target = lax.rem(me + k, groups)
-        start = edge - anchors[0, 1] + target * band
+        start = edge - anchors[0, 1] + (me ^ k) * band
         values = [frame[x, pl.ds(start, band), :] for x in range(row_count)]
         if k == 0:
             for x in range(row_count):
@@ -297,15 +337,9 @@
     return shot // (SIZE_Z * SIZE_C), lax.rem(shot // SIZE_C, SIZE_Z), lax.rem(shot, SIZE_C)
 
 
-def turn(axis, k):
-    pairs = []
-    for shot in range(SIZE_X * SIZE_Z * SIZE_C):
-        x, z, c = shot // (SIZE_Z * SIZE_C), shot // SIZE_C % SIZE_Z, shot % SIZE_C
-        x = (x + k) % SIZE_X if axis == "x" else x
-        z = (z + k) % SIZE_Z if axis == "z" else z
-        c = (c + k) % SIZE_C if axis == "c" else c
-        pairs.append((shot, (x * SIZE_Z + z) * SIZE_C + c))
-    return pairs
+def swap(axis, k):
+    bits = k * {"x": SIZE_Z * SIZE_C, "z": SIZE_C, "c": 1}[axis]
+    return [(shot, shot ^ bits) for shot in range(SIZE_X * SIZE_Z * SIZE_C)]
 
 
 def pick_kernel(layout, row_count, anchors, *refs):
@@ -322,8 +356,7 @@
     span = table.shape[0] // block
     for ref, owners in zip(ins, layout):
         for n, (dx, dz, dc) in enumerate(owners):
-            owner = lax.rem(x + dx, SIZE_X) * SIZE_Z + lax.rem(z + dz, SIZE_Z)
-            place = owner * SIZE_C + lax.rem(c + dc, SIZE_C) - first
+            place = ((x ^ dx) * SIZE_Z + (z ^ dz)) * SIZE_C + (c ^ dc) - first
 
             @pl.when((place >= 0) & (place < span))
             def _():
@@ -332,7 +365,7 @@
 
     offset = (anchor - first * own) * per
     for k in range(groups):
-        start = pl.multiple_of(offset + lax.rem(me + k, groups) * (row_count * per), 8)
+        start = pl.multiple_of(offset + (me ^ k) * (row_count * per), 8)
         outs[k][...] = table[pl.ds(start, row_count * per), :].astype(BF16)
 
 
@@ -346,11 +379,11 @@
     table[...] = jnp.zeros(table.shape, F32)
     offset = (anchor - first * (block // per)) * per
     for k in range(groups):
-        base = offset + lax.rem(me + groups - k, groups) * (row_count * per)
+        base = offset + (me ^ k) * (row_count * per)
         if k == 0:
             table[pl.ds(pl.multiple_of(base, 8), row_count * per), :] = own[...]
         else:
-            for n, value in enumerate(decode_rows(got[k - 1], row_count, per)):
+            for n, value in enumerate(decode_rows(got[-k], row_count, per)):
                 table[pl.ds(pl.multiple_of(base + n * per, 8), per), :] = value
     mine = lax.rem(c + first, SIZE_C)
     for i in range(keep.shape[0] // block):
@@ -372,7 +405,7 @@
     size = own.shape[0]
     own[...] = total[pl.ds(pl.multiple_of(x * size, 8), size), :]
     for k, send in enumerate(sends, 1):
-        start = lax.rem(x + k, SIZE_X) * size
+        start = (x ^ k) * size
         values = [total[pl.ds(pl.multiple_of(start + n * per, 8), per), :] for n in range(size // per)]
         code_rows(values, send, 0)
 
@@ -388,7 +421,7 @@
     size = own.shape[0]
     own[...] = total[pl.ds(pl.multiple_of(z * size, 8), size), :]
     for k, send in enumerate(sends, 1):
-        start = lax.rem(z + k, SIZE_Z) * size
+        start = (z ^ k) * size
         values = [total[pl.ds(pl.multiple_of(start + n * per, 8), per), :] for n in range(size // per)]
         code_rows(values, send, 0)
 
@@ -403,8 +436,19 @@
         out[pl.ds(n * per, per), :] = total
 
 
-def around(groups, k):
-    return [(i, (i + k) % groups) for i in range(groups)]
+def across(groups, k):
+    return [(i, i ^ k) for i in range(groups)]
+
+
+def far_first(values):
+    return sorted(values, reverse=True)
+
+
+def exchange(parts, axis, pairs):
+    got = {}
+    for k in far_first(range(1, len(parts) + 1)):
+        got[k] = lax.ppermute(parts[k - 1], axis, pairs(k))
+    return [got[k] for k in sorted(got)]
 
 
 def body(
@@ -430,9 +474,12 @@
     up = [(i, i + 1) for i in range(groups - 1)]
     down = [(b, a) for a, b in up]
 
+    along = {axis: functools.partial(swap, axis) for axis in "xzc"}
+    between = functools.partial(across, groups)
+
     local = velocity.reshape(block, count_z)
-    near = [local] + [lax.ppermute(local, "shot", turn("z", k)) for k in range(1, SIZE_Z)]
-    other = lax.ppermute(anchors, "shot", turn("c", 1))
+    other = lax.ppermute(anchors, "shot", swap("c", 1))
+    near = [local] + exchange([local] * (SIZE_Z - 1), "shot", along["z"])
 
     half = halo_rows(2 * HALO, count_y)
     code = struct((half, count_z), I16)
@@ -441,17 +488,15 @@
     from_low = lax.ppermute(high, "dom", up)
     from_high = lax.ppermute(low, "dom", down)
 
+    line = jnp.concatenate(near, axis=0)
+    line, other, low = lax.optimization_barrier((line, other, low))
     field = struct((row_count, count_y, count_z), F32)
     hits = call(hit_kernel, (field, field), (start_step, receivers[0], traces[0]), "svv")
-
-    line = jnp.concatenate(near, axis=0)
-    plane = [line] + [lax.ppermute(line, "shot", turn("x", k)) for k in range(1, SIZE_X)]
-    plane += [lax.ppermute(part, "shot", turn("c", 1)) for part in plane]
-    layout = [
-        [(-dx % SIZE_X, -dz % SIZE_Z, dc) for dz in range(SIZE_Z)]
-        for dc in range(SIZE_C)
-        for dx in range(SIZE_X)
-    ]
+    plane = [line] + exchange([line] * (SIZE_X - 1), "shot", along["x"])
+    plane = list(lax.optimization_barrier((*plane, hits[0])))[:SIZE_X]
+    plane += [lax.ppermute(part, "shot", swap("c", 1)) for part in plane]
+    *plane, from_low, from_high = lax.optimization_barrier((*plane, from_low, from_high))
+    layout = [[(dx, dz, dc) for dz in range(SIZE_Z)] for dc in range(SIZE_C) for dx in range(SIZE_X)]
     span = -(-(row_count * groups + own_rows - 1) // own_rows)
     span += span % SIZE_C
     table = pltpu.VMEM((span * block, count_z), F32)
@@ -462,20 +507,34 @@
         "s" + "v" * len(plane),
         (table,),
     )
-    pieces = [pieces[0]] + [lax.ppermute(pieces[k], "dom", around(groups, k)) for k in range(1, groups)]
+    pieces = [pieces[0]] + exchange(pieces[1:], "dom", between)[::-1]
 
     padded = pltpu.VMEM((row_count + 2 * HALO, count_y + 2 * PAD, count_z), F32)
     scale = pltpu.VMEM((2 * HALO * count_y // GROUP, count_z), F32)
     slab = pltpu.VMEM((row_count, groups * band, count_z), F32)
+    sums = call(
+        before_kernel,
+        (field,) * 4,
+        (p0, q0, p_prev, q_prev, from_low, from_high, hits[0]),
+        "v" * 7,
+        (padded, scale, scale),
+    )
     p1, q1, courant, low, high = call(
         functools.partial(first_kernel, groups),
         (field, field, field, code, code),
-        (*scalars, p0, q0, p_prev, q_prev, from_low, from_high, hits[0], *pieces),
-        "ssss" + "v" * (7 + groups),
-        (slab, padded, scale, scale, levels),
+        (*scalars, *sums, *pieces),
+        "ssss" + "v" * (4 + groups),
+        (slab, levels),
     )
     from_low = lax.ppermute(high, "dom", up)
     from_high = lax.ppermute(low, "dom", down)
+    part_f, part_a, bend = call(
+        between_kernel,
+        (field,) * 3,
+        (p1, q1, p0, q0, p_prev, courant, hits[1]),
+        "v" * 7,
+        (padded,),
+    )
 
     edge = groups * band - count_y
     coded = struct((code_rows_of(row_count, band), count_z), I16)
@@ -483,11 +542,11 @@
     p2, q2, own, *sends = call(
         functools.partial(second_kernel, groups),
         (field, field, struct((piece, count_z), F32), *[coded] * (groups - 1)),
-        (*scalars, p1, q1, p0, q0, p_prev, courant, from_low, from_high, hits[1]),
+        (*scalars, p1, q1, p0, courant, part_f, part_a, bend, from_low, from_high),
         "ssss" + "v" * 9,
-        (frame, padded, padded, scale, scale),
-    )
-    got = [lax.ppermute(send, "dom", around(groups, k)) for k, send in enumerate(sends, 1)]
+        (frame, scale, scale),
+    )
+    got = exchange(sends, "dom", between)[::-1]
 
     part = struct((span // SIZE_C * block, count_z), F32)
     keep, send = call(
@@ -497,7 +556,7 @@
         "s" + "v" * groups,
         (table,),
     )
-    got = lax.ppermute(send, "shot", turn("c", 1))
+    got = lax.ppermute(send, "shot", swap("c", 1))
 
     size = SIZE_Z * block
     coded = struct((code_rows_of(size // band, band), count_z), I16)
@@ -509,7 +568,7 @@
         "ssvv",
         (total,),
     )
-    got = [lax.ppermute(send, "shot", turn("x", k)) for k, send in enumerate(sends, 1)]
+    got = exchange(sends, "shot", along["x"])[::-1]
 
     coded = struct((code_rows_of(own_rows, band), count_z), I16)
     own, *sends = call(
@@ -519,7 +578,7 @@
         "v" * SIZE_X,
         (pltpu.VMEM((size, count_z), F32),),
     )
-    got = [lax.ppermute(send, "shot", turn("z", k)) for k, send in enumerate(sends, 1)]
+    got = exchange(sends, "shot", along["z"])[::-1]
 
     (gradient,) = call(
         functools.partial(along_z_kernel, band),

time: 192 us -> 181 us (0.943); the launches traced: 190 us -> 181 us
  Pallas kernels: 43.1 us -> 24.8 us
  starting transfers between devices: 95.1 us -> 110 us
  local copies, waits for them, and re-layouts: 6.56 us -> 3.14 us
  waiting for transfers between devices: 42.7 us -> 40.6 us
    pallas_call x9 -> x11, Pallas kernels: 43.1 us -> 24.8 us  [call(): pl.pallas_call(kernel, out_shape=list(outs), in_specs=[smem() if s == 's'...]
    ppermute x32, starting transfers between devices: 87.7 us -> 100 us  [the longest x26 99.3 us: exchange(): got[k] = lax.ppermute(parts[k - 1], axis, pairs(k))]
    ppermute x2, waiting for transfers between devices: 8.28 us -> 2.88 us  [body(): from_low = lax.ppermute(high, 'dom', up)]
    unnamed x73 -> x23, local copies, waits for them, and re-layouts: 6.56 us -> 3.14 us
    ppermute x32, waiting for transfers between devices: 30.4 us -> 33.6 us  [the longest x26 29.8 us: exchange(): got[k] = lax.ppermute(parts[k - 1], axis, pairs(k))]
    ppermute x2, starting transfers between devices: 4.81 us -> 7.02 us  [body(): from_low = lax.ppermute(high, 'dom', up)]
  transfers between devices with their start and end apart: 36 -> 36, of which waited for: 19 -> 18; matrix products, arithmetic and copies ran while one was open for 0% -> 0% of each run, Pallas kernels for 6% -> 9%
where the time goes in v2:
time: 181 us
  starting transfers between devices  110 us (61%)
  waiting for transfers between devices  40.6 us (22%)
  Pallas kernels  24.8 us (14%)
  local copies, waits for them, and re-layouts  3.14 us (2%)
    ppermute x26, starting transfers between devices, exchange(): got[k] = lax.ppermute(parts[k - 1], axis, pairs(k))  99.3 us
    ppermute x26, waiting for transfers between devices, exchange(): got[k] = lax.ppermute(parts[k - 1], axis, pairs(k))  29.8 us
    pallas_call x11, Pallas kernels, call(): pl.pallas_call(kernel, out_shape=list(outs), in_specs=[smem() if s == 's'...  24.8 us
    ppermute x2, starting transfers between devices, body(): from_low = lax.ppermute(high, 'dom', up)  7.02 us
    ppermute x2, waiting for transfers between devices, body(): from_high = lax.ppermute(low, 'dom', down)  4.15 us
  transfers between devices with their start and end apart: 36, of which 18 were waited for; matrix products, arithmetic and copies ran while one was open for 0% of the time, Pallas kernels for 9%

profile of v2, /device:TPU:6, one launch (start us, length us, event | category | flops | bytes accessed | tf_op | source)
XLA Modules:
  0.0 181.1 jit_solution(5899292472310712856)
XLA Ops:
  0.6 1.2 copy-done
  1.9 1.2 copy-done.2
  3.7 3.6 %collective-permute-start.11 = (s16[2112,128]{1,0:T(8,128)(2,1)S(1)}, s16[2112,128]{1,0:T(8,128)(2,1)S(1)}, u32[]{:S(2)}, u32[]{:S(2)}) collective-permute-start(s16[2112,128]{1,0:T(8,128)(2,1)S(1)} %get-tuple-element.70), channel_id=1, source_target_pairs={{0,1},{1,2},{2,3},{3,4},{4,5},{5,6},{6,7},{8,9},{9,10},{10,11},{11... | collective-permute-start | bytes 1622024 | tf_op jit(solution)/shard_map/ppermute | solution.py:488
  7.3 4.7 %collective-permute-start.2 = (bf16[240,128]{1,0:T(8,128)(2,1)}, bf16[240,128]{1,0:T(8,128)(2,1)S(1)}, u32[]{:S(2)}, u32[]{:S(2)}) collective-permute-start(bf16[240,128]{1,0:T(8,128)(2,1)} %bitcast.25), channel_id=1, source_target_pairs={{0,48},{8,56},{16,32},{24,40},{32,16},{40,24},{48,0},{56,8},{64,11... | collective-permute-start | bytes 184328 | tf_op jit(solution)/shard_map/ppermute | solution.py:450
  12.0 0.7 collective-permute-start
  12.7 2.4 %collective-permute-done.2 = bf16[240,128]{1,0:T(8,128)(2,1)S(1)} collective-permute-done((bf16[240,128]{1,0:T(8,128)(2,1)}, bf16[240,128]{1,0:T(8,128)(2,1)S(1)}, u32[]{:S(2)}, u32[]{:S(2)}) %collective-permute-start.2) | collective-permute-done | bytes 61472 | tf_op jit(solution)/shard_map/ppermute | solution.py:450
  15.1 1.4 collective-permute-start.12
  16.5 0.9 collective-permute-done.1
  17.6 0.9 pad_maximum_fusion.refs_0_
  19.0 2.4 %collective-permute-start.5 = (bf16[960,128]{1,0:T(8,128)(2,1)S(1)}, bf16[960,128]{1,0:T(8,128)(2,1)S(1)}, u32[]{:S(2)}, u32[]{:S(2)}) collective-permute-start(bf16[960,128]{1,0:T(8,128)(2,1)S(1)} %pad_maximum_fusion.refs_0_), channel_id=1, source_target_pairs={{0,128},{8,136},{16,144},{24,152},{32,160},{40,168},{48,176},{56,1... | collective-permute-start | bytes 737288 | tf_op jit(solution)/shard_map/ppermute | solution.py:450
  21.4 1.2 collective-permute-start.4
  23.4 3.4 %shard_map.131 = (f32[8,256,128]{2,1,0:T(8,128)S(1)}, f32[8,256,128]{2,1,0:T(8,128)S(1)}) custom-call(s32[1]{0:T(128)S(6)} %copy.17.begin, s32[3,512]{1,0:T(4,128)S(1)} %bitcast.23, f32[64,512]{1,0:T(8,128)S(1)} %bitcast.22), custom_call_target="tpu_custom_call" | custom-call | tf_op jit(solution)/shard_map/pallas_call | solution.py:36
  26.7 5.0 %collective-permute-done.6.refs_3_ = bf16[960,128]{1,0:T(8,128)(2,1)S(1)} collective-permute-done((bf16[960,128]{1,0:T(8,128)(2,1)S(1)}, bf16[960,128]{1,0:T(8,128)(2,1)S(1)}, u32[]{:S(2)}, u32[]{:S(2)}) %collective-permute-start.6) | collective-permute-done | bytes 245792 | tf_op jit(solution)/shard_map/ppermute | solution.py:450
  31.7 0.6 collective-permute-done.4.refs_1_
  34.9 1.0 shard_map.133
  35.9 8.1 %collective-permute-start.13 = (bf16[320,128]{1,0:T(8,128)(2,1)S(1)}, bf16[320,128]{1,0:T(8,128)(2,1)S(1)}, u32[]{:S(2)}, u32[]{:S(2)}) collective-permute-start(bf16[320,128]{1,0:T(8,128)(2,1)S(1)} %get-tuple-element.86), channel_id=1, source_target_pairs={{0,7},{1,6},{2,5},{3,4},{4,3},{5,2},{6,1},{7,0},{8,15},{9,14},{10,... | collective-permute-start | bytes 245768 | tf_op jit(solution)/shard_map/ppermute | solution.py:450
  44.0 0.9 collective-permute-start.14
  44.8 23.4 %collective-permute-start.15 = (bf16[320,128]{1,0:T(8,128)(2,1)S(1)}, bf16[320,128]{1,0:T(8,128)(2,1)S(1)}, u32[]{:S(2)}, u32[]{:S(2)}) collective-permute-start(bf16[320,128]{1,0:T(8,128)(2,1)S(1)} %get-tuple-element.88), channel_id=1, source_target_pairs={{0,5},{1,4},{2,7},{3,6},{4,1},{5,0},{6,3},{7,2},{8,13},{9,12},{10,... | collective-permute-start | bytes 245768 | tf_op jit(solution)/shard_map/ppermute | solution.py:450
  68.2 8.5 %collective-permute-start.17 = (bf16[320,128]{1,0:T(8,128)(2,1)S(1)}, bf16[320,128]{1,0:T(8,128)(2,1)S(1)}, u32[]{:S(2)}, u32[]{:S(2)}) collective-permute-start(bf16[320,128]{1,0:T(8,128)(2,1)S(1)} %get-tuple-element.90), channel_id=1, source_target_pairs={{0,3},{1,2},{2,1},{3,0},{4,7},{5,6},{6,5},{7,4},{8,11},{9,10},{10,... | collective-permute-start | bytes 245768 | tf_op jit(solution)/shard_map/ppermute | solution.py:450
  76.7 0.9 collective-permute-start.19
  77.6 6.1 %shard_map.132 = (f32[8,256,128]{2,1,0:T(8,128)S(1)}, f32[8,256,128]{2,1,0:T(8,128)S(1)}, f32[8,256,128]{2,1,0:T(8,128)S(1)}, f32[8,256,128]{2,1,0:T(8,128)S(1)}) custom-call(f32[8,256,128]{2,1,0:T(8,128)S(1)} %bitcast.13, f32[8,256,128]{2,1,0:T(8,128)S(1)} %bitcast.17, f32[8,256,128]{2,1,0:T(8,128)S(1)} %bitcast.19, f32[8,256,128]{2,1,0:T(8,128)S(1)} %bitcast.21, ...), custom_call_target="tpu_custom_call" | custom-call | tf_op jit(solution)/shard_map/pallas_call | solution.py:36
  83.8 0.6 copy-done.8
  84.5 1.6 shard_map.134
  86.1 3.4 %collective-permute-start.20 = (s16[2112,128]{1,0:T(8,128)(2,1)S(1)}, s16[2112,128]{1,0:T(8,128)(2,1)S(1)}, u32[]{:S(2)}, u32[]{:S(2)}) collective-permute-start(s16[2112,128]{1,0:T(8,128)(2,1)S(1)} %get-tuple-element.100), channel_id=1, source_target_pairs={{0,1},{1,2},{2,3},{3,4},{4,5},{5,6},{6,7},{8,9},{9,10},{10,11},{11... | collective-permute-start | bytes 1622024 | tf_op jit(solution)/shard_map/ppermute | solution.py:529
  89.5 1.3 collective-permute-start.21
  90.8 5.9 %shard_map.135 = (f32[8,256,128]{2,1,0:T(8,128)S(1)}, f32[8,256,128]{2,1,0:T(8,128)S(1)}, f32[8,256,128]{2,1,0:T(8,128)S(1)}) custom-call(f32[8,256,128]{2,1,0:T(8,128)S(1)} %get-tuple-element.93.p1, f32[8,256,128]{2,1,0:T(8,128)S(1)} %get-tuple-element.94.q1, f32[8,256,128]{2,1,0:T(8,128)S(1)} %bitcast.14, f32[8,256,128]{2,1,0:T(8,128)S(1)} %bitcast.18, ...), custom_call_target="tpu_custom_call" | custom-call | tf_op jit(solution)/shard_map/pallas_call | solution.py:36
  96.7 2.9 %collective-permute-done.20.low = s16[2112,128]{1,0:T(8,128)(2,1)S(1)} collective-permute-done((s16[2112,128]{1,0:T(8,128)(2,1)S(1)}, s16[2112,128]{1,0:T(8,128)(2,1)S(1)}, u32[]{:S(2)}, u32[]{:S(2)}) %collective-permute-start.20) | collective-permute-done | bytes 540704 | tf_op jit(solution)/shard_map/ppermute | solution.py:529
  99.6 4.1 %collective-permute-done.21.high = s16[2112,128]{1,0:T(8,128)(2,1)S(1)} collective-permute-done((s16[2112,128]{1,0:T(8,128)(2,1)S(1)}, s16[2112,128]{1,0:T(8,128)(2,1)S(1)}, u32[]{:S(2)}, u32[]{:S(2)}) %collective-permute-start.21) | collective-permute-done | bytes 540704 | tf_op jit(solution)/shard_map/ppermute | solution.py:530
  103.7 3.1 %shard_map.136 = (f32[8,256,128]{2,1,0:T(8,128)}, f32[8,256,128]{2,1,0:T(8,128)}, f32[320,128]{1,0:T(8,128)S(1)}, s16[336,128]{1,0:T(8,128)(2,1)S(1)}, s16[336,1...) custom-call(s32[1,2]{1,0:T(1,128)S(1)} %copy-done.7, ...), custom_call_target="tpu_custom_call" | custom-call | tf_op jit(solution)/shard_map/pallas_call | solution.py:36
  106.9 1.3 collective-permute-start.22
  108.1 6.8 %collective-permute-start.23 = (s16[336,128]{1,0:T(8,128)(2,1)S(1)}, s16[336,128]{1,0:T(8,128)(2,1)S(1)}, u32[]{:S(2)}, u32[]{:S(2)}) collective-permute-start(s16[336,128]{1,0:T(8,128)(2,1)S(1)} %get-tuple-element.107), channel_id=1, source_target_pairs={{0,6},{1,7},{2,4},{3,5},{4,2},{5,3},{6,0},{7,1},{8,14},{9,15},{10,... | collective-permute-start | bytes 258056 | tf_op jit(solution)/shard_map/ppermute | solution.py:450
  114.9 8.7 %collective-permute-start.24 = (s16[336,128]{1,0:T(8,128)(2,1)S(1)}, s16[336,128]{1,0:T(8,128)(2,1)S(1)}, u32[]{:S(2)}, u32[]{:S(2)}) collective-permute-start(s16[336,128]{1,0:T(8,128)(2,1)S(1)} %get-tuple-element.108), channel_id=1, source_target_pairs={{0,5},{1,4},{2,7},{3,6},{4,1},{5,0},{6,3},{7,2},{8,13},{9,12},{10,... | collective-permute-start | bytes 258056 | tf_op jit(solution)/shard_map/ppermute | solution.py:450
  123.7 8.6 %collective-permute-start.26 = (s16[336,128]{1,0:T(8,128)(2,1)S(1)}, s16[336,128]{1,0:T(8,128)(2,1)S(1)}, u32[]{:S(2)}, u32[]{:S(2)}) collective-permute-start(s16[336,128]{1,0:T(8,128)(2,1)S(1)} %get-tuple-element.110), channel_id=1, source_target_pairs={{0,3},{1,2},{2,1},{3,0},{4,7},{5,6},{6,5},{7,4},{8,11},{9,10},{10,... | collective-permute-start | bytes 258056 | tf_op jit(solution)/shard_map/ppermute | solution.py:450
  132.3 0.9 collective-permute-start.28
  133.1 2.1 %collective-permute-done.26.refs_4_ = s16[336,128]{1,0:T(8,128)(2,1)S(1)} collective-permute-done((s16[336,128]{1,0:T(8,128)(2,1)S(1)}, s16[336,128]{1,0:T(8,128)(2,1)S(1)}, u32[]{:S(2)}, u32[]{:S(2)}) %collective-permute-start.26) | collective-permute-done | bytes 86048 | tf_op jit(solution)/shard_map/ppermute | solution.py:450
  135.2 3.0 %collective-permute-done.27.refs_5_ = s16[336,128]{1,0:T(8,128)(2,1)S(1)} collective-permute-done((s16[336,128]{1,0:T(8,128)(2,1)S(1)}, s16[336,128]{1,0:T(8,128)(2,1)S(1)}, u32[]{:S(2)}, u32[]{:S(2)}) %collective-permute-start.27) | collective-permute-done | bytes 86048 | tf_op jit(solution)/shard_map/ppermute | solution.py:450
  138.3 0.9 shard_map.137
  139.2 2.2 %collective-permute-done.29.got = f32[1440,128]{1,0:T(8,128)S(1)} collective-permute-done((f32[1440,128]{1,0:T(8,128)S(1)}, f32[1440,128]{1,0:T(8,128)S(1)}, u32[]{:S(2)}, u32[]{:S(2)}) %collective-permute-start.29) | collective-permute-done | bytes 737312 | tf_op jit(solution)/shard_map/ppermute | solution.py:559
  141.4 1.2 shard_map.138
  143.2 2.4 %collective-permute-start.31 = (s16[992,128]{1,0:T(8,128)(2,1)S(1)}, s16[992,128]{1,0:T(8,128)(2,1)S(1)}, u32[]{:S(2)}, u32[]{:S(2)}) collective-permute-start(s16[992,128]{1,0:T(8,128)(2,1)S(1)} %get-tuple-element.117), channel_id=1, source_target_pairs={{0,128},{8,136},{16,144},{24,152},{32,160},{40,168},{48,176},{56,1... | collective-permute-start | bytes 761864 | tf_op jit(solution)/shard_map/ppermute | solution.py:450
  145.7 1.2 collective-permute-start.32
  146.8 10.7 %collective-permute-done.30.refs_0_ = s16[992,128]{1,0:T(8,128)(2,1)S(1)} collective-permute-done((s16[992,128]{1,0:T(8,128)(2,1)S(1)}, s16[992,128]{1,0:T(8,128)(2,1)S(1)}, u32[]{:S(2)}, u32[]{:S(2)}) %collective-permute-start.30) | collective-permute-done | bytes 253984 | tf_op jit(solution)/shard_map/ppermute | solution.py:450
  157.6 0.6 collective-permute-done.32.refs_2_
  158.5 2.1 %collective-permute-start.33 = (s16[256,128]{1,0:T(8,128)(2,1)S(1)}, s16[256,128]{1,0:T(8,128)(2,1)S(1)}, u32[]{:S(2)}, u32[]{:S(2)}) collective-permute-start(s16[256,128]{1,0:T(8,128)(2,1)S(1)} %get-tuple-element.120), channel_id=1, source_target_pairs={{0,48},{8,56},{16,32},{24,40},{32,16},{40,24},{48,0},{56,8},{64,11... | collective-permute-start | bytes 196616 | tf_op jit(solution)/shard_map/ppermute | solution.py:450
  160.6 15.5 %collective-permute-start.34 = (s16[256,128]{1,0:T(8,128)(2,1)S(1)}, s16[256,128]{1,0:T(8,128)(2,1)S(1)}, u32[]{:S(2)}, u32[]{:S(2)}) collective-permute-start(s16[256,128]{1,0:T(8,128)(2,1)S(1)} %get-tuple-element.121), channel_id=1, source_target_pairs={{0,32},{8,40},{16,48},{24,56},{32,0},{40,8},{48,16},{56,24},{64,96... | collective-permute-start | bytes 196616 | tf_op jit(solution)/shard_map/ppermute | solution.py:450
  176.1 3.3 %collective-permute-done.34.refs_1_ = s16[256,128]{1,0:T(8,128)(2,1)S(1)} collective-permute-done((s16[256,128]{1,0:T(8,128)(2,1)S(1)}, s16[256,128]{1,0:T(8,128)(2,1)S(1)}, u32[]{:S(2)}, u32[]{:S(2)}) %collective-permute-start.34) | collective-permute-done | bytes 65568 | tf_op jit(solution)/shard_map/ppermute | solution.py:450
  179.5 0.9 collective-permute-done.35.refs_2_
  180.4 0.7 shard_map.140
  (59 shorter events, 5.0 us)
Async XLA Ops:
  0.6 1.2 copy-start
  1.9 1.2 copy-start.2
  3.1 74.5 %copy-start.4 = (f32[1,8,256,128]{3,2,1,0:T(8,128)S(1)}, f32[1,8,256,128]{3,2,1,0:T(8,128)}, u32[]{:S(2)}) copy-start(f32[1,8,256,128]{3,2,1,0:T(8,128)} %param.18) | copy-start | bytes 3145732
  3.1 74.5 %copy-start.5 = (f32[1,8,256,128]{3,2,1,0:T(8,128)S(1)}, f32[1,8,256,128]{3,2,1,0:T(8,128)}, u32[]{:S(2)}) copy-start(f32[1,8,256,128]{3,2,1,0:T(8,128)} %param.20) | copy-start | bytes 3145732
  3.6 9.0 %copy-start.7 = (s32[1,2]{1,0:T(1,128)S(1)}, s32[1,2]{1,0:T(1,128)}, u32[]{:S(2)}) copy-start(s32[1,2]{1,0:T(1,128)} %anchors.9) | copy-start | bytes 28
  3.7 29.2 %collective-permute-start.11 = (s16[2112,128]{1,0:T(8,128)(2,1)S(1)}, s16[2112,128]{1,0:T(8,128)(2,1)S(1)}, u32[]{:S(2)}, u32[]{:S(2)}) collective-permute-start(s16[2112,128]{1,0:T(8,128)(2,1)S(1)} %get-tuple-element.70), channel_id=1, source_target_pairs={{0,1},{1,2},{2,3},{3,4},{4,5},{5,6},{6,7},{8,9},{9,10},{10,11},{11... | collective-permute-start | bytes 1622024 | tf_op jit(solution)/shard_map/ppermute | solution.py:488
  7.3 7.8 %collective-permute-start.2 = (bf16[240,128]{1,0:T(8,128)(2,1)}, bf16[240,128]{1,0:T(8,128)(2,1)S(1)}, u32[]{:S(2)}, u32[]{:S(2)}) collective-permute-start(bf16[240,128]{1,0:T(8,128)(2,1)} %bitcast.25), channel_id=1, source_target_pairs={{0,48},{8,56},{16,32},{24,40},{32,16},{40,24},{48,0},{56,8},{64,11... | collective-permute-start | bytes 184328 | tf_op jit(solution)/shard_map/ppermute | solution.py:450
  12.0 5.4 %collective-permute-start.1 = (bf16[240,128]{1,0:T(8,128)(2,1)}, bf16[240,128]{1,0:T(8,128)(2,1)S(1)}, u32[]{:S(2)}, u32[]{:S(2)}) collective-permute-start(bf16[240,128]{1,0:T(8,128)(2,1)} %bitcast.26), channel_id=1, source_target_pairs={{0,32},{8,40},{16,48},{24,56},{32,0},{40,8},{48,16},{56,24},{64,96... | collective-permute-start | bytes 184328 | tf_op jit(solution)/shard_map/ppermute | solution.py:450
  12.0 5.6 %collective-permute-start = (bf16[240,128]{1,0:T(8,128)(2,1)}, bf16[240,128]{1,0:T(8,128)(2,1)S(1)}, u32[]{:S(2)}, u32[]{:S(2)}) collective-permute-start(bf16[240,128]{1,0:T(8,128)(2,1)} %bitcast.27), channel_id=1, source_target_pairs={{0,16},{8,24},{16,0},{24,8},{32,48},{40,56},{48,32},{56,40},{64,80... | collective-permute-start | bytes 184328 | tf_op jit(solution)/shard_map/ppermute | solution.py:450
  12.7 5.8 %collective-permute-start.3 = (s32[1,2]{1,0:T(1,128)S(1)}, s32[1,2]{1,0:T(1,128)S(1)}, u32[]{:S(2)}, u32[]{:S(2)}) collective-permute-start(s32[1,2]{1,0:T(1,128)S(1)} %copy-done.7), channel_id=1, source_target_pairs={{0,8},{8,0},{16,24},{24,16},{32,40},{40,32},{48,56},{56,48},{64,72... | collective-permute-start | bytes 32 | tf_op jit(solution)/shard_map/ppermute | solution.py:481
  15.1 8.2 %copy-start.6 = (f32[1,64,512]{2,1,0:T(8,128)S(1)}, f32[1,64,512]{2,1,0:T(8,128)}, u32[]{:S(2)}) copy-start(f32[1,64,512]{2,1,0:T(8,128)} %param.16) | copy-start | bytes 393220
  15.1 18.2 %collective-permute-start.12 = (s16[2112,128]{1,0:T(8,128)(2,1)S(1)}, s16[2112,128]{1,0:T(8,128)(2,1)S(1)}, u32[]{:S(2)}, u32[]{:S(2)}) collective-permute-start(s16[2112,128]{1,0:T(8,128)(2,1)S(1)} %get-tuple-element.63), channel_id=1, source_target_pairs={{1,0},{2,1},{3,2},{4,3},{5,4},{6,5},{7,6},{9,8},{10,9},{11,10},{12... | collective-permute-start | bytes 1622024 | tf_op jit(solution)/shard_map/ppermute | solution.py:489
  17.6 5.7 %copy-start.10 = (s32[1,3,512]{2,0,1:T(1,128)S(1)}, s32[1,3,512]{2,0,1:T(1,128)}, u32[]{:S(2)}) copy-start(s32[1,3,512]{2,0,1:T(1,128)} %param.15) | copy-start | bytes 18436
  18.5 13.2 %collective-permute-start.6 = (bf16[960,128]{1,0:T(8,128)(2,1)S(1)}, bf16[960,128]{1,0:T(8,128)(2,1)S(1)}, u32[]{:S(2)}, u32[]{:S(2)}) collective-permute-start(bf16[960,128]{1,0:T(8,128)(2,1)S(1)} %pad_maximum_fusion.refs_0_), channel_id=1, source_target_pairs={{0,192},{8,200},{16,208},{24,216},{32,224},{40,232},{48,240},{56,2... | collective-permute-start | bytes 737288 | tf_op jit(solution)/shard_map/ppermute | solution.py:450
  19.0 12.7 %collective-permute-start.5 = (bf16[960,128]{1,0:T(8,128)(2,1)S(1)}, bf16[960,128]{1,0:T(8,128)(2,1)S(1)}, u32[]{:S(2)}, u32[]{:S(2)}) collective-permute-start(bf16[960,128]{1,0:T(8,128)(2,1)S(1)} %pad_maximum_fusion.refs_0_), channel_id=1, source_target_pairs={{0,128},{8,136},{16,144},{24,152},{32,160},{40,168},{48,176},{56,1... | collective-permute-start | bytes 737288 | tf_op jit(solution)/shard_map/ppermute | solution.py:450
  21.4 10.9 %collective-permute-start.4 = (bf16[960,128]{1,0:T(8,128)(2,1)S(1)}, bf16[960,128]{1,0:T(8,128)(2,1)S(1)}, u32[]{:S(2)}, u32[]{:S(2)}) collective-permute-start(bf16[960,128]{1,0:T(8,128)(2,1)S(1)} %pad_maximum_fusion.refs_0_), channel_id=1, source_target_pairs={{0,64},{8,72},{16,80},{24,88},{32,96},{40,104},{48,112},{56,120},{... | collective-permute-start | bytes 737288 | tf_op jit(solution)/shard_map/ppermute | solution.py:450
  23.3 54.3 %copy-start.1 = (f32[1,8,256,128]{3,2,1,0:T(8,128)S(1)}, f32[1,8,256,128]{3,2,1,0:T(8,128)}, u32[]{:S(2)}) copy-start(f32[1,8,256,128]{3,2,1,0:T(8,128)} %param.19) | copy-start | bytes 3145732
  23.3 54.2 %copy-start.3 = (f32[1,8,256,128]{3,2,1,0:T(8,128)S(1)}, f32[1,8,256,128]{3,2,1,0:T(8,128)}, u32[]{:S(2)}) copy-start(f32[1,8,256,128]{3,2,1,0:T(8,128)} %param.21) | copy-start | bytes 3145732
  32.3 1.5 collective-permute-start.7
  32.3 1.9 %collective-permute-start.8 = (bf16[960,128]{1,0:T(8,128)(2,1)S(1)}, bf16[960,128]{1,0:T(8,128)(2,1)S(1)}, u32[]{:S(2)}, u32[]{:S(2)}) collective-permute-start(bf16[960,128]{1,0:T(8,128)(2,1)S(1)} %collective-permute-done.4.refs_1_), channel_id=1, source_target_pairs={{0,8},{8,0},{16,24},{24,16},{32,40},{40,32},{48,56},{56,48},{64,72... | collective-permute-start | bytes 737288 | tf_op jit(solution)/shard_map/ppermute | solution.py:497
  32.8 1.7 collective-permute-start.9
  32.8 2.0 %collective-permute-start.10 = (bf16[960,128]{1,0:T(8,128)(2,1)S(1)}, bf16[960,128]{1,0:T(8,128)(2,1)S(1)}, u32[]{:S(2)}, u32[]{:S(2)}) collective-permute-start(bf16[960,128]{1,0:T(8,128)(2,1)S(1)} %collective-permute-done.6.refs_3_), channel_id=1, source_target_pairs={{0,8},{8,0},{16,24},{24,16},{32,40},{40,32},{48,56},{56,48},{64,72... | collective-permute-start | bytes 737288 | tf_op jit(solution)/shard_map/ppermute | solution.py:497
  35.9 40.8 %collective-permute-start.13 = (bf16[320,128]{1,0:T(8,128)(2,1)S(1)}, bf16[320,128]{1,0:T(8,128)(2,1)S(1)}, u32[]{:S(2)}, u32[]{:S(2)}) collective-permute-start(bf16[320,128]{1,0:T(8,128)(2,1)S(1)} %get-tuple-element.86), channel_id=1, source_target_pairs={{0,7},{1,6},{2,5},{3,4},{4,3},{5,2},{6,1},{7,0},{8,15},{9,14},{10,... | collective-permute-start | bytes 245768 | tf_op jit(solution)/shard_map/ppermute | solution.py:450
  44.0 32.7 %collective-permute-start.14 = (bf16[320,128]{1,0:T(8,128)(2,1)S(1)}, bf16[320,128]{1,0:T(8,128)(2,1)S(1)}, u32[]{:S(2)}, u32[]{:S(2)}) collective-permute-start(bf16[320,128]{1,0:T(8,128)(2,1)S(1)} %get-tuple-element.87), channel_id=1, source_target_pairs={{0,6},{1,7},{2,4},{3,5},{4,2},{5,3},{6,0},{7,1},{8,14},{9,15},{10,... | collective-permute-start | bytes 245768 | tf_op jit(solution)/shard_map/ppermute | solution.py:450
  44.8 38.9 %collective-permute-start.15 = (bf16[320,128]{1,0:T(8,128)(2,1)S(1)}, bf16[320,128]{1,0:T(8,128)(2,1)S(1)}, u32[]{:S(2)}, u32[]{:S(2)}) collective-permute-start(bf16[320,128]{1,0:T(8,128)(2,1)S(1)} %get-tuple-element.88), channel_id=1, source_target_pairs={{0,5},{1,4},{2,7},{3,6},{4,1},{5,0},{6,3},{7,2},{8,13},{9,12},{10,... | collective-permute-start | bytes 245768 | tf_op jit(solution)/shard_map/ppermute | solution.py:450
  68.2 15.6 %collective-permute-start.16 = (bf16[320,128]{1,0:T(8,128)(2,1)S(1)}, bf16[320,128]{1,0:T(8,128)(2,1)S(1)}, u32[]{:S(2)}, u32[]{:S(2)}) collective-permute-start(bf16[320,128]{1,0:T(8,128)(2,1)S(1)} %get-tuple-element.89), channel_id=1, source_target_pairs={{0,4},{1,5},{2,6},{3,7},{4,0},{5,1},{6,2},{7,3},{8,12},{9,13},{10,... | collective-permute-start | bytes 245768 | tf_op jit(solution)/shard_map/ppermute | solution.py:450
  68.2 15.6 %collective-permute-start.17 = (bf16[320,128]{1,0:T(8,128)(2,1)S(1)}, bf16[320,128]{1,0:T(8,128)(2,1)S(1)}, u32[]{:S(2)}, u32[]{:S(2)}) collective-permute-start(bf16[320,128]{1,0:T(8,128)(2,1)S(1)} %get-tuple-element.90), channel_id=1, source_target_pairs={{0,3},{1,2},{2,1},{3,0},{4,7},{5,6},{6,5},{7,4},{8,11},{9,10},{10,... | collective-permute-start | bytes 245768 | tf_op jit(solution)/shard_map/ppermute | solution.py:450
  76.7 7.1 %collective-permute-start.18 = (bf16[320,128]{1,0:T(8,128)(2,1)S(1)}, bf16[320,128]{1,0:T(8,128)(2,1)S(1)}, u32[]{:S(2)}, u32[]{:S(2)}) collective-permute-start(bf16[320,128]{1,0:T(8,128)(2,1)S(1)} %get-tuple-element.91), channel_id=1, source_target_pairs={{0,2},{1,3},{2,0},{3,1},{4,6},{5,7},{6,4},{7,5},{8,10},{9,11},{10,... | collective-permute-start | bytes 245768 | tf_op jit(solution)/shard_map/ppermute | solution.py:450
  76.7 7.1 %collective-permute-start.19 = (bf16[320,128]{1,0:T(8,128)(2,1)S(1)}, bf16[320,128]{1,0:T(8,128)(2,1)S(1)}, u32[]{:S(2)}, u32[]{:S(2)}) collective-permute-start(bf16[320,128]{1,0:T(8,128)(2,1)S(1)} %get-tuple-element.92), channel_id=1, source_target_pairs={{0,1},{1,0},{2,3},{3,2},{4,5},{5,4},{6,7},{7,6},{8,9},{9,8},{10,11... | collective-permute-start | bytes 245768 | tf_op jit(solution)/shard_map/ppermute | solution.py:450
  83.8 0.7 copy-start.8
  83.8 0.7 copy-start.9
  86.1 13.5 %collective-permute-start.20 = (s16[2112,128]{1,0:T(8,128)(2,1)S(1)}, s16[2112,128]{1,0:T(8,128)(2,1)S(1)}, u32[]{:S(2)}, u32[]{:S(2)}) collective-permute-start(s16[2112,128]{1,0:T(8,128)(2,1)S(1)} %get-tuple-element.100), channel_id=1, source_target_pairs={{0,1},{1,2},{2,3},{3,4},{4,5},{5,6},{6,7},{8,9},{9,10},{10,11},{11... | collective-permute-start | bytes 1622024 | tf_op jit(solution)/shard_map/ppermute | solution.py:529
  89.5 14.3 %collective-permute-start.21 = (s16[2112,128]{1,0:T(8,128)(2,1)S(1)}, s16[2112,128]{1,0:T(8,128)(2,1)S(1)}, u32[]{:S(2)}, u32[]{:S(2)}) collective-permute-start(s16[2112,128]{1,0:T(8,128)(2,1)S(1)} %get-tuple-element.101), channel_id=1, source_target_pairs={{1,0},{2,1},{3,2},{4,3},{5,4},{6,5},{7,6},{9,8},{10,9},{11,10},{12... | collective-permute-start | bytes 1622024 | tf_op jit(solution)/shard_map/ppermute | solution.py:530
  106.9 25.4 %collective-permute-start.22 = (s16[336,128]{1,0:T(8,128)(2,1)S(1)}, s16[336,128]{1,0:T(8,128)(2,1)S(1)}, u32[]{:S(2)}, u32[]{:S(2)}) collective-permute-start(s16[336,128]{1,0:T(8,128)(2,1)S(1)} %get-tuple-element.106), channel_id=1, source_target_pairs={{0,7},{1,6},{2,5},{3,4},{4,3},{5,2},{6,1},{7,0},{8,15},{9,14},{10,... | collective-permute-start | bytes 258056 | tf_op jit(solution)/shard_map/ppermute | solution.py:450
  108.1 24.1 %collective-permute-start.23 = (s16[336,128]{1,0:T(8,128)(2,1)S(1)}, s16[336,128]{1,0:T(8,128)(2,1)S(1)}, u32[]{:S(2)}, u32[]{:S(2)}) collective-permute-start(s16[336,128]{1,0:T(8,128)(2,1)S(1)} %get-tuple-element.107), channel_id=1, source_target_pairs={{0,6},{1,7},{2,4},{3,5},{4,2},{5,3},{6,0},{7,1},{8,14},{9,15},{10,... | collective-permute-start | bytes 258056 | tf_op jit(solution)/shard_map/ppermute | solution.py:450
  114.9 18.2 %collective-permute-start.24 = (s16[336,128]{1,0:T(8,128)(2,1)S(1)}, s16[336,128]{1,0:T(8,128)(2,1)S(1)}, u32[]{:S(2)}, u32[]{:S(2)}) collective-permute-start(s16[336,128]{1,0:T(8,128)(2,1)S(1)} %get-tuple-element.108), channel_id=1, source_target_pairs={{0,5},{1,4},{2,7},{3,6},{4,1},{5,0},{6,3},{7,2},{8,13},{9,12},{10,... | collective-permute-start | bytes 258056 | tf_op jit(solution)/shard_map/ppermute | solution.py:450
  123.7 9.5 %collective-permute-start.25 = (s16[336,128]{1,0:T(8,128)(2,1)S(1)}, s16[336,128]{1,0:T(8,128)(2,1)S(1)}, u32[]{:S(2)}, u32[]{:S(2)}) collective-permute-start(s16[336,128]{1,0:T(8,128)(2,1)S(1)} %get-tuple-element.109), channel_id=1, source_target_pairs={{0,4},{1,5},{2,6},{3,7},{4,0},{5,1},{6,2},{7,3},{8,12},{9,13},{10,... | collective-permute-start | bytes 258056 | tf_op jit(solution)/shard_map/ppermute | solution.py:450
  123.7 11.6 %collective-permute-start.26 = (s16[336,128]{1,0:T(8,128)(2,1)S(1)}, s16[336,128]{1,0:T(8,128)(2,1)S(1)}, u32[]{:S(2)}, u32[]{:S(2)}) collective-permute-start(s16[336,128]{1,0:T(8,128)(2,1)S(1)} %get-tuple-element.110), channel_id=1, source_target_pairs={{0,3},{1,2},{2,1},{3,0},{4,7},{5,6},{6,5},{7,4},{8,11},{9,10},{10,... | collective-permute-start | bytes 258056 | tf_op jit(solution)/shard_map/ppermute | solution.py:450
  132.3 6.0 %collective-permute-start.27 = (s16[336,128]{1,0:T(8,128)(2,1)S(1)}, s16[336,128]{1,0:T(8,128)(2,1)S(1)}, u32[]{:S(2)}, u32[]{:S(2)}) collective-permute-start(s16[336,128]{1,0:T(8,128)(2,1)S(1)} %get-tuple-element.111), channel_id=1, source_target_pairs={{0,2},{1,3},{2,0},{3,1},{4,6},{5,7},{6,4},{7,5},{8,10},{9,11},{10,... | collective-permute-start | bytes 258056 | tf_op jit(solution)/shard_map/ppermute | solution.py:450
  132.3 6.0 %collective-permute-start.28 = (s16[336,128]{1,0:T(8,128)(2,1)S(1)}, s16[336,128]{1,0:T(8,128)(2,1)S(1)}, u32[]{:S(2)}, u32[]{:S(2)}) collective-permute-start(s16[336,128]{1,0:T(8,128)(2,1)S(1)} %get-tuple-element.112), channel_id=1, source_target_pairs={{0,1},{1,0},{2,3},{3,2},{4,5},{5,4},{6,7},{7,6},{8,9},{9,8},{10,11... | collective-permute-start | bytes 258056 | tf_op jit(solution)/shard_map/ppermute | solution.py:450
  139.1 2.3 %collective-permute-start.29 = (f32[1440,128]{1,0:T(8,128)S(1)}, f32[1440,128]{1,0:T(8,128)S(1)}, u32[]{:S(2)}, u32[]{:S(2)}) collective-permute-start(f32[1440,128]{1,0:T(8,128)S(1)} %get-tuple-element.114), channel_id=1, source_target_pairs={{0,8},{8,0},{16,24},{24,16},{32,40},{40,32},{48,56},{56,48},{64,72... | collective-permute-start | bytes 2211848 | tf_op jit(solution)/shard_map/ppermute | solution.py:559
  142.7 14.9 %collective-permute-start.30 = (s16[992,128]{1,0:T(8,128)(2,1)S(1)}, s16[992,128]{1,0:T(8,128)(2,1)S(1)}, u32[]{:S(2)}, u32[]{:S(2)}) collective-permute-start(s16[992,128]{1,0:T(8,128)(2,1)S(1)} %get-tuple-element.116), channel_id=1, source_target_pairs={{0,192},{8,200},{16,208},{24,216},{32,224},{40,232},{48,240},{56,2... | collective-permute-start | bytes 761864 | tf_op jit(solution)/shard_map/ppermute | solution.py:450
  143.2 14.3 %collective-permute-start.31 = (s16[992,128]{1,0:T(8,128)(2,1)S(1)}, s16[992,128]{1,0:T(8,128)(2,1)S(1)}, u32[]{:S(2)}, u32[]{:S(2)}) collective-permute-start(s16[992,128]{1,0:T(8,128)(2,1)S(1)} %get-tuple-element.117), channel_id=1, source_target_pairs={{0,128},{8,136},{16,144},{24,152},{32,160},{40,168},{48,176},{56,1... | collective-permute-start | bytes 761864 | tf_op jit(solution)/shard_map/ppermute | solution.py:450
  145.7 12.5 %collective-permute-start.32 = (s16[992,128]{1,0:T(8,128)(2,1)S(1)}, s16[992,128]{1,0:T(8,128)(2,1)S(1)}, u32[]{:S(2)}, u32[]{:S(2)}) collective-permute-start(s16[992,128]{1,0:T(8,128)(2,1)S(1)} %get-tuple-element.118), channel_id=1, source_target_pairs={{0,64},{8,72},{16,80},{24,88},{32,96},{40,104},{48,112},{56,120},{... | collective-permute-start | bytes 761864 | tf_op jit(solution)/shard_map/ppermute | solution.py:450
  158.5 17.6 %collective-permute-start.33 = (s16[256,128]{1,0:T(8,128)(2,1)S(1)}, s16[256,128]{1,0:T(8,128)(2,1)S(1)}, u32[]{:S(2)}, u32[]{:S(2)}) collective-permute-start(s16[256,128]{1,0:T(8,128)(2,1)S(1)} %get-tuple-element.120), channel_id=1, source_target_pairs={{0,48},{8,56},{16,32},{24,40},{32,16},{40,24},{48,0},{56,8},{64,11... | collective-permute-start | bytes 196616 | tf_op jit(solution)/shard_map/ppermute | solution.py:450
  160.6 18.9 %collective-permute-start.34 = (s16[256,128]{1,0:T(8,128)(2,1)S(1)}, s16[256,128]{1,0:T(8,128)(2,1)S(1)}, u32[]{:S(2)}, u32[]{:S(2)}) collective-permute-start(s16[256,128]{1,0:T(8,128)(2,1)S(1)} %get-tuple-element.121), channel_id=1, source_target_pairs={{0,32},{8,40},{16,48},{24,56},{32,0},{40,8},{48,16},{56,24},{64,96... | collective-permute-start | bytes 196616 | tf_op jit(solution)/shard_map/ppermute | solution.py:450
  176.1 4.3 %collective-permute-start.35 = (s16[256,128]{1,0:T(8,128)(2,1)S(1)}, s16[256,128]{1,0:T(8,128)(2,1)S(1)}, u32[]{:S(2)}, u32[]{:S(2)}) collective-permute-start(s16[256,128]{1,0:T(8,128)(2,1)S(1)} %get-tuple-element.122), channel_id=1, source_target_pairs={{0,16},{8,24},{16,0},{24,8},{32,48},{40,56},{48,32},{56,40},{64,80... | collective-permute-start | bytes 196616 | tf_op jit(solution)/shard_map/ppermute | solution.py:450

commit v3 on v2

--- a/solution.py
+++ b/solution.py
@@ -102,13 +102,23 @@
     return groups * GROUP + groups
 
 
-def encode_kernel(now_f, now_a, low_ref, high_ref, level_ref):
-    count_y = now_f.shape[1]
+def odd_place():
+    return lax.rem(lax.axis_index("dom"), 2)
+
+
+def code_edges(fields, out_refs, level_ref):
+    row_count, count_y, _ = fields[0].shape
     per = HALO * count_y // GROUP
-    for out_ref, first in ((low_ref, 0), (high_ref, now_f.shape[0] - HALO)):
-        for f, ref in enumerate((now_f, now_a)):
-            code_halos(lambda x: ref[x], range(first, first + HALO), out_ref, level_ref, f * per)
+    odd = odd_place()
+    for out_ref, high in zip(out_refs, (1 - odd, odd)):
+        first = high * (row_count - HALO)
+        for f, ref in enumerate(fields):
+            code_halos(lambda x: ref[x], [first + n for n in range(HALO)], out_ref, level_ref, f * per)
         out_ref[2 * per * GROUP :, :] = level_ref[...].astype(I16)
+
+
+def encode_kernel(now_f, now_a, one, two, level_ref):
+    code_edges((now_f, now_a), (one, two), level_ref)
 
 
 def decode_halo(in_ref, scale_ref, pad_ref, f, first, count_y):
@@ -170,17 +180,18 @@
         ref[x, pl.ds(y, 1), :] = row + jnp.where(lane == source[0, 2], wave[start[0] + k], 0.0)
 
 
-def before_kernel(now_f, now_a, prev_f, prev_a, low, high, hit, *rest):
-    sum_f, sum_a, base_f, base_a, pad, scale_low, scale_high = rest
+def before_kernel(now_f, now_a, prev_f, prev_a, one, two, hit, *rest):
+    sum_f, sum_a, base_f, base_a, pad, scale_one, scale_two = rest
     row_count, count_y, count_z = now_f.shape
     masks = lane_masks(TILE, count_z)
-    load_scales(low, scale_low)
-    load_scales(high, scale_high)
+    load_scales(one, scale_one)
+    load_scales(two, scale_two)
+    odd = odd_place()
     fields = ((now_f, prev_f, sum_f, base_f), (now_a, prev_a, sum_a, base_a))
     for f, (now, prev, total, base) in enumerate(fields):
         fill(pad, now)
-        decode_halo(low, scale_low, pad, f, 0, count_y)
-        decode_halo(high, scale_high, pad, f, HALO + row_count, count_y)
+        decode_halo(one, scale_one, pad, f, (1 - odd) * (HALO + row_count), count_y)
+        decode_halo(two, scale_two, pad, f, odd * (HALO + row_count), count_y)
 
         @pl.loop(0, row_count)
         def _(x):
@@ -192,18 +203,20 @@
                 base[x, spot, :] = value + hit[x, spot, :] if f else value
 
 
-def first_kernel(groups, anchors, source, begin, wave, sum_f, sum_a, base_f, base_a, *rest):
-    pieces, rest = rest[:groups], rest[groups:]
-    next_f, next_a, courant, send_low, send_high, slab, level = rest
+def first_kernel(halves, anchors, source, begin, wave, sum_f, sum_a, base_f, base_a, *rest):
+    next_f, next_a, courant, one, two, slab, level = rest[-7:]
+    pieces = rest[:-7]
     row_count, count_y, _ = sum_f.shape
-    band = pieces[0].shape[0] // row_count
-    me = lax.axis_index("dom")
-    for k in range(groups):
-        start = pl.multiple_of((me ^ k) * band, 8)
-        for x in range(0, row_count, 2):
-            speed = pieces[-k][pl.ds(x * band, 2 * band), :].astype(F32)
-            slab[x, pl.ds(start, band), :] = jnp.square(speed[:band])
-            slab[x + 1, pl.ds(start, band), :] = jnp.square(speed[band:])
+    band = pieces[0].shape[0] // (row_count * halves)
+    side = len(pieces)
+    me = lax.rem(lax.axis_index("dom"), side)
+    for k in range(side):
+        for half in range(halves):
+            start = pl.multiple_of((half * side + (me ^ k)) * band, 8)
+            for x in range(0, row_count, 2):
+                speed = pieces[-k][pl.ds((half * row_count + x) * band, 2 * band), :].astype(F32)
+                slab[x, pl.ds(start, band), :] = jnp.square(speed[:band])
+                slab[x + 1, pl.ds(start, band), :] = jnp.square(speed[band:])
 
     @pl.loop(0, row_count)
     def _(x):
@@ -215,11 +228,7 @@
             next_a[x, spot, :] = base_a[x, spot, :] + factor * sum_a[x, spot, :]
 
     add_source(source, begin, wave, next_f, 0)
-    per = HALO * count_y // GROUP
-    for out_ref, first in ((send_low, 0), (send_high, row_count - HALO)):
-        for f, ref in enumerate((next_f, next_a)):
-            code_halos(lambda x: ref[x], range(first, first + HALO), out_ref, level, f * per)
-        out_ref[2 * per * GROUP :, :] = level[...].astype(I16)
+    code_edges((next_f, next_a), (one, two), level)
 
 
 def between_kernel(p1, q1, p0, q0, prev_f, courant, hit, part_f, part_a, bend, pad):
@@ -247,32 +256,32 @@
 def halo_terms(in_ref, scale_ref, f, spot_y, count_y, low):
     per = count_y // GROUP
     rows = []
-    for layer in range(HALO):
+    for j in range(HALO):
+        layer = j + low * (HALO - 1 - 2 * j)
         spot = (f * HALO + layer) * per + spot_y // GROUP
-        code = in_ref[pl.ds(spot * GROUP, GROUP), :].astype(I32).astype(F32)
+        code = in_ref[pl.ds(pl.multiple_of(spot * GROUP, GROUP), GROUP), :].astype(I32).astype(F32)
         rows.append(code * scale_ref[pl.ds(spot, 1), :])
-    if low:
-        rows = rows[::-1]
     return [sum(COEFFS[r + j] * rows[j] for j in range(HALO - r)) for r in range(HALO)]
 
 
-def second_kernel(groups, anchors, source, begin, wave, p1, q1, p0, courant, part_f, part_a, bend, low, high, *rest):
+def second_kernel(groups, anchors, source, begin, wave, p1, q1, p0, courant, part_f, part_a, bend, one, two, *rest):
     next_f, next_a, own = rest[:3]
     sends = rest[3 : 2 + groups]
-    frame, scale_low, scale_high = rest[2 + groups :]
+    frame, scale_one, scale_two = rest[2 + groups :]
     row_count, count_y, count_z = p1.shape
     band = own.shape[0] // row_count
-    load_scales(low, scale_low)
-    load_scales(high, scale_high)
+    load_scales(one, scale_one)
+    load_scales(two, scale_two)
+    odd = odd_place()
     edge = (frame.shape[1] - count_y) // 2
     frame[:, 0:edge, :] = jnp.zeros((row_count, edge, count_z), F32)
     frame[:, edge + count_y :, :] = jnp.zeros((row_count, edge, count_z), F32)
     for y in range(0, count_y, GROUP):
         spot = pl.ds(y, GROUP)
-        for ref, scale, side in ((low, scale_low, True), (high, scale_high, False)):
+        for ref, scale, low in ((one, scale_one, odd), (two, scale_two, 1 - odd)):
             for f in range(2):
-                for r, term in enumerate(halo_terms(ref, scale, f, y, count_y, side)):
-                    x = r if side else row_count - 1 - r
+                for r, term in enumerate(halo_terms(ref, scale, f, y, count_y, low)):
+                    x = row_count - 1 - r + low * (2 * r + 1 - row_count)
                     term = courant[x, spot, :] * term
                     if f == 0:
                         frame[x, pl.ds(edge + y, GROUP), :] = part_f[x, spot, :] + term
@@ -331,6 +340,7 @@
 
 
 SIZE_X, SIZE_Z, SIZE_C = 4, 4, 2
+HALVES = 2
 
 
 def place_of(shot):
@@ -342,31 +352,39 @@
     return [(shot, shot ^ bits) for shot in range(SIZE_X * SIZE_Z * SIZE_C)]
 
 
-def pick_kernel(layout, row_count, anchors, *refs):
+def join_kernel(*refs):
+    size = refs[0].shape[0]
+    for n, ref in enumerate(refs[:-1]):
+        refs[-1][pl.ds(n * size, size), :] = ref[...]
+
+
+def pick_kernel(layout, row_count, halves, anchors, *refs):
     count = len(layout)
     ins, outs, table = refs[:count], refs[count:-1], refs[-1]
-    groups = len(outs)
-    per = outs[0].shape[0] // row_count
+    side = len(outs)
+    piece = outs[0].shape[0] // halves
+    per = piece // row_count
     block = ins[0].shape[0] // len(layout[0])
     own = block // per
     x, z, c = place_of(lax.axis_index("shot"))
-    me = lax.axis_index("dom")
-    anchor = anchors[0, 0]
+    half, me = lax.axis_index("dom") // side, lax.rem(lax.axis_index("dom"), side)
+    anchor = anchors[0, 0] + half * (side * row_count)
     first = anchor // own
-    span = table.shape[0] // block
+    span = table.shape[1] // block
     for ref, owners in zip(ins, layout):
-        for n, (dx, dz, dc) in enumerate(owners):
+        for n, (dx, dz, dc, dh) in enumerate(owners):
             place = ((x ^ dx) * SIZE_Z + (z ^ dz)) * SIZE_C + (c ^ dc) - first
 
             @pl.when((place >= 0) & (place < span))
             def _():
                 start = pl.multiple_of(place * block, 8)
-                table[pl.ds(start, block), :] = ref[pl.ds(n * block, block), :].astype(F32)
+                table[half ^ dh, pl.ds(start, block), :] = ref[pl.ds(n * block, block), :].astype(F32)
 
     offset = (anchor - first * own) * per
-    for k in range(groups):
-        start = pl.multiple_of(offset + (me ^ k) * (row_count * per), 8)
-        outs[k][...] = table[pl.ds(start, row_count * per), :].astype(BF16)
+    for k in range(side):
+        start = pl.multiple_of(offset + (me ^ k) * piece, 8)
+        for h in range(halves):
+            outs[k][pl.ds(h * piece, piece), :] = table[h, pl.ds(start, piece), :].astype(BF16)
 
 
 def band_kernel(groups, row_count, block, anchors, own, *refs):
@@ -436,6 +454,15 @@
         out[pl.ds(n * per, per), :] = total
 
 
+def swap_z(groups, k):
+    shots, doms = (k % SIZE_Z) * SIZE_C, (k // SIZE_Z) * (groups // HALVES)
+    return [
+        (shot * groups + dom, (shot ^ shots) * groups + (dom ^ doms))
+        for shot in range(SIZE_X * SIZE_Z * SIZE_C)
+        for dom in range(groups)
+    ]
+
+
 def across(groups, k):
     return [(i, i ^ k) for i in range(groups)]
 
@@ -471,41 +498,47 @@
     piece = row_count * band
     p0, q0, p_prev, q_prev = fwd_now[0], adj_now[0], fwd_prev[0], adj_prev[0]
     scalars = (anchors, source, start_step, wavelet)
-    up = [(i, i + 1) for i in range(groups - 1)]
-    down = [(b, a) for a, b in up]
+    one_pairs = [(i, i ^ 1) for i in range(groups)]
+    two_pairs = [(i, i + 1) for i in range(1, groups - 1, 2)]
+    two_pairs += [(b, a) for a, b in two_pairs]
 
     along = {axis: functools.partial(swap, axis) for axis in "xzc"}
     between = functools.partial(across, groups)
 
     local = velocity.reshape(block, count_z)
     other = lax.ppermute(anchors, "shot", swap("c", 1))
-    near = [local] + exchange([local] * (SIZE_Z - 1), "shot", along["z"])
+    near = [local] + exchange([local] * (HALVES * SIZE_Z - 1), ("shot", "dom"), functools.partial(swap_z, groups))
 
     half = halo_rows(2 * HALO, count_y)
     code = struct((half, count_z), I16)
     levels = pltpu.VMEM((2 * HALO * count_y // GROUP, count_z), I32)
-    low, high = call(encode_kernel, (code, code), (p0, q0), "vv", (levels,))
-    from_low = lax.ppermute(high, "dom", up)
-    from_high = lax.ppermute(low, "dom", down)
-
-    line = jnp.concatenate(near, axis=0)
-    line, other, low = lax.optimization_barrier((line, other, low))
+    one, two = call(encode_kernel, (code, code), (p0, q0), "vv", (levels,))
+    from_one = lax.ppermute(one, "dom", one_pairs)
+    from_two = lax.ppermute(two, "dom", two_pairs)
+
+    (line,) = call(join_kernel, (struct((len(near) * block, count_z), BF16),), near, "v" * len(near))
+    line, other, one = lax.optimization_barrier((line, other, one))
     field = struct((row_count, count_y, count_z), F32)
     hits = call(hit_kernel, (field, field), (start_step, receivers[0], traces[0]), "svv")
     plane = [line] + exchange([line] * (SIZE_X - 1), "shot", along["x"])
     plane = list(lax.optimization_barrier((*plane, hits[0])))[:SIZE_X]
     plane += [lax.ppermute(part, "shot", swap("c", 1)) for part in plane]
-    *plane, from_low, from_high = lax.optimization_barrier((*plane, from_low, from_high))
-    layout = [[(dx, dz, dc) for dz in range(SIZE_Z)] for dc in range(SIZE_C) for dx in range(SIZE_X)]
+    *plane, from_one, from_two = lax.optimization_barrier((*plane, from_one, from_two))
+    layout = [
+        [(dx, k % SIZE_Z, dc, k // SIZE_Z) for k in range(HALVES * SIZE_Z)]
+        for dc in range(SIZE_C)
+        for dx in range(SIZE_X)
+    ]
     span = -(-(row_count * groups + own_rows - 1) // own_rows)
     span += span % SIZE_C
     table = pltpu.VMEM((span * block, count_z), F32)
+    side = groups // HALVES
     pieces = call(
-        functools.partial(pick_kernel, layout, row_count),
-        [struct((piece, count_z), BF16)] * groups,
+        functools.partial(pick_kernel, layout, row_count, HALVES),
+        [struct((HALVES * piece, count_z), BF16)] * side,
         (anchors, *plane),
         "s" + "v" * len(plane),
-        (table,),
+        (pltpu.VMEM((HALVES, -(-(row_count * side + own_rows - 1) // own_rows) * block, count_z), F32),),
     )
     pieces = [pieces[0]] + exchange(pieces[1:], "dom", between)[::-1]
 
@@ -515,19 +548,19 @@
     sums = call(
         before_kernel,
         (field,) * 4,
-        (p0, q0, p_prev, q_prev, from_low, from_high, hits[0]),
+        (p0, q0, p_prev, q_prev, from_one, from_two, hits[0]),
         "v" * 7,
         (padded, scale, scale),
     )
-    p1, q1, courant, low, high = call(
-        functools.partial(first_kernel, groups),
+    p1, q1, courant, one, two = call(
+        functools.partial(first_kernel, HALVES),
         (field, field, field, code, code),
         (*scalars, *sums, *pieces),
-        "ssss" + "v" * (4 + groups),
+        "ssss" + "v" * (4 + side),
         (slab, levels),
     )
-    from_low = lax.ppermute(high, "dom", up)
-    from_high = lax.ppermute(low, "dom", down)
+    from_one = lax.ppermute(one, "dom", one_pairs)
+    from_two = lax.ppermute(two, "dom", two_pairs)
     part_f, part_a, bend = call(
         between_kernel,
         (field,) * 3,
@@ -542,7 +575,7 @@
     p2, q2, own, *sends = call(
         functools.partial(second_kernel, groups),
         (field, field, struct((piece, count_z), F32), *[coded] * (groups - 1)),
-        (*scalars, p1, q1, p0, courant, part_f, part_a, bend, from_low, from_high),
+        (*scalars, p1, q1, p0, courant, part_f, part_a, bend, from_one, from_two),
         "ssss" + "v" * 9,
         (frame, scale, scale),
     )

time: 181 us -> 160 us (0.88)
  starting transfers between devices: 110 us -> 78.4 us
  waiting for transfers between devices: 40.6 us -> 51.2 us
    ppermute x26, starting transfers between devices: 99.3 us -> 72.8 us  [exchange(): got[k] = lax.ppermute(parts[k - 1], axis, pairs(k))]
    ppermute x26, waiting for transfers between devices: 29.8 us -> 40.1 us  [exchange(): got[k] = lax.ppermute(parts[k - 1], axis, pairs(k))]
    ppermute x4, starting transfers between devices: 9.72 us -> 4.47 us  [the longest x2 2.96 us: body(): from_one = lax.ppermute(one, 'dom', one_pairs)]
    pallas_call x11 -> x12, Pallas kernels: 24.8 us -> 24.9 us  [call(): pl.pallas_call(kernel, out_shape=list(outs), in_specs=[smem() if s == 's'...]
  transfers between devices with their start and end apart: 36 -> 36, of which waited for: 18 -> 20; matrix products, arithmetic and copies ran while one was open for 0% -> 0% of each run, Pallas kernels for 9% -> 10%
where the time goes in v3:
time: 160 us; the launch traced here: 159 us
  starting transfers between devices  78.4 us (49%)
  waiting for transfers between devices  51.2 us (32%)
  Pallas kernels  24.9 us (16%)
  local copies, waits for them, and re-layouts  3.16 us (2%)
    ppermute x26, starting transfers between devices, exchange(): got[k] = lax.ppermute(parts[k - 1], axis, pairs(k))  72.8 us
    ppermute x26, waiting for transfers between devices, exchange(): got[k] = lax.ppermute(parts[k - 1], axis, pairs(k))  40.1 us
    pallas_call x12, Pallas kernels, call(): pl.pallas_call(kernel, out_shape=list(outs), in_specs=[smem() if s == 's'...  24.9 us
    ppermute x2, waiting for transfers between devices, body(): from_one = lax.ppermute(one, 'dom', one_pairs)  6.01 us
  transfers between devices with their start and end apart: 36, of which 20 were waited for; matrix products, arithmetic and copies ran while one was open for 0% of the time, Pallas kernels for 10%

profile of v3, /device:TPU:6, one launch (start us, length us, event | category | flops | bytes accessed | tf_op | source)
XLA Modules:
  0.0 159.2 jit_solution(8660765407281779665)
XLA Ops:
  0.6 5.9 %collective-permute-start.6 = (bf16[240,128]{1,0:T(8,128)(2,1)}, bf16[240,128]{1,0:T(8,128)(2,1)S(1)}, u32[]{:S(2)}, u32[]{:S(2)}) collective-permute-start(bf16[240,128]{1,0:T(8,128)(2,1)} %bitcast.23), channel_id=1, source_target_pairs={{0,52},{1,53},{2,54},{3,55},{4,48},{5,49},{6,50},{7,51},{8,60},{9,... | collective-permute-start | bytes 184328 | tf_op jit(solution)/shard_map/ppermute | solution.py:477
  7.1 4.0 %collective-permute-start.4 = (bf16[240,128]{1,0:T(8,128)(2,1)}, bf16[240,128]{1,0:T(8,128)(2,1)S(1)}, u32[]{:S(2)}, u32[]{:S(2)}) collective-permute-start(bf16[240,128]{1,0:T(8,128)(2,1)} %bitcast.25), channel_id=1, source_target_pairs={{0,20},{1,21},{2,22},{3,23},{4,16},{5,17},{6,18},{7,19},{8,28},{9,... | collective-permute-start | bytes 184328 | tf_op jit(solution)/shard_map/ppermute | solution.py:477
  11.1 1.8 %collective-permute-start.3 = (bf16[240,128]{1,0:T(8,128)(2,1)}, bf16[240,128]{1,0:T(8,128)(2,1)S(1)}, u32[]{:S(2)}, u32[]{:S(2)}) collective-permute-start(bf16[240,128]{1,0:T(8,128)(2,1)} %bitcast.26), channel_id=1, source_target_pairs={{0,4},{1,5},{2,6},{3,7},{4,0},{5,1},{6,2},{7,3},{8,12},{9,13},{10,... | collective-permute-start | bytes 184328 | tf_op jit(solution)/shard_map/ppermute | solution.py:477
  13.0 1.9 %collective-permute-start.2 = (bf16[240,128]{1,0:T(8,128)(2,1)}, bf16[240,128]{1,0:T(8,128)(2,1)S(1)}, u32[]{:S(2)}, u32[]{:S(2)}) collective-permute-start(bf16[240,128]{1,0:T(8,128)(2,1)} %bitcast.27), channel_id=1, source_target_pairs={{0,48},{1,49},{2,50},{3,51},{4,52},{5,53},{6,54},{7,55},{8,56},{9,... | collective-permute-start | bytes 184328 | tf_op jit(solution)/shard_map/ppermute | solution.py:477
  15.1 2.3 %collective-permute-start = (bf16[240,128]{1,0:T(8,128)(2,1)}, bf16[240,128]{1,0:T(8,128)(2,1)S(1)}, u32[]{:S(2)}, u32[]{:S(2)}) collective-permute-start(bf16[240,128]{1,0:T(8,128)(2,1)} %bitcast.29), channel_id=1, source_target_pairs={{0,16},{1,17},{2,18},{3,19},{4,20},{5,21},{6,22},{7,23},{8,24},{9,... | collective-permute-start | bytes 184328 | tf_op jit(solution)/shard_map/ppermute | solution.py:477
  17.4 1.2 copy-done
  18.6 1.2 copy-done.2
  20.4 0.8 collective-permute-start.16
  21.5 3.2 %collective-permute-done.1.refs_2_ = bf16[240,128]{1,0:T(8,128)(2,1)S(1)} collective-permute-done((bf16[240,128]{1,0:T(8,128)(2,1)}, bf16[240,128]{1,0:T(8,128)(2,1)S(1)}, u32[]{:S(2)}, u32[]{:S(2)}) %collective-permute-start.1) | collective-permute-done | bytes 61472 | tf_op jit(solution)/shard_map/ppermute | solution.py:477
  25.3 2.4 %collective-permute-start.9 = (bf16[1920,128]{1,0:T(8,128)(2,1)S(1)}, bf16[1920,128]{1,0:T(8,128)(2,1)S(1)}, u32[]{:S(2)}, u32[]{:S(2)}) collective-permute-start(bf16[1920,128]{1,0:T(8,128)(2,1)S(1)} %shard_map.130.refs_0_), channel_id=1, source_target_pairs={{0,128},{8,136},{16,144},{24,152},{32,160},{40,168},{48,176},{56,1... | collective-permute-start | bytes 1474568 | tf_op jit(solution)/shard_map/ppermute | solution.py:477
  27.7 1.2 collective-permute-start.8
  28.9 2.0 %collective-permute-start.15 = (s16[2112,128]{1,0:T(8,128)(2,1)S(1)}, s16[2112,128]{1,0:T(8,128)(2,1)S(1)}, u32[]{:S(2)}, u32[]{:S(2)}) collective-permute-start(s16[2112,128]{1,0:T(8,128)(2,1)S(1)} %get-tuple-element.59), channel_id=1, source_target_pairs={{0,1},{1,0},{2,3},{3,2},{4,5},{5,4},{6,7},{7,6},{8,9},{9,8},{10,11... | collective-permute-start | bytes 1622024 | tf_op jit(solution)/shard_map/ppermute | solution.py:516
  31.6 3.4 %shard_map.132 = (f32[8,256,128]{2,1,0:T(8,128)S(1)}, f32[8,256,128]{2,1,0:T(8,128)S(1)}) custom-call(s32[1]{0:T(128)S(6)} %copy.17.begin, s32[3,512]{1,0:T(4,128)S(1)} %bitcast.31, f32[64,512]{1,0:T(8,128)S(1)} %bitcast.22), custom_call_target="tpu_custom_call" | custom-call | tf_op jit(solution)/shard_map/pallas_call | solution.py:36
  35.0 13.7 %collective-permute-done.10.refs_3_ = bf16[1920,128]{1,0:T(8,128)(2,1)S(1)} collective-permute-done((bf16[1920,128]{1,0:T(8,128)(2,1)S(1)}, bf16[1920,128]{1,0:T(8,128)(2,1)S(1)}, u32[]{:S(2)}, u32[]{:S(2)}) %collective-permute-start.10) | collective-permute-done | bytes 491552 | tf_op jit(solution)/shard_map/ppermute | solution.py:477
  50.3 0.8 collective-permute-done.11.refs_4_
  51.2 0.7 collective-permute-done.12.refs_5_
  51.9 0.7 collective-permute-done.13.refs_6_
  52.6 0.7 collective-permute-done.14.refs_7_
  53.3 1.1 shard_map.134
  54.4 9.2 %collective-permute-start.17 = (bf16[640,128]{1,0:T(8,128)(2,1)S(1)}, bf16[640,128]{1,0:T(8,128)(2,1)S(1)}, u32[]{:S(2)}, u32[]{:S(2)}) collective-permute-start(bf16[640,128]{1,0:T(8,128)(2,1)S(1)} %get-tuple-element.82), channel_id=1, source_target_pairs={{0,3},{1,2},{2,1},{3,0},{4,7},{5,6},{6,5},{7,4},{8,11},{9,10},{10,... | collective-permute-start | bytes 491528 | tf_op jit(solution)/shard_map/ppermute | solution.py:477
  63.6 1.1 collective-permute-start.19
  64.7 6.1 %shard_map.133 = (f32[8,256,128]{2,1,0:T(8,128)S(1)}, f32[8,256,128]{2,1,0:T(8,128)S(1)}, f32[8,256,128]{2,1,0:T(8,128)S(1)}, f32[8,256,128]{2,1,0:T(8,128)S(1)}) custom-call(f32[8,256,128]{2,1,0:T(8,128)S(1)} %bitcast.13, f32[8,256,128]{2,1,0:T(8,128)S(1)} %bitcast.17, f32[8,256,128]{2,1,0:T(8,128)S(1)} %bitcast.19, f32[8,256,128]{2,1,0:T(8,128)S(1)} %bitcast.21, ...), custom_call_target="tpu_custom_call" | custom-call | tf_op jit(solution)/shard_map/pallas_call | solution.py:36
  71.0 1.1 collective-permute-done.18.rest_2_
  72.5 0.7 copy-done.9
  73.2 1.6 shard_map.135
  74.7 0.9 collective-permute-start.20
  75.7 0.7 collective-permute-start.21
  76.4 5.9 %shard_map.136 = (f32[8,256,128]{2,1,0:T(8,128)S(1)}, f32[8,256,128]{2,1,0:T(8,128)S(1)}, f32[8,256,128]{2,1,0:T(8,128)S(1)}) custom-call(f32[8,256,128]{2,1,0:T(8,128)S(1)} %get-tuple-element.85.p1, f32[8,256,128]{2,1,0:T(8,128)S(1)} %get-tuple-element.86.q1, f32[8,256,128]{2,1,0:T(8,128)S(1)} %bitcast.14, f32[8,256,128]{2,1,0:T(8,128)S(1)} %bitcast.18, ...), custom_call_target="tpu_custom_call" | custom-call | tf_op jit(solution)/shard_map/pallas_call | solution.py:36
  82.3 6.0 %collective-permute-done.20.one = s16[2112,128]{1,0:T(8,128)(2,1)S(1)} collective-permute-done((s16[2112,128]{1,0:T(8,128)(2,1)S(1)}, s16[2112,128]{1,0:T(8,128)(2,1)S(1)}, u32[]{:S(2)}, u32[]{:S(2)}) %collective-permute-start.20) | collective-permute-done | bytes 540704 | tf_op jit(solution)/shard_map/ppermute | solution.py:562
  88.3 3.0 %shard_map.137 = (f32[8,256,128]{2,1,0:T(8,128)}, f32[8,256,128]{2,1,0:T(8,128)}, f32[320,128]{1,0:T(8,128)S(1)}, s16[336,128]{1,0:T(8,128)(2,1)S(1)}, s16[336,1...) custom-call(s32[1,2]{1,0:T(1,128)S(1)} %copy-done.8, ...), custom_call_target="tpu_custom_call" | custom-call | tf_op jit(solution)/shard_map/pallas_call | solution.py:36
  91.3 2.1 %collective-permute-start.22 = (s16[336,128]{1,0:T(8,128)(2,1)S(1)}, s16[336,128]{1,0:T(8,128)(2,1)S(1)}, u32[]{:S(2)}, u32[]{:S(2)}) collective-permute-start(s16[336,128]{1,0:T(8,128)(2,1)S(1)} %get-tuple-element.98), channel_id=1, source_target_pairs={{0,7},{1,6},{2,5},{3,4},{4,3},{5,2},{6,1},{7,0},{8,15},{9,14},{10,... | collective-permute-start | bytes 258056 | tf_op jit(solution)/shard_map/ppermute | solution.py:477
  93.4 8.5 %collective-permute-start.23 = (s16[336,128]{1,0:T(8,128)(2,1)S(1)}, s16[336,128]{1,0:T(8,128)(2,1)S(1)}, u32[]{:S(2)}, u32[]{:S(2)}) collective-permute-start(s16[336,128]{1,0:T(8,128)(2,1)S(1)} %get-tuple-element.99), channel_id=1, source_target_pairs={{0,6},{1,7},{2,4},{3,5},{4,2},{5,3},{6,0},{7,1},{8,14},{9,15},{10,... | collective-permute-start | bytes 258056 | tf_op jit(solution)/shard_map/ppermute | solution.py:477
  101.9 8.3 %collective-permute-start.24 = (s16[336,128]{1,0:T(8,128)(2,1)S(1)}, s16[336,128]{1,0:T(8,128)(2,1)S(1)}, u32[]{:S(2)}, u32[]{:S(2)}) collective-permute-start(s16[336,128]{1,0:T(8,128)(2,1)S(1)} %get-tuple-element.100), channel_id=1, source_target_pairs={{0,5},{1,4},{2,7},{3,6},{4,1},{5,0},{6,3},{7,2},{8,13},{9,12},{10,... | collective-permute-start | bytes 258056 | tf_op jit(solution)/shard_map/ppermute | solution.py:477
  110.3 5.8 %collective-permute-start.26 = (s16[336,128]{1,0:T(8,128)(2,1)S(1)}, s16[336,128]{1,0:T(8,128)(2,1)S(1)}, u32[]{:S(2)}, u32[]{:S(2)}) collective-permute-start(s16[336,128]{1,0:T(8,128)(2,1)S(1)} %get-tuple-element.102), channel_id=1, source_target_pairs={{0,3},{1,2},{2,1},{3,0},{4,7},{5,6},{6,5},{7,4},{8,11},{9,10},{10,... | collective-permute-start | bytes 258056 | tf_op jit(solution)/shard_map/ppermute | solution.py:477
  116.1 0.9 collective-permute-start.28
  116.9 1.8 %collective-permute-done.25.refs_3_ = s16[336,128]{1,0:T(8,128)(2,1)S(1)} collective-permute-done((s16[336,128]{1,0:T(8,128)(2,1)S(1)}, s16[336,128]{1,0:T(8,128)(2,1)S(1)}, u32[]{:S(2)}, u32[]{:S(2)}) %collective-permute-start.25) | collective-permute-done | bytes 86048 | tf_op jit(solution)/shard_map/ppermute | solution.py:477
  119.0 3.0 %collective-permute-done.27.refs_5_ = s16[336,128]{1,0:T(8,128)(2,1)S(1)} collective-permute-done((s16[336,128]{1,0:T(8,128)(2,1)S(1)}, s16[336,128]{1,0:T(8,128)(2,1)S(1)}, u32[]{:S(2)}, u32[]{:S(2)}) %collective-permute-start.27) | collective-permute-done | bytes 86048 | tf_op jit(solution)/shard_map/ppermute | solution.py:477
  122.1 0.9 shard_map.138
  123.0 2.2 %collective-permute-done.29.got = f32[1440,128]{1,0:T(8,128)S(1)} collective-permute-done((f32[1440,128]{1,0:T(8,128)S(1)}, f32[1440,128]{1,0:T(8,128)S(1)}, u32[]{:S(2)}, u32[]{:S(2)}) %collective-permute-start.29) | collective-permute-done | bytes 737312 | tf_op jit(solution)/shard_map/ppermute | solution.py:592
  125.2 1.2 shard_map.139
  127.0 2.5 %collective-permute-start.31 = (s16[992,128]{1,0:T(8,128)(2,1)S(1)}, s16[992,128]{1,0:T(8,128)(2,1)S(1)}, u32[]{:S(2)}, u32[]{:S(2)}) collective-permute-start(s16[992,128]{1,0:T(8,128)(2,1)S(1)} %get-tuple-element.109), channel_id=1, source_target_pairs={{0,128},{8,136},{16,144},{24,152},{32,160},{40,168},{48,176},{56,1... | collective-permute-start | bytes 761864 | tf_op jit(solution)/shard_map/ppermute | solution.py:477
  129.5 1.2 collective-permute-start.32
  130.7 10.7 %collective-permute-done.30.refs_0_ = s16[992,128]{1,0:T(8,128)(2,1)S(1)} collective-permute-done((s16[992,128]{1,0:T(8,128)(2,1)S(1)}, s16[992,128]{1,0:T(8,128)(2,1)S(1)}, u32[]{:S(2)}, u32[]{:S(2)}) %collective-permute-start.30) | collective-permute-done | bytes 253984 | tf_op jit(solution)/shard_map/ppermute | solution.py:477
  142.4 2.0 %collective-permute-start.33 = (s16[256,128]{1,0:T(8,128)(2,1)S(1)}, s16[256,128]{1,0:T(8,128)(2,1)S(1)}, u32[]{:S(2)}, u32[]{:S(2)}) collective-permute-start(s16[256,128]{1,0:T(8,128)(2,1)S(1)} %get-tuple-element.112), channel_id=1, source_target_pairs={{0,48},{8,56},{16,32},{24,40},{32,16},{40,24},{48,0},{56,8},{64,11... | collective-permute-start | bytes 196616 | tf_op jit(solution)/shard_map/ppermute | solution.py:477
  144.3 9.9 %collective-permute-start.34 = (s16[256,128]{1,0:T(8,128)(2,1)S(1)}, s16[256,128]{1,0:T(8,128)(2,1)S(1)}, u32[]{:S(2)}, u32[]{:S(2)}) collective-permute-start(s16[256,128]{1,0:T(8,128)(2,1)S(1)} %get-tuple-element.113), channel_id=1, source_target_pairs={{0,32},{8,40},{16,48},{24,56},{32,0},{40,8},{48,16},{56,24},{64,96... | collective-permute-start | bytes 196616 | tf_op jit(solution)/shard_map/ppermute | solution.py:477
  154.3 3.4 %collective-permute-done.34.refs_1_ = s16[256,128]{1,0:T(8,128)(2,1)S(1)} collective-permute-done((s16[256,128]{1,0:T(8,128)(2,1)S(1)}, s16[256,128]{1,0:T(8,128)(2,1)S(1)}, u32[]{:S(2)}, u32[]{:S(2)}) %collective-permute-start.34) | collective-permute-done | bytes 65568 | tf_op jit(solution)/shard_map/ppermute | solution.py:477
  157.6 0.9 collective-permute-done.35.refs_2_
  158.5 0.7 shard_map.141
  (61 shorter events, 6.2 us)
Async XLA Ops:
  0.6 14.2 %collective-permute-start.6 = (bf16[240,128]{1,0:T(8,128)(2,1)}, bf16[240,128]{1,0:T(8,128)(2,1)S(1)}, u32[]{:S(2)}, u32[]{:S(2)}) collective-permute-start(bf16[240,128]{1,0:T(8,128)(2,1)} %bitcast.23), channel_id=1, source_target_pairs={{0,52},{1,53},{2,54},{3,55},{4,48},{5,49},{6,50},{7,51},{8,60},{9,... | collective-permute-start | bytes 184328 | tf_op jit(solution)/shard_map/ppermute | solution.py:477
  6.6 8.5 %collective-permute-start.5 = (bf16[240,128]{1,0:T(8,128)(2,1)}, bf16[240,128]{1,0:T(8,128)(2,1)S(1)}, u32[]{:S(2)}, u32[]{:S(2)}) collective-permute-start(bf16[240,128]{1,0:T(8,128)(2,1)} %bitcast.24), channel_id=1, source_target_pairs={{0,36},{1,37},{2,38},{3,39},{4,32},{5,33},{6,34},{7,35},{8,44},{9,... | collective-permute-start | bytes 184328 | tf_op jit(solution)/shard_map/ppermute | solution.py:477
  7.1 13.3 %collective-permute-start.4 = (bf16[240,128]{1,0:T(8,128)(2,1)}, bf16[240,128]{1,0:T(8,128)(2,1)S(1)}, u32[]{:S(2)}, u32[]{:S(2)}) collective-permute-start(bf16[240,128]{1,0:T(8,128)(2,1)} %bitcast.25), channel_id=1, source_target_pairs={{0,20},{1,21},{2,22},{3,23},{4,16},{5,17},{6,18},{7,19},{8,28},{9,... | collective-permute-start | bytes 184328 | tf_op jit(solution)/shard_map/ppermute | solution.py:477
  11.1 10.3 %collective-permute-start.3 = (bf16[240,128]{1,0:T(8,128)(2,1)}, bf16[240,128]{1,0:T(8,128)(2,1)S(1)}, u32[]{:S(2)}, u32[]{:S(2)}) collective-permute-start(bf16[240,128]{1,0:T(8,128)(2,1)} %bitcast.26), channel_id=1, source_target_pairs={{0,4},{1,5},{2,6},{3,7},{4,0},{5,1},{6,2},{7,3},{8,12},{9,13},{10,... | collective-permute-start | bytes 184328 | tf_op jit(solution)/shard_map/ppermute | solution.py:477
  13.0 8.5 %collective-permute-start.2 = (bf16[240,128]{1,0:T(8,128)(2,1)}, bf16[240,128]{1,0:T(8,128)(2,1)S(1)}, u32[]{:S(2)}, u32[]{:S(2)}) collective-permute-start(bf16[240,128]{1,0:T(8,128)(2,1)} %bitcast.27), channel_id=1, source_target_pairs={{0,48},{1,49},{2,50},{3,51},{4,52},{5,53},{6,54},{7,55},{8,56},{9,... | collective-permute-start | bytes 184328 | tf_op jit(solution)/shard_map/ppermute | solution.py:477
  14.9 9.8 %collective-permute-start.1 = (bf16[240,128]{1,0:T(8,128)(2,1)}, bf16[240,128]{1,0:T(8,128)(2,1)S(1)}, u32[]{:S(2)}, u32[]{:S(2)}) collective-permute-start(bf16[240,128]{1,0:T(8,128)(2,1)} %bitcast.28), channel_id=1, source_target_pairs={{0,32},{1,33},{2,34},{3,35},{4,36},{5,37},{6,38},{7,39},{8,40},{9,... | collective-permute-start | bytes 184328 | tf_op jit(solution)/shard_map/ppermute | solution.py:477
  15.1 9.5 %collective-permute-start = (bf16[240,128]{1,0:T(8,128)(2,1)}, bf16[240,128]{1,0:T(8,128)(2,1)S(1)}, u32[]{:S(2)}, u32[]{:S(2)}) collective-permute-start(bf16[240,128]{1,0:T(8,128)(2,1)} %bitcast.29), channel_id=1, source_target_pairs={{0,16},{1,17},{2,18},{3,19},{4,20},{5,21},{6,22},{7,23},{8,24},{9,... | collective-permute-start | bytes 184328 | tf_op jit(solution)/shard_map/ppermute | solution.py:477
  17.4 1.2 copy-start
  18.6 1.2 copy-start.2
  19.8 4.8 %copy-start.7 = (bf16[6,40,128]{2,1,0:T(8,128)(2,1)S(1)}, bf16[6,40,128]{2,1,0:T(8,128)(2,1)}, u32[]{:S(2)}) copy-start(bf16[6,40,128]{2,1,0:T(8,128)(2,1)} %param.11) | copy-start | bytes 184324
  20.4 1.1 copy-start.8
  20.4 11.2 %copy-start.6 = (f32[1,64,512]{2,1,0:T(8,128)S(1)}, f32[1,64,512]{2,1,0:T(8,128)}, u32[]{:S(2)}) copy-start(f32[1,64,512]{2,1,0:T(8,128)} %param.16) | copy-start | bytes 393220
  20.4 29.5 %collective-permute-start.16 = (s16[2112,128]{1,0:T(8,128)(2,1)S(1)}, s16[2112,128]{1,0:T(8,128)(2,1)S(1)}, u32[]{:S(2)}, u32[]{:S(2)}) collective-permute-start(s16[2112,128]{1,0:T(8,128)(2,1)S(1)} %get-tuple-element.66), channel_id=1, source_target_pairs={{1,2},{3,4},{5,6},{2,1},{4,3},{6,5},{9,10},{11,12},{13,14},{10,9},... | collective-permute-start | bytes 1622024 | tf_op jit(solution)/shard_map/ppermute | solution.py:517
  21.5 3.2 %collective-permute-start.7 = (s32[1,2]{1,0:T(1,128)S(1)}, s32[1,2]{1,0:T(1,128)S(1)}, u32[]{:S(2)}, u32[]{:S(2)}) collective-permute-start(s32[1,2]{1,0:T(1,128)S(1)} %copy-done.8), channel_id=1, source_target_pairs={{0,8},{8,0},{16,24},{24,16},{32,40},{40,32},{48,56},{56,48},{64,72... | collective-permute-start | bytes 32 | tf_op jit(solution)/shard_map/ppermute | solution.py:509
  24.6 6.9 %copy-start.11 = (s32[1,3,512]{2,0,1:T(1,128)S(1)}, s32[1,3,512]{2,0,1:T(1,128)}, u32[]{:S(2)}) copy-start(s32[1,3,512]{2,0,1:T(1,128)} %param.15) | copy-start | bytes 18436
  24.6 40.1 %copy-start.5 = (f32[1,8,256,128]{3,2,1,0:T(8,128)S(1)}, f32[1,8,256,128]{3,2,1,0:T(8,128)}, u32[]{:S(2)}) copy-start(f32[1,8,256,128]{3,2,1,0:T(8,128)} %param.20) | copy-start | bytes 3145732
  24.7 24.0 %collective-permute-start.10 = (bf16[1920,128]{1,0:T(8,128)(2,1)S(1)}, bf16[1920,128]{1,0:T(8,128)(2,1)S(1)}, u32[]{:S(2)}, u32[]{:S(2)}) collective-permute-start(bf16[1920,128]{1,0:T(8,128)(2,1)S(1)} %shard_map.130.refs_0_), channel_id=1, source_target_pairs={{0,192},{8,200},{16,208},{24,216},{32,224},{40,232},{48,240},{56,2... | collective-permute-start | bytes 1474568 | tf_op jit(solution)/shard_map/ppermute | solution.py:477
  25.3 23.4 %collective-permute-start.9 = (bf16[1920,128]{1,0:T(8,128)(2,1)S(1)}, bf16[1920,128]{1,0:T(8,128)(2,1)S(1)}, u32[]{:S(2)}, u32[]{:S(2)}) collective-permute-start(bf16[1920,128]{1,0:T(8,128)(2,1)S(1)} %shard_map.130.refs_0_), channel_id=1, source_target_pairs={{0,128},{8,136},{16,144},{24,152},{32,160},{40,168},{48,176},{56,1... | collective-permute-start | bytes 1474568 | tf_op jit(solution)/shard_map/ppermute | solution.py:477
  27.7 21.6 %collective-permute-start.8 = (bf16[1920,128]{1,0:T(8,128)(2,1)S(1)}, bf16[1920,128]{1,0:T(8,128)(2,1)S(1)}, u32[]{:S(2)}, u32[]{:S(2)}) collective-permute-start(bf16[1920,128]{1,0:T(8,128)(2,1)S(1)} %shard_map.130.refs_0_), channel_id=1, source_target_pairs={{0,64},{8,72},{16,80},{24,88},{32,96},{40,104},{48,112},{56,120},{... | collective-permute-start | bytes 1474568 | tf_op jit(solution)/shard_map/ppermute | solution.py:477
  28.9 21.4 %collective-permute-start.15 = (s16[2112,128]{1,0:T(8,128)(2,1)S(1)}, s16[2112,128]{1,0:T(8,128)(2,1)S(1)}, u32[]{:S(2)}, u32[]{:S(2)}) collective-permute-start(s16[2112,128]{1,0:T(8,128)(2,1)S(1)} %get-tuple-element.59), channel_id=1, source_target_pairs={{0,1},{1,0},{2,3},{3,2},{4,5},{5,4},{6,7},{7,6},{8,9},{9,8},{10,11... | collective-permute-start | bytes 1622024 | tf_op jit(solution)/shard_map/ppermute | solution.py:516
  49.3 15.4 %copy-start.1 = (f32[1,8,256,128]{3,2,1,0:T(8,128)S(1)}, f32[1,8,256,128]{3,2,1,0:T(8,128)}, u32[]{:S(2)}) copy-start(f32[1,8,256,128]{3,2,1,0:T(8,128)} %param.19) | copy-start | bytes 3145732
  49.3 15.4 %copy-start.3 = (f32[1,8,256,128]{3,2,1,0:T(8,128)S(1)}, f32[1,8,256,128]{3,2,1,0:T(8,128)}, u32[]{:S(2)}) copy-start(f32[1,8,256,128]{3,2,1,0:T(8,128)} %param.21) | copy-start | bytes 3145732
  49.3 15.5 %copy-start.4 = (f32[1,8,256,128]{3,2,1,0:T(8,128)S(1)}, f32[1,8,256,128]{3,2,1,0:T(8,128)}, u32[]{:S(2)}) copy-start(f32[1,8,256,128]{3,2,1,0:T(8,128)} %param.18) | copy-start | bytes 3145732
  49.3 1.9 %collective-permute-start.11 = (bf16[1920,128]{1,0:T(8,128)(2,1)S(1)}, bf16[1920,128]{1,0:T(8,128)(2,1)S(1)}, u32[]{:S(2)}, u32[]{:S(2)}) collective-permute-start(bf16[1920,128]{1,0:T(8,128)(2,1)S(1)} %shard_map.130.refs_0_), channel_id=1, source_target_pairs={{0,8},{8,0},{16,24},{24,16},{32,40},{40,32},{48,56},{56,48},{64,72... | collective-permute-start | bytes 1474568 | tf_op jit(solution)/shard_map/ppermute | solution.py:525
  49.3 2.6 %collective-permute-start.12 = (bf16[1920,128]{1,0:T(8,128)(2,1)S(1)}, bf16[1920,128]{1,0:T(8,128)(2,1)S(1)}, u32[]{:S(2)}, u32[]{:S(2)}) collective-permute-start(bf16[1920,128]{1,0:T(8,128)(2,1)S(1)} %collective-permute-done.8.refs_1_), channel_id=1, source_target_pairs={{0,8},{8,0},{16,24},{24,16},{32,40},{40,32},{48,56},{56,48},{64,72... | collective-permute-start | bytes 1474568 | tf_op jit(solution)/shard_map/ppermute | solution.py:525
  49.8 2.8 %collective-permute-start.13 = (bf16[1920,128]{1,0:T(8,128)(2,1)S(1)}, bf16[1920,128]{1,0:T(8,128)(2,1)S(1)}, u32[]{:S(2)}, u32[]{:S(2)}) collective-permute-start(bf16[1920,128]{1,0:T(8,128)(2,1)S(1)} %collective-permute-done.9.refs_2_), channel_id=1, source_target_pairs={{0,8},{8,0},{16,24},{24,16},{32,40},{40,32},{48,56},{56,48},{64,72... | collective-permute-start | bytes 1474568 | tf_op jit(solution)/shard_map/ppermute | solution.py:525
  49.9 3.4 %collective-permute-start.14 = (bf16[1920,128]{1,0:T(8,128)(2,1)S(1)}, bf16[1920,128]{1,0:T(8,128)(2,1)S(1)}, u32[]{:S(2)}, u32[]{:S(2)}) collective-permute-start(bf16[1920,128]{1,0:T(8,128)(2,1)S(1)} %collective-permute-done.10.refs_3_), channel_id=1, source_target_pairs={{0,8},{8,0},{16,24},{24,16},{32,40},{40,32},{48,56},{56,48},{64,72... | collective-permute-start | bytes 1474568 | tf_op jit(solution)/shard_map/ppermute | solution.py:525
  54.4 16.6 %collective-permute-start.17 = (bf16[640,128]{1,0:T(8,128)(2,1)S(1)}, bf16[640,128]{1,0:T(8,128)(2,1)S(1)}, u32[]{:S(2)}, u32[]{:S(2)}) collective-permute-start(bf16[640,128]{1,0:T(8,128)(2,1)S(1)} %get-tuple-element.82), channel_id=1, source_target_pairs={{0,3},{1,2},{2,1},{3,0},{4,7},{5,6},{6,5},{7,4},{8,11},{9,10},{10,... | collective-permute-start | bytes 491528 | tf_op jit(solution)/shard_map/ppermute | solution.py:477
  63.6 8.6 %collective-permute-start.18 = (bf16[640,128]{1,0:T(8,128)(2,1)S(1)}, bf16[640,128]{1,0:T(8,128)(2,1)S(1)}, u32[]{:S(2)}, u32[]{:S(2)}) collective-permute-start(bf16[640,128]{1,0:T(8,128)(2,1)S(1)} %get-tuple-element.83), channel_id=1, source_target_pairs={{0,2},{1,3},{2,0},{3,1},{4,6},{5,7},{6,4},{7,5},{8,10},{9,11},{10,... | collective-permute-start | bytes 491528 | tf_op jit(solution)/shard_map/ppermute | solution.py:477
  63.6 8.9 %collective-permute-start.19 = (bf16[640,128]{1,0:T(8,128)(2,1)S(1)}, bf16[640,128]{1,0:T(8,128)(2,1)S(1)}, u32[]{:S(2)}, u32[]{:S(2)}) collective-permute-start(bf16[640,128]{1,0:T(8,128)(2,1)S(1)} %get-tuple-element.84), channel_id=1, source_target_pairs={{0,1},{1,0},{2,3},{3,2},{4,5},{5,4},{6,7},{7,6},{8,9},{9,8},{10,11... | collective-permute-start | bytes 491528 | tf_op jit(solution)/shard_map/ppermute | solution.py:477
  72.5 0.7 copy-start.9
  72.5 0.7 copy-start.10
  74.7 13.6 %collective-permute-start.20 = (s16[2112,128]{1,0:T(8,128)(2,1)S(1)}, s16[2112,128]{1,0:T(8,128)(2,1)S(1)}, u32[]{:S(2)}, u32[]{:S(2)}) collective-permute-start(s16[2112,128]{1,0:T(8,128)(2,1)S(1)} %get-tuple-element.92), channel_id=1, source_target_pairs={{0,1},{1,0},{2,3},{3,2},{4,5},{5,4},{6,7},{7,6},{8,9},{9,8},{10,11... | collective-permute-start | bytes 1622024 | tf_op jit(solution)/shard_map/ppermute | solution.py:562
  75.7 12.6 %collective-permute-start.21 = (s16[2112,128]{1,0:T(8,128)(2,1)S(1)}, s16[2112,128]{1,0:T(8,128)(2,1)S(1)}, u32[]{:S(2)}, u32[]{:S(2)}) collective-permute-start(s16[2112,128]{1,0:T(8,128)(2,1)S(1)} %get-tuple-element.93), channel_id=1, source_target_pairs={{1,2},{3,4},{5,6},{2,1},{4,3},{6,5},{9,10},{11,12},{13,14},{10,9},... | collective-permute-start | bytes 1622024 | tf_op jit(solution)/shard_map/ppermute | solution.py:563
  91.3 24.7 %collective-permute-start.22 = (s16[336,128]{1,0:T(8,128)(2,1)S(1)}, s16[336,128]{1,0:T(8,128)(2,1)S(1)}, u32[]{:S(2)}, u32[]{:S(2)}) collective-permute-start(s16[336,128]{1,0:T(8,128)(2,1)S(1)} %get-tuple-element.98), channel_id=1, source_target_pairs={{0,7},{1,6},{2,5},{3,4},{4,3},{5,2},{6,1},{7,0},{8,15},{9,14},{10,... | collective-permute-start | bytes 258056 | tf_op jit(solution)/shard_map/ppermute | solution.py:477
  93.4 22.7 %collective-permute-start.23 = (s16[336,128]{1,0:T(8,128)(2,1)S(1)}, s16[336,128]{1,0:T(8,128)(2,1)S(1)}, u32[]{:S(2)}, u32[]{:S(2)}) collective-permute-start(s16[336,128]{1,0:T(8,128)(2,1)S(1)} %get-tuple-element.99), channel_id=1, source_target_pairs={{0,6},{1,7},{2,4},{3,5},{4,2},{5,3},{6,0},{7,1},{8,14},{9,15},{10,... | collective-permute-start | bytes 258056 | tf_op jit(solution)/shard_map/ppermute | solution.py:477
  101.9 15.0 %collective-permute-start.24 = (s16[336,128]{1,0:T(8,128)(2,1)S(1)}, s16[336,128]{1,0:T(8,128)(2,1)S(1)}, u32[]{:S(2)}, u32[]{:S(2)}) collective-permute-start(s16[336,128]{1,0:T(8,128)(2,1)S(1)} %get-tuple-element.100), channel_id=1, source_target_pairs={{0,5},{1,4},{2,7},{3,6},{4,1},{5,0},{6,3},{7,2},{8,13},{9,12},{10,... | collective-permute-start | bytes 258056 | tf_op jit(solution)/shard_map/ppermute | solution.py:477
  110.3 8.5 %collective-permute-start.25 = (s16[336,128]{1,0:T(8,128)(2,1)S(1)}, s16[336,128]{1,0:T(8,128)(2,1)S(1)}, u32[]{:S(2)}, u32[]{:S(2)}) collective-permute-start(s16[336,128]{1,0:T(8,128)(2,1)S(1)} %get-tuple-element.101), channel_id=1, source_target_pairs={{0,4},{1,5},{2,6},{3,7},{4,0},{5,1},{6,2},{7,3},{8,12},{9,13},{10,... | collective-permute-start | bytes 258056 | tf_op jit(solution)/shard_map/ppermute | solution.py:477
  110.3 8.7 %collective-permute-start.26 = (s16[336,128]{1,0:T(8,128)(2,1)S(1)}, s16[336,128]{1,0:T(8,128)(2,1)S(1)}, u32[]{:S(2)}, u32[]{:S(2)}) collective-permute-start(s16[336,128]{1,0:T(8,128)(2,1)S(1)} %get-tuple-element.102), channel_id=1, source_target_pairs={{0,3},{1,2},{2,1},{3,0},{4,7},{5,6},{6,5},{7,4},{8,11},{9,10},{10,... | collective-permute-start | bytes 258056 | tf_op jit(solution)/shard_map/ppermute | solution.py:477
  116.1 6.0 %collective-permute-start.27 = (s16[336,128]{1,0:T(8,128)(2,1)S(1)}, s16[336,128]{1,0:T(8,128)(2,1)S(1)}, u32[]{:S(2)}, u32[]{:S(2)}) collective-permute-start(s16[336,128]{1,0:T(8,128)(2,1)S(1)} %get-tuple-element.103), channel_id=1, source_target_pairs={{0,2},{1,3},{2,0},{3,1},{4,6},{5,7},{6,4},{7,5},{8,10},{9,11},{10,... | collective-permute-start | bytes 258056 | tf_op jit(solution)/shard_map/ppermute | solution.py:477
  116.1 6.0 %collective-permute-start.28 = (s16[336,128]{1,0:T(8,128)(2,1)S(1)}, s16[336,128]{1,0:T(8,128)(2,1)S(1)}, u32[]{:S(2)}, u32[]{:S(2)}) collective-permute-start(s16[336,128]{1,0:T(8,128)(2,1)S(1)} %get-tuple-element.104), channel_id=1, source_target_pairs={{0,1},{1,0},{2,3},{3,2},{4,5},{5,4},{6,7},{7,6},{8,9},{9,8},{10,11... | collective-permute-start | bytes 258056 | tf_op jit(solution)/shard_map/ppermute | solution.py:477
  122.9 2.3 %collective-permute-start.29 = (f32[1440,128]{1,0:T(8,128)S(1)}, f32[1440,128]{1,0:T(8,128)S(1)}, u32[]{:S(2)}, u32[]{:S(2)}) collective-permute-start(f32[1440,128]{1,0:T(8,128)S(1)} %get-tuple-element.106), channel_id=1, source_target_pairs={{0,8},{8,0},{16,24},{24,16},{32,40},{40,32},{48,56},{56,48},{64,72... | collective-permute-start | bytes 2211848 | tf_op jit(solution)/shard_map/ppermute | solution.py:592
  126.5 14.9 %collective-permute-start.30 = (s16[992,128]{1,0:T(8,128)(2,1)S(1)}, s16[992,128]{1,0:T(8,128)(2,1)S(1)}, u32[]{:S(2)}, u32[]{:S(2)}) collective-permute-start(s16[992,128]{1,0:T(8,128)(2,1)S(1)} %get-tuple-element.108), channel_id=1, source_target_pairs={{0,192},{8,200},{16,208},{24,216},{32,224},{40,232},{48,240},{56,2... | collective-permute-start | bytes 761864 | tf_op jit(solution)/shard_map/ppermute | solution.py:477
  127.0 14.4 %collective-permute-start.31 = (s16[992,128]{1,0:T(8,128)(2,1)S(1)}, s16[992,128]{1,0:T(8,128)(2,1)S(1)}, u32[]{:S(2)}, u32[]{:S(2)}) collective-permute-start(s16[992,128]{1,0:T(8,128)(2,1)S(1)} %get-tuple-element.109), channel_id=1, source_target_pairs={{0,128},{8,136},{16,144},{24,152},{32,160},{40,168},{48,176},{56,1... | collective-permute-start | bytes 761864 | tf_op jit(solution)/shard_map/ppermute | solution.py:477
  129.5 12.6 %collective-permute-start.32 = (s16[992,128]{1,0:T(8,128)(2,1)S(1)}, s16[992,128]{1,0:T(8,128)(2,1)S(1)}, u32[]{:S(2)}, u32[]{:S(2)}) collective-permute-start(s16[992,128]{1,0:T(8,128)(2,1)S(1)} %get-tuple-element.110), channel_id=1, source_target_pairs={{0,64},{8,72},{16,80},{24,88},{32,96},{40,104},{48,112},{56,120},{... | collective-permute-start | bytes 761864 | tf_op jit(solution)/shard_map/ppermute | solution.py:477
  142.4 11.9 %collective-permute-start.33 = (s16[256,128]{1,0:T(8,128)(2,1)S(1)}, s16[256,128]{1,0:T(8,128)(2,1)S(1)}, u32[]{:S(2)}, u32[]{:S(2)}) collective-permute-start(s16[256,128]{1,0:T(8,128)(2,1)S(1)} %get-tuple-element.112), channel_id=1, source_target_pairs={{0,48},{8,56},{16,32},{24,40},{32,16},{40,24},{48,0},{56,8},{64,11... | collective-permute-start | bytes 196616 | tf_op jit(solution)/shard_map/ppermute | solution.py:477
  144.3 13.3 %collective-permute-start.34 = (s16[256,128]{1,0:T(8,128)(2,1)S(1)}, s16[256,128]{1,0:T(8,128)(2,1)S(1)}, u32[]{:S(2)}, u32[]{:S(2)}) collective-permute-start(s16[256,128]{1,0:T(8,128)(2,1)S(1)} %get-tuple-element.113), channel_id=1, source_target_pairs={{0,32},{8,40},{16,48},{24,56},{32,0},{40,8},{48,16},{56,24},{64,96... | collective-permute-start | bytes 196616 | tf_op jit(solution)/shard_map/ppermute | solution.py:477
  154.3 4.3 %collective-permute-start.35 = (s16[256,128]{1,0:T(8,128)(2,1)S(1)}, s16[256,128]{1,0:T(8,128)(2,1)S(1)}, u32[]{:S(2)}, u32[]{:S(2)}) collective-permute-start(s16[256,128]{1,0:T(8,128)(2,1)S(1)} %get-tuple-element.114), channel_id=1, source_target_pairs={{0,16},{8,24},{16,0},{24,8},{32,48},{40,56},{48,32},{56,40},{64,80... | collective-permute-start | bytes 196616 | tf_op jit(solution)/shard_map/ppermute | solution.py:477

commit v4 on v3

--- a/solution.py
+++ b/solution.py
@@ -121,15 +121,6 @@
     code_edges((now_f, now_a), (one, two), level_ref)
 
 
-def decode_halo(in_ref, scale_ref, pad_ref, f, first, count_y):
-    per = count_y // GROUP
-    for layer in range(HALO):
-        for g in range(per):
-            spot = (f * HALO + layer) * per + g
-            code = in_ref[pl.ds(spot * GROUP, GROUP), :].astype(I32).astype(F32)
-            pad_ref[first + layer, pl.ds(PAD + g * GROUP, GROUP), :] = code * scale_ref[pl.ds(spot, 1), :]
-
-
 PAD = 8
 
 
@@ -164,6 +155,12 @@
         pad_ref[HALO + x, PAD : PAD + count_y, :] = field_ref[x]
 
 
+def clear_outer(pad_ref):
+    outer = jnp.zeros((HALO, *pad_ref.shape[1:]), F32)
+    pad_ref[0:HALO] = outer
+    pad_ref[pad_ref.shape[0] - HALO :] = outer
+
+
 def load_scales(in_ref, scale_ref):
     groups = scale_ref.shape[0]
     scale_ref[...] = decode_scale(in_ref[groups * GROUP :, :])
@@ -180,18 +177,13 @@
         ref[x, pl.ds(y, 1), :] = row + jnp.where(lane == source[0, 2], wave[start[0] + k], 0.0)
 
 
-def before_kernel(now_f, now_a, prev_f, prev_a, one, two, hit, *rest):
-    sum_f, sum_a, base_f, base_a, pad, scale_one, scale_two = rest
+def before_kernel(now_f, now_a, prev_f, prev_a, hit, sum_f, sum_a, base_f, base_a, pad):
     row_count, count_y, count_z = now_f.shape
     masks = lane_masks(TILE, count_z)
-    load_scales(one, scale_one)
-    load_scales(two, scale_two)
-    odd = odd_place()
+    clear_outer(pad)
     fields = ((now_f, prev_f, sum_f, base_f), (now_a, prev_a, sum_a, base_a))
     for f, (now, prev, total, base) in enumerate(fields):
         fill(pad, now)
-        decode_halo(one, scale_one, pad, f, (1 - odd) * (HALO + row_count), count_y)
-        decode_halo(two, scale_two, pad, f, odd * (HALO + row_count), count_y)
 
         @pl.loop(0, row_count)
         def _(x):
@@ -203,9 +195,31 @@
                 base[x, spot, :] = value + hit[x, spot, :] if f else value
 
 
+def halo_terms(in_ref, scale_ref, f, spot_y, count_y, low):
+    per = count_y // GROUP
+    rows = []
+    for j in range(HALO):
+        layer = j + low * (HALO - 1 - 2 * j)
+        spot = (f * HALO + layer) * per + spot_y // GROUP
+        code = in_ref[pl.ds(pl.multiple_of(spot * GROUP, GROUP), GROUP), :].astype(I32).astype(F32)
+        rows.append(code * scale_ref[pl.ds(spot, 1), :])
+    return [sum(COEFFS[r + j] * rows[j] for j in range(HALO - r)) for r in range(HALO)]
+
+
+def halo_tiles(refs, scales, row_count, count_y):
+    for ref, scale in zip(refs, scales):
+        load_scales(ref, scale)
+    odd = odd_place()
+    for y in range(0, count_y, GROUP):
+        for ref, scale, low in zip(refs, scales, (odd, 1 - odd)):
+            terms = [halo_terms(ref, scale, f, y, count_y, low) for f in range(2)]
+            for r in range(HALO):
+                yield row_count - 1 - r + low * (2 * r + 1 - row_count), y, terms[0][r], terms[1][r]
+
+
 def first_kernel(halves, anchors, source, begin, wave, sum_f, sum_a, base_f, base_a, *rest):
-    next_f, next_a, courant, one, two, slab, level = rest[-7:]
-    pieces = rest[:-7]
+    next_f, next_a, courant, one, two, slab, level, scale_one, scale_two = rest[-9:]
+    halos, pieces = rest[:2], rest[2:-9]
     row_count, count_y, _ = sum_f.shape
     band = pieces[0].shape[0] // (row_count * halves)
     side = len(pieces)
@@ -218,14 +232,12 @@
                 slab[x, pl.ds(start, band), :] = jnp.square(speed[:band])
                 slab[x + 1, pl.ds(start, band), :] = jnp.square(speed[band:])
 
-    @pl.loop(0, row_count)
-    def _(x):
-        for y in range(0, count_y, TILE):
-            spot = pl.ds(y, TILE)
-            factor = slab[x, pl.ds(anchors[0, 1] + y, TILE), :]
-            courant[x, spot, :] = factor
-            next_f[x, spot, :] = base_f[x, spot, :] + factor * sum_f[x, spot, :]
-            next_a[x, spot, :] = base_a[x, spot, :] + factor * sum_a[x, spot, :]
+    for x, y, term_f, term_a in halo_tiles(halos, (scale_one, scale_two), row_count, count_y):
+        spot = pl.ds(y, GROUP)
+        factor = slab[x, pl.ds(anchors[0, 1] + y, GROUP), :]
+        courant[x, spot, :] = factor
+        next_f[x, spot, :] = base_f[x, spot, :] + factor * (sum_f[x, spot, :] + term_f)
+        next_a[x, spot, :] = base_a[x, spot, :] + factor * (sum_a[x, spot, :] + term_a)
 
     add_source(source, begin, wave, next_f, 0)
     code_edges((next_f, next_a), (one, two), level)
@@ -234,9 +246,7 @@
 def between_kernel(p1, q1, p0, q0, prev_f, courant, hit, part_f, part_a, bend, pad):
     row_count, count_y, count_z = p1.shape
     masks = lane_masks(TILE, count_z)
-    outer = jnp.zeros((HALO, pad.shape[1], count_z), F32)
-    pad[0:HALO] = outer
-    pad[HALO + row_count :] = outer
+    clear_outer(pad)
     for f, (now, out) in enumerate(((p1, part_f), (q1, part_a))):
         fill(pad, now)
 
@@ -253,40 +263,20 @@
                 out[x, spot, :] = value
 
 
-def halo_terms(in_ref, scale_ref, f, spot_y, count_y, low):
-    per = count_y // GROUP
-    rows = []
-    for j in range(HALO):
-        layer = j + low * (HALO - 1 - 2 * j)
-        spot = (f * HALO + layer) * per + spot_y // GROUP
-        code = in_ref[pl.ds(pl.multiple_of(spot * GROUP, GROUP), GROUP), :].astype(I32).astype(F32)
-        rows.append(code * scale_ref[pl.ds(spot, 1), :])
-    return [sum(COEFFS[r + j] * rows[j] for j in range(HALO - r)) for r in range(HALO)]
-
-
 def second_kernel(groups, anchors, source, begin, wave, p1, q1, p0, courant, part_f, part_a, bend, one, two, *rest):
     next_f, next_a, own = rest[:3]
     sends = rest[3 : 2 + groups]
     frame, scale_one, scale_two = rest[2 + groups :]
     row_count, count_y, count_z = p1.shape
     band = own.shape[0] // row_count
-    load_scales(one, scale_one)
-    load_scales(two, scale_two)
-    odd = odd_place()
     edge = (frame.shape[1] - count_y) // 2
     frame[:, 0:edge, :] = jnp.zeros((row_count, edge, count_z), F32)
     frame[:, edge + count_y :, :] = jnp.zeros((row_count, edge, count_z), F32)
-    for y in range(0, count_y, GROUP):
+    for x, y, term_f, term_a in halo_tiles((one, two), (scale_one, scale_two), row_count, count_y):
         spot = pl.ds(y, GROUP)
-        for ref, scale, low in ((one, scale_one, odd), (two, scale_two, 1 - odd)):
-            for f in range(2):
-                for r, term in enumerate(halo_terms(ref, scale, f, y, count_y, low)):
-                    x = row_count - 1 - r + low * (2 * r + 1 - row_count)
-                    term = courant[x, spot, :] * term
-                    if f == 0:
-                        frame[x, pl.ds(edge + y, GROUP), :] = part_f[x, spot, :] + term
-                    else:
-                        next_a[x, spot, :] = part_a[x, spot, :] + term
+        factor = courant[x, spot, :]
+        frame[x, pl.ds(edge + y, GROUP), :] = part_f[x, spot, :] + factor * term_f
+        next_a[x, spot, :] = part_a[x, spot, :] + factor * term_a
 
     add_source(source, begin, wave, frame, 1, edge)
 
@@ -516,22 +506,26 @@
     from_one = lax.ppermute(one, "dom", one_pairs)
     from_two = lax.ppermute(two, "dom", two_pairs)
 
-    (line,) = call(join_kernel, (struct((len(near) * block, count_z), BF16),), near, "v" * len(near))
-    line, other, one = lax.optimization_barrier((line, other, one))
+    lines = []
+    for part in range(HALVES):
+        blocks = near[part * SIZE_Z : (part + 1) * SIZE_Z]
+        lines += call(join_kernel, (struct((SIZE_Z * block, count_z), BF16),), blocks, "v" * SIZE_Z)
+    lines[1], other, one = lax.optimization_barrier((lines[1], other, one))
     field = struct((row_count, count_y, count_z), F32)
     hits = call(hit_kernel, (field, field), (start_step, receivers[0], traces[0]), "svv")
-    plane = [line] + exchange([line] * (SIZE_X - 1), "shot", along["x"])
-    plane = list(lax.optimization_barrier((*plane, hits[0])))[:SIZE_X]
+    padded = pltpu.VMEM((row_count + 2 * HALO, count_y + 2 * PAD, count_z), F32)
+    sums = call(before_kernel, (field,) * 4, (p0, q0, p_prev, q_prev, hits[0]), "v" * 5, (padded,))
+    planes = [[line] + exchange([line] * (SIZE_X - 1), "shot", along["x"]) for line in lines]
+    planes[1] = list(lax.optimization_barrier((*planes[1], sums[0])))[:SIZE_X]
+    plane = planes[0] + planes[1]
     plane += [lax.ppermute(part, "shot", swap("c", 1)) for part in plane]
     *plane, from_one, from_two = lax.optimization_barrier((*plane, from_one, from_two))
     layout = [
-        [(dx, k % SIZE_Z, dc, k // SIZE_Z) for k in range(HALVES * SIZE_Z)]
+        [(dx, dz, dc, dh) for dz in range(SIZE_Z)]
         for dc in range(SIZE_C)
+        for dh in range(HALVES)
         for dx in range(SIZE_X)
     ]
-    span = -(-(row_count * groups + own_rows - 1) // own_rows)
-    span += span % SIZE_C
-    table = pltpu.VMEM((span * block, count_z), F32)
     side = groups // HALVES
     pieces = call(
         functools.partial(pick_kernel, layout, row_count, HALVES),
@@ -542,22 +536,14 @@
     )
     pieces = [pieces[0]] + exchange(pieces[1:], "dom", between)[::-1]
 
-    padded = pltpu.VMEM((row_count + 2 * HALO, count_y + 2 * PAD, count_z), F32)
     scale = pltpu.VMEM((2 * HALO * count_y // GROUP, count_z), F32)
     slab = pltpu.VMEM((row_count, groups * band, count_z), F32)
-    sums = call(
-        before_kernel,
-        (field,) * 4,
-        (p0, q0, p_prev, q_prev, from_one, from_two, hits[0]),
-        "v" * 7,
-        (padded, scale, scale),
-    )
     p1, q1, courant, one, two = call(
         functools.partial(first_kernel, HALVES),
         (field, field, field, code, code),
-        (*scalars, *sums, *pieces),
-        "ssss" + "v" * (4 + side),
-        (slab, levels),
+        (*scalars, *sums, from_one, from_two, *pieces),
+        "ssss" + "v" * (6 + side),
+        (slab, levels, scale, scale),
     )
     from_one = lax.ppermute(one, "dom", one_pairs)
     from_two = lax.ppermute(two, "dom", two_pairs)
@@ -569,6 +555,9 @@
         (padded,),
     )
 
+    span = -(-(row_count * groups + own_rows - 1) // own_rows)
+    span += span % SIZE_C
+    table = pltpu.VMEM((span * block, count_z), F32)
     edge = groups * band - count_y
     coded = struct((code_rows_of(row_count, band), count_z), I16)
     frame = pltpu.VMEM((row_count, count_y + 2 * edge, count_z), F32)

time: 160 us -> 180 us (1.12)
  starting transfers between devices: 78.4 us -> 86.4 us
  waiting for transfers between devices: 51.2 us -> 58.6 us
  local copies, waits for them, and re-layouts: 3.16 us -> 5.59 us
    ppermute x26 -> x29, waiting for transfers between devices: 40.1 us -> 48.4 us  [exchange(): got[k] = lax.ppermute(parts[k - 1], axis, pairs(k))]
    ppermute x26 -> x29, starting transfers between devices: 72.8 us -> 78.6 us  [exchange(): got[k] = lax.ppermute(parts[k - 1], axis, pairs(k))]
    unnamed x25, local copies, waits for them, and re-layouts: 3.16 us -> 5.59 us
    pallas_call x12 -> x13, Pallas kernels: 24.9 us -> 26.2 us  [call(): pl.pallas_call(kernel, out_shape=list(outs), in_specs=[smem() if s == 's'...]
  transfers between devices with their start and end apart: 36 -> 43, of which waited for: 20 -> 22; matrix products, arithmetic and copies ran while one was open for 0% -> 0% of each run, Pallas kernels for 10% -> 9%
where the time goes in v4:
time: 180 us; the launch traced here: 178 us
  starting transfers between devices  86.4 us (48%)
  waiting for transfers between devices  58.6 us (33%)
  Pallas kernels  26.2 us (15%)
  local copies, waits for them, and re-layouts  5.59 us (3%)
    ppermute x29, starting transfers between devices, exchange(): got[k] = lax.ppermute(parts[k - 1], axis, pairs(k))  78.6 us
    ppermute x29, waiting for transfers between devices, exchange(): got[k] = lax.ppermute(parts[k - 1], axis, pairs(k))  48.4 us
    pallas_call x13, Pallas kernels, call(): pl.pallas_call(kernel, out_shape=list(outs), in_specs=[smem() if s == 's'...  26.2 us
    unnamed x25, local copies, waits for them, and re-layouts  5.59 us
    ppermute x2, waiting for transfers between devices, body(): from_one = lax.ppermute(one, 'dom', one_pairs)  5.33 us
    ppermute x2, starting transfers between devices, body(): from_one = lax.ppermute(one, 'dom', one_pairs)  4.33 us
  transfers between devices with their start and end apart: 43, of which 22 were waited for; matrix products, arithmetic and copies ran while one was open for 0% of the time, Pallas kernels for 9%

profile of v4, /device:TPU:6, one launch (start us, length us, event | category | flops | bytes accessed | tf_op | source)
XLA Modules:
  0.0 178.3 jit_solution(5873266452471069598)
XLA Ops:
  0.6 4.7 %collective-permute-start.2 = (bf16[240,128]{1,0:T(8,128)(2,1)}, bf16[240,128]{1,0:T(8,128)(2,1)S(1)}, u32[]{:S(2)}, u32[]{:S(2)}) collective-permute-start(bf16[240,128]{1,0:T(8,128)(2,1)} %bitcast.5.refs_0_), channel_id=1, source_target_pairs={{0,48},{1,49},{2,50},{3,51},{4,52},{5,53},{6,54},{7,55},{8,56},{9,... | collective-permute-start | bytes 184328 | tf_op jit(solution)/shard_map/ppermute | solution.py:467
  6.0 2.3 %collective-permute-done.2.refs_3_ = bf16[240,128]{1,0:T(8,128)(2,1)S(1)} collective-permute-done((bf16[240,128]{1,0:T(8,128)(2,1)}, bf16[240,128]{1,0:T(8,128)(2,1)S(1)}, u32[]{:S(2)}, u32[]{:S(2)}) %collective-permute-start.2) | collective-permute-done | bytes 61472 | tf_op jit(solution)/shard_map/ppermute | solution.py:467
  8.3 2.4 %collective-permute-done.1.refs_2_ = bf16[240,128]{1,0:T(8,128)(2,1)S(1)} collective-permute-done((bf16[240,128]{1,0:T(8,128)(2,1)}, bf16[240,128]{1,0:T(8,128)(2,1)S(1)}, u32[]{:S(2)}, u32[]{:S(2)}) %collective-permute-start.1) | collective-permute-done | bytes 61472 | tf_op jit(solution)/shard_map/ppermute | solution.py:467
  11.0 0.8 shard_map.132.refs_0_
  12.6 2.4 %collective-permute-start.4 = (bf16[960,128]{1,0:T(8,128)(2,1)S(1)}, bf16[960,128]{1,0:T(8,128)(2,1)S(1)}, u32[]{:S(2)}, u32[]{:S(2)}) collective-permute-start(bf16[960,128]{1,0:T(8,128)(2,1)S(1)} %shard_map.132.refs_0_), channel_id=1, source_target_pairs={{0,128},{8,136},{16,144},{24,152},{32,160},{40,168},{48,176},{56,1... | collective-permute-start | bytes 737288 | tf_op jit(solution)/shard_map/ppermute | solution.py:467
  15.0 4.4 %collective-permute-start.9 = (bf16[240,128]{1,0:T(8,128)(2,1)}, bf16[240,128]{1,0:T(8,128)(2,1)S(1)}, u32[]{:S(2)}, u32[]{:S(2)}) collective-permute-start(bf16[240,128]{1,0:T(8,128)(2,1)} %bitcast.5.refs_0_), channel_id=1, source_target_pairs={{0,52},{1,53},{2,54},{3,55},{4,48},{5,49},{6,50},{7,51},{8,60},{9,... | collective-permute-start | bytes 184328 | tf_op jit(solution)/shard_map/ppermute | solution.py:467
  19.4 1.1 collective-permute-done.10.other
  20.6 3.3 %collective-permute-done.9.refs_3_ = bf16[240,128]{1,0:T(8,128)(2,1)S(1)} collective-permute-done((bf16[240,128]{1,0:T(8,128)(2,1)}, bf16[240,128]{1,0:T(8,128)(2,1)S(1)}, u32[]{:S(2)}, u32[]{:S(2)}) %collective-permute-start.9) | collective-permute-done | bytes 61472 | tf_op jit(solution)/shard_map/ppermute | solution.py:467
  23.9 2.8 %collective-permute-start.7 = (bf16[240,128]{1,0:T(8,128)(2,1)}, bf16[240,128]{1,0:T(8,128)(2,1)S(1)}, u32[]{:S(2)}, u32[]{:S(2)}) collective-permute-start(bf16[240,128]{1,0:T(8,128)(2,1)} %bitcast.5.refs_0_), channel_id=1, source_target_pairs={{0,20},{1,21},{2,22},{3,23},{4,16},{5,17},{6,18},{7,19},{8,28},{9,... | collective-permute-start | bytes 184328 | tf_op jit(solution)/shard_map/ppermute | solution.py:467
  27.0 2.1 %collective-permute-start.6 = (bf16[240,128]{1,0:T(8,128)(2,1)}, bf16[240,128]{1,0:T(8,128)(2,1)S(1)}, u32[]{:S(2)}, u32[]{:S(2)}) collective-permute-start(bf16[240,128]{1,0:T(8,128)(2,1)} %bitcast.5.refs_0_), channel_id=1, source_target_pairs={{0,4},{1,5},{2,6},{3,7},{4,0},{5,1},{6,2},{7,3},{8,12},{9,13},{10,... | collective-permute-start | bytes 184328 | tf_op jit(solution)/shard_map/ppermute | solution.py:467
  29.1 1.2 copy-done
  30.3 1.2 copy-done.2
  33.0 2.4 %collective-permute-done.6.refs_0_ = bf16[240,128]{1,0:T(8,128)(2,1)S(1)} collective-permute-done((bf16[240,128]{1,0:T(8,128)(2,1)}, bf16[240,128]{1,0:T(8,128)(2,1)S(1)}, u32[]{:S(2)}, u32[]{:S(2)}) %collective-permute-start.6) | collective-permute-done | bytes 61472 | tf_op jit(solution)/shard_map/ppermute | solution.py:467
  35.4 2.1 %collective-permute-start.22 = (s16[2112,128]{1,0:T(8,128)(2,1)S(1)}, s16[2112,128]{1,0:T(8,128)(2,1)S(1)}, u32[]{:S(2)}, u32[]{:S(2)}) collective-permute-start(s16[2112,128]{1,0:T(8,128)(2,1)S(1)} %get-tuple-element.72), channel_id=1, source_target_pairs={{0,1},{1,0},{2,3},{3,2},{4,5},{5,4},{6,7},{7,6},{8,9},{9,8},{10,11... | collective-permute-start | bytes 1622024 | tf_op jit(solution)/shard_map/ppermute | solution.py:506
  37.5 1.2 collective-permute-start.13
  38.7 2.1 %collective-permute-start.12 = (bf16[960,128]{1,0:T(8,128)(2,1)S(1)}, bf16[960,128]{1,0:T(8,128)(2,1)S(1)}, u32[]{:S(2)}, u32[]{:S(2)}) collective-permute-start(bf16[960,128]{1,0:T(8,128)(2,1)S(1)} %shard_map.133.refs_4_), channel_id=1, source_target_pairs={{0,128},{8,136},{16,144},{24,152},{32,160},{40,168},{48,176},{56,1... | collective-permute-start | bytes 737288 | tf_op jit(solution)/shard_map/ppermute | solution.py:467
  41.7 8.0 %collective-permute-done.13.refs_7_ = bf16[960,128]{1,0:T(8,128)(2,1)S(1)} collective-permute-done((bf16[960,128]{1,0:T(8,128)(2,1)S(1)}, bf16[960,128]{1,0:T(8,128)(2,1)S(1)}, u32[]{:S(2)}, u32[]{:S(2)}) %collective-permute-start.13) | collective-permute-done | bytes 245792 | tf_op jit(solution)/shard_map/ppermute | solution.py:467
  51.0 3.4 %shard_map.130 = (f32[8,256,128]{2,1,0:T(8,128)S(1)}, f32[8,256,128]{2,1,0:T(8,128)S(1)}) custom-call(s32[1]{0:T(128)S(6)} %copy.17.begin, s32[3,512]{1,0:T(4,128)S(1)} %bitcast.23, f32[64,512]{1,0:T(8,128)S(1)} %bitcast.22), custom_call_target="tpu_custom_call" | custom-call | tf_op jit(solution)/shard_map/pallas_call | solution.py:36
  54.4 1.2 copy-done.4
  55.6 1.2 copy-done.6
  56.8 6.0 %shard_map.131 = (f32[8,256,128]{2,1,0:T(8,128)S(1)}, f32[8,256,128]{2,1,0:T(8,128)S(1)}, f32[8,256,128]{2,1,0:T(8,128)S(1)}, f32[8,256,128]{2,1,0:T(8,128)S(1)}) custom-call(f32[8,256,128]{2,1,0:T(8,128)S(1)} %bitcast.13, f32[8,256,128]{2,1,0:T(8,128)S(1)} %bitcast.17, f32[8,256,128]{2,1,0:T(8,128)S(1)} %bitcast.19, f32[8,256,128]{2,1,0:T(8,128)S(1)} %bitcast.21, ...), custom_call_target="tpu_custom_call" | custom-call | tf_op jit(solution)/shard_map/pallas_call | solution.py:36
  64.7 0.8 collective-permute-done.15.refs_9_
  66.2 1.2 shard_map.135
  67.4 4.3 %collective-permute-start.24 = (bf16[640,128]{1,0:T(8,128)(2,1)S(1)}, bf16[640,128]{1,0:T(8,128)(2,1)S(1)}, u32[]{:S(2)}, u32[]{:S(2)}) collective-permute-start(bf16[640,128]{1,0:T(8,128)(2,1)S(1)} %get-tuple-element.98), channel_id=1, source_target_pairs={{0,3},{1,2},{2,1},{3,0},{4,7},{5,6},{6,5},{7,4},{8,11},{9,10},{10,... | collective-permute-start | bytes 491528 | tf_op jit(solution)/shard_map/ppermute | solution.py:467
  71.8 1.2 collective-permute-start.25
  73.0 6.6 %collective-permute-done.24.rest_3_ = bf16[640,128]{1,0:T(8,128)(2,1)S(1)} collective-permute-done((bf16[640,128]{1,0:T(8,128)(2,1)S(1)}, bf16[640,128]{1,0:T(8,128)(2,1)S(1)}, u32[]{:S(2)}, u32[]{:S(2)}) %collective-permute-start.24) | collective-permute-done | bytes 163872 | tf_op jit(solution)/shard_map/ppermute | solution.py:467
  81.5 2.0 %shard_map.136 = (f32[8,256,128]{2,1,0:T(8,128)S(1)}, f32[8,256,128]{2,1,0:T(8,128)S(1)}, f32[8,256,128]{2,1,0:T(8,128)S(1)}, s16[2112,128]{1,0:T(8,128)(2,1)S(1)}, s16[2112,128]{1,0:T(8,128)(2,1)S(1)}) custom-call(s32[1,2]{1,0:T(1,128)S(1)} %copy-done.8, s32[1,3]{1,0:T(1,128)S(1)} %copy-done.9, s32[1]{0:T(128)S(6)} %copy.17.begin, f32[64]{0:T(128)S(1)} %copy-done.10, ...), custom_call_target="tpu_custom_call" | custom-call | tf_op jit(solution)/shard_map/pallas_call | solution.py:36
  83.5 2.2 %collective-permute-start.27 = (s16[2112,128]{1,0:T(8,128)(2,1)S(1)}, s16[2112,128]{1,0:T(8,128)(2,1)S(1)}, u32[]{:S(2)}, u32[]{:S(2)}) collective-permute-start(s16[2112,128]{1,0:T(8,128)(2,1)S(1)} %get-tuple-element.108), channel_id=1, source_target_pairs={{0,1},{1,0},{2,3},{3,2},{4,5},{5,4},{6,7},{7,6},{8,9},{9,8},{10,11... | collective-permute-start | bytes 1622024 | tf_op jit(solution)/shard_map/ppermute | solution.py:548
  86.4 5.9 %shard_map.137 = (f32[8,256,128]{2,1,0:T(8,128)S(1)}, f32[8,256,128]{2,1,0:T(8,128)S(1)}, f32[8,256,128]{2,1,0:T(8,128)S(1)}) custom-call(f32[8,256,128]{2,1,0:T(8,128)S(1)} %get-tuple-element.101.p1, f32[8,256,128]{2,1,0:T(8,128)S(1)} %get-tuple-element.102.q1, f32[8,256,128]{2,1,0:T(8,128)S(1)} %bitcast.14, f32[8,256,128]{2,1,0:T(8,128)S(1)} %bitcast.18, ...), custom_call_target="tpu_custom_call" | custom-call | tf_op jit(solution)/shard_map/pallas_call | solution.py:36
  92.4 5.3 %collective-permute-done.27.one = s16[2112,128]{1,0:T(8,128)(2,1)S(1)} collective-permute-done((s16[2112,128]{1,0:T(8,128)(2,1)S(1)}, s16[2112,128]{1,0:T(8,128)(2,1)S(1)}, u32[]{:S(2)}, u32[]{:S(2)}) %collective-permute-start.27) | collective-permute-done | bytes 540704 | tf_op jit(solution)/shard_map/ppermute | solution.py:548
  97.7 3.1 %shard_map.138 = (f32[8,256,128]{2,1,0:T(8,128)}, f32[8,256,128]{2,1,0:T(8,128)}, f32[320,128]{1,0:T(8,128)S(1)}, s16[336,128]{1,0:T(8,128)(2,1)S(1)}, s16[336,1...) custom-call(s32[1,2]{1,0:T(1,128)S(1)} %copy-done.8, ...), custom_call_target="tpu_custom_call" | custom-call | tf_op jit(solution)/shard_map/pallas_call | solution.py:36
  100.8 4.0 %collective-permute-start.29 = (s16[336,128]{1,0:T(8,128)(2,1)S(1)}, s16[336,128]{1,0:T(8,128)(2,1)S(1)}, u32[]{:S(2)}, u32[]{:S(2)}) collective-permute-start(s16[336,128]{1,0:T(8,128)(2,1)S(1)} %get-tuple-element.114), channel_id=1, source_target_pairs={{0,7},{1,6},{2,5},{3,4},{4,3},{5,2},{6,1},{7,0},{8,15},{9,14},{10,... | collective-permute-start | bytes 258056 | tf_op jit(solution)/shard_map/ppermute | solution.py:467
  104.8 6.5 %collective-permute-start.30 = (s16[336,128]{1,0:T(8,128)(2,1)S(1)}, s16[336,128]{1,0:T(8,128)(2,1)S(1)}, u32[]{:S(2)}, u32[]{:S(2)}) collective-permute-start(s16[336,128]{1,0:T(8,128)(2,1)S(1)} %get-tuple-element.115), channel_id=1, source_target_pairs={{0,6},{1,7},{2,4},{3,5},{4,2},{5,3},{6,0},{7,1},{8,14},{9,15},{10,... | collective-permute-start | bytes 258056 | tf_op jit(solution)/shard_map/ppermute | solution.py:467
  111.3 10.5 %collective-permute-start.31 = (s16[336,128]{1,0:T(8,128)(2,1)S(1)}, s16[336,128]{1,0:T(8,128)(2,1)S(1)}, u32[]{:S(2)}, u32[]{:S(2)}) collective-permute-start(s16[336,128]{1,0:T(8,128)(2,1)S(1)} %get-tuple-element.116), channel_id=1, source_target_pairs={{0,5},{1,4},{2,7},{3,6},{4,1},{5,0},{6,3},{7,2},{8,13},{9,12},{10,... | collective-permute-start | bytes 258056 | tf_op jit(solution)/shard_map/ppermute | solution.py:467
  121.9 4.6 %collective-permute-start.33 = (s16[336,128]{1,0:T(8,128)(2,1)S(1)}, s16[336,128]{1,0:T(8,128)(2,1)S(1)}, u32[]{:S(2)}, u32[]{:S(2)}) collective-permute-start(s16[336,128]{1,0:T(8,128)(2,1)S(1)} %get-tuple-element.118), channel_id=1, source_target_pairs={{0,3},{1,2},{2,1},{3,0},{4,7},{5,6},{6,5},{7,4},{8,11},{9,10},{10,... | collective-permute-start | bytes 258056 | tf_op jit(solution)/shard_map/ppermute | solution.py:467
  126.5 0.9 collective-permute-start.35
  127.3 2.9 %collective-permute-done.32.refs_3_ = s16[336,128]{1,0:T(8,128)(2,1)S(1)} collective-permute-done((s16[336,128]{1,0:T(8,128)(2,1)S(1)}, s16[336,128]{1,0:T(8,128)(2,1)S(1)}, u32[]{:S(2)}, u32[]{:S(2)}) %collective-permute-start.32) | collective-permute-done | bytes 86048 | tf_op jit(solution)/shard_map/ppermute | solution.py:467
  130.3 2.2 %collective-permute-done.34.refs_5_ = s16[336,128]{1,0:T(8,128)(2,1)S(1)} collective-permute-done((s16[336,128]{1,0:T(8,128)(2,1)S(1)}, s16[336,128]{1,0:T(8,128)(2,1)S(1)}, u32[]{:S(2)}, u32[]{:S(2)}) %collective-permute-start.34) | collective-permute-done | bytes 86048 | tf_op jit(solution)/shard_map/ppermute | solution.py:467
  132.5 0.9 shard_map.139
  133.4 2.2 %collective-permute-done.36.got = f32[1440,128]{1,0:T(8,128)S(1)} collective-permute-done((f32[1440,128]{1,0:T(8,128)S(1)}, f32[1440,128]{1,0:T(8,128)S(1)}, u32[]{:S(2)}, u32[]{:S(2)}) %collective-permute-start.36) | collective-permute-done | bytes 737312 | tf_op jit(solution)/shard_map/ppermute | solution.py:581
  135.6 1.3 shard_map.140
  136.9 3.1 %collective-permute-start.37 = (s16[992,128]{1,0:T(8,128)(2,1)S(1)}, s16[992,128]{1,0:T(8,128)(2,1)S(1)}, u32[]{:S(2)}, u32[]{:S(2)}) collective-permute-start(s16[992,128]{1,0:T(8,128)(2,1)S(1)} %get-tuple-element.124), channel_id=1, source_target_pairs={{0,192},{8,200},{16,208},{24,216},{32,224},{40,232},{48,240},{56,2... | collective-permute-start | bytes 761864 | tf_op jit(solution)/shard_map/ppermute | solution.py:467
  140.0 1.3 collective-permute-start.38
  141.3 10.5 %collective-permute-done.37.refs_0_ = s16[992,128]{1,0:T(8,128)(2,1)S(1)} collective-permute-done((s16[992,128]{1,0:T(8,128)(2,1)S(1)}, s16[992,128]{1,0:T(8,128)(2,1)S(1)}, u32[]{:S(2)}, u32[]{:S(2)}) %collective-permute-start.37) | collective-permute-done | bytes 253984 | tf_op jit(solution)/shard_map/ppermute | solution.py:467
  151.9 1.0 collective-permute-done.39.refs_2_
  153.2 2.0 %collective-permute-start.40 = (s16[256,128]{1,0:T(8,128)(2,1)S(1)}, s16[256,128]{1,0:T(8,128)(2,1)S(1)}, u32[]{:S(2)}, u32[]{:S(2)}) collective-permute-start(s16[256,128]{1,0:T(8,128)(2,1)S(1)} %get-tuple-element.128), channel_id=1, source_target_pairs={{0,48},{8,56},{16,32},{24,40},{32,16},{40,24},{48,0},{56,8},{64,11... | collective-permute-start | bytes 196616 | tf_op jit(solution)/shard_map/ppermute | solution.py:467
  155.2 18.1 %collective-permute-start.41 = (s16[256,128]{1,0:T(8,128)(2,1)S(1)}, s16[256,128]{1,0:T(8,128)(2,1)S(1)}, u32[]{:S(2)}, u32[]{:S(2)}) collective-permute-start(s16[256,128]{1,0:T(8,128)(2,1)S(1)} %get-tuple-element.129), channel_id=1, source_target_pairs={{0,32},{8,40},{16,48},{24,56},{32,0},{40,8},{48,16},{56,24},{64,96... | collective-permute-start | bytes 196616 | tf_op jit(solution)/shard_map/ppermute | solution.py:467
  173.3 4.3 %collective-permute-done.41.refs_1_ = s16[256,128]{1,0:T(8,128)(2,1)S(1)} collective-permute-done((s16[256,128]{1,0:T(8,128)(2,1)S(1)}, s16[256,128]{1,0:T(8,128)(2,1)S(1)}, u32[]{:S(2)}, u32[]{:S(2)}) %collective-permute-start.41) | collective-permute-done | bytes 65568 | tf_op jit(solution)/shard_map/ppermute | solution.py:467
  (76 shorter events, 11.3 us)
Async XLA Ops:
  0.6 18.7 %copy-start.8 = (s32[1,2]{1,0:T(1,128)S(1)}, s32[1,2]{1,0:T(1,128)}, u32[]{:S(2)}) copy-start(s32[1,2]{1,0:T(1,128)} %anchors.9) | copy-start | bytes 28
  0.6 7.7 %collective-permute-start.2 = (bf16[240,128]{1,0:T(8,128)(2,1)}, bf16[240,128]{1,0:T(8,128)(2,1)S(1)}, u32[]{:S(2)}, u32[]{:S(2)}) collective-permute-start(bf16[240,128]{1,0:T(8,128)(2,1)} %bitcast.5.refs_0_), channel_id=1, source_target_pairs={{0,48},{1,49},{2,50},{3,51},{4,52},{5,53},{6,54},{7,55},{8,56},{9,... | collective-permute-start | bytes 184328 | tf_op jit(solution)/shard_map/ppermute | solution.py:467
  5.4 5.4 %collective-permute-start.1 = (bf16[240,128]{1,0:T(8,128)(2,1)}, bf16[240,128]{1,0:T(8,128)(2,1)S(1)}, u32[]{:S(2)}, u32[]{:S(2)}) collective-permute-start(bf16[240,128]{1,0:T(8,128)(2,1)} %bitcast.5.refs_0_), channel_id=1, source_target_pairs={{0,32},{1,33},{2,34},{3,35},{4,36},{5,37},{6,38},{7,39},{8,40},{9,... | collective-permute-start | bytes 184328 | tf_op jit(solution)/shard_map/ppermute | solution.py:467
  5.4 5.7 %collective-permute-start = (bf16[240,128]{1,0:T(8,128)(2,1)}, bf16[240,128]{1,0:T(8,128)(2,1)S(1)}, u32[]{:S(2)}, u32[]{:S(2)}) collective-permute-start(bf16[240,128]{1,0:T(8,128)(2,1)} %bitcast.5.refs_0_), channel_id=1, source_target_pairs={{0,16},{1,17},{2,18},{3,19},{4,20},{5,21},{6,22},{7,23},{8,24},{9,... | collective-permute-start | bytes 184328 | tf_op jit(solution)/shard_map/ppermute | solution.py:467
  11.9 25.6 %collective-permute-start.14 = (bf16[960,128]{1,0:T(8,128)(2,1)S(1)}, bf16[960,128]{1,0:T(8,128)(2,1)S(1)}, u32[]{:S(2)}, u32[]{:S(2)}) collective-permute-start(bf16[960,128]{1,0:T(8,128)(2,1)S(1)} %shard_map.132.refs_0_), channel_id=1, source_target_pairs={{0,8},{8,0},{16,24},{24,16},{32,40},{40,32},{48,56},{56,48},{64,72... | collective-permute-start | bytes 737288 | tf_op jit(solution)/shard_map/ppermute | solution.py:521
  12.0 26.7 %collective-permute-start.5 = (bf16[960,128]{1,0:T(8,128)(2,1)S(1)}, bf16[960,128]{1,0:T(8,128)(2,1)S(1)}, u32[]{:S(2)}, u32[]{:S(2)}) collective-permute-start(bf16[960,128]{1,0:T(8,128)(2,1)S(1)} %shard_map.132.refs_0_), channel_id=1, source_target_pairs={{0,192},{8,200},{16,208},{24,216},{32,224},{40,232},{48,240},{56,2... | collective-permute-start | bytes 737288 | tf_op jit(solution)/shard_map/ppermute | solution.py:467
  12.6 28.2 %collective-permute-start.4 = (bf16[960,128]{1,0:T(8,128)(2,1)S(1)}, bf16[960,128]{1,0:T(8,128)(2,1)S(1)}, u32[]{:S(2)}, u32[]{:S(2)}) collective-permute-start(bf16[960,128]{1,0:T(8,128)(2,1)S(1)} %shard_map.132.refs_0_), channel_id=1, source_target_pairs={{0,128},{8,136},{16,144},{24,152},{32,160},{40,168},{48,176},{56,1... | collective-permute-start | bytes 737288 | tf_op jit(solution)/shard_map/ppermute | solution.py:467
  15.0 8.9 %collective-permute-start.9 = (bf16[240,128]{1,0:T(8,128)(2,1)}, bf16[240,128]{1,0:T(8,128)(2,1)S(1)}, u32[]{:S(2)}, u32[]{:S(2)}) collective-permute-start(bf16[240,128]{1,0:T(8,128)(2,1)} %bitcast.5.refs_0_), channel_id=1, source_target_pairs={{0,52},{1,53},{2,54},{3,55},{4,48},{5,49},{6,50},{7,51},{8,60},{9,... | collective-permute-start | bytes 184328 | tf_op jit(solution)/shard_map/ppermute | solution.py:467
  19.3 1.1 collective-permute-start.10
  20.5 6.5 %collective-permute-start.8 = (bf16[240,128]{1,0:T(8,128)(2,1)}, bf16[240,128]{1,0:T(8,128)(2,1)S(1)}, u32[]{:S(2)}, u32[]{:S(2)}) collective-permute-start(bf16[240,128]{1,0:T(8,128)(2,1)} %bitcast.5.refs_0_), channel_id=1, source_target_pairs={{0,36},{1,37},{2,38},{3,39},{4,32},{5,33},{6,34},{7,35},{8,44},{9,... | collective-permute-start | bytes 184328 | tf_op jit(solution)/shard_map/ppermute | solution.py:467
  23.9 8.2 %collective-permute-start.7 = (bf16[240,128]{1,0:T(8,128)(2,1)}, bf16[240,128]{1,0:T(8,128)(2,1)S(1)}, u32[]{:S(2)}, u32[]{:S(2)}) collective-permute-start(bf16[240,128]{1,0:T(8,128)(2,1)} %bitcast.5.refs_0_), channel_id=1, source_target_pairs={{0,20},{1,21},{2,22},{3,23},{4,16},{5,17},{6,18},{7,19},{8,28},{9,... | collective-permute-start | bytes 184328 | tf_op jit(solution)/shard_map/ppermute | solution.py:467
  27.0 8.4 %collective-permute-start.6 = (bf16[240,128]{1,0:T(8,128)(2,1)}, bf16[240,128]{1,0:T(8,128)(2,1)S(1)}, u32[]{:S(2)}, u32[]{:S(2)}) collective-permute-start(bf16[240,128]{1,0:T(8,128)(2,1)} %bitcast.5.refs_0_), channel_id=1, source_target_pairs={{0,4},{1,5},{2,6},{3,7},{4,0},{5,1},{6,2},{7,3},{8,12},{9,13},{10,... | collective-permute-start | bytes 184328 | tf_op jit(solution)/shard_map/ppermute | solution.py:467
  31.6 22.8 %copy-start.1 = (f32[1,8,256,128]{3,2,1,0:T(8,128)S(1)}, f32[1,8,256,128]{3,2,1,0:T(8,128)}, u32[]{:S(2)}) copy-start(f32[1,8,256,128]{3,2,1,0:T(8,128)} %param.19) | copy-start | bytes 3145732
  31.6 22.8 %copy-start.3 = (f32[1,8,256,128]{3,2,1,0:T(8,128)S(1)}, f32[1,8,256,128]{3,2,1,0:T(8,128)}, u32[]{:S(2)}) copy-start(f32[1,8,256,128]{3,2,1,0:T(8,128)} %param.21) | copy-start | bytes 3145732
  32.1 31.5 %collective-permute-start.23 = (s16[2112,128]{1,0:T(8,128)(2,1)S(1)}, s16[2112,128]{1,0:T(8,128)(2,1)S(1)}, u32[]{:S(2)}, u32[]{:S(2)}) collective-permute-start(s16[2112,128]{1,0:T(8,128)(2,1)S(1)} %get-tuple-element.78), channel_id=1, source_target_pairs={{1,2},{3,4},{5,6},{2,1},{4,3},{6,5},{9,10},{11,12},{13,14},{10,9},... | collective-permute-start | bytes 1622024 | tf_op jit(solution)/shard_map/ppermute | solution.py:507
  35.4 15.6 %copy-start.7 = (f32[1,64,512]{2,1,0:T(8,128)S(1)}, f32[1,64,512]{2,1,0:T(8,128)}, u32[]{:S(2)}) copy-start(f32[1,64,512]{2,1,0:T(8,128)} %param.16) | copy-start | bytes 393220
  35.4 28.4 %collective-permute-start.22 = (s16[2112,128]{1,0:T(8,128)(2,1)S(1)}, s16[2112,128]{1,0:T(8,128)(2,1)S(1)}, u32[]{:S(2)}, u32[]{:S(2)}) collective-permute-start(s16[2112,128]{1,0:T(8,128)(2,1)S(1)} %get-tuple-element.72), channel_id=1, source_target_pairs={{0,1},{1,0},{2,3},{3,2},{4,5},{5,4},{6,7},{7,6},{8,9},{9,8},{10,11... | collective-permute-start | bytes 1622024 | tf_op jit(solution)/shard_map/ppermute | solution.py:506
  37.5 13.5 %copy-start.11 = (s32[1,3,512]{2,0,1:T(1,128)S(1)}, s32[1,3,512]{2,0,1:T(1,128)}, u32[]{:S(2)}) copy-start(s32[1,3,512]{2,0,1:T(1,128)} %param.15) | copy-start | bytes 18436
  37.5 12.2 %collective-permute-start.13 = (bf16[960,128]{1,0:T(8,128)(2,1)S(1)}, bf16[960,128]{1,0:T(8,128)(2,1)S(1)}, u32[]{:S(2)}, u32[]{:S(2)}) collective-permute-start(bf16[960,128]{1,0:T(8,128)(2,1)S(1)} %shard_map.133.refs_4_), channel_id=1, source_target_pairs={{0,192},{8,200},{16,208},{24,216},{32,224},{40,232},{48,240},{56,2... | collective-permute-start | bytes 737288 | tf_op jit(solution)/shard_map/ppermute | solution.py:467
  38.7 11.0 %collective-permute-start.12 = (bf16[960,128]{1,0:T(8,128)(2,1)S(1)}, bf16[960,128]{1,0:T(8,128)(2,1)S(1)}, u32[]{:S(2)}, u32[]{:S(2)}) collective-permute-start(bf16[960,128]{1,0:T(8,128)(2,1)S(1)} %shard_map.133.refs_4_), channel_id=1, source_target_pairs={{0,128},{8,136},{16,144},{24,152},{32,160},{40,168},{48,176},{56,1... | collective-permute-start | bytes 737288 | tf_op jit(solution)/shard_map/ppermute | solution.py:467
  40.8 9.4 %collective-permute-start.11 = (bf16[960,128]{1,0:T(8,128)(2,1)S(1)}, bf16[960,128]{1,0:T(8,128)(2,1)S(1)}, u32[]{:S(2)}, u32[]{:S(2)}) collective-permute-start(bf16[960,128]{1,0:T(8,128)(2,1)S(1)} %shard_map.133.refs_4_), channel_id=1, source_target_pairs={{0,64},{8,72},{16,80},{24,88},{32,96},{40,104},{48,112},{56,120},{... | collective-permute-start | bytes 737288 | tf_op jit(solution)/shard_map/ppermute | solution.py:467
  49.7 13.2 %collective-permute-start.3 = (bf16[960,128]{1,0:T(8,128)(2,1)S(1)}, bf16[960,128]{1,0:T(8,128)(2,1)S(1)}, u32[]{:S(2)}, u32[]{:S(2)}) collective-permute-start(bf16[960,128]{1,0:T(8,128)(2,1)S(1)} %shard_map.132.refs_0_), channel_id=1, source_target_pairs={{0,64},{8,72},{16,80},{24,88},{32,96},{40,104},{48,112},{56,120},{... | collective-permute-start | bytes 737288 | tf_op jit(solution)/shard_map/ppermute | solution.py:467
  49.7 14.5 %collective-permute-start.17 = (bf16[960,128]{1,0:T(8,128)(2,1)S(1)}, bf16[960,128]{1,0:T(8,128)(2,1)S(1)}, u32[]{:S(2)}, u32[]{:S(2)}) collective-permute-start(bf16[960,128]{1,0:T(8,128)(2,1)S(1)} %collective-permute-done.5.refs_3_), channel_id=1, source_target_pairs={{0,8},{8,0},{16,24},{24,16},{32,40},{40,32},{48,56},{56,48},{64,72... | collective-permute-start | bytes 737288 | tf_op jit(solution)/shard_map/ppermute | solution.py:521
  50.3 14.0 %collective-permute-start.16 = (bf16[960,128]{1,0:T(8,128)(2,1)S(1)}, bf16[960,128]{1,0:T(8,128)(2,1)S(1)}, u32[]{:S(2)}, u32[]{:S(2)}) collective-permute-start(bf16[960,128]{1,0:T(8,128)(2,1)S(1)} %collective-permute-done.4.refs_2_), channel_id=1, source_target_pairs={{0,8},{8,0},{16,24},{24,16},{32,40},{40,32},{48,56},{56,48},{64,72... | collective-permute-start | bytes 737288 | tf_op jit(solution)/shard_map/ppermute | solution.py:521
  62.9 2.6 %collective-permute-start.18 = (bf16[960,128]{1,0:T(8,128)(2,1)S(1)}, bf16[960,128]{1,0:T(8,128)(2,1)S(1)}, u32[]{:S(2)}, u32[]{:S(2)}) collective-permute-start(bf16[960,128]{1,0:T(8,128)(2,1)S(1)} %shard_map.133.refs_4_), channel_id=1, source_target_pairs={{0,8},{8,0},{16,24},{24,16},{32,40},{40,32},{48,56},{56,48},{64,72... | collective-permute-start | bytes 737288 | tf_op jit(solution)/shard_map/ppermute | solution.py:521
  63.6 1.9 %collective-permute-start.19 = (bf16[960,128]{1,0:T(8,128)(2,1)S(1)}, bf16[960,128]{1,0:T(8,128)(2,1)S(1)}, u32[]{:S(2)}, u32[]{:S(2)}) collective-permute-start(bf16[960,128]{1,0:T(8,128)(2,1)S(1)} %collective-permute-done.11.refs_5_), channel_id=1, source_target_pairs={{0,8},{8,0},{16,24},{24,16},{32,40},{40,32},{48,56},{56,48},{64,72... | collective-permute-start | bytes 737288 | tf_op jit(solution)/shard_map/ppermute | solution.py:521
  63.7 1.8 collective-permute-start.15
  64.2 1.7 collective-permute-start.20
  64.3 1.9 %collective-permute-start.21 = (bf16[960,128]{1,0:T(8,128)(2,1)S(1)}, bf16[960,128]{1,0:T(8,128)(2,1)S(1)}, u32[]{:S(2)}, u32[]{:S(2)}) collective-permute-start(bf16[960,128]{1,0:T(8,128)(2,1)S(1)} %collective-permute-done.13.refs_7_), channel_id=1, source_target_pairs={{0,8},{8,0},{16,24},{24,16},{32,40},{40,32},{48,56},{56,48},{64,72... | collective-permute-start | bytes 737288 | tf_op jit(solution)/shard_map/ppermute | solution.py:521
  67.4 12.2 %collective-permute-start.24 = (bf16[640,128]{1,0:T(8,128)(2,1)S(1)}, bf16[640,128]{1,0:T(8,128)(2,1)S(1)}, u32[]{:S(2)}, u32[]{:S(2)}) collective-permute-start(bf16[640,128]{1,0:T(8,128)(2,1)S(1)} %get-tuple-element.98), channel_id=1, source_target_pairs={{0,3},{1,2},{2,1},{3,0},{4,7},{5,6},{6,5},{7,4},{8,11},{9,10},{10,... | collective-permute-start | bytes 491528 | tf_op jit(solution)/shard_map/ppermute | solution.py:467
  71.8 8.6 %collective-permute-start.25 = (bf16[640,128]{1,0:T(8,128)(2,1)S(1)}, bf16[640,128]{1,0:T(8,128)(2,1)S(1)}, u32[]{:S(2)}, u32[]{:S(2)}) collective-permute-start(bf16[640,128]{1,0:T(8,128)(2,1)S(1)} %get-tuple-element.99), channel_id=1, source_target_pairs={{0,2},{1,3},{2,0},{3,1},{4,6},{5,7},{6,4},{7,5},{8,10},{9,11},{10,... | collective-permute-start | bytes 491528 | tf_op jit(solution)/shard_map/ppermute | solution.py:467
  73.0 7.8 %collective-permute-start.26 = (bf16[640,128]{1,0:T(8,128)(2,1)S(1)}, bf16[640,128]{1,0:T(8,128)(2,1)S(1)}, u32[]{:S(2)}, u32[]{:S(2)}) collective-permute-start(bf16[640,128]{1,0:T(8,128)(2,1)S(1)} %get-tuple-element.100), channel_id=1, source_target_pairs={{0,1},{1,0},{2,3},{3,2},{4,5},{5,4},{6,7},{7,6},{8,9},{9,8},{10,11... | collective-permute-start | bytes 491528 | tf_op jit(solution)/shard_map/ppermute | solution.py:467
  83.5 14.2 %collective-permute-start.27 = (s16[2112,128]{1,0:T(8,128)(2,1)S(1)}, s16[2112,128]{1,0:T(8,128)(2,1)S(1)}, u32[]{:S(2)}, u32[]{:S(2)}) collective-permute-start(s16[2112,128]{1,0:T(8,128)(2,1)S(1)} %get-tuple-element.108), channel_id=1, source_target_pairs={{0,1},{1,0},{2,3},{3,2},{4,5},{5,4},{6,7},{7,6},{8,9},{9,8},{10,11... | collective-permute-start | bytes 1622024 | tf_op jit(solution)/shard_map/ppermute | solution.py:548
  85.7 12.0 %collective-permute-start.28 = (s16[2112,128]{1,0:T(8,128)(2,1)S(1)}, s16[2112,128]{1,0:T(8,128)(2,1)S(1)}, u32[]{:S(2)}, u32[]{:S(2)}) collective-permute-start(s16[2112,128]{1,0:T(8,128)(2,1)S(1)} %get-tuple-element.109), channel_id=1, source_target_pairs={{1,2},{3,4},{5,6},{2,1},{4,3},{6,5},{9,10},{11,12},{13,14},{10,9},... | collective-permute-start | bytes 1622024 | tf_op jit(solution)/shard_map/ppermute | solution.py:549
  100.8 25.7 %collective-permute-start.29 = (s16[336,128]{1,0:T(8,128)(2,1)S(1)}, s16[336,128]{1,0:T(8,128)(2,1)S(1)}, u32[]{:S(2)}, u32[]{:S(2)}) collective-permute-start(s16[336,128]{1,0:T(8,128)(2,1)S(1)} %get-tuple-element.114), channel_id=1, source_target_pairs={{0,7},{1,6},{2,5},{3,4},{4,3},{5,2},{6,1},{7,0},{8,15},{9,14},{10,... | collective-permute-start | bytes 258056 | tf_op jit(solution)/shard_map/ppermute | solution.py:467
  104.8 21.7 %collective-permute-start.30 = (s16[336,128]{1,0:T(8,128)(2,1)S(1)}, s16[336,128]{1,0:T(8,128)(2,1)S(1)}, u32[]{:S(2)}, u32[]{:S(2)}) collective-permute-start(s16[336,128]{1,0:T(8,128)(2,1)S(1)} %get-tuple-element.115), channel_id=1, source_target_pairs={{0,6},{1,7},{2,4},{3,5},{4,2},{5,3},{6,0},{7,1},{8,14},{9,15},{10,... | collective-permute-start | bytes 258056 | tf_op jit(solution)/shard_map/ppermute | solution.py:467
  111.3 16.0 %collective-permute-start.31 = (s16[336,128]{1,0:T(8,128)(2,1)S(1)}, s16[336,128]{1,0:T(8,128)(2,1)S(1)}, u32[]{:S(2)}, u32[]{:S(2)}) collective-permute-start(s16[336,128]{1,0:T(8,128)(2,1)S(1)} %get-tuple-element.116), channel_id=1, source_target_pairs={{0,5},{1,4},{2,7},{3,6},{4,1},{5,0},{6,3},{7,2},{8,13},{9,12},{10,... | collective-permute-start | bytes 258056 | tf_op jit(solution)/shard_map/ppermute | solution.py:467
  121.9 8.4 %collective-permute-start.32 = (s16[336,128]{1,0:T(8,128)(2,1)S(1)}, s16[336,128]{1,0:T(8,128)(2,1)S(1)}, u32[]{:S(2)}, u32[]{:S(2)}) collective-permute-start(s16[336,128]{1,0:T(8,128)(2,1)S(1)} %get-tuple-element.117), channel_id=1, source_target_pairs={{0,4},{1,5},{2,6},{3,7},{4,0},{5,1},{6,2},{7,3},{8,12},{9,13},{10,... | collective-permute-start | bytes 258056 | tf_op jit(solution)/shard_map/ppermute | solution.py:467
  121.9 8.4 %collective-permute-start.33 = (s16[336,128]{1,0:T(8,128)(2,1)S(1)}, s16[336,128]{1,0:T(8,128)(2,1)S(1)}, u32[]{:S(2)}, u32[]{:S(2)}) collective-permute-start(s16[336,128]{1,0:T(8,128)(2,1)S(1)} %get-tuple-element.118), channel_id=1, source_target_pairs={{0,3},{1,2},{2,1},{3,0},{4,7},{5,6},{6,5},{7,4},{8,11},{9,10},{10,... | collective-permute-start | bytes 258056 | tf_op jit(solution)/shard_map/ppermute | solution.py:467
  126.5 6.0 %collective-permute-start.34 = (s16[336,128]{1,0:T(8,128)(2,1)S(1)}, s16[336,128]{1,0:T(8,128)(2,1)S(1)}, u32[]{:S(2)}, u32[]{:S(2)}) collective-permute-start(s16[336,128]{1,0:T(8,128)(2,1)S(1)} %get-tuple-element.119), channel_id=1, source_target_pairs={{0,2},{1,3},{2,0},{3,1},{4,6},{5,7},{6,4},{7,5},{8,10},{9,11},{10,... | collective-permute-start | bytes 258056 | tf_op jit(solution)/shard_map/ppermute | solution.py:467
  126.5 6.0 %collective-permute-start.35 = (s16[336,128]{1,0:T(8,128)(2,1)S(1)}, s16[336,128]{1,0:T(8,128)(2,1)S(1)}, u32[]{:S(2)}, u32[]{:S(2)}) collective-permute-start(s16[336,128]{1,0:T(8,128)(2,1)S(1)} %get-tuple-element.120), channel_id=1, source_target_pairs={{0,1},{1,0},{2,3},{3,2},{4,5},{5,4},{6,7},{7,6},{8,9},{9,8},{10,11... | collective-permute-start | bytes 258056 | tf_op jit(solution)/shard_map/ppermute | solution.py:467
  133.3 2.3 %collective-permute-start.36 = (f32[1440,128]{1,0:T(8,128)S(1)}, f32[1440,128]{1,0:T(8,128)S(1)}, u32[]{:S(2)}, u32[]{:S(2)}) collective-permute-start(f32[1440,128]{1,0:T(8,128)S(1)} %get-tuple-element.122), channel_id=1, source_target_pairs={{0,8},{8,0},{16,24},{24,16},{32,40},{40,32},{48,56},{56,48},{64,72... | collective-permute-start | bytes 2211848 | tf_op jit(solution)/shard_map/ppermute | solution.py:581
  136.9 15.0 %collective-permute-start.37 = (s16[992,128]{1,0:T(8,128)(2,1)S(1)}, s16[992,128]{1,0:T(8,128)(2,1)S(1)}, u32[]{:S(2)}, u32[]{:S(2)}) collective-permute-start(s16[992,128]{1,0:T(8,128)(2,1)S(1)} %get-tuple-element.124), channel_id=1, source_target_pairs={{0,192},{8,200},{16,208},{24,216},{32,224},{40,232},{48,240},{56,2... | collective-permute-start | bytes 761864 | tf_op jit(solution)/shard_map/ppermute | solution.py:467
  140.0 11.9 %collective-permute-start.38 = (s16[992,128]{1,0:T(8,128)(2,1)S(1)}, s16[992,128]{1,0:T(8,128)(2,1)S(1)}, u32[]{:S(2)}, u32[]{:S(2)}) collective-permute-start(s16[992,128]{1,0:T(8,128)(2,1)S(1)} %get-tuple-element.125), channel_id=1, source_target_pairs={{0,128},{8,136},{16,144},{24,152},{32,160},{40,168},{48,176},{56,1... | collective-permute-start | bytes 761864 | tf_op jit(solution)/shard_map/ppermute | solution.py:467
  141.3 11.5 %collective-permute-start.39 = (s16[992,128]{1,0:T(8,128)(2,1)S(1)}, s16[992,128]{1,0:T(8,128)(2,1)S(1)}, u32[]{:S(2)}, u32[]{:S(2)}) collective-permute-start(s16[992,128]{1,0:T(8,128)(2,1)S(1)} %get-tuple-element.126), channel_id=1, source_target_pairs={{0,64},{8,72},{16,80},{24,88},{32,96},{40,104},{48,112},{56,120},{... | collective-permute-start | bytes 761864 | tf_op jit(solution)/shard_map/ppermute | solution.py:467
  153.2 20.2 %collective-permute-start.40 = (s16[256,128]{1,0:T(8,128)(2,1)S(1)}, s16[256,128]{1,0:T(8,128)(2,1)S(1)}, u32[]{:S(2)}, u32[]{:S(2)}) collective-permute-start(s16[256,128]{1,0:T(8,128)(2,1)S(1)} %get-tuple-element.128), channel_id=1, source_target_pairs={{0,48},{8,56},{16,32},{24,40},{32,16},{40,24},{48,0},{56,8},{64,11... | collective-permute-start | bytes 196616 | tf_op jit(solution)/shard_map/ppermute | solution.py:467
  155.2 22.4 %collective-permute-start.41 = (s16[256,128]{1,0:T(8,128)(2,1)S(1)}, s16[256,128]{1,0:T(8,128)(2,1)S(1)}, u32[]{:S(2)}, u32[]{:S(2)}) collective-permute-start(s16[256,128]{1,0:T(8,128)(2,1)S(1)} %get-tuple-element.129), channel_id=1, source_target_pairs={{0,32},{8,40},{16,48},{24,56},{32,0},{40,8},{48,16},{56,24},{64,96... | collective-permute-start | bytes 196616 | tf_op jit(solution)/shard_map/ppermute | solution.py:467
  173.3 4.3 %collective-permute-start.42 = (s16[256,128]{1,0:T(8,128)(2,1)S(1)}, s16[256,128]{1,0:T(8,128)(2,1)S(1)}, u32[]{:S(2)}, u32[]{:S(2)}) collective-permute-start(s16[256,128]{1,0:T(8,128)(2,1)S(1)} %get-tuple-element.130), channel_id=1, source_target_pairs={{0,16},{8,24},{16,0},{24,8},{32,48},{40,56},{48,32},{56,40},{64,80... | collective-permute-start | bytes 196616 | tf_op jit(solution)/shard_map/ppermute | solution.py:467
  (7 other events, 11.2 us)

commit v5 on v4

--- a/solution.py
+++ b/solution.py
@@ -19,6 +19,7 @@
 VMEM_LIMIT = 32 * 1024 * 1024
 FLOOR = 1e-33
 TOP = 32700.0
+MICROSECOND = 3_690_000
 HALO = 4
 GROUP = 32
 
@@ -31,8 +32,7 @@
     return pl.BlockSpec(memory_space=pltpu.SMEM)
 
 
-def call(kernel, outs, args, spaces, scratch=(), cost=1_000_000):
-    moved = sum(a.size * a.dtype.itemsize for a in (*outs, *args))
+def call(kernel, outs, args, spaces, scratch=(), work=0):
     return pl.pallas_call(
         kernel,
         out_shape=list(outs),
@@ -40,7 +40,7 @@
         out_specs=[vmem()] * len(outs),
         scratch_shapes=list(scratch),
         compiler_params=pltpu.CompilerParams(vmem_limit_bytes=VMEM_LIMIT),
-        cost_estimate=pl.CostEstimate(flops=0, bytes_accessed=0, transcendentals=0),
+        cost_estimate=pl.CostEstimate(flops=0, bytes_accessed=work * MICROSECOND, transcendentals=0),
     )(*args)
 
 
@@ -496,34 +496,30 @@
     between = functools.partial(across, groups)
 
     local = velocity.reshape(block, count_z)
-    other = lax.ppermute(anchors, "shot", swap("c", 1))
     near = [local] + exchange([local] * (HALVES * SIZE_Z - 1), ("shot", "dom"), functools.partial(swap_z, groups))
 
     half = halo_rows(2 * HALO, count_y)
     code = struct((half, count_z), I16)
     levels = pltpu.VMEM((2 * HALO * count_y // GROUP, count_z), I32)
+    (line,) = call(join_kernel, (struct((len(near) * block, count_z), BF16),), near, "v" * len(near))
+
+    p0, line = lax.optimization_barrier((p0, line))
     one, two = call(encode_kernel, (code, code), (p0, q0), "vv", (levels,))
     from_one = lax.ppermute(one, "dom", one_pairs)
     from_two = lax.ppermute(two, "dom", two_pairs)
-
-    lines = []
-    for part in range(HALVES):
-        blocks = near[part * SIZE_Z : (part + 1) * SIZE_Z]
-        lines += call(join_kernel, (struct((SIZE_Z * block, count_z), BF16),), blocks, "v" * SIZE_Z)
-    lines[1], other, one = lax.optimization_barrier((lines[1], other, one))
+    anchors, line = lax.optimization_barrier((anchors, line))
+    other = lax.ppermute(anchors, "shot", swap("c", 1))
     field = struct((row_count, count_y, count_z), F32)
-    hits = call(hit_kernel, (field, field), (start_step, receivers[0], traces[0]), "svv")
+    hits = call(hit_kernel, (field, field), (start_step, receivers[0], traces[0]), "svv", work=4)
     padded = pltpu.VMEM((row_count + 2 * HALO, count_y + 2 * PAD, count_z), F32)
-    sums = call(before_kernel, (field,) * 4, (p0, q0, p_prev, q_prev, hits[0]), "v" * 5, (padded,))
-    planes = [[line] + exchange([line] * (SIZE_X - 1), "shot", along["x"]) for line in lines]
-    planes[1] = list(lax.optimization_barrier((*planes[1], sums[0])))[:SIZE_X]
-    plane = planes[0] + planes[1]
+    sums = call(before_kernel, (field,) * 4, (p0, q0, p_prev, q_prev, hits[0]), "v" * 5, (padded,), work=6)
+    plane = [line] + exchange([line] * (SIZE_X - 1), "shot", along["x"])
+    plane, other = lax.optimization_barrier((plane, sums[0], other))[::2]
     plane += [lax.ppermute(part, "shot", swap("c", 1)) for part in plane]
-    *plane, from_one, from_two = lax.optimization_barrier((*plane, from_one, from_two))
+    *plane, from_two, from_one = lax.optimization_barrier((*plane, from_two, from_one))
     layout = [
-        [(dx, dz, dc, dh) for dz in range(SIZE_Z)]
+        [(dx, k % SIZE_Z, dc, k // SIZE_Z) for k in range(HALVES * SIZE_Z)]
         for dc in range(SIZE_C)
-        for dh in range(HALVES)
         for dx in range(SIZE_X)
     ]
     side = groups // HALVES
@@ -553,6 +549,7 @@
         (p1, q1, p0, q0, p_prev, courant, hits[1]),
         "v" * 7,
         (padded,),
+        work=6,
     )
 
     span = -(-(row_count * groups + own_rows - 1) // own_rows)

time: 180 us -> 167 us (0.928)
  waiting for transfers between devices: 58.6 us -> 50.4 us
  starting transfers between devices: 86.4 us -> 82.6 us
    ppermute x29 -> x26, waiting for transfers between devices: 48.4 us -> 38.4 us  [exchange(): got[k] = lax.ppermute(parts[k - 1], axis, pairs(k))]
    ppermute x29 -> x26, starting transfers between devices: 78.6 us -> 74.5 us  [exchange(): got[k] = lax.ppermute(parts[k - 1], axis, pairs(k))]
    pallas_call x13 -> x12, Pallas kernels: 26.2 us -> 25.3 us  [call(): pl.pallas_call(kernel, out_shape=list(outs), in_specs=[smem() if s == 's'...]
    unnamed x25 -> x27, local copies, waits for them, and re-layouts: 5.59 us -> 6.45 us
  transfers between devices with their start and end apart: 43 -> 36, of which waited for: 22 -> 20; matrix products, arithmetic and copies ran while one was open for 0% -> 0% of each run, Pallas kernels for 9% -> 9%
where the time goes in v5:
time: 167 us; the launch traced here: 166 us
  starting transfers between devices  82.6 us (49%)
  waiting for transfers between devices  50.4 us (30%)
  Pallas kernels  25.3 us (15%)
  local copies, waits for them, and re-layouts  6.45 us (4%)
    ppermute x26, starting transfers between devices, exchange(): got[k] = lax.ppermute(parts[k - 1], axis, pairs(k))  74.5 us
    ppermute x26, waiting for transfers between devices, exchange(): got[k] = lax.ppermute(parts[k - 1], axis, pairs(k))  38.4 us
    pallas_call x12, Pallas kernels, call(): pl.pallas_call(kernel, out_shape=list(outs), in_specs=[smem() if s == 's'...  25.3 us
    unnamed x27, local copies, waits for them, and re-layouts  6.45 us
    ppermute x2, waiting for transfers between devices, body(): from_one = lax.ppermute(one, 'dom', one_pairs)  5.81 us
    ppermute x2, starting transfers between devices, body(): from_one = lax.ppermute(one, 'dom', one_pairs)  5.48 us
  transfers between devices with their start and end apart: 36, of which 20 were waited for; matrix products, arithmetic and copies ran while one was open for 0% of the time, Pallas kernels for 9%

profile of v5, /device:TPU:6, one launch (start us, length us, event | category | flops | bytes accessed | tf_op | source)
XLA Modules:
  0.0 166.2 jit_solution(3449884199193427031)
XLA Ops:
  0.6 5.9 %collective-permute-start.6 = (bf16[240,128]{1,0:T(8,128)(2,1)}, bf16[240,128]{1,0:T(8,128)(2,1)S(1)}, u32[]{:S(2)}, u32[]{:S(2)}) collective-permute-start(bf16[240,128]{1,0:T(8,128)(2,1)} %bitcast.23), channel_id=1, source_target_pairs={{0,52},{1,53},{2,54},{3,55},{4,48},{5,49},{6,50},{7,51},{8,60},{9,... | collective-permute-start | bytes 184328 | tf_op jit(solution)/shard_map/ppermute | solution.py:467
  7.1 4.0 %collective-permute-start.4 = (bf16[240,128]{1,0:T(8,128)(2,1)}, bf16[240,128]{1,0:T(8,128)(2,1)S(1)}, u32[]{:S(2)}, u32[]{:S(2)}) collective-permute-start(bf16[240,128]{1,0:T(8,128)(2,1)} %bitcast.25), channel_id=1, source_target_pairs={{0,20},{1,21},{2,22},{3,23},{4,16},{5,17},{6,18},{7,19},{8,28},{9,... | collective-permute-start | bytes 184328 | tf_op jit(solution)/shard_map/ppermute | solution.py:467
  11.1 1.8 %collective-permute-start.3 = (bf16[240,128]{1,0:T(8,128)(2,1)}, bf16[240,128]{1,0:T(8,128)(2,1)S(1)}, u32[]{:S(2)}, u32[]{:S(2)}) collective-permute-start(bf16[240,128]{1,0:T(8,128)(2,1)} %bitcast.26), channel_id=1, source_target_pairs={{0,4},{1,5},{2,6},{3,7},{4,0},{5,1},{6,2},{7,3},{8,12},{9,13},{10,... | collective-permute-start | bytes 184328 | tf_op jit(solution)/shard_map/ppermute | solution.py:467
  13.0 1.9 %collective-permute-start.2 = (bf16[240,128]{1,0:T(8,128)(2,1)}, bf16[240,128]{1,0:T(8,128)(2,1)S(1)}, u32[]{:S(2)}, u32[]{:S(2)}) collective-permute-start(bf16[240,128]{1,0:T(8,128)(2,1)} %bitcast.27), channel_id=1, source_target_pairs={{0,48},{1,49},{2,50},{3,51},{4,52},{5,53},{6,54},{7,55},{8,56},{9,... | collective-permute-start | bytes 184328 | tf_op jit(solution)/shard_map/ppermute | solution.py:467
  15.1 2.3 %collective-permute-start = (bf16[240,128]{1,0:T(8,128)(2,1)}, bf16[240,128]{1,0:T(8,128)(2,1)S(1)}, u32[]{:S(2)}, u32[]{:S(2)}) collective-permute-start(bf16[240,128]{1,0:T(8,128)(2,1)} %bitcast.29), channel_id=1, source_target_pairs={{0,16},{1,17},{2,18},{3,19},{4,20},{5,21},{6,22},{7,23},{8,24},{9,... | collective-permute-start | bytes 184328 | tf_op jit(solution)/shard_map/ppermute | solution.py:467
  17.4 4.1 %collective-permute-done.3.refs_4_ = bf16[240,128]{1,0:T(8,128)(2,1)S(1)} collective-permute-done((bf16[240,128]{1,0:T(8,128)(2,1)}, bf16[240,128]{1,0:T(8,128)(2,1)S(1)}, u32[]{:S(2)}, u32[]{:S(2)}) %collective-permute-start.3) | collective-permute-done | bytes 61472 | tf_op jit(solution)/shard_map/ppermute | solution.py:467
  21.5 3.2 %collective-permute-done.1.refs_2_ = bf16[240,128]{1,0:T(8,128)(2,1)S(1)} collective-permute-done((bf16[240,128]{1,0:T(8,128)(2,1)}, bf16[240,128]{1,0:T(8,128)(2,1)S(1)}, u32[]{:S(2)}, u32[]{:S(2)}) %collective-permute-start.1) | collective-permute-done | bytes 61472 | tf_op jit(solution)/shard_map/ppermute | solution.py:467
  24.6 0.8 copy-done.8
  25.5 1.3 copy-done
  26.8 1.2 copy-done.2
  28.6 0.8 collective-permute-start.15
  30.0 2.4 %collective-permute-start.8 = (bf16[1920,128]{1,0:T(8,128)(2,1)S(1)}, bf16[1920,128]{1,0:T(8,128)(2,1)S(1)}, u32[]{:S(2)}, u32[]{:S(2)}) collective-permute-start(bf16[1920,128]{1,0:T(8,128)(2,1)S(1)} %shard_map.130.refs_0_), channel_id=1, source_target_pairs={{0,128},{8,136},{16,144},{24,152},{32,160},{40,168},{48,176},{56,1... | collective-permute-start | bytes 1474568 | tf_op jit(solution)/shard_map/ppermute | solution.py:467
  32.4 1.2 collective-permute-start.7
  33.6 1.1 collective-permute-done.10.other
  34.7 4.4 %collective-permute-start.16 = (s16[2112,128]{1,0:T(8,128)(2,1)S(1)}, s16[2112,128]{1,0:T(8,128)(2,1)S(1)}, u32[]{:S(2)}, u32[]{:S(2)}) collective-permute-start(s16[2112,128]{1,0:T(8,128)(2,1)S(1)} %get-tuple-element.76), channel_id=1, source_target_pairs={{0,1},{1,0},{2,3},{3,2},{4,5},{5,4},{6,7},{7,6},{8,9},{9,8},{10,11... | collective-permute-start | bytes 1622024 | tf_op jit(solution)/shard_map/ppermute | solution.py:508
  39.8 3.4 %shard_map.131 = (f32[8,256,128]{2,1,0:T(8,128)S(1)}, f32[8,256,128]{2,1,0:T(8,128)S(1)}) custom-call(s32[1]{0:T(128)S(6)} %copy.17.begin, s32[3,512]{1,0:T(4,128)S(1)} %bitcast.31, f32[64,512]{1,0:T(8,128)S(1)} %bitcast.22), custom_call_target="tpu_custom_call" | custom-call | bytes 14760000 | tf_op jit(solution)/shard_map/pallas_call | solution.py:36
  43.2 1.2 copy-done.4
  44.4 1.2 copy-done.6
  45.6 6.0 %shard_map.132 = (f32[8,256,128]{2,1,0:T(8,128)S(1)}, f32[8,256,128]{2,1,0:T(8,128)S(1)}, f32[8,256,128]{2,1,0:T(8,128)S(1)}, f32[8,256,128]{2,1,0:T(8,128)S(1)}) custom-call(f32[8,256,128]{2,1,0:T(8,128)S(1)} %bitcast.13, f32[8,256,128]{2,1,0:T(8,128)S(1)} %bitcast.17, f32[8,256,128]{2,1,0:T(8,128)S(1)} %bitcast.19, f32[8,256,128]{2,1,0:T(8,128)S(1)} %bitcast.21, ...), custom_call_target="tpu_custom_call" | custom-call | bytes 22140000 | tf_op jit(solution)/shard_map/pallas_call | solution.py:36
  51.6 1.7 %collective-permute-done.9.refs_3_ = bf16[1920,128]{1,0:T(8,128)(2,1)S(1)} collective-permute-done((bf16[1920,128]{1,0:T(8,128)(2,1)S(1)}, bf16[1920,128]{1,0:T(8,128)(2,1)S(1)}, u32[]{:S(2)}, u32[]{:S(2)}) %collective-permute-start.9) | collective-permute-done | bytes 491552 | tf_op jit(solution)/shard_map/ppermute | solution.py:467
  55.0 0.8 collective-permute-done.11.refs_4_
  58.0 1.1 shard_map.134
  59.1 7.9 %collective-permute-start.17 = (bf16[640,128]{1,0:T(8,128)(2,1)S(1)}, bf16[640,128]{1,0:T(8,128)(2,1)S(1)}, u32[]{:S(2)}, u32[]{:S(2)}) collective-permute-start(bf16[640,128]{1,0:T(8,128)(2,1)S(1)} %get-tuple-element.88), channel_id=1, source_target_pairs={{0,3},{1,2},{2,1},{3,0},{4,7},{5,6},{6,5},{7,4},{8,11},{9,10},{10,... | collective-permute-start | bytes 491528 | tf_op jit(solution)/shard_map/ppermute | solution.py:467
  67.0 1.0 collective-permute-start.19
  67.9 6.5 %collective-permute-done.17.rest_3_ = bf16[640,128]{1,0:T(8,128)(2,1)S(1)} collective-permute-done((bf16[640,128]{1,0:T(8,128)(2,1)S(1)}, bf16[640,128]{1,0:T(8,128)(2,1)S(1)}, u32[]{:S(2)}, u32[]{:S(2)}) %collective-permute-start.17) | collective-permute-done | bytes 163872 | tf_op jit(solution)/shard_map/ppermute | solution.py:467
  74.4 1.2 collective-permute-done.18.rest_4_
  76.4 2.0 %shard_map.135 = (f32[8,256,128]{2,1,0:T(8,128)S(1)}, f32[8,256,128]{2,1,0:T(8,128)S(1)}, f32[8,256,128]{2,1,0:T(8,128)S(1)}, s16[2112,128]{1,0:T(8,128)(2,1)S(1)}, s16[2112,128]{1,0:T(8,128)(2,1)S(1)}) custom-call(s32[1,2]{1,0:T(1,128)S(1)} %copy-done.9, s32[1,3]{1,0:T(1,128)S(1)} %copy-done.10, s32[1]{0:T(128)S(6)} %copy.17.begin, f32[64]{0:T(128)S(1)} %copy-done.11, ...), custom_call_target="tpu_custom_call" | custom-call | tf_op jit(solution)/shard_map/pallas_call | solution.py:36
  78.4 1.1 collective-permute-start.20
  80.2 5.9 %shard_map.136 = (f32[8,256,128]{2,1,0:T(8,128)S(1)}, f32[8,256,128]{2,1,0:T(8,128)S(1)}, f32[8,256,128]{2,1,0:T(8,128)S(1)}) custom-call(f32[8,256,128]{2,1,0:T(8,128)S(1)} %get-tuple-element.91.p1, f32[8,256,128]{2,1,0:T(8,128)S(1)} %get-tuple-element.92.q1, f32[8,256,128]{2,1,0:T(8,128)S(1)} %bitcast.14, f32[8,256,128]{2,1,0:T(8,128)S(1)} %bitcast.18, ...), custom_call_target="tpu_custom_call" | custom-call | bytes 22140000 | tf_op jit(solution)/shard_map/pallas_call | solution.py:36
  86.1 5.8 %collective-permute-done.20.one = s16[2112,128]{1,0:T(8,128)(2,1)S(1)} collective-permute-done((s16[2112,128]{1,0:T(8,128)(2,1)S(1)}, s16[2112,128]{1,0:T(8,128)(2,1)S(1)}, u32[]{:S(2)}, u32[]{:S(2)}) %collective-permute-start.20) | collective-permute-done | bytes 540704 | tf_op jit(solution)/shard_map/ppermute | solution.py:544
  91.9 3.1 %shard_map.137 = (f32[8,256,128]{2,1,0:T(8,128)}, f32[8,256,128]{2,1,0:T(8,128)}, f32[320,128]{1,0:T(8,128)S(1)}, s16[336,128]{1,0:T(8,128)(2,1)S(1)}, s16[336,1...) custom-call(s32[1,2]{1,0:T(1,128)S(1)} %copy-done.9, ...), custom_call_target="tpu_custom_call" | custom-call | tf_op jit(solution)/shard_map/pallas_call | solution.py:36
  95.0 4.4 %collective-permute-start.22 = (s16[336,128]{1,0:T(8,128)(2,1)S(1)}, s16[336,128]{1,0:T(8,128)(2,1)S(1)}, u32[]{:S(2)}, u32[]{:S(2)}) collective-permute-start(s16[336,128]{1,0:T(8,128)(2,1)S(1)} %get-tuple-element.104), channel_id=1, source_target_pairs={{0,7},{1,6},{2,5},{3,4},{4,3},{5,2},{6,1},{7,0},{8,15},{9,14},{10,... | collective-permute-start | bytes 258056 | tf_op jit(solution)/shard_map/ppermute | solution.py:467
  99.4 6.4 %collective-permute-start.23 = (s16[336,128]{1,0:T(8,128)(2,1)S(1)}, s16[336,128]{1,0:T(8,128)(2,1)S(1)}, u32[]{:S(2)}, u32[]{:S(2)}) collective-permute-start(s16[336,128]{1,0:T(8,128)(2,1)S(1)} %get-tuple-element.105), channel_id=1, source_target_pairs={{0,6},{1,7},{2,4},{3,5},{4,2},{5,3},{6,0},{7,1},{8,14},{9,15},{10,... | collective-permute-start | bytes 258056 | tf_op jit(solution)/shard_map/ppermute | solution.py:467
  105.7 9.9 %collective-permute-start.24 = (s16[336,128]{1,0:T(8,128)(2,1)S(1)}, s16[336,128]{1,0:T(8,128)(2,1)S(1)}, u32[]{:S(2)}, u32[]{:S(2)}) collective-permute-start(s16[336,128]{1,0:T(8,128)(2,1)S(1)} %get-tuple-element.106), channel_id=1, source_target_pairs={{0,5},{1,4},{2,7},{3,6},{4,1},{5,0},{6,3},{7,2},{8,13},{9,12},{10,... | collective-permute-start | bytes 258056 | tf_op jit(solution)/shard_map/ppermute | solution.py:467
  115.7 4.2 %collective-permute-start.26 = (s16[336,128]{1,0:T(8,128)(2,1)S(1)}, s16[336,128]{1,0:T(8,128)(2,1)S(1)}, u32[]{:S(2)}, u32[]{:S(2)}) collective-permute-start(s16[336,128]{1,0:T(8,128)(2,1)S(1)} %get-tuple-element.108), channel_id=1, source_target_pairs={{0,3},{1,2},{2,1},{3,0},{4,7},{5,6},{6,5},{7,4},{8,11},{9,10},{10,... | collective-permute-start | bytes 258056 | tf_op jit(solution)/shard_map/ppermute | solution.py:467
  119.9 0.9 collective-permute-start.28
  120.8 3.4 %collective-permute-done.25.refs_3_ = s16[336,128]{1,0:T(8,128)(2,1)S(1)} collective-permute-done((s16[336,128]{1,0:T(8,128)(2,1)S(1)}, s16[336,128]{1,0:T(8,128)(2,1)S(1)}, u32[]{:S(2)}, u32[]{:S(2)}) %collective-permute-start.25) | collective-permute-done | bytes 86048 | tf_op jit(solution)/shard_map/ppermute | solution.py:467
  124.2 1.7 %collective-permute-done.27.refs_5_ = s16[336,128]{1,0:T(8,128)(2,1)S(1)} collective-permute-done((s16[336,128]{1,0:T(8,128)(2,1)S(1)}, s16[336,128]{1,0:T(8,128)(2,1)S(1)}, u32[]{:S(2)}, u32[]{:S(2)}) %collective-permute-start.27) | collective-permute-done | bytes 86048 | tf_op jit(solution)/shard_map/ppermute | solution.py:467
  125.9 0.9 shard_map.138
  126.8 2.2 %collective-permute-done.29.got = f32[1440,128]{1,0:T(8,128)S(1)} collective-permute-done((f32[1440,128]{1,0:T(8,128)S(1)}, f32[1440,128]{1,0:T(8,128)S(1)}, u32[]{:S(2)}, u32[]{:S(2)}) %collective-permute-start.29) | collective-permute-done | bytes 737312 | tf_op jit(solution)/shard_map/ppermute | solution.py:578
  129.1 1.2 shard_map.139
  130.8 2.4 %collective-permute-start.31 = (s16[992,128]{1,0:T(8,128)(2,1)S(1)}, s16[992,128]{1,0:T(8,128)(2,1)S(1)}, u32[]{:S(2)}, u32[]{:S(2)}) collective-permute-start(s16[992,128]{1,0:T(8,128)(2,1)S(1)} %get-tuple-element.115), channel_id=1, source_target_pairs={{0,128},{8,136},{16,144},{24,152},{32,160},{40,168},{48,176},{56,1... | collective-permute-start | bytes 761864 | tf_op jit(solution)/shard_map/ppermute | solution.py:467
  133.3 1.2 collective-permute-start.32
  134.5 10.7 %collective-permute-done.30.refs_0_ = s16[992,128]{1,0:T(8,128)(2,1)S(1)} collective-permute-done((s16[992,128]{1,0:T(8,128)(2,1)S(1)}, s16[992,128]{1,0:T(8,128)(2,1)S(1)}, u32[]{:S(2)}, u32[]{:S(2)}) %collective-permute-start.30) | collective-permute-done | bytes 253984 | tf_op jit(solution)/shard_map/ppermute | solution.py:467
  146.2 2.0 %collective-permute-start.33 = (s16[256,128]{1,0:T(8,128)(2,1)S(1)}, s16[256,128]{1,0:T(8,128)(2,1)S(1)}, u32[]{:S(2)}, u32[]{:S(2)}) collective-permute-start(s16[256,128]{1,0:T(8,128)(2,1)S(1)} %get-tuple-element.118), channel_id=1, source_target_pairs={{0,48},{8,56},{16,32},{24,40},{32,16},{40,24},{48,0},{56,8},{64,11... | collective-permute-start | bytes 196616 | tf_op jit(solution)/shard_map/ppermute | solution.py:467
  148.2 12.8 %collective-permute-start.34 = (s16[256,128]{1,0:T(8,128)(2,1)S(1)}, s16[256,128]{1,0:T(8,128)(2,1)S(1)}, u32[]{:S(2)}, u32[]{:S(2)}) collective-permute-start(s16[256,128]{1,0:T(8,128)(2,1)S(1)} %get-tuple-element.119), channel_id=1, source_target_pairs={{0,32},{8,40},{16,48},{24,56},{32,0},{40,8},{48,16},{56,24},{64,96... | collective-permute-start | bytes 196616 | tf_op jit(solution)/shard_map/ppermute | solution.py:467
  161.0 3.8 %collective-permute-done.34.refs_1_ = s16[256,128]{1,0:T(8,128)(2,1)S(1)} collective-permute-done((s16[256,128]{1,0:T(8,128)(2,1)S(1)}, s16[256,128]{1,0:T(8,128)(2,1)S(1)}, u32[]{:S(2)}, u32[]{:S(2)}) %collective-permute-start.34) | collective-permute-done | bytes 65568 | tf_op jit(solution)/shard_map/ppermute | solution.py:467
  165.5 0.7 shard_map.141
  (63 shorter events, 9.5 us)
Async XLA Ops:
  0.6 14.2 %collective-permute-start.6 = (bf16[240,128]{1,0:T(8,128)(2,1)}, bf16[240,128]{1,0:T(8,128)(2,1)S(1)}, u32[]{:S(2)}, u32[]{:S(2)}) collective-permute-start(bf16[240,128]{1,0:T(8,128)(2,1)} %bitcast.23), channel_id=1, source_target_pairs={{0,52},{1,53},{2,54},{3,55},{4,48},{5,49},{6,50},{7,51},{8,60},{9,... | collective-permute-start | bytes 184328 | tf_op jit(solution)/shard_map/ppermute | solution.py:467
  6.6 8.5 %collective-permute-start.5 = (bf16[240,128]{1,0:T(8,128)(2,1)}, bf16[240,128]{1,0:T(8,128)(2,1)S(1)}, u32[]{:S(2)}, u32[]{:S(2)}) collective-permute-start(bf16[240,128]{1,0:T(8,128)(2,1)} %bitcast.24), channel_id=1, source_target_pairs={{0,36},{1,37},{2,38},{3,39},{4,32},{5,33},{6,34},{7,35},{8,44},{9,... | collective-permute-start | bytes 184328 | tf_op jit(solution)/shard_map/ppermute | solution.py:467
  7.1 10.2 %collective-permute-start.4 = (bf16[240,128]{1,0:T(8,128)(2,1)}, bf16[240,128]{1,0:T(8,128)(2,1)S(1)}, u32[]{:S(2)}, u32[]{:S(2)}) collective-permute-start(bf16[240,128]{1,0:T(8,128)(2,1)} %bitcast.25), channel_id=1, source_target_pairs={{0,20},{1,21},{2,22},{3,23},{4,16},{5,17},{6,18},{7,19},{8,28},{9,... | collective-permute-start | bytes 184328 | tf_op jit(solution)/shard_map/ppermute | solution.py:467
  11.1 10.3 %collective-permute-start.3 = (bf16[240,128]{1,0:T(8,128)(2,1)}, bf16[240,128]{1,0:T(8,128)(2,1)S(1)}, u32[]{:S(2)}, u32[]{:S(2)}) collective-permute-start(bf16[240,128]{1,0:T(8,128)(2,1)} %bitcast.26), channel_id=1, source_target_pairs={{0,4},{1,5},{2,6},{3,7},{4,0},{5,1},{6,2},{7,3},{8,12},{9,13},{10,... | collective-permute-start | bytes 184328 | tf_op jit(solution)/shard_map/ppermute | solution.py:467
  13.0 8.5 %collective-permute-start.2 = (bf16[240,128]{1,0:T(8,128)(2,1)}, bf16[240,128]{1,0:T(8,128)(2,1)S(1)}, u32[]{:S(2)}, u32[]{:S(2)}) collective-permute-start(bf16[240,128]{1,0:T(8,128)(2,1)} %bitcast.27), channel_id=1, source_target_pairs={{0,48},{1,49},{2,50},{3,51},{4,52},{5,53},{6,54},{7,55},{8,56},{9,... | collective-permute-start | bytes 184328 | tf_op jit(solution)/shard_map/ppermute | solution.py:467
  14.9 9.8 %collective-permute-start.1 = (bf16[240,128]{1,0:T(8,128)(2,1)}, bf16[240,128]{1,0:T(8,128)(2,1)S(1)}, u32[]{:S(2)}, u32[]{:S(2)}) collective-permute-start(bf16[240,128]{1,0:T(8,128)(2,1)} %bitcast.28), channel_id=1, source_target_pairs={{0,32},{1,33},{2,34},{3,35},{4,36},{5,37},{6,38},{7,39},{8,40},{9,... | collective-permute-start | bytes 184328 | tf_op jit(solution)/shard_map/ppermute | solution.py:467
  15.1 9.5 %collective-permute-start = (bf16[240,128]{1,0:T(8,128)(2,1)}, bf16[240,128]{1,0:T(8,128)(2,1)S(1)}, u32[]{:S(2)}, u32[]{:S(2)}) collective-permute-start(bf16[240,128]{1,0:T(8,128)(2,1)} %bitcast.29), channel_id=1, source_target_pairs={{0,16},{1,17},{2,18},{3,19},{4,20},{5,21},{6,22},{7,23},{8,24},{9,... | collective-permute-start | bytes 184328 | tf_op jit(solution)/shard_map/ppermute | solution.py:467
  24.6 0.8 copy-start.8
  25.5 14.3 %copy-start.12 = (s32[1,3,512]{2,0,1:T(1,128)S(1)}, s32[1,3,512]{2,0,1:T(1,128)}, u32[]{:S(2)}) copy-start(s32[1,3,512]{2,0,1:T(1,128)} %param.15) | copy-start | bytes 18436
  25.5 14.3 %copy-start.7 = (f32[1,64,512]{2,1,0:T(8,128)S(1)}, f32[1,64,512]{2,1,0:T(8,128)}, u32[]{:S(2)}) copy-start(f32[1,64,512]{2,1,0:T(8,128)} %param.16) | copy-start | bytes 393220
  25.5 1.3 copy-start
  26.8 1.2 copy-start.2
  28.0 15.1 %copy-start.1 = (f32[1,8,256,128]{3,2,1,0:T(8,128)S(1)}, f32[1,8,256,128]{3,2,1,0:T(8,128)}, u32[]{:S(2)}) copy-start(f32[1,8,256,128]{3,2,1,0:T(8,128)} %param.19) | copy-start | bytes 3145732
  28.0 15.1 %copy-start.3 = (f32[1,8,256,128]{3,2,1,0:T(8,128)S(1)}, f32[1,8,256,128]{3,2,1,0:T(8,128)}, u32[]{:S(2)}) copy-start(f32[1,8,256,128]{3,2,1,0:T(8,128)} %param.21) | copy-start | bytes 3145732
  28.6 5.0 %copy-start.9 = (s32[1,2]{1,0:T(1,128)S(1)}, s32[1,2]{1,0:T(1,128)}, u32[]{:S(2)}) copy-start(s32[1,2]{1,0:T(1,128)} %anchors.6) | copy-start | bytes 28
  28.6 25.9 %collective-permute-start.15 = (s16[2112,128]{1,0:T(8,128)(2,1)S(1)}, s16[2112,128]{1,0:T(8,128)(2,1)S(1)}, u32[]{:S(2)}, u32[]{:S(2)}) collective-permute-start(s16[2112,128]{1,0:T(8,128)(2,1)S(1)} %get-tuple-element.75), channel_id=1, source_target_pairs={{1,2},{3,4},{5,6},{2,1},{4,3},{6,5},{9,10},{11,12},{13,14},{10,9},... | collective-permute-start | bytes 1622024 | tf_op jit(solution)/shard_map/ppermute | solution.py:509
  29.4 24.0 %collective-permute-start.9 = (bf16[1920,128]{1,0:T(8,128)(2,1)S(1)}, bf16[1920,128]{1,0:T(8,128)(2,1)S(1)}, u32[]{:S(2)}, u32[]{:S(2)}) collective-permute-start(bf16[1920,128]{1,0:T(8,128)(2,1)S(1)} %shard_map.130.refs_0_), channel_id=1, source_target_pairs={{0,192},{8,200},{16,208},{24,216},{32,224},{40,232},{48,240},{56,2... | collective-permute-start | bytes 1474568 | tf_op jit(solution)/shard_map/ppermute | solution.py:467
  30.0 23.4 %collective-permute-start.8 = (bf16[1920,128]{1,0:T(8,128)(2,1)S(1)}, bf16[1920,128]{1,0:T(8,128)(2,1)S(1)}, u32[]{:S(2)}, u32[]{:S(2)}) collective-permute-start(bf16[1920,128]{1,0:T(8,128)(2,1)S(1)} %shard_map.130.refs_0_), channel_id=1, source_target_pairs={{0,128},{8,136},{16,144},{24,152},{32,160},{40,168},{48,176},{56,1... | collective-permute-start | bytes 1474568 | tf_op jit(solution)/shard_map/ppermute | solution.py:467
  32.4 21.6 %collective-permute-start.7 = (bf16[1920,128]{1,0:T(8,128)(2,1)S(1)}, bf16[1920,128]{1,0:T(8,128)(2,1)S(1)}, u32[]{:S(2)}, u32[]{:S(2)}) collective-permute-start(bf16[1920,128]{1,0:T(8,128)(2,1)S(1)} %shard_map.130.refs_0_), channel_id=1, source_target_pairs={{0,64},{8,72},{16,80},{24,88},{32,96},{40,104},{48,112},{56,120},{... | collective-permute-start | bytes 1474568 | tf_op jit(solution)/shard_map/ppermute | solution.py:467
  33.6 1.1 collective-permute-start.10
  34.7 20.3 %collective-permute-start.16 = (s16[2112,128]{1,0:T(8,128)(2,1)S(1)}, s16[2112,128]{1,0:T(8,128)(2,1)S(1)}, u32[]{:S(2)}, u32[]{:S(2)}) collective-permute-start(s16[2112,128]{1,0:T(8,128)(2,1)S(1)} %get-tuple-element.76), channel_id=1, source_target_pairs={{0,1},{1,0},{2,3},{3,2},{4,5},{5,4},{6,7},{7,6},{8,9},{9,8},{10,11... | collective-permute-start | bytes 1622024 | tf_op jit(solution)/shard_map/ppermute | solution.py:508
  43.1 1.2 copy-start.4
  44.4 1.2 copy-start.6
  54.0 1.9 %collective-permute-start.11 = (bf16[1920,128]{1,0:T(8,128)(2,1)S(1)}, bf16[1920,128]{1,0:T(8,128)(2,1)S(1)}, u32[]{:S(2)}, u32[]{:S(2)}) collective-permute-start(bf16[1920,128]{1,0:T(8,128)(2,1)S(1)} %shard_map.130.refs_0_), channel_id=1, source_target_pairs={{0,8},{8,0},{16,24},{24,16},{32,40},{40,32},{48,56},{56,48},{64,72... | collective-permute-start | bytes 1474568 | tf_op jit(solution)/shard_map/ppermute | solution.py:518
  54.0 2.6 %collective-permute-start.12 = (bf16[1920,128]{1,0:T(8,128)(2,1)S(1)}, bf16[1920,128]{1,0:T(8,128)(2,1)S(1)}, u32[]{:S(2)}, u32[]{:S(2)}) collective-permute-start(bf16[1920,128]{1,0:T(8,128)(2,1)S(1)} %collective-permute-done.7.refs_1_), channel_id=1, source_target_pairs={{0,8},{8,0},{16,24},{24,16},{32,40},{40,32},{48,56},{56,48},{64,72... | collective-permute-start | bytes 1474568 | tf_op jit(solution)/shard_map/ppermute | solution.py:518
  54.5 2.8 %collective-permute-start.13 = (bf16[1920,128]{1,0:T(8,128)(2,1)S(1)}, bf16[1920,128]{1,0:T(8,128)(2,1)S(1)}, u32[]{:S(2)}, u32[]{:S(2)}) collective-permute-start(bf16[1920,128]{1,0:T(8,128)(2,1)S(1)} %collective-permute-done.8.refs_2_), channel_id=1, source_target_pairs={{0,8},{8,0},{16,24},{24,16},{32,40},{40,32},{48,56},{56,48},{64,72... | collective-permute-start | bytes 1474568 | tf_op jit(solution)/shard_map/ppermute | solution.py:518
  54.5 3.5 %collective-permute-start.14 = (bf16[1920,128]{1,0:T(8,128)(2,1)S(1)}, bf16[1920,128]{1,0:T(8,128)(2,1)S(1)}, u32[]{:S(2)}, u32[]{:S(2)}) collective-permute-start(bf16[1920,128]{1,0:T(8,128)(2,1)S(1)} %collective-permute-done.9.refs_3_), channel_id=1, source_target_pairs={{0,8},{8,0},{16,24},{24,16},{32,40},{40,32},{48,56},{56,48},{64,72... | collective-permute-start | bytes 1474568 | tf_op jit(solution)/shard_map/ppermute | solution.py:518
  59.1 15.3 %collective-permute-start.17 = (bf16[640,128]{1,0:T(8,128)(2,1)S(1)}, bf16[640,128]{1,0:T(8,128)(2,1)S(1)}, u32[]{:S(2)}, u32[]{:S(2)}) collective-permute-start(bf16[640,128]{1,0:T(8,128)(2,1)S(1)} %get-tuple-element.88), channel_id=1, source_target_pairs={{0,3},{1,2},{2,1},{3,0},{4,7},{5,6},{6,5},{7,4},{8,11},{9,10},{10,... | collective-permute-start | bytes 491528 | tf_op jit(solution)/shard_map/ppermute | solution.py:467
  67.0 8.6 %collective-permute-start.18 = (bf16[640,128]{1,0:T(8,128)(2,1)S(1)}, bf16[640,128]{1,0:T(8,128)(2,1)S(1)}, u32[]{:S(2)}, u32[]{:S(2)}) collective-permute-start(bf16[640,128]{1,0:T(8,128)(2,1)S(1)} %get-tuple-element.89), channel_id=1, source_target_pairs={{0,2},{1,3},{2,0},{3,1},{4,6},{5,7},{6,4},{7,5},{8,10},{9,11},{10,... | collective-permute-start | bytes 491528 | tf_op jit(solution)/shard_map/ppermute | solution.py:467
  67.0 8.7 %collective-permute-start.19 = (bf16[640,128]{1,0:T(8,128)(2,1)S(1)}, bf16[640,128]{1,0:T(8,128)(2,1)S(1)}, u32[]{:S(2)}, u32[]{:S(2)}) collective-permute-start(bf16[640,128]{1,0:T(8,128)(2,1)S(1)} %get-tuple-element.90), channel_id=1, source_target_pairs={{0,1},{1,0},{2,3},{3,2},{4,5},{5,4},{6,7},{7,6},{8,9},{9,8},{10,11... | collective-permute-start | bytes 491528 | tf_op jit(solution)/shard_map/ppermute | solution.py:467
  75.7 0.7 copy-start.11
  76.4 3.8 %copy-start.5 = (f32[1,8,256,128]{3,2,1,0:T(8,128)S(1)}, f32[1,8,256,128]{3,2,1,0:T(8,128)}, u32[]{:S(2)}) copy-start(f32[1,8,256,128]{3,2,1,0:T(8,128)} %param.18) | copy-start | bytes 3145732
  78.4 13.6 %collective-permute-start.20 = (s16[2112,128]{1,0:T(8,128)(2,1)S(1)}, s16[2112,128]{1,0:T(8,128)(2,1)S(1)}, u32[]{:S(2)}, u32[]{:S(2)}) collective-permute-start(s16[2112,128]{1,0:T(8,128)(2,1)S(1)} %get-tuple-element.98), channel_id=1, source_target_pairs={{0,1},{1,0},{2,3},{3,2},{4,5},{5,4},{6,7},{7,6},{8,9},{9,8},{10,11... | collective-permute-start | bytes 1622024 | tf_op jit(solution)/shard_map/ppermute | solution.py:544
  79.5 12.5 %collective-permute-start.21 = (s16[2112,128]{1,0:T(8,128)(2,1)S(1)}, s16[2112,128]{1,0:T(8,128)(2,1)S(1)}, u32[]{:S(2)}, u32[]{:S(2)}) collective-permute-start(s16[2112,128]{1,0:T(8,128)(2,1)S(1)} %get-tuple-element.99), channel_id=1, source_target_pairs={{1,2},{3,4},{5,6},{2,1},{4,3},{6,5},{9,10},{11,12},{13,14},{10,9},... | collective-permute-start | bytes 1622024 | tf_op jit(solution)/shard_map/ppermute | solution.py:545
  95.0 24.9 %collective-permute-start.22 = (s16[336,128]{1,0:T(8,128)(2,1)S(1)}, s16[336,128]{1,0:T(8,128)(2,1)S(1)}, u32[]{:S(2)}, u32[]{:S(2)}) collective-permute-start(s16[336,128]{1,0:T(8,128)(2,1)S(1)} %get-tuple-element.104), channel_id=1, source_target_pairs={{0,7},{1,6},{2,5},{3,4},{4,3},{5,2},{6,1},{7,0},{8,15},{9,14},{10,... | collective-permute-start | bytes 258056 | tf_op jit(solution)/shard_map/ppermute | solution.py:467
  99.4 20.5 %collective-permute-start.23 = (s16[336,128]{1,0:T(8,128)(2,1)S(1)}, s16[336,128]{1,0:T(8,128)(2,1)S(1)}, u32[]{:S(2)}, u32[]{:S(2)}) collective-permute-start(s16[336,128]{1,0:T(8,128)(2,1)S(1)} %get-tuple-element.105), channel_id=1, source_target_pairs={{0,6},{1,7},{2,4},{3,5},{4,2},{5,3},{6,0},{7,1},{8,14},{9,15},{10,... | collective-permute-start | bytes 258056 | tf_op jit(solution)/shard_map/ppermute | solution.py:467
  105.7 15.0 %collective-permute-start.24 = (s16[336,128]{1,0:T(8,128)(2,1)S(1)}, s16[336,128]{1,0:T(8,128)(2,1)S(1)}, u32[]{:S(2)}, u32[]{:S(2)}) collective-permute-start(s16[336,128]{1,0:T(8,128)(2,1)S(1)} %get-tuple-element.106), channel_id=1, source_target_pairs={{0,5},{1,4},{2,7},{3,6},{4,1},{5,0},{6,3},{7,2},{8,13},{9,12},{10,... | collective-permute-start | bytes 258056 | tf_op jit(solution)/shard_map/ppermute | solution.py:467
  115.7 8.5 %collective-permute-start.25 = (s16[336,128]{1,0:T(8,128)(2,1)S(1)}, s16[336,128]{1,0:T(8,128)(2,1)S(1)}, u32[]{:S(2)}, u32[]{:S(2)}) collective-permute-start(s16[336,128]{1,0:T(8,128)(2,1)S(1)} %get-tuple-element.107), channel_id=1, source_target_pairs={{0,4},{1,5},{2,6},{3,7},{4,0},{5,1},{6,2},{7,3},{8,12},{9,13},{10,... | collective-permute-start | bytes 258056 | tf_op jit(solution)/shard_map/ppermute | solution.py:467
  115.7 8.5 %collective-permute-start.26 = (s16[336,128]{1,0:T(8,128)(2,1)S(1)}, s16[336,128]{1,0:T(8,128)(2,1)S(1)}, u32[]{:S(2)}, u32[]{:S(2)}) collective-permute-start(s16[336,128]{1,0:T(8,128)(2,1)S(1)} %get-tuple-element.108), channel_id=1, source_target_pairs={{0,3},{1,2},{2,1},{3,0},{4,7},{5,6},{6,5},{7,4},{8,11},{9,10},{10,... | collective-permute-start | bytes 258056 | tf_op jit(solution)/shard_map/ppermute | solution.py:467
  119.9 6.0 %collective-permute-start.27 = (s16[336,128]{1,0:T(8,128)(2,1)S(1)}, s16[336,128]{1,0:T(8,128)(2,1)S(1)}, u32[]{:S(2)}, u32[]{:S(2)}) collective-permute-start(s16[336,128]{1,0:T(8,128)(2,1)S(1)} %get-tuple-element.109), channel_id=1, source_target_pairs={{0,2},{1,3},{2,0},{3,1},{4,6},{5,7},{6,4},{7,5},{8,10},{9,11},{10,... | collective-permute-start | bytes 258056 | tf_op jit(solution)/shard_map/ppermute | solution.py:467
  119.9 6.0 %collective-permute-start.28 = (s16[336,128]{1,0:T(8,128)(2,1)S(1)}, s16[336,128]{1,0:T(8,128)(2,1)S(1)}, u32[]{:S(2)}, u32[]{:S(2)}) collective-permute-start(s16[336,128]{1,0:T(8,128)(2,1)S(1)} %get-tuple-element.110), channel_id=1, source_target_pairs={{0,1},{1,0},{2,3},{3,2},{4,5},{5,4},{6,7},{7,6},{8,9},{9,8},{10,11... | collective-permute-start | bytes 258056 | tf_op jit(solution)/shard_map/ppermute | solution.py:467
  126.7 2.3 %collective-permute-start.29 = (f32[1440,128]{1,0:T(8,128)S(1)}, f32[1440,128]{1,0:T(8,128)S(1)}, u32[]{:S(2)}, u32[]{:S(2)}) collective-permute-start(f32[1440,128]{1,0:T(8,128)S(1)} %get-tuple-element.112), channel_id=1, source_target_pairs={{0,8},{8,0},{16,24},{24,16},{32,40},{40,32},{48,56},{56,48},{64,72... | collective-permute-start | bytes 2211848 | tf_op jit(solution)/shard_map/ppermute | solution.py:578
  130.3 14.9 %collective-permute-start.30 = (s16[992,128]{1,0:T(8,128)(2,1)S(1)}, s16[992,128]{1,0:T(8,128)(2,1)S(1)}, u32[]{:S(2)}, u32[]{:S(2)}) collective-permute-start(s16[992,128]{1,0:T(8,128)(2,1)S(1)} %get-tuple-element.114), channel_id=1, source_target_pairs={{0,192},{8,200},{16,208},{24,216},{32,224},{40,232},{48,240},{56,2... | collective-permute-start | bytes 761864 | tf_op jit(solution)/shard_map/ppermute | solution.py:467
  130.8 14.4 %collective-permute-start.31 = (s16[992,128]{1,0:T(8,128)(2,1)S(1)}, s16[992,128]{1,0:T(8,128)(2,1)S(1)}, u32[]{:S(2)}, u32[]{:S(2)}) collective-permute-start(s16[992,128]{1,0:T(8,128)(2,1)S(1)} %get-tuple-element.115), channel_id=1, source_target_pairs={{0,128},{8,136},{16,144},{24,152},{32,160},{40,168},{48,176},{56,1... | collective-permute-start | bytes 761864 | tf_op jit(solution)/shard_map/ppermute | solution.py:467
  133.3 12.6 %collective-permute-start.32 = (s16[992,128]{1,0:T(8,128)(2,1)S(1)}, s16[992,128]{1,0:T(8,128)(2,1)S(1)}, u32[]{:S(2)}, u32[]{:S(2)}) collective-permute-start(s16[992,128]{1,0:T(8,128)(2,1)S(1)} %get-tuple-element.116), channel_id=1, source_target_pairs={{0,64},{8,72},{16,80},{24,88},{32,96},{40,104},{48,112},{56,120},{... | collective-permute-start | bytes 761864 | tf_op jit(solution)/shard_map/ppermute | solution.py:467
  146.2 14.8 %collective-permute-start.33 = (s16[256,128]{1,0:T(8,128)(2,1)S(1)}, s16[256,128]{1,0:T(8,128)(2,1)S(1)}, u32[]{:S(2)}, u32[]{:S(2)}) collective-permute-start(s16[256,128]{1,0:T(8,128)(2,1)S(1)} %get-tuple-element.118), channel_id=1, source_target_pairs={{0,48},{8,56},{16,32},{24,40},{32,16},{40,24},{48,0},{56,8},{64,11... | collective-permute-start | bytes 196616 | tf_op jit(solution)/shard_map/ppermute | solution.py:467
  148.2 16.6 %collective-permute-start.34 = (s16[256,128]{1,0:T(8,128)(2,1)S(1)}, s16[256,128]{1,0:T(8,128)(2,1)S(1)}, u32[]{:S(2)}, u32[]{:S(2)}) collective-permute-start(s16[256,128]{1,0:T(8,128)(2,1)S(1)} %get-tuple-element.119), channel_id=1, source_target_pairs={{0,32},{8,40},{16,48},{24,56},{32,0},{40,8},{48,16},{56,24},{64,96... | collective-permute-start | bytes 196616 | tf_op jit(solution)/shard_map/ppermute | solution.py:467
  161.0 4.5 %collective-permute-start.35 = (s16[256,128]{1,0:T(8,128)(2,1)S(1)}, s16[256,128]{1,0:T(8,128)(2,1)S(1)}, u32[]{:S(2)}, u32[]{:S(2)}) collective-permute-start(s16[256,128]{1,0:T(8,128)(2,1)S(1)} %get-tuple-element.120), channel_id=1, source_target_pairs={{0,16},{8,24},{16,0},{24,8},{32,48},{40,56},{48,32},{56,40},{64,80... | collective-permute-start | bytes 196616 | tf_op jit(solution)/shard_map/ppermute | solution.py:467
  (1 other events, 0.7 us)

commit v6 on v5

--- a/solution.py
+++ b/solution.py
@@ -496,33 +496,36 @@
     between = functools.partial(across, groups)
 
     local = velocity.reshape(block, count_z)
-    near = [local] + exchange([local] * (HALVES * SIZE_Z - 1), ("shot", "dom"), functools.partial(swap_z, groups))
+    side = groups // HALVES
+    far = lax.ppermute(local, "dom", between(side))
+    lines = []
+    for mine in (local, far):
+        blocks = [mine] + exchange([mine] * (SIZE_Z - 1), "shot", along["z"])
+        lines += call(join_kernel, (struct((SIZE_Z * block, count_z), BF16),), blocks, "v" * SIZE_Z)
 
     half = halo_rows(2 * HALO, count_y)
     code = struct((half, count_z), I16)
     levels = pltpu.VMEM((2 * HALO * count_y // GROUP, count_z), I32)
-    (line,) = call(join_kernel, (struct((len(near) * block, count_z), BF16),), near, "v" * len(near))
-
-    p0, line = lax.optimization_barrier((p0, line))
     one, two = call(encode_kernel, (code, code), (p0, q0), "vv", (levels,))
     from_one = lax.ppermute(one, "dom", one_pairs)
     from_two = lax.ppermute(two, "dom", two_pairs)
-    anchors, line = lax.optimization_barrier((anchors, line))
-    other = lax.ppermute(anchors, "shot", swap("c", 1))
+    near_anchors, _ = lax.optimization_barrier((anchors, lines[0]))
+    other = lax.ppermute(near_anchors, "shot", swap("c", 1))
     field = struct((row_count, count_y, count_z), F32)
     hits = call(hit_kernel, (field, field), (start_step, receivers[0], traces[0]), "svv", work=4)
     padded = pltpu.VMEM((row_count + 2 * HALO, count_y + 2 * PAD, count_z), F32)
     sums = call(before_kernel, (field,) * 4, (p0, q0, p_prev, q_prev, hits[0]), "v" * 5, (padded,), work=6)
-    plane = [line] + exchange([line] * (SIZE_X - 1), "shot", along["x"])
-    plane, other = lax.optimization_barrier((plane, sums[0], other))[::2]
+    plane = []
+    for line in lines:
+        plane += [line] + exchange([line] * (SIZE_X - 1), "shot", along["x"])
+    plane, _, other, from_two, from_one = lax.optimization_barrier((plane, sums[0], other, from_two, from_one))
     plane += [lax.ppermute(part, "shot", swap("c", 1)) for part in plane]
-    *plane, from_two, from_one = lax.optimization_barrier((*plane, from_two, from_one))
     layout = [
-        [(dx, k % SIZE_Z, dc, k // SIZE_Z) for k in range(HALVES * SIZE_Z)]
+        [(dx, dz, dc, dh) for dz in range(SIZE_Z)]
         for dc in range(SIZE_C)
+        for dh in range(HALVES)
         for dx in range(SIZE_X)
     ]
-    side = groups // HALVES
     pieces = call(
         functools.partial(pick_kernel, layout, row_count, HALVES),
         [struct((HALVES * piece, count_z), BF16)] * side,

time: 167 us -> 175 us (1.048)
  starting transfers between devices: 82.6 us -> 90.9 us
    ppermute x1 -> x2, starting transfers between devices: 0.01 us -> 7.37 us  [the longest x1 7.28 us: body(): far = lax.ppermute(local, 'dom', between(side))]
    ppermute x26 -> x28, starting transfers between devices: 74.5 us -> 73.7 us  [exchange(): got[k] = lax.ppermute(parts[k - 1], axis, pairs(k))]
    ppermute x26 -> x28, waiting for transfers between devices: 38.4 us -> 38.8 us  [exchange(): got[k] = lax.ppermute(parts[k - 1], axis, pairs(k))]
    unnamed x27 -> x23, local copies, waits for them, and re-layouts: 6.45 us -> 6.78 us
    pallas_call x12 -> x13, Pallas kernels: 25.3 us -> 25.3 us  [call(): pl.pallas_call(kernel, out_shape=list(outs), in_specs=[smem() if s == 's'...]
  transfers between devices with their start and end apart: 36 -> 43, of which waited for: 20 -> 21; matrix products, arithmetic and copies ran while one was open for 0% -> 0% of each run, Pallas kernels for 9% -> 9%
where the time goes in v6:
time: 175 us; the launch traced here: 174 us
  starting transfers between devices  90.9 us (52%)
  waiting for transfers between devices  49.8 us (28%)
  Pallas kernels  25.3 us (14%)
  local copies, waits for them, and re-layouts  6.78 us (4%)
    ppermute x28, starting transfers between devices, exchange(): got[k] = lax.ppermute(parts[k - 1], axis, pairs(k))  73.7 us
    ppermute x28, waiting for transfers between devices, exchange(): got[k] = lax.ppermute(parts[k - 1], axis, pairs(k))  38.8 us
    pallas_call x13, Pallas kernels, call(): pl.pallas_call(kernel, out_shape=list(outs), in_specs=[smem() if s == 's'...  25.3 us
    ppermute x1, starting transfers between devices, body(): far = lax.ppermute(local, 'dom', between(side))  7.28 us
    unnamed x23, local copies, waits for them, and re-layouts  6.78 us
    ppermute x2, starting transfers between devices, body(): from_one = lax.ppermute(one, 'dom', one_pairs)  6.62 us
    ppermute x2, waiting for transfers between devices, body(): from_one = lax.ppermute(one, 'dom', one_pairs)  5.13 us
  transfers between devices with their start and end apart: 43, of which 21 were waited for; matrix products, arithmetic and copies ran while one was open for 0% of the time, Pallas kernels for 9%

profile of v6, /device:TPU:6, one launch (start us, length us, event | category | flops | bytes accessed | tf_op | source)
XLA Modules:
  0.0 174.4 jit_solution(163153774114708658)
XLA Ops:
  0.6 7.3 %collective-permute-start.6 = (bf16[240,128]{1,0:T(8,128)(2,1)}, bf16[240,128]{1,0:T(8,128)(2,1)S(1)}, u32[]{:S(2)}, u32[]{:S(2)}) collective-permute-start(bf16[240,128]{1,0:T(8,128)(2,1)} %bitcast.23), channel_id=1, source_target_pairs={{0,4},{1,5},{2,6},{3,7},{4,0},{5,1},{6,2},{7,3},{8,12},{9,13},{10,... | collective-permute-start | bytes 184328 | tf_op jit(solution)/shard_map/ppermute | solution.py:500
  7.9 1.9 %collective-permute-start.2 = (bf16[240,128]{1,0:T(8,128)(2,1)}, bf16[240,128]{1,0:T(8,128)(2,1)S(1)}, u32[]{:S(2)}, u32[]{:S(2)}) collective-permute-start(bf16[240,128]{1,0:T(8,128)(2,1)} %bitcast.24), channel_id=1, source_target_pairs={{0,48},{8,56},{16,32},{24,40},{32,16},{40,24},{48,0},{56,8},{64,11... | collective-permute-start | bytes 184328 | tf_op jit(solution)/shard_map/ppermute | solution.py:467
  10.4 1.9 %collective-permute-start = (bf16[240,128]{1,0:T(8,128)(2,1)}, bf16[240,128]{1,0:T(8,128)(2,1)S(1)}, u32[]{:S(2)}, u32[]{:S(2)}) collective-permute-start(bf16[240,128]{1,0:T(8,128)(2,1)} %bitcast.26), channel_id=1, source_target_pairs={{0,16},{8,24},{16,0},{24,8},{32,48},{40,56},{48,32},{56,40},{64,80... | collective-permute-start | bytes 184328 | tf_op jit(solution)/shard_map/ppermute | solution.py:467
  12.3 2.2 %collective-permute-start.9 = (bf16[240,128]{1,0:T(8,128)(2,1)S(1)}, bf16[240,128]{1,0:T(8,128)(2,1)S(1)}, u32[]{:S(2)}, u32[]{:S(2)}) collective-permute-start(bf16[240,128]{1,0:T(8,128)(2,1)S(1)} %collective-permute-done.6.refs_0_), channel_id=1, source_target_pairs={{0,48},{8,56},{16,32},{24,40},{32,16},{40,24},{48,0},{56,8},{64,11... | collective-permute-start | bytes 184328 | tf_op jit(solution)/shard_map/ppermute | solution.py:467
  14.6 3.5 %collective-permute-start.7 = (bf16[240,128]{1,0:T(8,128)(2,1)S(1)}, bf16[240,128]{1,0:T(8,128)(2,1)S(1)}, u32[]{:S(2)}, u32[]{:S(2)}) collective-permute-start(bf16[240,128]{1,0:T(8,128)(2,1)S(1)} %collective-permute-done.6.refs_0_), channel_id=1, source_target_pairs={{0,16},{8,24},{16,0},{24,8},{32,48},{40,56},{48,32},{56,40},{64,80... | collective-permute-start | bytes 184328 | tf_op jit(solution)/shard_map/ppermute | solution.py:467
  18.1 1.2 copy-done
  19.3 1.2 copy-done.2
  21.1 0.8 collective-permute-start.14
  22.0 0.8 copy-done.7
  22.9 1.2 collective-permute-done.13.other
  24.2 4.4 %collective-permute-start.15 = (s16[2112,128]{1,0:T(8,128)(2,1)S(1)}, s16[2112,128]{1,0:T(8,128)(2,1)S(1)}, u32[]{:S(2)}, u32[]{:S(2)}) collective-permute-start(s16[2112,128]{1,0:T(8,128)(2,1)S(1)} %get-tuple-element.62), channel_id=1, source_target_pairs={{0,1},{1,0},{2,3},{3,2},{4,5},{5,4},{6,7},{7,6},{8,9},{9,8},{10,11... | collective-permute-start | bytes 1622024 | tf_op jit(solution)/shard_map/ppermute | solution.py:510
  29.0 2.4 %collective-permute-start.4 = (bf16[960,128]{1,0:T(8,128)(2,1)S(1)}, bf16[960,128]{1,0:T(8,128)(2,1)S(1)}, u32[]{:S(2)}, u32[]{:S(2)}) collective-permute-start(bf16[960,128]{1,0:T(8,128)(2,1)S(1)} %shard_map.132.refs_0_), channel_id=1, source_target_pairs={{0,128},{8,136},{16,144},{24,152},{32,160},{40,168},{48,176},{56,1... | collective-permute-start | bytes 737288 | tf_op jit(solution)/shard_map/ppermute | solution.py:467
  31.5 1.2 collective-permute-start.3
  32.7 10.1 %collective-permute-done.5.refs_3_ = bf16[960,128]{1,0:T(8,128)(2,1)S(1)} collective-permute-done((bf16[960,128]{1,0:T(8,128)(2,1)S(1)}, bf16[960,128]{1,0:T(8,128)(2,1)S(1)}, u32[]{:S(2)}, u32[]{:S(2)}) %collective-permute-start.5) | collective-permute-done | bytes 245792 | tf_op jit(solution)/shard_map/ppermute | solution.py:467
  43.3 1.2 collective-permute-start.11
  44.5 2.4 %collective-permute-start.10 = (bf16[960,128]{1,0:T(8,128)(2,1)S(1)}, bf16[960,128]{1,0:T(8,128)(2,1)S(1)}, u32[]{:S(2)}, u32[]{:S(2)}) collective-permute-start(bf16[960,128]{1,0:T(8,128)(2,1)S(1)} %shard_map.133.refs_4_), channel_id=1, source_target_pairs={{0,64},{8,72},{16,80},{24,88},{32,96},{40,104},{48,112},{56,120},{... | collective-permute-start | bytes 737288 | tf_op jit(solution)/shard_map/ppermute | solution.py:467
  47.6 0.7 copy.16
  48.3 0.9 copy-done.6
  49.2 3.4 %shard_map.130 = (f32[8,256,128]{2,1,0:T(8,128)S(1)}, f32[8,256,128]{2,1,0:T(8,128)S(1)}) custom-call(s32[1]{0:T(128)S(6)} %copy.17.begin, s32[3,512]{1,0:T(4,128)S(1)} %bitcast.28, f32[64,512]{1,0:T(8,128)S(1)} %bitcast.22), custom_call_target="tpu_custom_call" | custom-call | bytes 14760000 | tf_op jit(solution)/shard_map/pallas_call | solution.py:36
  52.6 1.2 copy-done.5
  53.8 6.0 %shard_map.131 = (f32[8,256,128]{2,1,0:T(8,128)S(1)}, f32[8,256,128]{2,1,0:T(8,128)S(1)}, f32[8,256,128]{2,1,0:T(8,128)S(1)}, f32[8,256,128]{2,1,0:T(8,128)S(1)}) custom-call(f32[8,256,128]{2,1,0:T(8,128)S(1)} %bitcast.13, f32[8,256,128]{2,1,0:T(8,128)S(1)} %bitcast.17, f32[8,256,128]{2,1,0:T(8,128)S(1)} %bitcast.19, f32[8,256,128]{2,1,0:T(8,128)S(1)} %bitcast.21, ...), custom_call_target="tpu_custom_call" | custom-call | bytes 22140000 | tf_op jit(solution)/shard_map/pallas_call | solution.py:36
  64.0 1.2 shard_map.135
  65.2 3.5 %collective-permute-start.24 = (bf16[640,128]{1,0:T(8,128)(2,1)S(1)}, bf16[640,128]{1,0:T(8,128)(2,1)S(1)}, u32[]{:S(2)}, u32[]{:S(2)}) collective-permute-start(bf16[640,128]{1,0:T(8,128)(2,1)S(1)} %get-tuple-element.74), channel_id=1, source_target_pairs={{0,3},{1,2},{2,1},{3,0},{4,7},{5,6},{6,5},{7,4},{8,11},{9,10},{10,... | collective-permute-start | bytes 491528 | tf_op jit(solution)/shard_map/ppermute | solution.py:467
  68.7 1.3 collective-permute-start.25
  70.0 6.2 %collective-permute-done.24.rest_3_ = bf16[640,128]{1,0:T(8,128)(2,1)S(1)} collective-permute-done((bf16[640,128]{1,0:T(8,128)(2,1)S(1)}, bf16[640,128]{1,0:T(8,128)(2,1)S(1)}, u32[]{:S(2)}, u32[]{:S(2)}) %collective-permute-start.24) | collective-permute-done | bytes 163872 | tf_op jit(solution)/shard_map/ppermute | solution.py:467
  76.2 1.1 collective-permute-done.25.rest_4_
  78.3 2.0 %shard_map.136 = (f32[8,256,128]{2,1,0:T(8,128)S(1)}, f32[8,256,128]{2,1,0:T(8,128)S(1)}, f32[8,256,128]{2,1,0:T(8,128)S(1)}, s16[2112,128]{1,0:T(8,128)(2,1)S(1)}, s16[2112,128]{1,0:T(8,128)(2,1)S(1)}) custom-call(s32[1,2]{1,0:T(1,128)S(1)} %copy-done.8, s32[1,3]{1,0:T(1,128)S(1)} %copy-done.9, s32[1]{0:T(128)S(6)} %copy.17.begin, f32[64]{0:T(128)S(1)} %copy-done.10, ...), custom_call_target="tpu_custom_call" | custom-call | tf_op jit(solution)/shard_map/pallas_call | solution.py:36
  80.3 2.3 %collective-permute-start.27 = (s16[2112,128]{1,0:T(8,128)(2,1)S(1)}, s16[2112,128]{1,0:T(8,128)(2,1)S(1)}, u32[]{:S(2)}, u32[]{:S(2)}) collective-permute-start(s16[2112,128]{1,0:T(8,128)(2,1)S(1)} %get-tuple-element.84), channel_id=1, source_target_pairs={{0,1},{1,0},{2,3},{3,2},{4,5},{5,4},{6,7},{7,6},{8,9},{9,8},{10,11... | collective-permute-start | bytes 1622024 | tf_op jit(solution)/shard_map/ppermute | solution.py:547
  83.2 5.9 %shard_map.137 = (f32[8,256,128]{2,1,0:T(8,128)S(1)}, f32[8,256,128]{2,1,0:T(8,128)S(1)}, f32[8,256,128]{2,1,0:T(8,128)S(1)}) custom-call(f32[8,256,128]{2,1,0:T(8,128)S(1)} %get-tuple-element.77.p1, f32[8,256,128]{2,1,0:T(8,128)S(1)} %get-tuple-element.78.q1, f32[8,256,128]{2,1,0:T(8,128)S(1)} %bitcast.14, f32[8,256,128]{2,1,0:T(8,128)S(1)} %bitcast.18, ...), custom_call_target="tpu_custom_call" | custom-call | bytes 22140000 | tf_op jit(solution)/shard_map/pallas_call | solution.py:36
  89.2 5.1 %collective-permute-done.27.one = s16[2112,128]{1,0:T(8,128)(2,1)S(1)} collective-permute-done((s16[2112,128]{1,0:T(8,128)(2,1)S(1)}, s16[2112,128]{1,0:T(8,128)(2,1)S(1)}, u32[]{:S(2)}, u32[]{:S(2)}) %collective-permute-start.27) | collective-permute-done | bytes 540704 | tf_op jit(solution)/shard_map/ppermute | solution.py:547
  94.3 3.1 %shard_map.138 = (f32[8,256,128]{2,1,0:T(8,128)}, f32[8,256,128]{2,1,0:T(8,128)}, f32[320,128]{1,0:T(8,128)S(1)}, s16[336,128]{1,0:T(8,128)(2,1)S(1)}, s16[336,1...) custom-call(s32[1,2]{1,0:T(1,128)S(1)} %copy-done.8, ...), custom_call_target="tpu_custom_call" | custom-call | tf_op jit(solution)/shard_map/pallas_call | solution.py:36
  97.4 4.8 %collective-permute-start.29 = (s16[336,128]{1,0:T(8,128)(2,1)S(1)}, s16[336,128]{1,0:T(8,128)(2,1)S(1)}, u32[]{:S(2)}, u32[]{:S(2)}) collective-permute-start(s16[336,128]{1,0:T(8,128)(2,1)S(1)} %get-tuple-element.90), channel_id=1, source_target_pairs={{0,7},{1,6},{2,5},{3,4},{4,3},{5,2},{6,1},{7,0},{8,15},{9,14},{10,... | collective-permute-start | bytes 258056 | tf_op jit(solution)/shard_map/ppermute | solution.py:467
  102.2 5.7 %collective-permute-start.30 = (s16[336,128]{1,0:T(8,128)(2,1)S(1)}, s16[336,128]{1,0:T(8,128)(2,1)S(1)}, u32[]{:S(2)}, u32[]{:S(2)}) collective-permute-start(s16[336,128]{1,0:T(8,128)(2,1)S(1)} %get-tuple-element.91), channel_id=1, source_target_pairs={{0,6},{1,7},{2,4},{3,5},{4,2},{5,3},{6,0},{7,1},{8,14},{9,15},{10,... | collective-permute-start | bytes 258056 | tf_op jit(solution)/shard_map/ppermute | solution.py:467
  107.9 11.4 %collective-permute-start.31 = (s16[336,128]{1,0:T(8,128)(2,1)S(1)}, s16[336,128]{1,0:T(8,128)(2,1)S(1)}, u32[]{:S(2)}, u32[]{:S(2)}) collective-permute-start(s16[336,128]{1,0:T(8,128)(2,1)S(1)} %get-tuple-element.92), channel_id=1, source_target_pairs={{0,5},{1,4},{2,7},{3,6},{4,1},{5,0},{6,3},{7,2},{8,13},{9,12},{10,... | collective-permute-start | bytes 258056 | tf_op jit(solution)/shard_map/ppermute | solution.py:467
  119.3 3.8 %collective-permute-start.33 = (s16[336,128]{1,0:T(8,128)(2,1)S(1)}, s16[336,128]{1,0:T(8,128)(2,1)S(1)}, u32[]{:S(2)}, u32[]{:S(2)}) collective-permute-start(s16[336,128]{1,0:T(8,128)(2,1)S(1)} %get-tuple-element.94), channel_id=1, source_target_pairs={{0,3},{1,2},{2,1},{3,0},{4,7},{5,6},{6,5},{7,4},{8,11},{9,10},{10,... | collective-permute-start | bytes 258056 | tf_op jit(solution)/shard_map/ppermute | solution.py:467
  123.1 0.9 collective-permute-start.35
  124.0 3.7 %collective-permute-done.32.refs_3_ = s16[336,128]{1,0:T(8,128)(2,1)S(1)} collective-permute-done((s16[336,128]{1,0:T(8,128)(2,1)S(1)}, s16[336,128]{1,0:T(8,128)(2,1)S(1)}, u32[]{:S(2)}, u32[]{:S(2)}) %collective-permute-start.32) | collective-permute-done | bytes 86048 | tf_op jit(solution)/shard_map/ppermute | solution.py:467
  127.7 1.4 collective-permute-done.34.refs_5_
  129.1 0.9 shard_map.139
  130.1 2.2 %collective-permute-done.36.got = f32[1440,128]{1,0:T(8,128)S(1)} collective-permute-done((f32[1440,128]{1,0:T(8,128)S(1)}, f32[1440,128]{1,0:T(8,128)S(1)}, u32[]{:S(2)}, u32[]{:S(2)}) %collective-permute-start.36) | collective-permute-done | bytes 737312 | tf_op jit(solution)/shard_map/ppermute | solution.py:581
  132.3 1.2 shard_map.140
  133.9 1.8 %collective-permute-start.38 = (s16[992,128]{1,0:T(8,128)(2,1)S(1)}, s16[992,128]{1,0:T(8,128)(2,1)S(1)}, u32[]{:S(2)}, u32[]{:S(2)}) collective-permute-start(s16[992,128]{1,0:T(8,128)(2,1)S(1)} %get-tuple-element.101), channel_id=1, source_target_pairs={{0,128},{8,136},{16,144},{24,152},{32,160},{40,168},{48,176},{56,1... | collective-permute-start | bytes 761864 | tf_op jit(solution)/shard_map/ppermute | solution.py:467
  135.6 2.0 %collective-permute-start.39 = (s16[992,128]{1,0:T(8,128)(2,1)S(1)}, s16[992,128]{1,0:T(8,128)(2,1)S(1)}, u32[]{:S(2)}, u32[]{:S(2)}) collective-permute-start(s16[992,128]{1,0:T(8,128)(2,1)S(1)} %get-tuple-element.102), channel_id=1, source_target_pairs={{0,64},{8,72},{16,80},{24,88},{32,96},{40,104},{48,112},{56,120},{... | collective-permute-start | bytes 761864 | tf_op jit(solution)/shard_map/ppermute | solution.py:467
  137.7 10.7 %collective-permute-done.37.refs_0_ = s16[992,128]{1,0:T(8,128)(2,1)S(1)} collective-permute-done((s16[992,128]{1,0:T(8,128)(2,1)S(1)}, s16[992,128]{1,0:T(8,128)(2,1)S(1)}, u32[]{:S(2)}, u32[]{:S(2)}) %collective-permute-start.37) | collective-permute-done | bytes 253984 | tf_op jit(solution)/shard_map/ppermute | solution.py:467
  149.4 2.4 %collective-permute-start.40 = (s16[256,128]{1,0:T(8,128)(2,1)S(1)}, s16[256,128]{1,0:T(8,128)(2,1)S(1)}, u32[]{:S(2)}, u32[]{:S(2)}) collective-permute-start(s16[256,128]{1,0:T(8,128)(2,1)S(1)} %get-tuple-element.104), channel_id=1, source_target_pairs={{0,48},{8,56},{16,32},{24,40},{32,16},{40,24},{48,0},{56,8},{64,11... | collective-permute-start | bytes 196616 | tf_op jit(solution)/shard_map/ppermute | solution.py:467
  151.7 17.4 %collective-permute-start.41 = (s16[256,128]{1,0:T(8,128)(2,1)S(1)}, s16[256,128]{1,0:T(8,128)(2,1)S(1)}, u32[]{:S(2)}, u32[]{:S(2)}) collective-permute-start(s16[256,128]{1,0:T(8,128)(2,1)S(1)} %get-tuple-element.105), channel_id=1, source_target_pairs={{0,32},{8,40},{16,48},{24,56},{32,0},{40,8},{48,16},{56,24},{64,96... | collective-permute-start | bytes 196616 | tf_op jit(solution)/shard_map/ppermute | solution.py:467
  169.1 3.8 %collective-permute-done.41.refs_1_ = s16[256,128]{1,0:T(8,128)(2,1)S(1)} collective-permute-done((s16[256,128]{1,0:T(8,128)(2,1)S(1)}, s16[256,128]{1,0:T(8,128)(2,1)S(1)}, u32[]{:S(2)}, u32[]{:S(2)}) %collective-permute-start.41) | collective-permute-done | bytes 65568 | tf_op jit(solution)/shard_map/ppermute | solution.py:467
  173.7 0.7 shard_map.142
  (74 shorter events, 10.3 us)
Async XLA Ops:
  0.6 11.7 %collective-permute-start.6 = (bf16[240,128]{1,0:T(8,128)(2,1)}, bf16[240,128]{1,0:T(8,128)(2,1)S(1)}, u32[]{:S(2)}, u32[]{:S(2)}) collective-permute-start(bf16[240,128]{1,0:T(8,128)(2,1)} %bitcast.23), channel_id=1, source_target_pairs={{0,4},{1,5},{2,6},{3,7},{4,0},{5,1},{6,2},{7,3},{8,12},{9,13},{10,... | collective-permute-start | bytes 184328 | tf_op jit(solution)/shard_map/ppermute | solution.py:500
  7.9 6.7 %collective-permute-start.2 = (bf16[240,128]{1,0:T(8,128)(2,1)}, bf16[240,128]{1,0:T(8,128)(2,1)S(1)}, u32[]{:S(2)}, u32[]{:S(2)}) collective-permute-start(bf16[240,128]{1,0:T(8,128)(2,1)} %bitcast.24), channel_id=1, source_target_pairs={{0,48},{8,56},{16,32},{24,40},{32,16},{40,24},{48,0},{56,8},{64,11... | collective-permute-start | bytes 184328 | tf_op jit(solution)/shard_map/ppermute | solution.py:467
  9.8 11.3 %collective-permute-start.1 = (bf16[240,128]{1,0:T(8,128)(2,1)}, bf16[240,128]{1,0:T(8,128)(2,1)S(1)}, u32[]{:S(2)}, u32[]{:S(2)}) collective-permute-start(bf16[240,128]{1,0:T(8,128)(2,1)} %bitcast.25), channel_id=1, source_target_pairs={{0,32},{8,40},{16,48},{24,56},{32,0},{40,8},{48,16},{56,24},{64,96... | collective-permute-start | bytes 184328 | tf_op jit(solution)/shard_map/ppermute | solution.py:467
  10.4 11.6 %collective-permute-start = (bf16[240,128]{1,0:T(8,128)(2,1)}, bf16[240,128]{1,0:T(8,128)(2,1)S(1)}, u32[]{:S(2)}, u32[]{:S(2)}) collective-permute-start(bf16[240,128]{1,0:T(8,128)(2,1)} %bitcast.26), channel_id=1, source_target_pairs={{0,16},{8,24},{16,0},{24,8},{32,48},{40,56},{48,32},{56,40},{64,80... | collective-permute-start | bytes 184328 | tf_op jit(solution)/shard_map/ppermute | solution.py:467
  12.3 16.3 %collective-permute-start.9 = (bf16[240,128]{1,0:T(8,128)(2,1)S(1)}, bf16[240,128]{1,0:T(8,128)(2,1)S(1)}, u32[]{:S(2)}, u32[]{:S(2)}) collective-permute-start(bf16[240,128]{1,0:T(8,128)(2,1)S(1)} %collective-permute-done.6.refs_0_), channel_id=1, source_target_pairs={{0,48},{8,56},{16,32},{24,40},{32,16},{40,24},{48,0},{56,8},{64,11... | collective-permute-start | bytes 184328 | tf_op jit(solution)/shard_map/ppermute | solution.py:467
  14.4 14.6 %collective-permute-start.8 = (bf16[240,128]{1,0:T(8,128)(2,1)S(1)}, bf16[240,128]{1,0:T(8,128)(2,1)S(1)}, u32[]{:S(2)}, u32[]{:S(2)}) collective-permute-start(bf16[240,128]{1,0:T(8,128)(2,1)S(1)} %collective-permute-done.6.refs_0_), channel_id=1, source_target_pairs={{0,32},{8,40},{16,48},{24,56},{32,0},{40,8},{48,16},{56,24},{64,96... | collective-permute-start | bytes 184328 | tf_op jit(solution)/shard_map/ppermute | solution.py:467
  14.6 16.9 %collective-permute-start.7 = (bf16[240,128]{1,0:T(8,128)(2,1)S(1)}, bf16[240,128]{1,0:T(8,128)(2,1)S(1)}, u32[]{:S(2)}, u32[]{:S(2)}) collective-permute-start(bf16[240,128]{1,0:T(8,128)(2,1)S(1)} %collective-permute-done.6.refs_0_), channel_id=1, source_target_pairs={{0,16},{8,24},{16,0},{24,8},{32,48},{40,56},{48,32},{56,40},{64,80... | collective-permute-start | bytes 184328 | tf_op jit(solution)/shard_map/ppermute | solution.py:467
  20.6 32.0 %copy-start.3 = (f32[1,8,256,128]{3,2,1,0:T(8,128)S(1)}, f32[1,8,256,128]{3,2,1,0:T(8,128)}, u32[]{:S(2)}) copy-start(f32[1,8,256,128]{3,2,1,0:T(8,128)} %param.21) | copy-start | bytes 3145732
  20.6 32.0 %copy-start.4 = (f32[1,8,256,128]{3,2,1,0:T(8,128)S(1)}, f32[1,8,256,128]{3,2,1,0:T(8,128)}, u32[]{:S(2)}) copy-start(f32[1,8,256,128]{3,2,1,0:T(8,128)} %param.18) | copy-start | bytes 3145732
  21.1 31.4 %copy-start.1 = (f32[1,8,256,128]{3,2,1,0:T(8,128)S(1)}, f32[1,8,256,128]{3,2,1,0:T(8,128)}, u32[]{:S(2)}) copy-start(f32[1,8,256,128]{3,2,1,0:T(8,128)} %param.19) | copy-start | bytes 3145732
  21.1 38.7 %collective-permute-start.14 = (s16[2112,128]{1,0:T(8,128)(2,1)S(1)}, s16[2112,128]{1,0:T(8,128)(2,1)S(1)}, u32[]{:S(2)}, u32[]{:S(2)}) collective-permute-start(s16[2112,128]{1,0:T(8,128)(2,1)S(1)} %get-tuple-element.61), channel_id=1, source_target_pairs={{1,2},{3,4},{5,6},{2,1},{4,3},{6,5},{9,10},{11,12},{13,14},{10,9},... | collective-permute-start | bytes 1622024 | tf_op jit(solution)/shard_map/ppermute | solution.py:511
  22.8 1.3 collective-permute-start.13
  24.2 35.7 %collective-permute-start.15 = (s16[2112,128]{1,0:T(8,128)(2,1)S(1)}, s16[2112,128]{1,0:T(8,128)(2,1)S(1)}, u32[]{:S(2)}, u32[]{:S(2)}) collective-permute-start(s16[2112,128]{1,0:T(8,128)(2,1)S(1)} %get-tuple-element.62), channel_id=1, source_target_pairs={{0,1},{1,0},{2,3},{3,2},{4,5},{5,4},{6,7},{7,6},{8,9},{9,8},{10,11... | collective-permute-start | bytes 1622024 | tf_op jit(solution)/shard_map/ppermute | solution.py:510
  28.6 14.3 %collective-permute-start.5 = (bf16[960,128]{1,0:T(8,128)(2,1)S(1)}, bf16[960,128]{1,0:T(8,128)(2,1)S(1)}, u32[]{:S(2)}, u32[]{:S(2)}) collective-permute-start(bf16[960,128]{1,0:T(8,128)(2,1)S(1)} %shard_map.132.refs_0_), channel_id=1, source_target_pairs={{0,192},{8,200},{16,208},{24,216},{32,224},{40,232},{48,240},{56,2... | collective-permute-start | bytes 737288 | tf_op jit(solution)/shard_map/ppermute | solution.py:467
  29.0 14.3 %collective-permute-start.4 = (bf16[960,128]{1,0:T(8,128)(2,1)S(1)}, bf16[960,128]{1,0:T(8,128)(2,1)S(1)}, u32[]{:S(2)}, u32[]{:S(2)}) collective-permute-start(bf16[960,128]{1,0:T(8,128)(2,1)S(1)} %shard_map.132.refs_0_), channel_id=1, source_target_pairs={{0,128},{8,136},{16,144},{24,152},{32,160},{40,168},{48,176},{56,1... | collective-permute-start | bytes 737288 | tf_op jit(solution)/shard_map/ppermute | solution.py:467
  31.5 13.1 %collective-permute-start.3 = (bf16[960,128]{1,0:T(8,128)(2,1)S(1)}, bf16[960,128]{1,0:T(8,128)(2,1)S(1)}, u32[]{:S(2)}, u32[]{:S(2)}) collective-permute-start(bf16[960,128]{1,0:T(8,128)(2,1)S(1)} %shard_map.132.refs_0_), channel_id=1, source_target_pairs={{0,64},{8,72},{16,80},{24,88},{32,96},{40,104},{48,112},{56,120},{... | collective-permute-start | bytes 737288 | tf_op jit(solution)/shard_map/ppermute | solution.py:467
  42.8 17.0 %collective-permute-start.12 = (bf16[960,128]{1,0:T(8,128)(2,1)S(1)}, bf16[960,128]{1,0:T(8,128)(2,1)S(1)}, u32[]{:S(2)}, u32[]{:S(2)}) collective-permute-start(bf16[960,128]{1,0:T(8,128)(2,1)S(1)} %shard_map.133.refs_4_), channel_id=1, source_target_pairs={{0,192},{8,200},{16,208},{24,216},{32,224},{40,232},{48,240},{56,2... | collective-permute-start | bytes 737288 | tf_op jit(solution)/shard_map/ppermute | solution.py:467
  43.3 16.6 %collective-permute-start.11 = (bf16[960,128]{1,0:T(8,128)(2,1)S(1)}, bf16[960,128]{1,0:T(8,128)(2,1)S(1)}, u32[]{:S(2)}, u32[]{:S(2)}) collective-permute-start(bf16[960,128]{1,0:T(8,128)(2,1)S(1)} %shard_map.133.refs_4_), channel_id=1, source_target_pairs={{0,128},{8,136},{16,144},{24,152},{32,160},{40,168},{48,176},{56,1... | collective-permute-start | bytes 737288 | tf_op jit(solution)/shard_map/ppermute | solution.py:467
  44.5 15.4 %collective-permute-start.10 = (bf16[960,128]{1,0:T(8,128)(2,1)S(1)}, bf16[960,128]{1,0:T(8,128)(2,1)S(1)}, u32[]{:S(2)}, u32[]{:S(2)}) collective-permute-start(bf16[960,128]{1,0:T(8,128)(2,1)S(1)} %shard_map.133.refs_4_), channel_id=1, source_target_pairs={{0,64},{8,72},{16,80},{24,88},{32,96},{40,104},{48,112},{56,120},{... | collective-permute-start | bytes 737288 | tf_op jit(solution)/shard_map/ppermute | solution.py:467
  52.6 1.2 copy-start.5
  59.8 4.1 %copy-start.8 = (s32[1,2]{1,0:T(1,128)S(1)}, s32[1,2]{1,0:T(1,128)}, u32[]{:S(2)}) copy-start(s32[1,2]{1,0:T(1,128)} %anchors.9) | copy-start | bytes 28
  59.9 1.6 collective-permute-start.16
  60.0 1.9 %collective-permute-start.17 = (bf16[960,128]{1,0:T(8,128)(2,1)S(1)}, bf16[960,128]{1,0:T(8,128)(2,1)S(1)}, u32[]{:S(2)}, u32[]{:S(2)}) collective-permute-start(bf16[960,128]{1,0:T(8,128)(2,1)S(1)} %collective-permute-done.3.refs_1_), channel_id=1, source_target_pairs={{0,8},{8,0},{16,24},{24,16},{32,40},{40,32},{48,56},{56,48},{64,72... | collective-permute-start | bytes 737288 | tf_op jit(solution)/shard_map/ppermute | solution.py:522
  60.5 1.7 collective-permute-start.18
  60.6 2.0 %collective-permute-start.19 = (bf16[960,128]{1,0:T(8,128)(2,1)S(1)}, bf16[960,128]{1,0:T(8,128)(2,1)S(1)}, u32[]{:S(2)}, u32[]{:S(2)}) collective-permute-start(bf16[960,128]{1,0:T(8,128)(2,1)S(1)} %collective-permute-done.5.refs_3_), channel_id=1, source_target_pairs={{0,8},{8,0},{16,24},{24,16},{32,40},{40,32},{48,56},{56,48},{64,72... | collective-permute-start | bytes 737288 | tf_op jit(solution)/shard_map/ppermute | solution.py:522
  61.0 1.9 %collective-permute-start.20 = (bf16[960,128]{1,0:T(8,128)(2,1)S(1)}, bf16[960,128]{1,0:T(8,128)(2,1)S(1)}, u32[]{:S(2)}, u32[]{:S(2)}) collective-permute-start(bf16[960,128]{1,0:T(8,128)(2,1)S(1)} %shard_map.133.refs_4_), channel_id=1, source_target_pairs={{0,8},{8,0},{16,24},{24,16},{32,40},{40,32},{48,56},{56,48},{64,72... | collective-permute-start | bytes 737288 | tf_op jit(solution)/shard_map/ppermute | solution.py:522
  61.5 1.8 %collective-permute-start.21 = (bf16[960,128]{1,0:T(8,128)(2,1)S(1)}, bf16[960,128]{1,0:T(8,128)(2,1)S(1)}, u32[]{:S(2)}, u32[]{:S(2)}) collective-permute-start(bf16[960,128]{1,0:T(8,128)(2,1)S(1)} %collective-permute-done.10.refs_5_), channel_id=1, source_target_pairs={{0,8},{8,0},{16,24},{24,16},{32,40},{40,32},{48,56},{56,48},{64,72... | collective-permute-start | bytes 737288 | tf_op jit(solution)/shard_map/ppermute | solution.py:522
  61.9 1.8 %collective-permute-start.22 = (bf16[960,128]{1,0:T(8,128)(2,1)S(1)}, bf16[960,128]{1,0:T(8,128)(2,1)S(1)}, u32[]{:S(2)}, u32[]{:S(2)}) collective-permute-start(bf16[960,128]{1,0:T(8,128)(2,1)S(1)} %collective-permute-done.11.refs_6_), channel_id=1, source_target_pairs={{0,8},{8,0},{16,24},{24,16},{32,40},{40,32},{48,56},{56,48},{64,72... | collective-permute-start | bytes 737288 | tf_op jit(solution)/shard_map/ppermute | solution.py:522
  62.2 1.8 %collective-permute-start.23 = (bf16[960,128]{1,0:T(8,128)(2,1)S(1)}, bf16[960,128]{1,0:T(8,128)(2,1)S(1)}, u32[]{:S(2)}, u32[]{:S(2)}) collective-permute-start(bf16[960,128]{1,0:T(8,128)(2,1)S(1)} %collective-permute-done.12.refs_7_), channel_id=1, source_target_pairs={{0,8},{8,0},{16,24},{24,16},{32,40},{40,32},{48,56},{56,48},{64,72... | collective-permute-start | bytes 737288 | tf_op jit(solution)/shard_map/ppermute | solution.py:522
  65.2 11.0 %collective-permute-start.24 = (bf16[640,128]{1,0:T(8,128)(2,1)S(1)}, bf16[640,128]{1,0:T(8,128)(2,1)S(1)}, u32[]{:S(2)}, u32[]{:S(2)}) collective-permute-start(bf16[640,128]{1,0:T(8,128)(2,1)S(1)} %get-tuple-element.74), channel_id=1, source_target_pairs={{0,3},{1,2},{2,1},{3,0},{4,7},{5,6},{6,5},{7,4},{8,11},{9,10},{10,... | collective-permute-start | bytes 491528 | tf_op jit(solution)/shard_map/ppermute | solution.py:467
  68.7 8.6 %collective-permute-start.25 = (bf16[640,128]{1,0:T(8,128)(2,1)S(1)}, bf16[640,128]{1,0:T(8,128)(2,1)S(1)}, u32[]{:S(2)}, u32[]{:S(2)}) collective-permute-start(bf16[640,128]{1,0:T(8,128)(2,1)S(1)} %get-tuple-element.75), channel_id=1, source_target_pairs={{0,2},{1,3},{2,0},{3,1},{4,6},{5,7},{6,4},{7,5},{8,10},{9,11},{10,... | collective-permute-start | bytes 491528 | tf_op jit(solution)/shard_map/ppermute | solution.py:467
  70.0 7.7 %collective-permute-start.26 = (bf16[640,128]{1,0:T(8,128)(2,1)S(1)}, bf16[640,128]{1,0:T(8,128)(2,1)S(1)}, u32[]{:S(2)}, u32[]{:S(2)}) collective-permute-start(bf16[640,128]{1,0:T(8,128)(2,1)S(1)} %get-tuple-element.76), channel_id=1, source_target_pairs={{0,1},{1,0},{2,3},{3,2},{4,5},{5,4},{6,7},{7,6},{8,9},{9,8},{10,11... | collective-permute-start | bytes 491528 | tf_op jit(solution)/shard_map/ppermute | solution.py:467
  80.3 14.0 %collective-permute-start.27 = (s16[2112,128]{1,0:T(8,128)(2,1)S(1)}, s16[2112,128]{1,0:T(8,128)(2,1)S(1)}, u32[]{:S(2)}, u32[]{:S(2)}) collective-permute-start(s16[2112,128]{1,0:T(8,128)(2,1)S(1)} %get-tuple-element.84), channel_id=1, source_target_pairs={{0,1},{1,0},{2,3},{3,2},{4,5},{5,4},{6,7},{7,6},{8,9},{9,8},{10,11... | collective-permute-start | bytes 1622024 | tf_op jit(solution)/shard_map/ppermute | solution.py:547
  82.5 11.8 %collective-permute-start.28 = (s16[2112,128]{1,0:T(8,128)(2,1)S(1)}, s16[2112,128]{1,0:T(8,128)(2,1)S(1)}, u32[]{:S(2)}, u32[]{:S(2)}) collective-permute-start(s16[2112,128]{1,0:T(8,128)(2,1)S(1)} %get-tuple-element.85), channel_id=1, source_target_pairs={{1,2},{3,4},{5,6},{2,1},{4,3},{6,5},{9,10},{11,12},{13,14},{10,9},... | collective-permute-start | bytes 1622024 | tf_op jit(solution)/shard_map/ppermute | solution.py:548
  97.4 25.7 %collective-permute-start.29 = (s16[336,128]{1,0:T(8,128)(2,1)S(1)}, s16[336,128]{1,0:T(8,128)(2,1)S(1)}, u32[]{:S(2)}, u32[]{:S(2)}) collective-permute-start(s16[336,128]{1,0:T(8,128)(2,1)S(1)} %get-tuple-element.90), channel_id=1, source_target_pairs={{0,7},{1,6},{2,5},{3,4},{4,3},{5,2},{6,1},{7,0},{8,15},{9,14},{10,... | collective-permute-start | bytes 258056 | tf_op jit(solution)/shard_map/ppermute | solution.py:467
  102.2 20.9 %collective-permute-start.30 = (s16[336,128]{1,0:T(8,128)(2,1)S(1)}, s16[336,128]{1,0:T(8,128)(2,1)S(1)}, u32[]{:S(2)}, u32[]{:S(2)}) collective-permute-start(s16[336,128]{1,0:T(8,128)(2,1)S(1)} %get-tuple-element.91), channel_id=1, source_target_pairs={{0,6},{1,7},{2,4},{3,5},{4,2},{5,3},{6,0},{7,1},{8,14},{9,15},{10,... | collective-permute-start | bytes 258056 | tf_op jit(solution)/shard_map/ppermute | solution.py:467
  107.9 16.1 %collective-permute-start.31 = (s16[336,128]{1,0:T(8,128)(2,1)S(1)}, s16[336,128]{1,0:T(8,128)(2,1)S(1)}, u32[]{:S(2)}, u32[]{:S(2)}) collective-permute-start(s16[336,128]{1,0:T(8,128)(2,1)S(1)} %get-tuple-element.92), channel_id=1, source_target_pairs={{0,5},{1,4},{2,7},{3,6},{4,1},{5,0},{6,3},{7,2},{8,13},{9,12},{10,... | collective-permute-start | bytes 258056 | tf_op jit(solution)/shard_map/ppermute | solution.py:467
  119.3 8.4 %collective-permute-start.32 = (s16[336,128]{1,0:T(8,128)(2,1)S(1)}, s16[336,128]{1,0:T(8,128)(2,1)S(1)}, u32[]{:S(2)}, u32[]{:S(2)}) collective-permute-start(s16[336,128]{1,0:T(8,128)(2,1)S(1)} %get-tuple-element.93), channel_id=1, source_target_pairs={{0,4},{1,5},{2,6},{3,7},{4,0},{5,1},{6,2},{7,3},{8,12},{9,13},{10,... | collective-permute-start | bytes 258056 | tf_op jit(solution)/shard_map/ppermute | solution.py:467
  119.3 8.4 %collective-permute-start.33 = (s16[336,128]{1,0:T(8,128)(2,1)S(1)}, s16[336,128]{1,0:T(8,128)(2,1)S(1)}, u32[]{:S(2)}, u32[]{:S(2)}) collective-permute-start(s16[336,128]{1,0:T(8,128)(2,1)S(1)} %get-tuple-element.94), channel_id=1, source_target_pairs={{0,3},{1,2},{2,1},{3,0},{4,7},{5,6},{6,5},{7,4},{8,11},{9,10},{10,... | collective-permute-start | bytes 258056 | tf_op jit(solution)/shard_map/ppermute | solution.py:467
  123.1 6.0 %collective-permute-start.34 = (s16[336,128]{1,0:T(8,128)(2,1)S(1)}, s16[336,128]{1,0:T(8,128)(2,1)S(1)}, u32[]{:S(2)}, u32[]{:S(2)}) collective-permute-start(s16[336,128]{1,0:T(8,128)(2,1)S(1)} %get-tuple-element.95), channel_id=1, source_target_pairs={{0,2},{1,3},{2,0},{3,1},{4,6},{5,7},{6,4},{7,5},{8,10},{9,11},{10,... | collective-permute-start | bytes 258056 | tf_op jit(solution)/shard_map/ppermute | solution.py:467
  123.1 6.0 %collective-permute-start.35 = (s16[336,128]{1,0:T(8,128)(2,1)S(1)}, s16[336,128]{1,0:T(8,128)(2,1)S(1)}, u32[]{:S(2)}, u32[]{:S(2)}) collective-permute-start(s16[336,128]{1,0:T(8,128)(2,1)S(1)} %get-tuple-element.96), channel_id=1, source_target_pairs={{0,1},{1,0},{2,3},{3,2},{4,5},{5,4},{6,7},{7,6},{8,9},{9,8},{10,11... | collective-permute-start | bytes 258056 | tf_op jit(solution)/shard_map/ppermute | solution.py:467
  130.0 2.3 %collective-permute-start.36 = (f32[1440,128]{1,0:T(8,128)S(1)}, f32[1440,128]{1,0:T(8,128)S(1)}, u32[]{:S(2)}, u32[]{:S(2)}) collective-permute-start(f32[1440,128]{1,0:T(8,128)S(1)} %get-tuple-element.98), channel_id=1, source_target_pairs={{0,8},{8,0},{16,24},{24,16},{32,40},{40,32},{48,56},{56,48},{64,72... | collective-permute-start | bytes 2211848 | tf_op jit(solution)/shard_map/ppermute | solution.py:581
  133.5 14.9 %collective-permute-start.37 = (s16[992,128]{1,0:T(8,128)(2,1)S(1)}, s16[992,128]{1,0:T(8,128)(2,1)S(1)}, u32[]{:S(2)}, u32[]{:S(2)}) collective-permute-start(s16[992,128]{1,0:T(8,128)(2,1)S(1)} %get-tuple-element.100), channel_id=1, source_target_pairs={{0,192},{8,200},{16,208},{24,216},{32,224},{40,232},{48,240},{56,2... | collective-permute-start | bytes 761864 | tf_op jit(solution)/shard_map/ppermute | solution.py:467
  133.9 14.5 %collective-permute-start.38 = (s16[992,128]{1,0:T(8,128)(2,1)S(1)}, s16[992,128]{1,0:T(8,128)(2,1)S(1)}, u32[]{:S(2)}, u32[]{:S(2)}) collective-permute-start(s16[992,128]{1,0:T(8,128)(2,1)S(1)} %get-tuple-element.101), channel_id=1, source_target_pairs={{0,128},{8,136},{16,144},{24,152},{32,160},{40,168},{48,176},{56,1... | collective-permute-start | bytes 761864 | tf_op jit(solution)/shard_map/ppermute | solution.py:467
  135.6 13.4 %collective-permute-start.39 = (s16[992,128]{1,0:T(8,128)(2,1)S(1)}, s16[992,128]{1,0:T(8,128)(2,1)S(1)}, u32[]{:S(2)}, u32[]{:S(2)}) collective-permute-start(s16[992,128]{1,0:T(8,128)(2,1)S(1)} %get-tuple-element.102), channel_id=1, source_target_pairs={{0,64},{8,72},{16,80},{24,88},{32,96},{40,104},{48,112},{56,120},{... | collective-permute-start | bytes 761864 | tf_op jit(solution)/shard_map/ppermute | solution.py:467
  149.4 19.8 %collective-permute-start.40 = (s16[256,128]{1,0:T(8,128)(2,1)S(1)}, s16[256,128]{1,0:T(8,128)(2,1)S(1)}, u32[]{:S(2)}, u32[]{:S(2)}) collective-permute-start(s16[256,128]{1,0:T(8,128)(2,1)S(1)} %get-tuple-element.104), channel_id=1, source_target_pairs={{0,48},{8,56},{16,32},{24,40},{32,16},{40,24},{48,0},{56,8},{64,11... | collective-permute-start | bytes 196616 | tf_op jit(solution)/shard_map/ppermute | solution.py:467
  151.7 21.3 %collective-permute-start.41 = (s16[256,128]{1,0:T(8,128)(2,1)S(1)}, s16[256,128]{1,0:T(8,128)(2,1)S(1)}, u32[]{:S(2)}, u32[]{:S(2)}) collective-permute-start(s16[256,128]{1,0:T(8,128)(2,1)S(1)} %get-tuple-element.105), channel_id=1, source_target_pairs={{0,32},{8,40},{16,48},{24,56},{32,0},{40,8},{48,16},{56,24},{64,96... | collective-permute-start | bytes 196616 | tf_op jit(solution)/shard_map/ppermute | solution.py:467
  169.1 4.5 %collective-permute-start.42 = (s16[256,128]{1,0:T(8,128)(2,1)S(1)}, s16[256,128]{1,0:T(8,128)(2,1)S(1)}, u32[]{:S(2)}, u32[]{:S(2)}) collective-permute-start(s16[256,128]{1,0:T(8,128)(2,1)S(1)} %get-tuple-element.106), channel_id=1, source_target_pairs={{0,16},{8,24},{16,0},{24,8},{32,48},{40,56},{48,32},{56,40},{64,80... | collective-permute-start | bytes 196616 | tf_op jit(solution)/shard_map/ppermute | solution.py:467
  (6 other events, 5.5 us)

commit v7 on v5

--- a/solution.py
+++ b/solution.py
@@ -19,28 +19,26 @@
 VMEM_LIMIT = 32 * 1024 * 1024
 FLOOR = 1e-33
 TOP = 32700.0
-MICROSECOND = 3_690_000
 HALO = 4
 GROUP = 32
 
 
-def vmem():
-    return pl.BlockSpec(memory_space=pltpu.VMEM)
-
-
-def smem():
-    return pl.BlockSpec(memory_space=pltpu.SMEM)
-
-
-def call(kernel, outs, args, spaces, scratch=(), work=0):
+SPACES = {
+    "v": pl.BlockSpec(memory_space=pltpu.VMEM),
+    "s": pl.BlockSpec(memory_space=pltpu.SMEM),
+    "a": pl.BlockSpec(memory_space=pl.ANY),
+}
+
+
+def call(kernel, outs, args, spaces, scratch=()):
     return pl.pallas_call(
         kernel,
         out_shape=list(outs),
-        in_specs=[smem() if s == "s" else vmem() for s in spaces],
-        out_specs=[vmem()] * len(outs),
+        in_specs=[SPACES[s] for s in spaces],
+        out_specs=[SPACES["v"]] * len(outs),
         scratch_shapes=list(scratch),
         compiler_params=pltpu.CompilerParams(vmem_limit_bytes=VMEM_LIMIT),
-        cost_estimate=pl.CostEstimate(flops=0, bytes_accessed=work * MICROSECOND, transcendentals=0),
+        cost_estimate=pl.CostEstimate(flops=0, bytes_accessed=0, transcendentals=0),
     )(*args)
 
 
@@ -86,15 +84,16 @@
     return jnp.exp2(levels.astype(I32).astype(F32) * (1.0 / 256.0)) * (1.0 / TOP)
 
 
-def code_halos(field, rows, out_ref, level_ref, base):
-    for n, layer in enumerate(rows):
-        value = field(layer)
+def code_layers(layers, out_ref, level_ref):
+    for n, (ref, layer) in enumerate(layers):
+        value = ref[layer]
         count = value.shape[0] // GROUP
         for g in range(count):
             code, level = code_group(value[g * GROUP : (g + 1) * GROUP])
-            spot = base + n * count + g
-            out_ref[pl.ds(spot * GROUP, GROUP), :] = code.astype(I16)
-            level_ref[pl.ds(spot, 1), :] = level
+            out_ref[pl.ds((n * count + g) * GROUP, GROUP), :] = code.astype(I16)
+            level_ref[pl.ds(n * count + g, 1), :] = level
+    groups = len(layers) * count
+    out_ref[groups * GROUP :, :] = level_ref[0:groups, :].astype(I16)
 
 
 def halo_rows(layers, count_y):
@@ -106,19 +105,37 @@
     return lax.rem(lax.axis_index("dom"), 2)
 
 
-def code_edges(fields, out_refs, level_ref):
-    row_count, count_y, _ = fields[0].shape
-    per = HALO * count_y // GROUP
+def at_border():
+    me, middle = lax.axis_index("dom"), lax.axis_size("dom") // 2
+    return (me == middle) | (me == middle - 1)
+
+
+def encode_kernel(now_f, now_a, prev_f, prev_a, one, two, wide, hold_f, hold_a, past_f, past_a, level_ref, arrived):
     odd = odd_place()
-    for out_ref, high in zip(out_refs, (1 - odd, odd)):
-        first = high * (row_count - HALO)
-        for f, ref in enumerate(fields):
-            code_halos(lambda x: ref[x], [first + n for n in range(HALO)], out_ref, level_ref, f * per)
-        out_ref[2 * per * GROUP :, :] = level_ref[...].astype(I16)
-
-
-def encode_kernel(now_f, now_a, one, two, level_ref):
-    code_edges((now_f, now_a), (one, two), level_ref)
+    edge = pl.ds(odd * HALO, HALO)
+    loads = [
+        pltpu.make_async_copy(source, target, arrived.at[n])
+        for n, (source, target) in enumerate(
+            ((now_f, hold_f), (now_a, hold_a), (prev_f.at[edge], past_f), (prev_a.at[edge], past_a))
+        )
+    ]
+    for load in loads:
+        load.start()
+    for load in loads:
+        load.wait()
+    near_one = [(ref, (1 - odd) * HALO + n) for ref in (hold_f, hold_a) for n in range(HALO)]
+    near_two = [(ref, odd * HALO + n) for ref in (hold_f, hold_a) for n in range(HALO)]
+    past_two = [(ref, n) for ref in (past_f, past_a) for n in range(HALO)]
+
+    @pl.when(at_border())
+    def _():
+        code_layers(near_two + near_one + past_two, wide, level_ref)
+
+    @pl.when(jnp.logical_not(at_border()))
+    def _():
+        code_layers(near_two, two, level_ref)
+
+    code_layers(near_one, one, level_ref)
 
 
 PAD = 8
@@ -163,11 +180,27 @@
 
 def load_scales(in_ref, scale_ref):
     groups = scale_ref.shape[0]
-    scale_ref[...] = decode_scale(in_ref[groups * GROUP :, :])
-
-
-def add_source(source, start, wave, ref, k, edge=0):
-    x = source[0, 0] - lax.axis_index("dom") * ref.shape[0]
+    base = in_ref.shape[0] // (GROUP + 1) * GROUP
+    scale_ref[...] = decode_scale(in_ref[base : base + groups, :])
+
+
+def load_codes(in_ref, code_ref, scale_ref):
+    code_ref[...] = in_ref[0 : code_ref.shape[0], :]
+    load_scales(in_ref, scale_ref)
+
+
+def load_second(two, wide, code_ref, scale_ref):
+    @pl.when(jnp.logical_not(at_border()))
+    def _():
+        load_codes(two, code_ref, scale_ref)
+
+    @pl.when(at_border())
+    def _():
+        load_codes(wide, code_ref, scale_ref)
+
+
+def add_source(source, start, wave, ref, k, first, edge=0):
+    x = source[0, 0] - first
     lane = lax.broadcasted_iota(I32, (1, ref.shape[2]), 1)
 
     @pl.when((x >= 0) & (x < ref.shape[0]))
@@ -206,21 +239,15 @@
     return [sum(COEFFS[r + j] * rows[j] for j in range(HALO - r)) for r in range(HALO)]
 
 
-def halo_tiles(refs, scales, row_count, count_y):
-    for ref, scale in zip(refs, scales):
-        load_scales(ref, scale)
-    odd = odd_place()
+def halo_tiles(ref, scale, low, row_count, count_y):
     for y in range(0, count_y, GROUP):
-        for ref, scale, low in zip(refs, scales, (odd, 1 - odd)):
-            terms = [halo_terms(ref, scale, f, y, count_y, low) for f in range(2)]
-            for r in range(HALO):
-                yield row_count - 1 - r + low * (2 * r + 1 - row_count), y, terms[0][r], terms[1][r]
-
-
-def first_kernel(halves, anchors, source, begin, wave, sum_f, sum_a, base_f, base_a, *rest):
-    next_f, next_a, courant, one, two, slab, level, scale_one, scale_two = rest[-9:]
-    halos, pieces = rest[:2], rest[2:-9]
-    row_count, count_y, _ = sum_f.shape
+        terms = [halo_terms(ref, scale, f, y, count_y, low) for f in range(2)]
+        for r in range(HALO):
+            yield row_count - 1 - r + low * (2 * r + 1 - row_count), y, terms[0][r], terms[1][r]
+
+
+def square_speed(pieces, halves, slab):
+    row_count = slab.shape[0]
     band = pieces[0].shape[0] // (row_count * halves)
     side = len(pieces)
     me = lax.rem(lax.axis_index("dom"), side)
@@ -232,15 +259,84 @@
                 slab[x, pl.ds(start, band), :] = jnp.square(speed[:band])
                 slab[x + 1, pl.ds(start, band), :] = jnp.square(speed[band:])
 
-    for x, y, term_f, term_a in halo_tiles(halos, (scale_one, scale_two), row_count, count_y):
+
+def step_rows(ref, scale, low, anchors, slab, terms, nexts, courant, shift):
+    sum_f, sum_a, base_f, base_a = terms
+    row_count, count_y, _ = sum_f.shape
+    for x, y, term_f, term_a in halo_tiles(ref, scale, low, row_count, count_y):
         spot = pl.ds(y, GROUP)
         factor = slab[x, pl.ds(anchors[0, 1] + y, GROUP), :]
-        courant[x, spot, :] = factor
-        next_f[x, spot, :] = base_f[x, spot, :] + factor * (sum_f[x, spot, :] + term_f)
-        next_a[x, spot, :] = base_a[x, spot, :] + factor * (sum_a[x, spot, :] + term_a)
-
-    add_source(source, begin, wave, next_f, 0)
-    code_edges((next_f, next_a), (one, two), level)
+        courant[x - shift, spot, :] = factor
+        nexts[0][x - shift, spot, :] = base_f[x, spot, :] + factor * (sum_f[x, spot, :] + term_f)
+        nexts[1][x - shift, spot, :] = base_a[x, spot, :] + factor * (sum_a[x, spot, :] + term_a)
+
+
+def first_kernel(halves, anchors, source, begin, wave, *rest):
+    next_f, next_a, courant, one, slab, level, scale = rest[-7:]
+    terms, halo, pieces = rest[:4], rest[4], rest[5:-7]
+    row_count = terms[0].shape[0]
+    square_speed(pieces, halves, slab)
+    load_scales(halo, scale)
+    odd = odd_place()
+    shift = (1 - odd) * HALO
+    step_rows(halo, scale, odd, anchors, slab, terms, (next_f, next_a), courant, shift)
+    add_source(source, begin, wave, next_f, 0, lax.axis_index("dom") * row_count + shift)
+    code_layers([(ref, n) for ref in (next_f, next_a) for n in range(HALO)], one, level)
+
+
+def other_kernel(halves, side, anchors, source, begin, wave, *rest):
+    (sum_f, sum_a, base_f, base_a, two, wide, now_f, now_a, edge_f, edge_a, edge_c, hit), rest = rest[:12], rest[12:]
+    pieces, extra, rest = rest[:side], rest[side : 2 * side], rest[2 * side :]
+    next_f, next_a, courant, send, beyond, slab, extra_slab, pad, out_f, out_a, codes, scale, far_scale, level = rest
+    row_count, count_y, count_z = sum_f.shape
+    odd = odd_place()
+    me = lax.axis_index("dom")
+    square_speed(pieces, halves, slab)
+    load_second(two, wide, codes, scale)
+    step_rows(codes, scale, 1 - odd, anchors, slab, (sum_f, sum_a, base_f, base_a), (next_f, next_a), courant, 0)
+    add_source(source, begin, wave, next_f, 0, me * row_count)
+    for n in range(HALO):
+        x = (1 - odd) * HALO + n
+        next_f[x] = edge_f[n]
+        next_a[x] = edge_a[n]
+        courant[x] = edge_c[n]
+    near = [(ref, odd * HALO + n) for ref in (next_f, next_a) for n in range(HALO)]
+
+    @pl.when(jnp.logical_not(at_border()))
+    def _():
+        code_layers(near, send, level)
+
+    @pl.when(at_border())
+    def _():
+        square_speed(extra, halves, extra_slab)
+        load_scales(wide, far_scale)
+        masks = lane_masks(TILE, count_z)
+        per = count_y // GROUP
+        ends = jnp.zeros((pad.shape[0], PAD, count_z), F32)
+        pad[:, 0:PAD, :] = ends
+        pad[:, PAD + count_y :, :] = ends
+        first = me * row_count + odd * (row_count + HALO) - HALO
+
+        def decoded(n, y):
+            spot = n * per + y // GROUP
+            code = wide[pl.ds(spot * GROUP, GROUP), :].astype(I32).astype(F32)
+            return code * far_scale[pl.ds(spot, 1), :]
+
+        for f, (now, out) in enumerate(((now_f, out_f), (now_a, out_a))):
+            for n in range(HALO):
+                pad[(1 - odd) * 2 * HALO + n, PAD : PAD + count_y, :] = now[odd * HALO + n]
+                for y in range(0, count_y, GROUP):
+                    pad[HALO + n, pl.ds(PAD + y, GROUP), :] = decoded(f * HALO + n, y)
+                    pad[odd * 2 * HALO + n, pl.ds(PAD + y, GROUP), :] = decoded((2 + f) * HALO + n, y)
+            for n in range(HALO):
+                for y in range(0, count_y, TILE):
+                    spot = pl.ds(y, TILE)
+                    middle, summed = laplace_tile(pad, HALO + n, y, TILE, masks)
+                    value = 2.0 * middle - decoded((4 + f) * HALO + n, y)
+                    value += extra_slab[n, pl.ds(anchors[0, 1] + y, TILE), :] * summed
+                    out[n, spot, :] = value + hit[n, spot, :] if f else value
+        add_source(source, begin, wave, out_f, 0, first)
+        code_layers([(ref, n) for ref in (out_f, out_a) for n in range(HALO)], beyond, level)
 
 
 def between_kernel(p1, q1, p0, q0, prev_f, courant, hit, part_f, part_a, bend, pad):
@@ -263,22 +359,26 @@
                 out[x, spot, :] = value
 
 
-def second_kernel(groups, anchors, source, begin, wave, p1, q1, p0, courant, part_f, part_a, bend, one, two, *rest):
+def second_kernel(groups, anchors, source, begin, wave, p1, q1, p0, courant, part_f, part_a, bend, one, two, beyond, *rest):
     next_f, next_a, own = rest[:3]
     sends = rest[3 : 2 + groups]
-    frame, scale_one, scale_two = rest[2 + groups :]
+    frame, codes, scale_one, scale_two = rest[2 + groups :]
     row_count, count_y, count_z = p1.shape
     band = own.shape[0] // row_count
     edge = (frame.shape[1] - count_y) // 2
     frame[:, 0:edge, :] = jnp.zeros((row_count, edge, count_z), F32)
     frame[:, edge + count_y :, :] = jnp.zeros((row_count, edge, count_z), F32)
-    for x, y, term_f, term_a in halo_tiles((one, two), (scale_one, scale_two), row_count, count_y):
-        spot = pl.ds(y, GROUP)
-        factor = courant[x, spot, :]
-        frame[x, pl.ds(edge + y, GROUP), :] = part_f[x, spot, :] + factor * term_f
-        next_a[x, spot, :] = part_a[x, spot, :] + factor * term_a
-
-    add_source(source, begin, wave, frame, 1, edge)
+    odd = odd_place()
+    load_scales(one, scale_one)
+    load_second(two, beyond, codes, scale_two)
+    for ref, scale, low in ((one, scale_one, odd), (codes, scale_two, 1 - odd)):
+        for x, y, term_f, term_a in halo_tiles(ref, scale, low, row_count, count_y):
+            spot = pl.ds(y, GROUP)
+            factor = courant[x, spot, :]
+            frame[x, pl.ds(edge + y, GROUP), :] = part_f[x, spot, :] + factor * term_f
+            next_a[x, spot, :] = part_a[x, spot, :] + factor * term_a
+
+    add_source(source, begin, wave, frame, 1, lax.axis_index("dom") * row_count, edge)
 
     @pl.loop(0, row_count)
     def _(x):
@@ -300,12 +400,9 @@
             code_rows(values, sends[k - 1], 0)
 
 
-def hit_kernel(begin, cells, traces, first, second):
+def hit_kernel(begin, cells, traces, first, second, beyond):
     row_count, count_y, count_z = first.shape
-    x = cells[0:1, :] - lax.axis_index("dom") * row_count
-    inside = (x >= 0) & (x < row_count)
-    row = jnp.where(inside, x * count_y + cells[1:2, :], -1)
-    depth = lax.broadcasted_iota(I32, (count_z, row.shape[1]), 0)
+    depth = lax.broadcasted_iota(I32, (count_z, cells.shape[1]), 0)
     at_depth = depth == cells[2:3, :]
     parts = []
     for k in range(STEPS):
@@ -314,19 +411,29 @@
             part = left.astype(BF16).astype(F32)
             parts.append(jnp.where(at_depth, part, 0.0).astype(BF16))
             left = left - part
-    right = jnp.concatenate(parts, axis=0)
-
-    @pl.loop(0, row_count)
-    def _(i):
-        cell = i * count_y + lax.broadcasted_iota(I32, (count_y, row.shape[1]), 0)
-        left = jnp.where(cell == row, 1.0, 0.0).astype(BF16)
-        got = lax.dot_general(left, right, (((1,), (1,)), ((), ())), preferred_element_type=F32)
-        for k, out in enumerate((first, second)):
-            base = 3 * k * count_z
-            high = got[:, base : base + count_z]
-            middle = got[:, base + count_z : base + 2 * count_z]
-            low = got[:, base + 2 * count_z : base + 3 * count_z]
-            out[i] = high + (middle + low)
+
+    def add_up(start, outs):
+        right = jnp.concatenate(parts[: 3 * len(outs)], axis=0)
+
+        @pl.loop(0, outs[0].shape[0])
+        def _(i):
+            row = jnp.where(cells[0:1, :] == start + i, cells[1:2, :], -1)
+            cell = lax.broadcasted_iota(I32, (count_y, cells.shape[1]), 0)
+            left = jnp.where(cell == row, 1.0, 0.0).astype(BF16)
+            got = lax.dot_general(left, right, (((1,), (1,)), ((), ())), preferred_element_type=F32)
+            for k, out in enumerate(outs):
+                base = 3 * k * count_z
+                high = got[:, base : base + count_z]
+                middle = got[:, base + count_z : base + 2 * count_z]
+                low = got[:, base + 2 * count_z : base + 3 * count_z]
+                out[i] = high + (middle + low)
+
+    start = lax.axis_index("dom") * row_count
+    add_up(start, (first, second))
+
+    @pl.when(at_border())
+    def _():
+        add_up(start + odd_place() * (row_count + HALO) - HALO, (beyond,))
 
 
 SIZE_X, SIZE_Z, SIZE_C = 4, 4, 2
@@ -350,7 +457,7 @@
 
 def pick_kernel(layout, row_count, halves, anchors, *refs):
     count = len(layout)
-    ins, outs, table = refs[:count], refs[count:-1], refs[-1]
+    ins, outs, extra, table = refs[:count], refs[count:-2], refs[-2], refs[-1]
     side = len(outs)
     piece = outs[0].shape[0] // halves
     per = piece // row_count
@@ -358,7 +465,7 @@
     own = block // per
     x, z, c = place_of(lax.axis_index("shot"))
     half, me = lax.axis_index("dom") // side, lax.rem(lax.axis_index("dom"), side)
-    anchor = anchors[0, 0] + half * (side * row_count)
+    anchor = anchors[0, 0] + half * (side * row_count - HALO)
     first = anchor // own
     span = table.shape[1] // block
     for ref, owners in zip(ins, layout):
@@ -371,10 +478,12 @@
                 table[half ^ dh, pl.ds(start, block), :] = ref[pl.ds(n * block, block), :].astype(F32)
 
     offset = (anchor - first * own) * per
-    for k in range(side):
-        start = pl.multiple_of(offset + (me ^ k) * piece, 8)
+    starts = [offset + half * (HALO * per) + (me ^ k) * piece for k in range(side)]
+    starts.append(offset + (1 - half) * (side * piece))
+    for start, out in zip(starts, (*outs, extra)):
+        size = out.shape[0] // halves
         for h in range(halves):
-            outs[k][pl.ds(h * piece, piece), :] = table[h, pl.ds(start, piece), :].astype(BF16)
+            out[pl.ds(h * size, size), :] = table[h, pl.ds(pl.multiple_of(start, 8), size), :].astype(BF16)
 
 
 def band_kernel(groups, row_count, block, anchors, own, *refs):
@@ -490,6 +599,9 @@
     scalars = (anchors, source, start_step, wavelet)
     one_pairs = [(i, i ^ 1) for i in range(groups)]
     two_pairs = [(i, i + 1) for i in range(1, groups - 1, 2)]
+    side = groups // HALVES
+    border = [(side - 1, side), (side, side - 1)]
+    two_pairs = [(a, b) for a, b in two_pairs if a != side - 1]
     two_pairs += [(b, a) for a, b in two_pairs]
 
     along = {axis: functools.partial(swap, axis) for axis in "xzc"}
@@ -498,50 +610,79 @@
     local = velocity.reshape(block, count_z)
     near = [local] + exchange([local] * (HALVES * SIZE_Z - 1), ("shot", "dom"), functools.partial(swap_z, groups))
 
-    half = halo_rows(2 * HALO, count_y)
-    code = struct((half, count_z), I16)
-    levels = pltpu.VMEM((2 * HALO * count_y // GROUP, count_z), I32)
-    (line,) = call(join_kernel, (struct((len(near) * block, count_z), BF16),), near, "v" * len(near))
-
-    p0, line = lax.optimization_barrier((p0, line))
-    one, two = call(encode_kernel, (code, code), (p0, q0), "vv", (levels,))
+    code = struct((halo_rows(2 * HALO, count_y), count_z), I16)
+    wide = struct((halo_rows(6 * HALO, count_y), count_z), I16)
+    groups_of = lambda layers: layers * count_y // GROUP
+    levels = pltpu.VMEM((groups_of(2 * HALO), count_z), I32)
+    scale = pltpu.VMEM((groups_of(2 * HALO), count_z), F32)
+    wide_levels = pltpu.VMEM((groups_of(6 * HALO), count_z), I32)
+    wide_scale = pltpu.VMEM((groups_of(6 * HALO), count_z), F32)
+    codes = pltpu.VMEM((groups_of(2 * HALO) * GROUP, count_z), I16)
+    fields = (p0, q0, p_prev, q_prev)
+    strip = struct((HALO, count_y, count_z), F32)
+    strips = pltpu.VMEM(strip.shape, F32)
+    hold = pltpu.VMEM(p0.shape, F32)
+    scratch = (hold, hold, strips, strips, wide_levels, pltpu.SemaphoreType.DMA((4,)))
+    one, two, wide = call(encode_kernel, (code, code, wide), fields, "aaaa", scratch)
+    from_wide = lax.ppermute(wide, "dom", border)
     from_one = lax.ppermute(one, "dom", one_pairs)
     from_two = lax.ppermute(two, "dom", two_pairs)
+
+    (line,) = call(join_kernel, (struct((len(near) * block, count_z), BF16),), near, "v" * len(near))
+
     anchors, line = lax.optimization_barrier((anchors, line))
     other = lax.ppermute(anchors, "shot", swap("c", 1))
     field = struct((row_count, count_y, count_z), F32)
-    hits = call(hit_kernel, (field, field), (start_step, receivers[0], traces[0]), "svv", work=4)
+    hits = call(hit_kernel, (field, field, strip), (start_step, receivers[0], traces[0]), "svv")
     padded = pltpu.VMEM((row_count + 2 * HALO, count_y + 2 * PAD, count_z), F32)
-    sums = call(before_kernel, (field,) * 4, (p0, q0, p_prev, q_prev, hits[0]), "v" * 5, (padded,), work=6)
+    sums = call(before_kernel, (field,) * 4, (p0, q0, p_prev, q_prev, hits[0]), "v" * 5, (padded,))
     plane = [line] + exchange([line] * (SIZE_X - 1), "shot", along["x"])
     plane, other = lax.optimization_barrier((plane, sums[0], other))[::2]
     plane += [lax.ppermute(part, "shot", swap("c", 1)) for part in plane]
-    *plane, from_two, from_one = lax.optimization_barrier((*plane, from_two, from_one))
     layout = [
         [(dx, k % SIZE_Z, dc, k // SIZE_Z) for k in range(HALVES * SIZE_Z)]
         for dc in range(SIZE_C)
         for dx in range(SIZE_X)
     ]
-    side = groups // HALVES
-    pieces = call(
+    *pieces, extra = call(
         functools.partial(pick_kernel, layout, row_count, HALVES),
-        [struct((HALVES * piece, count_z), BF16)] * side,
+        (*[struct((HALVES * piece, count_z), BF16)] * side, struct((HALVES * HALO * band, count_z), BF16)),
         (anchors, *plane),
         "s" + "v" * len(plane),
-        (pltpu.VMEM((HALVES, -(-(row_count * side + own_rows - 1) // own_rows) * block, count_z), F32),),
+        (pltpu.VMEM((HALVES, -(-(row_count * side + HALO + own_rows - 1) // own_rows) * block, count_z), F32),),
     )
     pieces = [pieces[0]] + exchange(pieces[1:], "dom", between)[::-1]
-
-    scale = pltpu.VMEM((2 * HALO * count_y // GROUP, count_z), F32)
+    *pieces, from_wide = lax.optimization_barrier((*pieces, from_wide))
+    to_border = lambda k: [(a ^ k, a) for a, _ in border]
+    extras = [extra] + exchange([extra] * (side - 1), "dom", to_border)[::-1]
+
     slab = pltpu.VMEM((row_count, groups * band, count_z), F32)
-    p1, q1, courant, one, two = call(
+    edge_f, edge_a, edge_c, one = call(
         functools.partial(first_kernel, HALVES),
+        (strip, strip, strip, code),
+        (*scalars, *sums, from_one, *pieces),
+        "ssss" + "v" * (5 + side),
+        (slab, levels, scale),
+    )
+    from_one = lax.ppermute(one, "dom", one_pairs)
+    extra_slab = pltpu.VMEM((HALO, groups * band, count_z), F32)
+    p1, q1, courant, two, beyond = call(
+        functools.partial(other_kernel, HALVES, side),
         (field, field, field, code, code),
-        (*scalars, *sums, from_one, from_two, *pieces),
-        "ssss" + "v" * (6 + side),
-        (slab, levels, scale, scale),
-    )
-    from_one = lax.ppermute(one, "dom", one_pairs)
+        (*scalars, *sums, from_two, from_wide, p0, q0, edge_f, edge_a, edge_c, hits[2], *pieces, *extras),
+        "ssss" + "v" * (12 + 2 * side),
+        (
+            slab,
+            extra_slab,
+            pltpu.VMEM((3 * HALO, count_y + 2 * PAD, count_z), F32),
+            strips,
+            strips,
+            codes,
+            scale,
+            wide_scale,
+            levels,
+        ),
+    )
     from_two = lax.ppermute(two, "dom", two_pairs)
     part_f, part_a, bend = call(
         between_kernel,
@@ -549,7 +690,6 @@
         (p1, q1, p0, q0, p_prev, courant, hits[1]),
         "v" * 7,
         (padded,),
-        work=6,
     )
 
     span = -(-(row_count * groups + own_rows - 1) // own_rows)
@@ -561,9 +701,9 @@
     p2, q2, own, *sends = call(
         functools.partial(second_kernel, groups),
         (field, field, struct((piece, count_z), F32), *[coded] * (groups - 1)),
-        (*scalars, p1, q1, p0, courant, part_f, part_a, bend, from_one, from_two),
-        "ssss" + "v" * 9,
-        (frame, scale, scale),
+        (*scalars, p1, q1, p0, courant, part_f, part_a, bend, from_one, from_two, beyond),
+        "ssss" + "v" * 10,
+        (frame, codes, scale, scale),
     )
     got = exchange(sends, "dom", between)[::-1]
 

time: 167 us -> 239 us (1.43)
  waiting for transfers between devices: 50.4 us -> 118 us
  starting transfers between devices: 82.6 us -> 86.9 us
    ppermute x26 -> x29, waiting for transfers between devices: 38.4 us -> 109 us  [exchange(): got[k] = lax.ppermute(parts[k - 1], axis, pairs(k))]
    ppermute x26 -> x29, starting transfers between devices: 74.5 us -> 82.4 us  [exchange(): got[k] = lax.ppermute(parts[k - 1], axis, pairs(k))]
    ppermute x2, starting transfers between devices: 5.48 us -> 0.95 us  [body(): from_one = lax.ppermute(one, 'dom', one_pairs)]
    pallas_call x12 -> x13, Pallas kernels: 25.3 us -> 26.7 us  [call(): pl.pallas_call(kernel, out_shape=list(outs), in_specs=[SPACES[s] for s in...]
  transfers between devices with their start and end apart: 36 -> 40, of which waited for: 20 -> 22; matrix products, arithmetic and copies ran while one was open for 0% -> 0% of each run, Pallas kernels for 9% -> 8%
where the time goes in v7:
time: 239 us
  waiting for transfers between devices  118 us (49%)
  starting transfers between devices  86.9 us (36%)
  Pallas kernels  26.7 us (11%)
  local copies, waits for them, and re-layouts  4.94 us (2%)
    ppermute x29, waiting for transfers between devices, exchange(): got[k] = lax.ppermute(parts[k - 1], axis, pairs(k))  109 us
    ppermute x29, starting transfers between devices, exchange(): got[k] = lax.ppermute(parts[k - 1], axis, pairs(k))  82.4 us
    pallas_call x13, Pallas kernels, call(): pl.pallas_call(kernel, out_shape=list(outs), in_specs=[SPACES[s] for s in...  26.7 us
    unnamed x27, local copies, waits for them, and re-layouts  4.94 us
  transfers between devices with their start and end apart: 40, of which 22 were waited for; matrix products, arithmetic and copies ran while one was open for 0% of the time, Pallas kernels for 8%

profile of v7, /device:TPU:6, one launch (start us, length us, event | category | flops | bytes accessed | tf_op | source)
XLA Modules:
  0.0 238.6 jit_solution(16207055999554942981)
XLA Ops:
  0.6 1.2 copy-done
  1.9 1.2 copy-done.2
  3.1 1.2 copy-done.4
  4.3 1.2 copy-done.6
  6.4 0.9 collective-permute-start.19
  7.3 11.5 %collective-permute-start.7 = (bf16[240,128]{1,0:T(8,128)(2,1)S(1)}, bf16[240,128]{1,0:T(8,128)(2,1)S(1)}, u32[]{:S(2)}, u32[]{:S(2)}) collective-permute-start(bf16[240,128]{1,0:T(8,128)(2,1)S(1)} %bitcast.27), channel_id=1, source_target_pairs={{0,52},{1,53},{2,54},{3,55},{4,48},{5,49},{6,50},{7,51},{8,60},{9,... | collective-permute-start | bytes 184328 | tf_op jit(solution)/shard_map/ppermute | solution.py:576
  18.9 1.9 collective-permute-start.5
  20.8 4.2 %collective-permute-start.4 = (bf16[240,128]{1,0:T(8,128)(2,1)S(1)}, bf16[240,128]{1,0:T(8,128)(2,1)S(1)}, u32[]{:S(2)}, u32[]{:S(2)}) collective-permute-start(bf16[240,128]{1,0:T(8,128)(2,1)S(1)} %bitcast.30), channel_id=1, source_target_pairs={{0,4},{1,5},{2,6},{3,7},{4,0},{5,1},{6,2},{7,3},{8,12},{9,13},{10,... | collective-permute-start | bytes 184328 | tf_op jit(solution)/shard_map/ppermute | solution.py:576
  24.9 70.4 %collective-permute-done.7.refs_7_ = bf16[240,128]{1,0:T(8,128)(2,1)S(1)} collective-permute-done((bf16[240,128]{1,0:T(8,128)(2,1)S(1)}, bf16[240,128]{1,0:T(8,128)(2,1)S(1)}, u32[]{:S(2)}, u32[]{:S(2)}) %collective-permute-start.7) | collective-permute-done | bytes 61472 | tf_op jit(solution)/shard_map/ppermute | solution.py:576
  95.3 1.5 collective-permute-start.3
  96.9 1.3 collective-permute-start.2
  98.2 1.5 collective-permute-start.1
  99.7 2.0 collective-permute-done.3.refs_3_
  101.8 1.5 collective-permute-done.2.refs_2_
  103.9 2.4 %collective-permute-start.9 = (bf16[1920,128]{1,0:T(8,128)(2,1)S(1)}, bf16[1920,128]{1,0:T(8,128)(2,1)S(1)}, u32[]{:S(2)}, u32[]{:S(2)}) collective-permute-start(bf16[1920,128]{1,0:T(8,128)(2,1)S(1)} %shard_map.133.refs_0_), channel_id=1, source_target_pairs={{0,128},{8,136},{16,144},{24,152},{32,160},{40,168},{48,176},{56,1... | collective-permute-start | bytes 1474568 | tf_op jit(solution)/shard_map/ppermute | solution.py:576
  106.3 1.2 collective-permute-start.8
  108.2 3.4 %shard_map.130 = (f32[8,256,128]{2,1,0:T(8,128)S(1)}, f32[8,256,128]{2,1,0:T(8,128)S(1)}, f32[4,256,128]{2,1,0:T(8,128)S(1)}) custom-call(s32[1]{0:T(128)S(6)} %copy.17.begin, s32[3,512]{1,0:T(4,128)S(1)} %bitcast.35, f32[64,512]{1,0:T(8,128)S(1)} %bitcast.26), custom_call_target="tpu_custom_call" | custom-call | tf_op jit(solution)/shard_map/pallas_call | solution.py:34
  111.6 6.1 %shard_map.131 = (f32[8,256,128]{2,1,0:T(8,128)S(1)}, f32[8,256,128]{2,1,0:T(8,128)S(1)}, f32[8,256,128]{2,1,0:T(8,128)S(1)}, f32[8,256,128]{2,1,0:T(8,128)S(1)}) custom-call(f32[8,256,128]{2,1,0:T(8,128)S(1)} %bitcast.13, f32[8,256,128]{2,1,0:T(8,128)S(1)} %bitcast.18, f32[8,256,128]{2,1,0:T(8,128)S(1)} %bitcast.22, f32[8,256,128]{2,1,0:T(8,128)S(1)} %bitcast.25, ...), custom_call_target="tpu_custom_call" | custom-call | tf_op jit(solution)/shard_map/pallas_call | solution.py:34
  117.8 1.1 collective-permute-done.11.other
  119.0 7.7 %collective-permute-done.10.refs_3_ = bf16[1920,128]{1,0:T(8,128)(2,1)S(1)} collective-permute-done((bf16[1920,128]{1,0:T(8,128)(2,1)S(1)}, bf16[1920,128]{1,0:T(8,128)(2,1)S(1)}, u32[]{:S(2)}, u32[]{:S(2)}) %collective-permute-start.10) | collective-permute-done | bytes 491552 | tf_op jit(solution)/shard_map/ppermute | solution.py:576
  131.2 1.2 shard_map.134
  132.4 2.2 collective-permute-start.16
  134.6 3.5 %collective-permute-start.17 = (bf16[640,128]{1,0:T(8,128)(2,1)S(1)}, bf16[640,128]{1,0:T(8,128)(2,1)S(1)}, u32[]{:S(2)}, u32[]{:S(2)}) collective-permute-start(bf16[640,128]{1,0:T(8,128)(2,1)S(1)} %get-tuple-element.76), channel_id=1, source_target_pairs={{0,2},{1,3},{2,0},{3,1},{4,6},{5,7},{6,4},{7,5},{8,10},{9,11},{10,... | collective-permute-start | bytes 491528 | tf_op jit(solution)/shard_map/ppermute | solution.py:576
  138.0 1.9 collective-permute-done.16.rest_6_.rest_13_
  139.9 14.3 %collective-permute-start.18 = (bf16[640,128]{1,0:T(8,128)(2,1)S(1)}, bf16[640,128]{1,0:T(8,128)(2,1)S(1)}, u32[]{:S(2)}, u32[]{:S(2)}) collective-permute-start(bf16[640,128]{1,0:T(8,128)(2,1)S(1)} %get-tuple-element.77), channel_id=1, source_target_pairs={{0,1},{1,0},{2,3},{3,2},{4,5},{5,4},{6,7},{7,6},{8,9},{9,8},{10,11... | collective-permute-start | bytes 491528 | tf_op jit(solution)/shard_map/ppermute | solution.py:576
  154.9 2.7 %collective-permute-done.18.rest_8_.rest_15_ = bf16[640,128]{1,0:T(8,128)(2,1)S(1)} collective-permute-done((bf16[640,128]{1,0:T(8,128)(2,1)S(1)}, bf16[640,128]{1,0:T(8,128)(2,1)S(1)}, u32[]{:S(2)}, u32[]{:S(2)}) %collective-permute-start.18) | collective-permute-done | bytes 163872 | tf_op jit(solution)/shard_map/ppermute | solution.py:576
  158.2 4.8 %collective-permute-start.21 = (bf16[320,128]{1,0:T(8,128)(2,1)S(1)}, bf16[320,128]{1,0:T(8,128)(2,1)S(1)}, u32[]{:S(2)}, u32[]{:S(2)}) collective-permute-start(bf16[320,128]{1,0:T(8,128)(2,1)S(1)} %get-tuple-element.89.rest_16_), channel_id=1, source_target_pairs={{0,3},{7,4},{8,11},{15,12},{16,19},{23,20},{24,27},{31,28},{32,35}... | collective-permute-start | bytes 245768 | tf_op jit(solution)/shard_map/ppermute | solution.py:576
  163.0 1.3 shard_map.135
  165.0 1.5 shard_map.136
  167.3 1.0 collective-permute-start.24
  168.2 6.0 %shard_map.137 = (f32[8,256,128]{2,1,0:T(8,128)S(1)}, f32[8,256,128]{2,1,0:T(8,128)S(1)}, f32[8,256,128]{2,1,0:T(8,128)S(1)}) custom-call(f32[8,256,128]{2,1,0:T(8,128)S(1)} %get-tuple-element.90.p1, f32[8,256,128]{2,1,0:T(8,128)S(1)} %get-tuple-element.91.q1, f32[8,256,128]{2,1,0:T(8,128)S(1)} %bitcast.15, f32[8,256,128]{2,1,0:T(8,128)S(1)} %bitcast.20, ...), custom_call_target="tpu_custom_call" | custom-call | tf_op jit(solution)/shard_map/pallas_call | solution.py:34
  174.2 4.4 %collective-permute-done.24.one = s16[2112,128]{1,0:T(8,128)(2,1)S(1)} collective-permute-done((s16[2112,128]{1,0:T(8,128)(2,1)S(1)}, s16[2112,128]{1,0:T(8,128)(2,1)S(1)}, u32[]{:S(2)}, u32[]{:S(2)}) %collective-permute-start.24) | collective-permute-done | bytes 540704 | tf_op jit(solution)/shard_map/ppermute | solution.py:667
  178.7 3.2 %shard_map.138 = (f32[8,256,128]{2,1,0:T(8,128)}, f32[8,256,128]{2,1,0:T(8,128)}, f32[320,128]{1,0:T(8,128)S(1)}, s16[336,128]{1,0:T(8,128)(2,1)S(1)}, s16[336,1...) custom-call(s32[1,2]{1,0:T(1,128)S(1)} %copy-done.9, ...), custom_call_target="tpu_custom_call" | custom-call | tf_op jit(solution)/shard_map/pallas_call | solution.py:34
  181.8 5.5 %collective-permute-start.26 = (s16[336,128]{1,0:T(8,128)(2,1)S(1)}, s16[336,128]{1,0:T(8,128)(2,1)S(1)}, u32[]{:S(2)}, u32[]{:S(2)}) collective-permute-start(s16[336,128]{1,0:T(8,128)(2,1)S(1)} %get-tuple-element.104), channel_id=1, source_target_pairs={{0,7},{1,6},{2,5},{3,4},{4,3},{5,2},{6,1},{7,0},{8,15},{9,14},{10,... | collective-permute-start | bytes 258056 | tf_op jit(solution)/shard_map/ppermute | solution.py:576
  187.3 2.8 %collective-permute-start.27 = (s16[336,128]{1,0:T(8,128)(2,1)S(1)}, s16[336,128]{1,0:T(8,128)(2,1)S(1)}, u32[]{:S(2)}, u32[]{:S(2)}) collective-permute-start(s16[336,128]{1,0:T(8,128)(2,1)S(1)} %get-tuple-element.105), channel_id=1, source_target_pairs={{0,6},{1,7},{2,4},{3,5},{4,2},{5,3},{6,0},{7,1},{8,14},{9,15},{10,... | collective-permute-start | bytes 258056 | tf_op jit(solution)/shard_map/ppermute | solution.py:576
  190.1 9.1 %collective-permute-start.28 = (s16[336,128]{1,0:T(8,128)(2,1)S(1)}, s16[336,128]{1,0:T(8,128)(2,1)S(1)}, u32[]{:S(2)}, u32[]{:S(2)}) collective-permute-start(s16[336,128]{1,0:T(8,128)(2,1)S(1)} %get-tuple-element.106), channel_id=1, source_target_pairs={{0,5},{1,4},{2,7},{3,6},{4,1},{5,0},{6,3},{7,2},{8,13},{9,12},{10,... | collective-permute-start | bytes 258056 | tf_op jit(solution)/shard_map/ppermute | solution.py:576
  199.3 3.1 %collective-permute-start.30 = (s16[336,128]{1,0:T(8,128)(2,1)S(1)}, s16[336,128]{1,0:T(8,128)(2,1)S(1)}, u32[]{:S(2)}, u32[]{:S(2)}) collective-permute-start(s16[336,128]{1,0:T(8,128)(2,1)S(1)} %get-tuple-element.108), channel_id=1, source_target_pairs={{0,3},{1,2},{2,1},{3,0},{4,7},{5,6},{6,5},{7,4},{8,11},{9,10},{10,... | collective-permute-start | bytes 258056 | tf_op jit(solution)/shard_map/ppermute | solution.py:576
  202.4 1.0 collective-permute-start.32
  203.4 1.9 collective-permute-done.28.refs_2_
  205.3 2.4 %collective-permute-done.29.refs_3_ = s16[336,128]{1,0:T(8,128)(2,1)S(1)} collective-permute-done((s16[336,128]{1,0:T(8,128)(2,1)S(1)}, s16[336,128]{1,0:T(8,128)(2,1)S(1)}, u32[]{:S(2)}, u32[]{:S(2)}) %collective-permute-start.29) | collective-permute-done | bytes 86048 | tf_op jit(solution)/shard_map/ppermute | solution.py:576
  209.4 2.2 collective-permute-done.33.got
  211.6 1.2 shard_map.140
  213.4 2.4 %collective-permute-start.35 = (s16[992,128]{1,0:T(8,128)(2,1)S(1)}, s16[992,128]{1,0:T(8,128)(2,1)S(1)}, u32[]{:S(2)}, u32[]{:S(2)}) collective-permute-start(s16[992,128]{1,0:T(8,128)(2,1)S(1)} %get-tuple-element.115), channel_id=1, source_target_pairs={{0,128},{8,136},{16,144},{24,152},{32,160},{40,168},{48,176},{56,1... | collective-permute-start | bytes 761864 | tf_op jit(solution)/shard_map/ppermute | solution.py:576
  215.8 1.2 collective-permute-start.36
  217.0 10.7 %collective-permute-done.34.refs_0_ = s16[992,128]{1,0:T(8,128)(2,1)S(1)} collective-permute-done((s16[992,128]{1,0:T(8,128)(2,1)S(1)}, s16[992,128]{1,0:T(8,128)(2,1)S(1)}, u32[]{:S(2)}, u32[]{:S(2)}) %collective-permute-start.34) | collective-permute-done | bytes 253984 | tf_op jit(solution)/shard_map/ppermute | solution.py:576
  228.7 3.8 %collective-permute-start.37 = (s16[256,128]{1,0:T(8,128)(2,1)S(1)}, s16[256,128]{1,0:T(8,128)(2,1)S(1)}, u32[]{:S(2)}, u32[]{:S(2)}) collective-permute-start(s16[256,128]{1,0:T(8,128)(2,1)S(1)} %get-tuple-element.118), channel_id=1, source_target_pairs={{0,48},{8,56},{16,32},{24,40},{32,16},{40,24},{48,0},{56,8},{64,11... | collective-permute-start | bytes 196616 | tf_op jit(solution)/shard_map/ppermute | solution.py:576
  233.2 1.8 collective-permute-done.37.refs_0_
  235.0 2.7 %collective-permute-done.38.refs_1_ = s16[256,128]{1,0:T(8,128)(2,1)S(1)} collective-permute-done((s16[256,128]{1,0:T(8,128)(2,1)S(1)}, s16[256,128]{1,0:T(8,128)(2,1)S(1)}, u32[]{:S(2)}, u32[]{:S(2)}) %collective-permute-start.38) | collective-permute-done | bytes 65568 | tf_op jit(solution)/shard_map/ppermute | solution.py:576
  (72 shorter events, 13.6 us)
Async XLA Ops:
  5.5 102.6 %copy-start.12 = (s32[1,3,512]{2,0,1:T(1,128)S(1)}, s32[1,3,512]{2,0,1:T(1,128)}, u32[]{:S(2)}) copy-start(s32[1,3,512]{2,0,1:T(1,128)} %param.15) | copy-start | bytes 18436
  5.5 102.7 %copy-start.7 = (f32[1,64,512]{2,1,0:T(8,128)S(1)}, f32[1,64,512]{2,1,0:T(8,128)}, u32[]{:S(2)}) copy-start(f32[1,64,512]{2,1,0:T(8,128)} %param.16) | copy-start | bytes 393220
  5.5 106.1 %copy-start.3 = (f32[1,8,256,128]{3,2,1,0:T(8,128)S(1)}, f32[1,8,256,128]{3,2,1,0:T(8,128)}, u32[]{:S(2)}) copy-start(f32[1,8,256,128]{3,2,1,0:T(8,128)} %param.21) | copy-start | bytes 3145732
  5.5 106.1 %copy-start.5 = (f32[1,8,256,128]{3,2,1,0:T(8,128)S(1)}, f32[1,8,256,128]{3,2,1,0:T(8,128)}, u32[]{:S(2)}) copy-start(f32[1,8,256,128]{3,2,1,0:T(8,128)} %param.18) | copy-start | bytes 3145732
  6.4 105.2 %copy-start.1 = (f32[1,8,256,128]{3,2,1,0:T(8,128)S(1)}, f32[1,8,256,128]{3,2,1,0:T(8,128)}, u32[]{:S(2)}) copy-start(f32[1,8,256,128]{3,2,1,0:T(8,128)} %param.19) | copy-start | bytes 3145732
  6.4 151.8 %collective-permute-start.19 = (s16[6336,128]{1,0:T(8,128)(2,1)S(1)}, s16[6336,128]{1,0:T(8,128)(2,1)S(1)}, u32[]{:S(2)}, u32[]{:S(2)}) collective-permute-start(s16[6336,128]{1,0:T(8,128)(2,1)S(1)} %get-tuple-element.78), channel_id=1, source_target_pairs={{3,4},{4,3},{11,12},{12,11},{19,20},{20,19},{27,28},{28,27},{35,36... | collective-permute-start | bytes 4866056 | tf_op jit(solution)/shard_map/ppermute | solution.py:627
  7.3 88.0 %collective-permute-start.7 = (bf16[240,128]{1,0:T(8,128)(2,1)S(1)}, bf16[240,128]{1,0:T(8,128)(2,1)S(1)}, u32[]{:S(2)}, u32[]{:S(2)}) collective-permute-start(bf16[240,128]{1,0:T(8,128)(2,1)S(1)} %bitcast.27), channel_id=1, source_target_pairs={{0,52},{1,53},{2,54},{3,55},{4,48},{5,49},{6,50},{7,51},{8,60},{9,... | collective-permute-start | bytes 184328 | tf_op jit(solution)/shard_map/ppermute | solution.py:576
  18.9 78.0 %collective-permute-start.6 = (bf16[240,128]{1,0:T(8,128)(2,1)S(1)}, bf16[240,128]{1,0:T(8,128)(2,1)S(1)}, u32[]{:S(2)}, u32[]{:S(2)}) collective-permute-start(bf16[240,128]{1,0:T(8,128)(2,1)S(1)} %bitcast.28), channel_id=1, source_target_pairs={{0,36},{1,37},{2,38},{3,39},{4,32},{5,33},{6,34},{7,35},{8,44},{9,... | collective-permute-start | bytes 184328 | tf_op jit(solution)/shard_map/ppermute | solution.py:576
  18.9 79.3 %collective-permute-start.5 = (bf16[240,128]{1,0:T(8,128)(2,1)S(1)}, bf16[240,128]{1,0:T(8,128)(2,1)S(1)}, u32[]{:S(2)}, u32[]{:S(2)}) collective-permute-start(bf16[240,128]{1,0:T(8,128)(2,1)S(1)} %bitcast.29), channel_id=1, source_target_pairs={{0,20},{1,21},{2,22},{3,23},{4,16},{5,17},{6,18},{7,19},{8,28},{9,... | collective-permute-start | bytes 184328 | tf_op jit(solution)/shard_map/ppermute | solution.py:576
  20.8 79.0 %collective-permute-start.4 = (bf16[240,128]{1,0:T(8,128)(2,1)S(1)}, bf16[240,128]{1,0:T(8,128)(2,1)S(1)}, u32[]{:S(2)}, u32[]{:S(2)}) collective-permute-start(bf16[240,128]{1,0:T(8,128)(2,1)S(1)} %bitcast.30), channel_id=1, source_target_pairs={{0,4},{1,5},{2,6},{3,7},{4,0},{5,1},{6,2},{7,3},{8,12},{9,13},{10,... | collective-permute-start | bytes 184328 | tf_op jit(solution)/shard_map/ppermute | solution.py:576
  95.3 6.4 %collective-permute-start.3 = (bf16[240,128]{1,0:T(8,128)(2,1)S(1)}, bf16[240,128]{1,0:T(8,128)(2,1)S(1)}, u32[]{:S(2)}, u32[]{:S(2)}) collective-permute-start(bf16[240,128]{1,0:T(8,128)(2,1)S(1)} %bitcast.31), channel_id=1, source_target_pairs={{0,48},{1,49},{2,50},{3,51},{4,52},{5,53},{6,54},{7,55},{8,56},{9,... | collective-permute-start | bytes 184328 | tf_op jit(solution)/shard_map/ppermute | solution.py:576
  96.9 6.5 %collective-permute-start.2 = (bf16[240,128]{1,0:T(8,128)(2,1)S(1)}, bf16[240,128]{1,0:T(8,128)(2,1)S(1)}, u32[]{:S(2)}, u32[]{:S(2)}) collective-permute-start(bf16[240,128]{1,0:T(8,128)(2,1)S(1)} %bitcast.32), channel_id=1, source_target_pairs={{0,32},{1,33},{2,34},{3,35},{4,36},{5,37},{6,38},{7,39},{8,40},{9,... | collective-permute-start | bytes 184328 | tf_op jit(solution)/shard_map/ppermute | solution.py:576
  98.2 5.1 %collective-permute-start.1 = (bf16[240,128]{1,0:T(8,128)(2,1)S(1)}, bf16[240,128]{1,0:T(8,128)(2,1)S(1)}, u32[]{:S(2)}, u32[]{:S(2)}) collective-permute-start(bf16[240,128]{1,0:T(8,128)(2,1)S(1)} %bitcast.33), channel_id=1, source_target_pairs={{0,16},{1,17},{2,18},{3,19},{4,20},{5,21},{6,22},{7,23},{8,24},{9,... | collective-permute-start | bytes 184328 | tf_op jit(solution)/shard_map/ppermute | solution.py:576
  103.3 23.3 %collective-permute-start.10 = (bf16[1920,128]{1,0:T(8,128)(2,1)S(1)}, bf16[1920,128]{1,0:T(8,128)(2,1)S(1)}, u32[]{:S(2)}, u32[]{:S(2)}) collective-permute-start(bf16[1920,128]{1,0:T(8,128)(2,1)S(1)} %shard_map.133.refs_0_), channel_id=1, source_target_pairs={{0,192},{8,200},{16,208},{24,216},{32,224},{40,232},{48,240},{56,2... | collective-permute-start | bytes 1474568 | tf_op jit(solution)/shard_map/ppermute | solution.py:576
  103.9 22.7 %collective-permute-start.9 = (bf16[1920,128]{1,0:T(8,128)(2,1)S(1)}, bf16[1920,128]{1,0:T(8,128)(2,1)S(1)}, u32[]{:S(2)}, u32[]{:S(2)}) collective-permute-start(bf16[1920,128]{1,0:T(8,128)(2,1)S(1)} %shard_map.133.refs_0_), channel_id=1, source_target_pairs={{0,128},{8,136},{16,144},{24,152},{32,160},{40,168},{48,176},{56,1... | collective-permute-start | bytes 1474568 | tf_op jit(solution)/shard_map/ppermute | solution.py:576
  106.3 20.9 %collective-permute-start.8 = (bf16[1920,128]{1,0:T(8,128)(2,1)S(1)}, bf16[1920,128]{1,0:T(8,128)(2,1)S(1)}, u32[]{:S(2)}, u32[]{:S(2)}) collective-permute-start(bf16[1920,128]{1,0:T(8,128)(2,1)S(1)} %shard_map.133.refs_0_), channel_id=1, source_target_pairs={{0,64},{8,72},{16,80},{24,88},{32,96},{40,104},{48,112},{56,120},{... | collective-permute-start | bytes 1474568 | tf_op jit(solution)/shard_map/ppermute | solution.py:576
  111.6 6.1 %copy-start.9 = (s32[1,2]{1,0:T(1,128)S(1)}, s32[1,2]{1,0:T(1,128)}, u32[]{:S(2)}) copy-start(s32[1,2]{1,0:T(1,128)} %anchors.8) | copy-start | bytes 28
  117.7 1.2 collective-permute-start.11
  127.2 1.9 collective-permute-start.12
  127.2 2.6 %collective-permute-start.13 = (bf16[1920,128]{1,0:T(8,128)(2,1)S(1)}, bf16[1920,128]{1,0:T(8,128)(2,1)S(1)}, u32[]{:S(2)}, u32[]{:S(2)}) collective-permute-start(bf16[1920,128]{1,0:T(8,128)(2,1)S(1)} %collective-permute-done.8.refs_1_), channel_id=1, source_target_pairs={{0,8},{8,0},{16,24},{24,16},{32,40},{40,32},{48,56},{56,48},{64,72... | collective-permute-start | bytes 1474568 | tf_op jit(solution)/shard_map/ppermute | solution.py:641
  127.7 2.9 %collective-permute-start.14 = (bf16[1920,128]{1,0:T(8,128)(2,1)S(1)}, bf16[1920,128]{1,0:T(8,128)(2,1)S(1)}, u32[]{:S(2)}, u32[]{:S(2)}) collective-permute-start(bf16[1920,128]{1,0:T(8,128)(2,1)S(1)} %collective-permute-done.9.refs_2_), channel_id=1, source_target_pairs={{0,8},{8,0},{16,24},{24,16},{32,40},{40,32},{48,56},{56,48},{64,72... | collective-permute-start | bytes 1474568 | tf_op jit(solution)/shard_map/ppermute | solution.py:641
  127.7 3.5 %collective-permute-start.15 = (bf16[1920,128]{1,0:T(8,128)(2,1)S(1)}, bf16[1920,128]{1,0:T(8,128)(2,1)S(1)}, u32[]{:S(2)}, u32[]{:S(2)}) collective-permute-start(bf16[1920,128]{1,0:T(8,128)(2,1)S(1)} %collective-permute-done.10.refs_3_), channel_id=1, source_target_pairs={{0,8},{8,0},{16,24},{24,16},{32,40},{40,32},{48,56},{56,48},{64,72... | collective-permute-start | bytes 1474568 | tf_op jit(solution)/shard_map/ppermute | solution.py:641
  129.1 33.9 %collective-permute-start.20 = (s16[2112,128]{1,0:T(8,128)(2,1)S(1)}, s16[2112,128]{1,0:T(8,128)(2,1)S(1)}, u32[]{:S(2)}, u32[]{:S(2)}) collective-permute-start(s16[2112,128]{1,0:T(8,128)(2,1)S(1)} %get-tuple-element.80), channel_id=1, source_target_pairs={{0,1},{1,0},{2,3},{3,2},{4,5},{5,4},{6,7},{7,6},{8,9},{9,8},{10,11... | collective-permute-start | bytes 1622024 | tf_op jit(solution)/shard_map/ppermute | solution.py:628
  129.8 33.2 %copy-start.10 = (s32[1,3]{1,0:T(1,128)S(1)}, s32[1,3]{1,0:T(1,128)}, u32[]{:S(2)}) copy-start(s32[1,3]{1,0:T(1,128)} %source.5) | copy-start | bytes 40
  129.8 33.2 %copy-start.11 = (f32[64]{0:T(128)S(1)}, f32[64]{0:T(128)}, u32[]{:S(2)}) copy-start(f32[64]{0:T(128)} %wave.5) | copy-start | bytes 772
  129.8 34.6 %collective-permute-start = (s16[2112,128]{1,0:T(8,128)(2,1)S(1)}, s16[2112,128]{1,0:T(8,128)(2,1)S(1)}, u32[]{:S(2)}, u32[]{:S(2)}) collective-permute-start(s16[2112,128]{1,0:T(8,128)(2,1)S(1)} %get-tuple-element.67), channel_id=1, source_target_pairs={{1,2},{5,6},{2,1},{6,5},{9,10},{13,14},{10,9},{14,13},{17,18},{21,... | collective-permute-start | bytes 1622024 | tf_op jit(solution)/shard_map/ppermute | solution.py:629
  132.4 7.6 %collective-permute-start.16 = (bf16[640,128]{1,0:T(8,128)(2,1)S(1)}, bf16[640,128]{1,0:T(8,128)(2,1)S(1)}, u32[]{:S(2)}, u32[]{:S(2)}) collective-permute-start(bf16[640,128]{1,0:T(8,128)(2,1)S(1)} %get-tuple-element.75), channel_id=1, source_target_pairs={{0,3},{1,2},{2,1},{3,0},{4,7},{5,6},{6,5},{7,4},{8,11},{9,10},{10,... | collective-permute-start | bytes 491528 | tf_op jit(solution)/shard_map/ppermute | solution.py:576
  134.6 19.6 %collective-permute-start.17 = (bf16[640,128]{1,0:T(8,128)(2,1)S(1)}, bf16[640,128]{1,0:T(8,128)(2,1)S(1)}, u32[]{:S(2)}, u32[]{:S(2)}) collective-permute-start(bf16[640,128]{1,0:T(8,128)(2,1)S(1)} %get-tuple-element.76), channel_id=1, source_target_pairs={{0,2},{1,3},{2,0},{3,1},{4,6},{5,7},{6,4},{7,5},{8,10},{9,11},{10,... | collective-permute-start | bytes 491528 | tf_op jit(solution)/shard_map/ppermute | solution.py:576
  139.9 17.6 %collective-permute-start.18 = (bf16[640,128]{1,0:T(8,128)(2,1)S(1)}, bf16[640,128]{1,0:T(8,128)(2,1)S(1)}, u32[]{:S(2)}, u32[]{:S(2)}) collective-permute-start(bf16[640,128]{1,0:T(8,128)(2,1)S(1)} %get-tuple-element.77), channel_id=1, source_target_pairs={{0,1},{1,0},{2,3},{3,2},{4,5},{5,4},{6,7},{7,6},{8,9},{9,8},{10,11... | collective-permute-start | bytes 491528 | tf_op jit(solution)/shard_map/ppermute | solution.py:576
  154.2 10.2 %collective-permute-start.23 = (bf16[320,128]{1,0:T(8,128)(2,1)S(1)}, bf16[320,128]{1,0:T(8,128)(2,1)S(1)}, u32[]{:S(2)}, u32[]{:S(2)}) collective-permute-start(bf16[320,128]{1,0:T(8,128)(2,1)S(1)} %get-tuple-element.89.rest_16_), channel_id=1, source_target_pairs={{2,3},{5,4},{10,11},{13,12},{18,19},{21,20},{26,27},{29,28},{34,35... | collective-permute-start | bytes 245768 | tf_op jit(solution)/shard_map/ppermute | solution.py:576
  157.6 6.8 %collective-permute-start.22 = (bf16[320,128]{1,0:T(8,128)(2,1)S(1)}, bf16[320,128]{1,0:T(8,128)(2,1)S(1)}, u32[]{:S(2)}, u32[]{:S(2)}) collective-permute-start(bf16[320,128]{1,0:T(8,128)(2,1)S(1)} %get-tuple-element.89.rest_16_), channel_id=1, source_target_pairs={{1,3},{6,4},{9,11},{14,12},{17,19},{22,20},{25,27},{30,28},{33,35}... | collective-permute-start | bytes 245768 | tf_op jit(solution)/shard_map/ppermute | solution.py:576
  158.2 6.8 %collective-permute-start.21 = (bf16[320,128]{1,0:T(8,128)(2,1)S(1)}, bf16[320,128]{1,0:T(8,128)(2,1)S(1)}, u32[]{:S(2)}, u32[]{:S(2)}) collective-permute-start(bf16[320,128]{1,0:T(8,128)(2,1)S(1)} %get-tuple-element.89.rest_16_), channel_id=1, source_target_pairs={{0,3},{7,4},{8,11},{15,12},{16,19},{23,20},{24,27},{31,28},{32,35}... | collective-permute-start | bytes 245768 | tf_op jit(solution)/shard_map/ppermute | solution.py:576
  166.6 7.7 %collective-permute-start.25 = (s16[2112,128]{1,0:T(8,128)(2,1)S(1)}, s16[2112,128]{1,0:T(8,128)(2,1)S(1)}, u32[]{:S(2)}, u32[]{:S(2)}) collective-permute-start(s16[2112,128]{1,0:T(8,128)(2,1)S(1)} %get-tuple-element.98), channel_id=1, source_target_pairs={{1,2},{5,6},{2,1},{6,5},{9,10},{13,14},{10,9},{14,13},{17,18},{21,... | collective-permute-start | bytes 1622024 | tf_op jit(solution)/shard_map/ppermute | solution.py:686
  167.3 11.4 %collective-permute-start.24 = (s16[2112,128]{1,0:T(8,128)(2,1)S(1)}, s16[2112,128]{1,0:T(8,128)(2,1)S(1)}, u32[]{:S(2)}, u32[]{:S(2)}) collective-permute-start(s16[2112,128]{1,0:T(8,128)(2,1)S(1)} %get-tuple-element.97), channel_id=1, source_target_pairs={{0,1},{1,0},{2,3},{3,2},{4,5},{5,4},{6,7},{7,6},{8,9},{9,8},{10,11... | collective-permute-start | bytes 1622024 | tf_op jit(solution)/shard_map/ppermute | solution.py:667
  181.8 20.6 %collective-permute-start.26 = (s16[336,128]{1,0:T(8,128)(2,1)S(1)}, s16[336,128]{1,0:T(8,128)(2,1)S(1)}, u32[]{:S(2)}, u32[]{:S(2)}) collective-permute-start(s16[336,128]{1,0:T(8,128)(2,1)S(1)} %get-tuple-element.104), channel_id=1, source_target_pairs={{0,7},{1,6},{2,5},{3,4},{4,3},{5,2},{6,1},{7,0},{8,15},{9,14},{10,... | collective-permute-start | bytes 258056 | tf_op jit(solution)/shard_map/ppermute | solution.py:576
  187.3 15.1 %collective-permute-start.27 = (s16[336,128]{1,0:T(8,128)(2,1)S(1)}, s16[336,128]{1,0:T(8,128)(2,1)S(1)}, u32[]{:S(2)}, u32[]{:S(2)}) collective-permute-start(s16[336,128]{1,0:T(8,128)(2,1)S(1)} %get-tuple-element.105), channel_id=1, source_target_pairs={{0,6},{1,7},{2,4},{3,5},{4,2},{5,3},{6,0},{7,1},{8,14},{9,15},{10,... | collective-permute-start | bytes 258056 | tf_op jit(solution)/shard_map/ppermute | solution.py:576
  190.1 15.2 %collective-permute-start.28 = (s16[336,128]{1,0:T(8,128)(2,1)S(1)}, s16[336,128]{1,0:T(8,128)(2,1)S(1)}, u32[]{:S(2)}, u32[]{:S(2)}) collective-permute-start(s16[336,128]{1,0:T(8,128)(2,1)S(1)} %get-tuple-element.106), channel_id=1, source_target_pairs={{0,5},{1,4},{2,7},{3,6},{4,1},{5,0},{6,3},{7,2},{8,13},{9,12},{10,... | collective-permute-start | bytes 258056 | tf_op jit(solution)/shard_map/ppermute | solution.py:576
  199.3 8.5 %collective-permute-start.29 = (s16[336,128]{1,0:T(8,128)(2,1)S(1)}, s16[336,128]{1,0:T(8,128)(2,1)S(1)}, u32[]{:S(2)}, u32[]{:S(2)}) collective-permute-start(s16[336,128]{1,0:T(8,128)(2,1)S(1)} %get-tuple-element.107), channel_id=1, source_target_pairs={{0,4},{1,5},{2,6},{3,7},{4,0},{5,1},{6,2},{7,3},{8,12},{9,13},{10,... | collective-permute-start | bytes 258056 | tf_op jit(solution)/shard_map/ppermute | solution.py:576
  199.3 8.5 %collective-permute-start.30 = (s16[336,128]{1,0:T(8,128)(2,1)S(1)}, s16[336,128]{1,0:T(8,128)(2,1)S(1)}, u32[]{:S(2)}, u32[]{:S(2)}) collective-permute-start(s16[336,128]{1,0:T(8,128)(2,1)S(1)} %get-tuple-element.108), channel_id=1, source_target_pairs={{0,3},{1,2},{2,1},{3,0},{4,7},{5,6},{6,5},{7,4},{8,11},{9,10},{10,... | collective-permute-start | bytes 258056 | tf_op jit(solution)/shard_map/ppermute | solution.py:576
  202.4 6.0 %collective-permute-start.31 = (s16[336,128]{1,0:T(8,128)(2,1)S(1)}, s16[336,128]{1,0:T(8,128)(2,1)S(1)}, u32[]{:S(2)}, u32[]{:S(2)}) collective-permute-start(s16[336,128]{1,0:T(8,128)(2,1)S(1)} %get-tuple-element.109), channel_id=1, source_target_pairs={{0,2},{1,3},{2,0},{3,1},{4,6},{5,7},{6,4},{7,5},{8,10},{9,11},{10,... | collective-permute-start | bytes 258056 | tf_op jit(solution)/shard_map/ppermute | solution.py:576
  202.4 6.0 %collective-permute-start.32 = (s16[336,128]{1,0:T(8,128)(2,1)S(1)}, s16[336,128]{1,0:T(8,128)(2,1)S(1)}, u32[]{:S(2)}, u32[]{:S(2)}) collective-permute-start(s16[336,128]{1,0:T(8,128)(2,1)S(1)} %get-tuple-element.110), channel_id=1, source_target_pairs={{0,1},{1,0},{2,3},{3,2},{4,5},{5,4},{6,7},{7,6},{8,9},{9,8},{10,11... | collective-permute-start | bytes 258056 | tf_op jit(solution)/shard_map/ppermute | solution.py:576
  209.3 2.3 collective-permute-start.33
  212.8 14.9 %collective-permute-start.34 = (s16[992,128]{1,0:T(8,128)(2,1)S(1)}, s16[992,128]{1,0:T(8,128)(2,1)S(1)}, u32[]{:S(2)}, u32[]{:S(2)}) collective-permute-start(s16[992,128]{1,0:T(8,128)(2,1)S(1)} %get-tuple-element.114), channel_id=1, source_target_pairs={{0,192},{8,200},{16,208},{24,216},{32,224},{40,232},{48,240},{56,2... | collective-permute-start | bytes 761864 | tf_op jit(solution)/shard_map/ppermute | solution.py:576
  213.4 14.4 %collective-permute-start.35 = (s16[992,128]{1,0:T(8,128)(2,1)S(1)}, s16[992,128]{1,0:T(8,128)(2,1)S(1)}, u32[]{:S(2)}, u32[]{:S(2)}) collective-permute-start(s16[992,128]{1,0:T(8,128)(2,1)S(1)} %get-tuple-element.115), channel_id=1, source_target_pairs={{0,128},{8,136},{16,144},{24,152},{32,160},{40,168},{48,176},{56,1... | collective-permute-start | bytes 761864 | tf_op jit(solution)/shard_map/ppermute | solution.py:576
  215.8 12.6 %collective-permute-start.36 = (s16[992,128]{1,0:T(8,128)(2,1)S(1)}, s16[992,128]{1,0:T(8,128)(2,1)S(1)}, u32[]{:S(2)}, u32[]{:S(2)}) collective-permute-start(s16[992,128]{1,0:T(8,128)(2,1)S(1)} %get-tuple-element.116), channel_id=1, source_target_pairs={{0,64},{8,72},{16,80},{24,88},{32,96},{40,104},{48,112},{56,120},{... | collective-permute-start | bytes 761864 | tf_op jit(solution)/shard_map/ppermute | solution.py:576
  228.7 6.3 %collective-permute-start.37 = (s16[256,128]{1,0:T(8,128)(2,1)S(1)}, s16[256,128]{1,0:T(8,128)(2,1)S(1)}, u32[]{:S(2)}, u32[]{:S(2)}) collective-permute-start(s16[256,128]{1,0:T(8,128)(2,1)S(1)} %get-tuple-element.118), channel_id=1, source_target_pairs={{0,48},{8,56},{16,32},{24,40},{32,16},{40,24},{48,0},{56,8},{64,11... | collective-permute-start | bytes 196616 | tf_op jit(solution)/shard_map/ppermute | solution.py:576
  232.5 5.2 %collective-permute-start.38 = (s16[256,128]{1,0:T(8,128)(2,1)S(1)}, s16[256,128]{1,0:T(8,128)(2,1)S(1)}, u32[]{:S(2)}, u32[]{:S(2)}) collective-permute-start(s16[256,128]{1,0:T(8,128)(2,1)S(1)} %get-tuple-element.119), channel_id=1, source_target_pairs={{0,32},{8,40},{16,48},{24,56},{32,0},{40,8},{48,16},{56,24},{64,96... | collective-permute-start | bytes 196616 | tf_op jit(solution)/shard_map/ppermute | solution.py:576
  232.5 5.4 %collective-permute-start.39 = (s16[256,128]{1,0:T(8,128)(2,1)S(1)}, s16[256,128]{1,0:T(8,128)(2,1)S(1)}, u32[]{:S(2)}, u32[]{:S(2)}) collective-permute-start(s16[256,128]{1,0:T(8,128)(2,1)S(1)} %get-tuple-element.120), channel_id=1, source_target_pairs={{0,16},{8,24},{16,0},{24,8},{32,48},{40,56},{48,32},{56,40},{64,80... | collective-permute-start | bytes 196616 | tf_op jit(solution)/shard_map/ppermute | solution.py:576
  (5 other events, 6.7 us)

commit v8 on v4

--- a/solution.py
+++ b/solution.py
@@ -31,8 +31,7 @@
     return pl.BlockSpec(memory_space=pltpu.SMEM)
 
 
-def call(kernel, outs, args, spaces, scratch=(), cost=1_000_000):
-    moved = sum(a.size * a.dtype.itemsize for a in (*outs, *args))
+def call(kernel, outs, args, spaces, scratch=()):
     return pl.pallas_call(
         kernel,
         out_shape=list(outs),
@@ -219,7 +218,7 @@
 
 def first_kernel(halves, anchors, source, begin, wave, sum_f, sum_a, base_f, base_a, *rest):
     next_f, next_a, courant, one, two, slab, level, scale_one, scale_two = rest[-9:]
-    halos, pieces = rest[:2], rest[2:-9]
+    halos, pieces = rest[1::-1], rest[2:-9]
     row_count, count_y, _ = sum_f.shape
     band = pieces[0].shape[0] // (row_count * halves)
     side = len(pieces)
@@ -263,7 +262,7 @@
                 out[x, spot, :] = value
 
 
-def second_kernel(groups, anchors, source, begin, wave, p1, q1, p0, courant, part_f, part_a, bend, one, two, *rest):
+def second_kernel(groups, anchors, source, begin, wave, p1, q1, p0, courant, part_f, part_a, bend, two, one, *rest):
     next_f, next_a, own = rest[:3]
     sends = rest[3 : 2 + groups]
     frame, scale_one, scale_two = rest[2 + groups :]
@@ -342,38 +341,64 @@
     return [(shot, shot ^ bits) for shot in range(SIZE_X * SIZE_Z * SIZE_C)]
 
 
-def join_kernel(*refs):
-    size = refs[0].shape[0]
-    for n, ref in enumerate(refs[:-1]):
-        refs[-1][pl.ds(n * size, size), :] = ref[...]
-
-
-def pick_kernel(layout, row_count, halves, anchors, *refs):
-    count = len(layout)
-    ins, outs, table = refs[:count], refs[count:-1], refs[-1]
+def nearest_x(anchor, z, c, own):
+    reach = SIZE_Z * SIZE_C * own
+    least = anchor - (own - 1) - (z * SIZE_C + c) * own
+    return jnp.clip((least + reach - 1 + reach) // reach - 1, 0, SIZE_X - 1)
+
+
+def select_kernel(own, window, places, *refs):
+    count = SIZE_X
+    ins, outs = refs[:count], refs[count:]
+    block = ins[0].shape[0]
+    x, z, c = place_of(lax.axis_index("shot"))
+    half = lax.axis_index("dom") // (lax.axis_size("dom") // HALVES)
+    for k, out in enumerate(outs):
+        for n in range(SIZE_C):
+            anchor = places[k % SIZE_Z, n] + (half ^ (k // SIZE_Z)) * window
+            apart = nearest_x(anchor, z, c, own) ^ x
+            for dx in range(SIZE_X):
+
+                @pl.when(apart == dx)
+                def _():
+                    out[pl.ds(n * block, block), :] = ins[dx][...]
+
+
+def share_kernel(*refs):
+    ins, (mine, theirs) = refs[:-2], refs[-2:]
+    block = ins[0].shape[0] // SIZE_C
+    for k in range(len(ins)):
+        n, ref = k, ins[-k]
+        mine[pl.ds(n * block, block), :] = ref[0:block, :]
+        theirs[pl.ds(n * block, block), :] = ref[block : 2 * block, :]
+
+
+def pick_kernel(row_count, anchors, mine, theirs, *refs):
+    outs, table = refs[:-1], refs[-1]
     side = len(outs)
-    piece = outs[0].shape[0] // halves
+    piece = outs[0].shape[0] // HALVES
     per = piece // row_count
-    block = ins[0].shape[0] // len(layout[0])
+    block = mine.shape[0] // (HALVES * SIZE_Z)
     own = block // per
     x, z, c = place_of(lax.axis_index("shot"))
     half, me = lax.axis_index("dom") // side, lax.rem(lax.axis_index("dom"), side)
     anchor = anchors[0, 0] + half * (side * row_count)
     first = anchor // own
     span = table.shape[1] // block
-    for ref, owners in zip(ins, layout):
-        for n, (dx, dz, dc, dh) in enumerate(owners):
-            place = ((x ^ dx) * SIZE_Z + (z ^ dz)) * SIZE_C + (c ^ dc) - first
+    for dc, ref in enumerate((mine, theirs)):
+        for k in range(HALVES * SIZE_Z):
+            from_z, from_c = z ^ (k % SIZE_Z), c ^ dc
+            place = (nearest_x(anchor, from_z, from_c, own) * SIZE_Z + from_z) * SIZE_C + from_c - first
 
             @pl.when((place >= 0) & (place < span))
             def _():
                 start = pl.multiple_of(place * block, 8)
-                table[half ^ dh, pl.ds(start, block), :] = ref[pl.ds(n * block, block), :].astype(F32)
+                table[half ^ (k // SIZE_Z), pl.ds(start, block), :] = ref[pl.ds(k * block, block), :].astype(F32)
 
     offset = (anchor - first * own) * per
     for k in range(side):
         start = pl.multiple_of(offset + (me ^ k) * piece, 8)
-        for h in range(halves):
+        for h in range(HALVES):
             outs[k][pl.ds(h * piece, piece), :] = table[h, pl.ds(start, piece), :].astype(BF16)
 
 
@@ -497,7 +522,27 @@
 
     local = velocity.reshape(block, count_z)
     other = lax.ppermute(anchors, "shot", swap("c", 1))
-    near = [local] + exchange([local] * (HALVES * SIZE_Z - 1), ("shot", "dom"), functools.partial(swap_z, groups))
+    row = [local] + exchange([local] * (SIZE_X - 1), "shot", along["x"])
+    pair = jnp.concatenate([anchors[:, 0], other[:, 0]])
+    places = jnp.stack([pair] + exchange([pair] * (SIZE_Z - 1), "shot", along["z"]))
+    side = groups // HALVES
+    window = side * row_count
+    needed = call(
+        functools.partial(select_kernel, own_rows, window),
+        [struct((SIZE_C * block, count_z), BF16)] * (HALVES * SIZE_Z),
+        (places, *row),
+        "s" + "v" * SIZE_X,
+    )
+    along_z = functools.partial(swap_z, groups)
+    column = [needed[0]] + exchange(needed[1:], ("shot", "dom"), along_z)[::-1]
+
+    field = struct((row_count, count_y, count_z), F32)
+    hits = call(hit_kernel, (field, field), (start_step, receivers[0], traces[0]), "svv")
+    padded = pltpu.VMEM((row_count + 2 * HALO, count_y + 2 * PAD, count_z), F32)
+    sums = call(before_kernel, (field,) * 4, (p0, q0, p_prev, q_prev, hits[0]), "v" * 5, (padded,))
+    column, _ = lax.optimization_barrier((column, sums[0]))
+    shared = struct((HALVES * SIZE_Z * block, count_z), BF16)
+    mine, theirs = call(share_kernel, (shared, shared), column, "v" * len(column))
 
     half = halo_rows(2 * HALO, count_y)
     code = struct((half, count_z), I16)
@@ -505,34 +550,14 @@
     one, two = call(encode_kernel, (code, code), (p0, q0), "vv", (levels,))
     from_one = lax.ppermute(one, "dom", one_pairs)
     from_two = lax.ppermute(two, "dom", two_pairs)
-
-    lines = []
-    for part in range(HALVES):
-        blocks = near[part * SIZE_Z : (part + 1) * SIZE_Z]
-        lines += call(join_kernel, (struct((SIZE_Z * block, count_z), BF16),), blocks, "v" * SIZE_Z)
-    lines[1], other, one = lax.optimization_barrier((lines[1], other, one))
-    field = struct((row_count, count_y, count_z), F32)
-    hits = call(hit_kernel, (field, field), (start_step, receivers[0], traces[0]), "svv")
-    padded = pltpu.VMEM((row_count + 2 * HALO, count_y + 2 * PAD, count_z), F32)
-    sums = call(before_kernel, (field,) * 4, (p0, q0, p_prev, q_prev, hits[0]), "v" * 5, (padded,))
-    planes = [[line] + exchange([line] * (SIZE_X - 1), "shot", along["x"]) for line in lines]
-    planes[1] = list(lax.optimization_barrier((*planes[1], sums[0])))[:SIZE_X]
-    plane = planes[0] + planes[1]
-    plane += [lax.ppermute(part, "shot", swap("c", 1)) for part in plane]
-    *plane, from_one, from_two = lax.optimization_barrier((*plane, from_one, from_two))
-    layout = [
-        [(dx, dz, dc, dh) for dz in range(SIZE_Z)]
-        for dc in range(SIZE_C)
-        for dh in range(HALVES)
-        for dx in range(SIZE_X)
-    ]
-    side = groups // HALVES
+    theirs = lax.ppermute(theirs, "shot", swap("c", 1))
+    reach = -(-(window + own_rows - 1) // own_rows) * block
     pieces = call(
-        functools.partial(pick_kernel, layout, row_count, HALVES),
+        functools.partial(pick_kernel, row_count),
         [struct((HALVES * piece, count_z), BF16)] * side,
-        (anchors, *plane),
-        "s" + "v" * len(plane),
-        (pltpu.VMEM((HALVES, -(-(row_count * side + own_rows - 1) // own_rows) * block, count_z), F32),),
+        (anchors, mine, theirs),
+        "svv",
+        (pltpu.VMEM((HALVES, reach, count_z), F32),),
     )
     pieces = [pieces[0]] + exchange(pieces[1:], "dom", between)[::-1]
 
@@ -541,7 +566,7 @@
     p1, q1, courant, one, two = call(
         functools.partial(first_kernel, HALVES),
         (field, field, field, code, code),
-        (*scalars, *sums, from_one, from_two, *pieces),
+        (*scalars, *sums, from_two, from_one, *pieces),
         "ssss" + "v" * (6 + side),
         (slab, levels, scale, scale),
     )
@@ -564,7 +589,7 @@
     p2, q2, own, *sends = call(
         functools.partial(second_kernel, groups),
         (field, field, struct((piece, count_z), F32), *[coded] * (groups - 1)),
-        (*scalars, p1, q1, p0, courant, part_f, part_a, bend, from_one, from_two),
+        (*scalars, p1, q1, p0, courant, part_f, part_a, bend, from_two, from_one),
         "ssss" + "v" * 9,
         (frame, scale, scale),
     )

time: 180 us -> 185 us (1.028)
  starting transfers between devices: 86.4 us -> 93.3 us
  waiting for transfers between devices: 58.6 us -> 56.7 us
    ppermute x29, waiting for transfers between devices: 48.4 us -> 40.5 us  [exchange(): got[k] = lax.ppermute(parts[k - 1], axis, pairs(k))]
    ppermute x2, waiting for transfers between devices: 5.33 us -> 12.9 us  [body(): from_one = lax.ppermute(one, 'dom', one_pairs)]
    ppermute x29, starting transfers between devices: 78.6 us -> 85.1 us  [exchange(): got[k] = lax.ppermute(parts[k - 1], axis, pairs(k))]
    ppermute x2, starting transfers between devices: 4.33 us -> 6.65 us  [body(): from_one = lax.ppermute(one, 'dom', one_pairs)]
    unnamed x25 -> x27, local copies, waits for them, and re-layouts: 5.59 us -> 6.44 us
  transfers between devices with their start and end apart: 43 -> 36, of which waited for: 22 -> 14; matrix products, arithmetic and copies ran while one was open for 0% -> 0% of each run, Pallas kernels for 9% -> 9%
where the time goes in v8:
time: 185 us
  starting transfers between devices  93.3 us (50%)
  waiting for transfers between devices  56.7 us (31%)
  Pallas kernels  26.3 us (14%)
  local copies, waits for them, and re-layouts  6.44 us (3%)
    ppermute x29, starting transfers between devices, exchange(): got[k] = lax.ppermute(parts[k - 1], axis, pairs(k))  85.1 us
    ppermute x29, waiting for transfers between devices, exchange(): got[k] = lax.ppermute(parts[k - 1], axis, pairs(k))  40.5 us
    pallas_call x13, Pallas kernels, call(): pl.pallas_call(kernel, out_shape=list(outs), in_specs=[smem() if s == 's'...  26.3 us
    ppermute x2, waiting for transfers between devices, body(): from_one = lax.ppermute(one, 'dom', one_pairs)  12.9 us
    ppermute x2, starting transfers between devices, body(): from_one = lax.ppermute(one, 'dom', one_pairs)  6.65 us
    unnamed x27, local copies, waits for them, and re-layouts  6.44 us
  transfers between devices with their start and end apart: 36, of which 14 were waited for; matrix products, arithmetic and copies ran while one was open for 0% of the time, Pallas kernels for 9%

profile of v8, /device:TPU:6, one launch (start us, length us, event | category | flops | bytes accessed | tf_op | source)
XLA Modules:
  0.0 184.6 jit_solution(18180949570915888455)
XLA Ops:
  0.6 2.3 %collective-permute-start.8 = (bf16[240,128]{1,0:T(8,128)(2,1)}, bf16[240,128]{1,0:T(8,128)(2,1)S(1)}, u32[]{:S(2)}, u32[]{:S(2)}) collective-permute-start(bf16[240,128]{1,0:T(8,128)(2,1)} %bitcast.32), channel_id=1, source_target_pairs={{0,192},{8,200},{16,208},{24,216},{32,224},{40,232},{48,240},{56,2... | collective-permute-start | bytes 184328 | tf_op jit(solution)/shard_map/ppermute | solution.py:492
  3.6 1.2 collective-permute-start.6
  4.8 1.1 collective-permute-done.2.other
  6.2 3.3 %collective-permute-start.4 = (s32[2]{0:T(128)S(1)}, s32[2]{0:T(128)S(1)}, u32[]{:S(2)}, u32[]{:S(2)}) collective-permute-start(s32[2]{0:T(128)S(1)} %pad_add_fusion.1), channel_id=1, source_target_pairs={{0,32},{8,40},{16,48},{24,56},{32,0},{40,8},{48,16},{56,24},{64,96... | collective-permute-start | bytes 32 | tf_op jit(solution)/shard_map/ppermute | solution.py:492
  9.5 1.9 %collective-permute-start.3 = (s32[2]{0:T(128)S(1)}, s32[2]{0:T(128)S(1)}, u32[]{:S(2)}, u32[]{:S(2)}) collective-permute-start(s32[2]{0:T(128)S(1)} %pad_add_fusion.1), channel_id=1, source_target_pairs={{0,16},{8,24},{16,0},{24,8},{32,48},{40,56},{48,32},{56,40},{64,80... | collective-permute-start | bytes 32 | tf_op jit(solution)/shard_map/ppermute | solution.py:492
  11.4 3.9 %collective-permute-start.5 = (s32[2]{0:T(128)S(1)}, s32[2]{0:T(128)S(1)}, u32[]{:S(2)}, u32[]{:S(2)}) collective-permute-start(s32[2]{0:T(128)S(1)} %pad_add_fusion.1), channel_id=1, source_target_pairs={{0,48},{8,56},{16,32},{24,40},{32,16},{40,24},{48,0},{56,8},{64,11... | collective-permute-start | bytes 32 | tf_op jit(solution)/shard_map/ppermute | solution.py:492
  15.3 1.5 collective-permute-done.5
  17.7 1.2 shard_map.133
  18.9 5.1 %collective-permute-start.9 = (bf16[480,128]{1,0:T(8,128)(2,1)S(1)}, bf16[480,128]{1,0:T(8,128)(2,1)S(1)}, u32[]{:S(2)}, u32[]{:S(2)}) collective-permute-start(bf16[480,128]{1,0:T(8,128)(2,1)S(1)} %get-tuple-element.69), channel_id=1, source_target_pairs={{0,52},{1,53},{2,54},{3,55},{4,48},{5,49},{6,50},{7,51},{8,60},{9,... | collective-permute-start | bytes 368648 | tf_op jit(solution)/shard_map/ppermute | solution.py:492
  24.1 4.6 %collective-permute-start.11 = (bf16[480,128]{1,0:T(8,128)(2,1)S(1)}, bf16[480,128]{1,0:T(8,128)(2,1)S(1)}, u32[]{:S(2)}, u32[]{:S(2)}) collective-permute-start(bf16[480,128]{1,0:T(8,128)(2,1)S(1)} %get-tuple-element.71), channel_id=1, source_target_pairs={{0,20},{1,21},{2,22},{3,23},{4,16},{5,17},{6,18},{7,19},{8,28},{9,... | collective-permute-start | bytes 368648 | tf_op jit(solution)/shard_map/ppermute | solution.py:492
  28.6 1.5 collective-permute-start.12
  30.1 1.9 %collective-permute-start.13 = (bf16[480,128]{1,0:T(8,128)(2,1)S(1)}, bf16[480,128]{1,0:T(8,128)(2,1)S(1)}, u32[]{:S(2)}, u32[]{:S(2)}) collective-permute-start(bf16[480,128]{1,0:T(8,128)(2,1)S(1)} %get-tuple-element.73), channel_id=1, source_target_pairs={{0,48},{1,49},{2,50},{3,51},{4,52},{5,53},{6,54},{7,55},{8,56},{9,... | collective-permute-start | bytes 368648 | tf_op jit(solution)/shard_map/ppermute | solution.py:492
  32.0 5.0 %collective-permute-done.9.refs_1_ = bf16[480,128]{1,0:T(8,128)(2,1)S(1)} collective-permute-done((bf16[480,128]{1,0:T(8,128)(2,1)S(1)}, bf16[480,128]{1,0:T(8,128)(2,1)S(1)}, u32[]{:S(2)}, u32[]{:S(2)}) %collective-permute-start.9) | collective-permute-done | bytes 122912 | tf_op jit(solution)/shard_map/ppermute | solution.py:492
  37.0 2.8 %collective-permute-done.10.refs_2_ = bf16[480,128]{1,0:T(8,128)(2,1)S(1)} collective-permute-done((bf16[480,128]{1,0:T(8,128)(2,1)S(1)}, bf16[480,128]{1,0:T(8,128)(2,1)S(1)}, u32[]{:S(2)}, u32[]{:S(2)}) %collective-permute-start.10) | collective-permute-done | bytes 122912 | tf_op jit(solution)/shard_map/ppermute | solution.py:492
  39.9 3.0 %collective-permute-start.15 = (bf16[480,128]{1,0:T(8,128)(2,1)S(1)}, bf16[480,128]{1,0:T(8,128)(2,1)S(1)}, u32[]{:S(2)}, u32[]{:S(2)}) collective-permute-start(bf16[480,128]{1,0:T(8,128)(2,1)S(1)} %get-tuple-element.75), channel_id=1, source_target_pairs={{0,16},{1,17},{2,18},{3,19},{4,20},{5,21},{6,22},{7,23},{8,24},{9,... | collective-permute-start | bytes 368648 | tf_op jit(solution)/shard_map/ppermute | solution.py:492
  43.5 3.4 %shard_map.130 = (f32[8,256,128]{2,1,0:T(8,128)S(1)}, f32[8,256,128]{2,1,0:T(8,128)S(1)}) custom-call(s32[1]{0:T(128)S(6)} %copy.17.begin, s32[3,512]{1,0:T(4,128)S(1)} %bitcast.36, f32[64,512]{1,0:T(8,128)S(1)} %bitcast.31), custom_call_target="tpu_custom_call" | custom-call | tf_op jit(solution)/shard_map/pallas_call | solution.py:35
  46.9 1.2 copy-done
  48.1 1.2 copy-done.2
  49.3 1.2 copy-done.4
  50.6 1.2 copy-done.6
  51.8 6.0 %shard_map.131 = (f32[8,256,128]{2,1,0:T(8,128)S(1)}, f32[8,256,128]{2,1,0:T(8,128)S(1)}, f32[8,256,128]{2,1,0:T(8,128)S(1)}, f32[8,256,128]{2,1,0:T(8,128)S(1)}) custom-call(f32[8,256,128]{2,1,0:T(8,128)S(1)} %bitcast.21, f32[8,256,128]{2,1,0:T(8,128)S(1)} %bitcast.25, f32[8,256,128]{2,1,0:T(8,128)S(1)} %bitcast.28, f32[8,256,128]{2,1,0:T(8,128)S(1)} %bitcast.30, ...), custom_call_target="tpu_custom_call" | custom-call | tf_op jit(solution)/shard_map/pallas_call | solution.py:35
  59.3 4.5 %collective-permute-start.1 = (s16[2112,128]{1,0:T(8,128)(2,1)S(1)}, s16[2112,128]{1,0:T(8,128)(2,1)S(1)}, u32[]{:S(2)}, u32[]{:S(2)}) collective-permute-start(s16[2112,128]{1,0:T(8,128)(2,1)S(1)} %get-tuple-element.67), channel_id=1, source_target_pairs={{0,1},{1,0},{2,3},{3,2},{4,5},{5,4},{6,7},{7,6},{8,9},{9,8},{10,11... | collective-permute-start | bytes 1622024 | tf_op jit(solution)/shard_map/ppermute | solution.py:551
  63.8 1.0 shard_map.135
  64.8 3.6 %collective-permute-start.17 = (bf16[640,128]{1,0:T(8,128)(2,1)S(1)}, bf16[640,128]{1,0:T(8,128)(2,1)S(1)}, u32[]{:S(2)}, u32[]{:S(2)}) collective-permute-start(bf16[640,128]{1,0:T(8,128)(2,1)S(1)} %get-tuple-element.87), channel_id=1, source_target_pairs={{0,3},{1,2},{2,1},{3,0},{4,7},{5,6},{6,5},{7,4},{8,11},{9,10},{10,... | collective-permute-start | bytes 491528 | tf_op jit(solution)/shard_map/ppermute | solution.py:492
  68.3 1.5 collective-permute-start.18
  69.9 7.0 %collective-permute-done.1.rest_1_ = s16[2112,128]{1,0:T(8,128)(2,1)S(1)} collective-permute-done((s16[2112,128]{1,0:T(8,128)(2,1)S(1)}, s16[2112,128]{1,0:T(8,128)(2,1)S(1)}, u32[]{:S(2)}, u32[]{:S(2)}) %collective-permute-start.1) | collective-permute-done | bytes 540704 | tf_op jit(solution)/shard_map/ppermute | solution.py:551
  76.9 10.4 %collective-permute-done.17.rest_3_ = bf16[640,128]{1,0:T(8,128)(2,1)S(1)} collective-permute-done((bf16[640,128]{1,0:T(8,128)(2,1)S(1)}, bf16[640,128]{1,0:T(8,128)(2,1)S(1)}, u32[]{:S(2)}, u32[]{:S(2)}) %collective-permute-start.17) | collective-permute-done | bytes 163872 | tf_op jit(solution)/shard_map/ppermute | solution.py:492
  87.9 2.0 %shard_map.136 = (f32[8,256,128]{2,1,0:T(8,128)S(1)}, f32[8,256,128]{2,1,0:T(8,128)S(1)}, f32[8,256,128]{2,1,0:T(8,128)S(1)}, s16[2112,128]{1,0:T(8,128)(2,1)S(1)}, s16[2112,128]{1,0:T(8,128)(2,1)S(1)}) custom-call(s32[1,2]{1,0:T(1,128)S(1)} %copy-done.9, s32[1,3]{1,0:T(1,128)S(1)} %copy-done.10, s32[1]{0:T(128)S(6)} %copy.17.begin, f32[64]{0:T(128)S(1)} %copy-done.11, ...), custom_call_target="tpu_custom_call" | custom-call | tf_op jit(solution)/shard_map/pallas_call | solution.py:35
  90.6 2.2 %collective-permute-start.21 = (s16[2112,128]{1,0:T(8,128)(2,1)S(1)}, s16[2112,128]{1,0:T(8,128)(2,1)S(1)}, u32[]{:S(2)}, u32[]{:S(2)}) collective-permute-start(s16[2112,128]{1,0:T(8,128)(2,1)S(1)} %get-tuple-element.98), channel_id=1, source_target_pairs={{0,1},{1,0},{2,3},{3,2},{4,5},{5,4},{6,7},{7,6},{8,9},{9,8},{10,11... | collective-permute-start | bytes 1622024 | tf_op jit(solution)/shard_map/ppermute | solution.py:573
  92.8 5.9 %shard_map.137 = (f32[8,256,128]{2,1,0:T(8,128)S(1)}, f32[8,256,128]{2,1,0:T(8,128)S(1)}, f32[8,256,128]{2,1,0:T(8,128)S(1)}) custom-call(f32[8,256,128]{2,1,0:T(8,128)S(1)} %get-tuple-element.90.p1, f32[8,256,128]{2,1,0:T(8,128)S(1)} %get-tuple-element.91.q1, f32[8,256,128]{2,1,0:T(8,128)S(1)} %bitcast.23, f32[8,256,128]{2,1,0:T(8,128)S(1)} %bitcast.27, ...), custom_call_target="tpu_custom_call" | custom-call | tf_op jit(solution)/shard_map/pallas_call | solution.py:35
  98.7 5.9 %collective-permute-done.21.one = s16[2112,128]{1,0:T(8,128)(2,1)S(1)} collective-permute-done((s16[2112,128]{1,0:T(8,128)(2,1)S(1)}, s16[2112,128]{1,0:T(8,128)(2,1)S(1)}, u32[]{:S(2)}, u32[]{:S(2)}) %collective-permute-start.21) | collective-permute-done | bytes 540704 | tf_op jit(solution)/shard_map/ppermute | solution.py:573
  104.6 3.1 %shard_map.138 = (f32[8,256,128]{2,1,0:T(8,128)}, f32[8,256,128]{2,1,0:T(8,128)}, f32[320,128]{1,0:T(8,128)S(1)}, s16[336,128]{1,0:T(8,128)(2,1)S(1)}, s16[336,1...) custom-call(s32[1,2]{1,0:T(1,128)S(1)} %copy-done.9, ...), custom_call_target="tpu_custom_call" | custom-call | tf_op jit(solution)/shard_map/pallas_call | solution.py:35
  107.7 4.7 %collective-permute-start.22 = (s16[336,128]{1,0:T(8,128)(2,1)S(1)}, s16[336,128]{1,0:T(8,128)(2,1)S(1)}, u32[]{:S(2)}, u32[]{:S(2)}) collective-permute-start(s16[336,128]{1,0:T(8,128)(2,1)S(1)} %get-tuple-element.102), channel_id=1, source_target_pairs={{0,7},{1,6},{2,5},{3,4},{4,3},{5,2},{6,1},{7,0},{8,15},{9,14},{10,... | collective-permute-start | bytes 258056 | tf_op jit(solution)/shard_map/ppermute | solution.py:492
  112.4 3.9 %collective-permute-start.23 = (s16[336,128]{1,0:T(8,128)(2,1)S(1)}, s16[336,128]{1,0:T(8,128)(2,1)S(1)}, u32[]{:S(2)}, u32[]{:S(2)}) collective-permute-start(s16[336,128]{1,0:T(8,128)(2,1)S(1)} %get-tuple-element.103), channel_id=1, source_target_pairs={{0,6},{1,7},{2,4},{3,5},{4,2},{5,3},{6,0},{7,1},{8,14},{9,15},{10,... | collective-permute-start | bytes 258056 | tf_op jit(solution)/shard_map/ppermute | solution.py:492
  116.3 12.1 %collective-permute-start.24 = (s16[336,128]{1,0:T(8,128)(2,1)S(1)}, s16[336,128]{1,0:T(8,128)(2,1)S(1)}, u32[]{:S(2)}, u32[]{:S(2)}) collective-permute-start(s16[336,128]{1,0:T(8,128)(2,1)S(1)} %get-tuple-element.104), channel_id=1, source_target_pairs={{0,5},{1,4},{2,7},{3,6},{4,1},{5,0},{6,3},{7,2},{8,13},{9,12},{10,... | collective-permute-start | bytes 258056 | tf_op jit(solution)/shard_map/ppermute | solution.py:492
  128.4 4.4 %collective-permute-start.26 = (s16[336,128]{1,0:T(8,128)(2,1)S(1)}, s16[336,128]{1,0:T(8,128)(2,1)S(1)}, u32[]{:S(2)}, u32[]{:S(2)}) collective-permute-start(s16[336,128]{1,0:T(8,128)(2,1)S(1)} %get-tuple-element.106), channel_id=1, source_target_pairs={{0,3},{1,2},{2,1},{3,0},{4,7},{5,6},{6,5},{7,4},{8,11},{9,10},{10,... | collective-permute-start | bytes 258056 | tf_op jit(solution)/shard_map/ppermute | solution.py:492
  132.8 0.9 collective-permute-start.28
  133.7 3.1 %collective-permute-done.25.refs_3_ = s16[336,128]{1,0:T(8,128)(2,1)S(1)} collective-permute-done((s16[336,128]{1,0:T(8,128)(2,1)S(1)}, s16[336,128]{1,0:T(8,128)(2,1)S(1)}, u32[]{:S(2)}, u32[]{:S(2)}) %collective-permute-start.25) | collective-permute-done | bytes 86048 | tf_op jit(solution)/shard_map/ppermute | solution.py:492
  136.8 2.0 %collective-permute-done.27.refs_5_ = s16[336,128]{1,0:T(8,128)(2,1)S(1)} collective-permute-done((s16[336,128]{1,0:T(8,128)(2,1)S(1)}, s16[336,128]{1,0:T(8,128)(2,1)S(1)}, u32[]{:S(2)}, u32[]{:S(2)}) %collective-permute-start.27) | collective-permute-done | bytes 86048 | tf_op jit(solution)/shard_map/ppermute | solution.py:492
  138.8 0.9 shard_map.139
  139.8 2.2 %collective-permute-done.29.got = f32[1440,128]{1,0:T(8,128)S(1)} collective-permute-done((f32[1440,128]{1,0:T(8,128)S(1)}, f32[1440,128]{1,0:T(8,128)S(1)}, u32[]{:S(2)}, u32[]{:S(2)}) %collective-permute-start.29) | collective-permute-done | bytes 737312 | tf_op jit(solution)/shard_map/ppermute | solution.py:606
  142.0 1.2 shard_map.140
  143.8 2.4 %collective-permute-start.31 = (s16[992,128]{1,0:T(8,128)(2,1)S(1)}, s16[992,128]{1,0:T(8,128)(2,1)S(1)}, u32[]{:S(2)}, u32[]{:S(2)}) collective-permute-start(s16[992,128]{1,0:T(8,128)(2,1)S(1)} %get-tuple-element.113), channel_id=1, source_target_pairs={{0,128},{8,136},{16,144},{24,152},{32,160},{40,168},{48,176},{56,1... | collective-permute-start | bytes 761864 | tf_op jit(solution)/shard_map/ppermute | solution.py:492
  146.2 1.2 collective-permute-start.32
  147.4 10.7 %collective-permute-done.30.refs_0_ = s16[992,128]{1,0:T(8,128)(2,1)S(1)} collective-permute-done((s16[992,128]{1,0:T(8,128)(2,1)S(1)}, s16[992,128]{1,0:T(8,128)(2,1)S(1)}, u32[]{:S(2)}, u32[]{:S(2)}) %collective-permute-start.30) | collective-permute-done | bytes 253984 | tf_op jit(solution)/shard_map/ppermute | solution.py:492
  159.1 1.9 %collective-permute-start.33 = (s16[256,128]{1,0:T(8,128)(2,1)S(1)}, s16[256,128]{1,0:T(8,128)(2,1)S(1)}, u32[]{:S(2)}, u32[]{:S(2)}) collective-permute-start(s16[256,128]{1,0:T(8,128)(2,1)S(1)} %get-tuple-element.116), channel_id=1, source_target_pairs={{0,48},{8,56},{16,32},{24,40},{32,16},{40,24},{48,0},{56,8},{64,11... | collective-permute-start | bytes 196616 | tf_op jit(solution)/shard_map/ppermute | solution.py:492
  161.0 18.6 %collective-permute-start.34 = (s16[256,128]{1,0:T(8,128)(2,1)S(1)}, s16[256,128]{1,0:T(8,128)(2,1)S(1)}, u32[]{:S(2)}, u32[]{:S(2)}) collective-permute-start(s16[256,128]{1,0:T(8,128)(2,1)S(1)} %get-tuple-element.117), channel_id=1, source_target_pairs={{0,32},{8,40},{16,48},{24,56},{32,0},{40,8},{48,16},{56,24},{64,96... | collective-permute-start | bytes 196616 | tf_op jit(solution)/shard_map/ppermute | solution.py:492
  179.6 3.5 %collective-permute-done.34.refs_1_ = s16[256,128]{1,0:T(8,128)(2,1)S(1)} collective-permute-done((s16[256,128]{1,0:T(8,128)(2,1)S(1)}, s16[256,128]{1,0:T(8,128)(2,1)S(1)}, u32[]{:S(2)}, u32[]{:S(2)}) %collective-permute-start.34) | collective-permute-done | bytes 65568 | tf_op jit(solution)/shard_map/ppermute | solution.py:492
  (67 shorter events, 7.7 us)
Async XLA Ops:
  0.6 4.2 %copy-start.9 = (s32[1,2]{1,0:T(1,128)S(1)}, s32[1,2]{1,0:T(1,128)}, u32[]{:S(2)}) copy-start(s32[1,2]{1,0:T(1,128)} %anchors.9) | copy-start | bytes 28
  0.6 16.2 %collective-permute-start.8 = (bf16[240,128]{1,0:T(8,128)(2,1)}, bf16[240,128]{1,0:T(8,128)(2,1)S(1)}, u32[]{:S(2)}, u32[]{:S(2)}) collective-permute-start(bf16[240,128]{1,0:T(8,128)(2,1)} %bitcast.32), channel_id=1, source_target_pairs={{0,192},{8,200},{16,208},{24,216},{32,224},{40,232},{48,240},{56,2... | collective-permute-start | bytes 184328 | tf_op jit(solution)/shard_map/ppermute | solution.py:492
  2.9 13.9 %collective-permute-start.7 = (bf16[240,128]{1,0:T(8,128)(2,1)}, bf16[240,128]{1,0:T(8,128)(2,1)S(1)}, u32[]{:S(2)}, u32[]{:S(2)}) collective-permute-start(bf16[240,128]{1,0:T(8,128)(2,1)} %bitcast.33), channel_id=1, source_target_pairs={{0,128},{8,136},{16,144},{24,152},{32,160},{40,168},{48,176},{56,1... | collective-permute-start | bytes 184328 | tf_op jit(solution)/shard_map/ppermute | solution.py:492
  3.6 13.2 %collective-permute-start.6 = (bf16[240,128]{1,0:T(8,128)(2,1)}, bf16[240,128]{1,0:T(8,128)(2,1)S(1)}, u32[]{:S(2)}, u32[]{:S(2)}) collective-permute-start(bf16[240,128]{1,0:T(8,128)(2,1)} %bitcast.34), channel_id=1, source_target_pairs={{0,64},{8,72},{16,80},{24,88},{32,96},{40,104},{48,112},{56,120},{... | collective-permute-start | bytes 184328 | tf_op jit(solution)/shard_map/ppermute | solution.py:492
  4.8 1.1 collective-permute-start.2
  6.2 5.2 %collective-permute-start.4 = (s32[2]{0:T(128)S(1)}, s32[2]{0:T(128)S(1)}, u32[]{:S(2)}, u32[]{:S(2)}) collective-permute-start(s32[2]{0:T(128)S(1)} %pad_add_fusion.1), channel_id=1, source_target_pairs={{0,32},{8,40},{16,48},{24,56},{32,0},{40,8},{48,16},{56,24},{64,96... | collective-permute-start | bytes 32 | tf_op jit(solution)/shard_map/ppermute | solution.py:492
  9.5 5.8 %collective-permute-start.3 = (s32[2]{0:T(128)S(1)}, s32[2]{0:T(128)S(1)}, u32[]{:S(2)}, u32[]{:S(2)}) collective-permute-start(s32[2]{0:T(128)S(1)} %pad_add_fusion.1), channel_id=1, source_target_pairs={{0,16},{8,24},{16,0},{24,8},{32,48},{40,56},{48,32},{56,40},{64,80... | collective-permute-start | bytes 32 | tf_op jit(solution)/shard_map/ppermute | solution.py:492
  11.4 5.4 %collective-permute-start.5 = (s32[2]{0:T(128)S(1)}, s32[2]{0:T(128)S(1)}, u32[]{:S(2)}, u32[]{:S(2)}) collective-permute-start(s32[2]{0:T(128)S(1)} %pad_add_fusion.1), channel_id=1, source_target_pairs={{0,48},{8,56},{16,32},{24,40},{32,16},{40,24},{48,0},{56,8},{64,11... | collective-permute-start | bytes 32 | tf_op jit(solution)/shard_map/ppermute | solution.py:492
  16.8 26.7 %copy-start.7 = (f32[1,64,512]{2,1,0:T(8,128)S(1)}, f32[1,64,512]{2,1,0:T(8,128)}, u32[]{:S(2)}) copy-start(f32[1,64,512]{2,1,0:T(8,128)} %param.16) | copy-start | bytes 393220
  16.8 0.9 copy-start.8
  18.9 18.1 %collective-permute-start.9 = (bf16[480,128]{1,0:T(8,128)(2,1)S(1)}, bf16[480,128]{1,0:T(8,128)(2,1)S(1)}, u32[]{:S(2)}, u32[]{:S(2)}) collective-permute-start(bf16[480,128]{1,0:T(8,128)(2,1)S(1)} %get-tuple-element.69), channel_id=1, source_target_pairs={{0,52},{1,53},{2,54},{3,55},{4,48},{5,49},{6,50},{7,51},{8,60},{9,... | collective-permute-start | bytes 368648 | tf_op jit(solution)/shard_map/ppermute | solution.py:492
  24.1 19.4 %copy-start.12 = (s32[1,3,512]{2,0,1:T(1,128)S(1)}, s32[1,3,512]{2,0,1:T(1,128)}, u32[]{:S(2)}) copy-start(s32[1,3,512]{2,0,1:T(1,128)} %param.15) | copy-start | bytes 18436
  24.1 15.8 %collective-permute-start.10 = (bf16[480,128]{1,0:T(8,128)(2,1)S(1)}, bf16[480,128]{1,0:T(8,128)(2,1)S(1)}, u32[]{:S(2)}, u32[]{:S(2)}) collective-permute-start(bf16[480,128]{1,0:T(8,128)(2,1)S(1)} %get-tuple-element.70), channel_id=1, source_target_pairs={{0,36},{1,37},{2,38},{3,39},{4,32},{5,33},{6,34},{7,35},{8,44},{9,... | collective-permute-start | bytes 368648 | tf_op jit(solution)/shard_map/ppermute | solution.py:492
  24.1 33.8 %collective-permute-start.11 = (bf16[480,128]{1,0:T(8,128)(2,1)S(1)}, bf16[480,128]{1,0:T(8,128)(2,1)S(1)}, u32[]{:S(2)}, u32[]{:S(2)}) collective-permute-start(bf16[480,128]{1,0:T(8,128)(2,1)S(1)} %get-tuple-element.71), channel_id=1, source_target_pairs={{0,20},{1,21},{2,22},{3,23},{4,16},{5,17},{6,18},{7,19},{8,28},{9,... | collective-permute-start | bytes 368648 | tf_op jit(solution)/shard_map/ppermute | solution.py:492
  28.6 29.2 %collective-permute-start.12 = (bf16[480,128]{1,0:T(8,128)(2,1)S(1)}, bf16[480,128]{1,0:T(8,128)(2,1)S(1)}, u32[]{:S(2)}, u32[]{:S(2)}) collective-permute-start(bf16[480,128]{1,0:T(8,128)(2,1)S(1)} %get-tuple-element.72), channel_id=1, source_target_pairs={{0,4},{1,5},{2,6},{3,7},{4,0},{5,1},{6,2},{7,3},{8,12},{9,13},{10,... | collective-permute-start | bytes 368648 | tf_op jit(solution)/shard_map/ppermute | solution.py:492
  30.1 27.7 %collective-permute-start.13 = (bf16[480,128]{1,0:T(8,128)(2,1)S(1)}, bf16[480,128]{1,0:T(8,128)(2,1)S(1)}, u32[]{:S(2)}, u32[]{:S(2)}) collective-permute-start(bf16[480,128]{1,0:T(8,128)(2,1)S(1)} %get-tuple-element.73), channel_id=1, source_target_pairs={{0,48},{1,49},{2,50},{3,51},{4,52},{5,53},{6,54},{7,55},{8,56},{9,... | collective-permute-start | bytes 368648 | tf_op jit(solution)/shard_map/ppermute | solution.py:492
  37.0 20.8 %collective-permute-start.14 = (bf16[480,128]{1,0:T(8,128)(2,1)S(1)}, bf16[480,128]{1,0:T(8,128)(2,1)S(1)}, u32[]{:S(2)}, u32[]{:S(2)}) collective-permute-start(bf16[480,128]{1,0:T(8,128)(2,1)S(1)} %get-tuple-element.74), channel_id=1, source_target_pairs={{0,32},{1,33},{2,34},{3,35},{4,36},{5,37},{6,38},{7,39},{8,40},{9,... | collective-permute-start | bytes 368648 | tf_op jit(solution)/shard_map/ppermute | solution.py:492
  39.9 18.0 %collective-permute-start.15 = (bf16[480,128]{1,0:T(8,128)(2,1)S(1)}, bf16[480,128]{1,0:T(8,128)(2,1)S(1)}, u32[]{:S(2)}, u32[]{:S(2)}) collective-permute-start(bf16[480,128]{1,0:T(8,128)(2,1)S(1)} %get-tuple-element.75), channel_id=1, source_target_pairs={{0,16},{1,17},{2,18},{3,19},{4,20},{5,21},{6,22},{7,23},{8,24},{9,... | collective-permute-start | bytes 368648 | tf_op jit(solution)/shard_map/ppermute | solution.py:492
  46.9 1.2 copy-start
  48.1 1.2 copy-start.2
  49.3 1.2 copy-start.4
  50.6 1.2 copy-start.6
  51.8 6.3 %copy-start.1 = (f32[1,8,256,128]{3,2,1,0:T(8,128)S(1)}, f32[1,8,256,128]{3,2,1,0:T(8,128)}, u32[]{:S(2)}) copy-start(f32[1,8,256,128]{3,2,1,0:T(8,128)} %param.19) | copy-start | bytes 3145732
  51.8 6.3 %copy-start.3 = (f32[1,8,256,128]{3,2,1,0:T(8,128)S(1)}, f32[1,8,256,128]{3,2,1,0:T(8,128)}, u32[]{:S(2)}) copy-start(f32[1,8,256,128]{3,2,1,0:T(8,128)} %param.21) | copy-start | bytes 3145732
  57.9 5.8 %collective-permute-start.16 = (bf16[1920,128]{1,0:T(8,128)(2,1)S(1)}, bf16[1920,128]{1,0:T(8,128)(2,1)S(1)}, u32[]{:S(2)}, u32[]{:S(2)}) collective-permute-start(bf16[1920,128]{1,0:T(8,128)(2,1)S(1)} %get-tuple-element.85), channel_id=1, source_target_pairs={{0,8},{8,0},{16,24},{24,16},{32,40},{40,32},{48,56},{56,48},{64,72... | collective-permute-start | bytes 1474568 | tf_op jit(solution)/shard_map/ppermute | solution.py:553
  58.6 11.2 %collective-permute-start = (s16[2112,128]{1,0:T(8,128)(2,1)S(1)}, s16[2112,128]{1,0:T(8,128)(2,1)S(1)}, u32[]{:S(2)}, u32[]{:S(2)}) collective-permute-start(s16[2112,128]{1,0:T(8,128)(2,1)S(1)} %get-tuple-element.66), channel_id=1, source_target_pairs={{1,2},{3,4},{5,6},{2,1},{4,3},{6,5},{9,10},{11,12},{13,14},{10,9},... | collective-permute-start | bytes 1622024 | tf_op jit(solution)/shard_map/ppermute | solution.py:552
  59.3 17.5 %collective-permute-start.1 = (s16[2112,128]{1,0:T(8,128)(2,1)S(1)}, s16[2112,128]{1,0:T(8,128)(2,1)S(1)}, u32[]{:S(2)}, u32[]{:S(2)}) collective-permute-start(s16[2112,128]{1,0:T(8,128)(2,1)S(1)} %get-tuple-element.67), channel_id=1, source_target_pairs={{0,1},{1,0},{2,3},{3,2},{4,5},{5,4},{6,7},{7,6},{8,9},{9,8},{10,11... | collective-permute-start | bytes 1622024 | tf_op jit(solution)/shard_map/ppermute | solution.py:551
  64.8 22.5 %collective-permute-start.17 = (bf16[640,128]{1,0:T(8,128)(2,1)S(1)}, bf16[640,128]{1,0:T(8,128)(2,1)S(1)}, u32[]{:S(2)}, u32[]{:S(2)}) collective-permute-start(bf16[640,128]{1,0:T(8,128)(2,1)S(1)} %get-tuple-element.87), channel_id=1, source_target_pairs={{0,3},{1,2},{2,1},{3,0},{4,7},{5,6},{6,5},{7,4},{8,11},{9,10},{10,... | collective-permute-start | bytes 491528 | tf_op jit(solution)/shard_map/ppermute | solution.py:492
  68.3 18.9 %collective-permute-start.18 = (bf16[640,128]{1,0:T(8,128)(2,1)S(1)}, bf16[640,128]{1,0:T(8,128)(2,1)S(1)}, u32[]{:S(2)}, u32[]{:S(2)}) collective-permute-start(bf16[640,128]{1,0:T(8,128)(2,1)S(1)} %get-tuple-element.88), channel_id=1, source_target_pairs={{0,2},{1,3},{2,0},{3,1},{4,6},{5,7},{6,4},{7,5},{8,10},{9,11},{10,... | collective-permute-start | bytes 491528 | tf_op jit(solution)/shard_map/ppermute | solution.py:492
  69.9 17.4 %collective-permute-start.19 = (bf16[640,128]{1,0:T(8,128)(2,1)S(1)}, bf16[640,128]{1,0:T(8,128)(2,1)S(1)}, u32[]{:S(2)}, u32[]{:S(2)}) collective-permute-start(bf16[640,128]{1,0:T(8,128)(2,1)S(1)} %get-tuple-element.89), channel_id=1, source_target_pairs={{0,1},{1,0},{2,3},{3,2},{4,5},{5,4},{6,7},{7,6},{8,9},{9,8},{10,11... | collective-permute-start | bytes 491528 | tf_op jit(solution)/shard_map/ppermute | solution.py:492
  87.2 0.7 copy-start.11
  87.9 4.9 %copy-start.5 = (f32[1,8,256,128]{3,2,1,0:T(8,128)S(1)}, f32[1,8,256,128]{3,2,1,0:T(8,128)}, u32[]{:S(2)}) copy-start(f32[1,8,256,128]{3,2,1,0:T(8,128)} %param.18) | copy-start | bytes 3145732
  89.9 8.8 %collective-permute-start.20 = (s16[2112,128]{1,0:T(8,128)(2,1)S(1)}, s16[2112,128]{1,0:T(8,128)(2,1)S(1)}, u32[]{:S(2)}, u32[]{:S(2)}) collective-permute-start(s16[2112,128]{1,0:T(8,128)(2,1)S(1)} %get-tuple-element.97), channel_id=1, source_target_pairs={{1,2},{3,4},{5,6},{2,1},{4,3},{6,5},{9,10},{11,12},{13,14},{10,9},... | collective-permute-start | bytes 1622024 | tf_op jit(solution)/shard_map/ppermute | solution.py:574
  90.6 14.0 %collective-permute-start.21 = (s16[2112,128]{1,0:T(8,128)(2,1)S(1)}, s16[2112,128]{1,0:T(8,128)(2,1)S(1)}, u32[]{:S(2)}, u32[]{:S(2)}) collective-permute-start(s16[2112,128]{1,0:T(8,128)(2,1)S(1)} %get-tuple-element.98), channel_id=1, source_target_pairs={{0,1},{1,0},{2,3},{3,2},{4,5},{5,4},{6,7},{7,6},{8,9},{9,8},{10,11... | collective-permute-start | bytes 1622024 | tf_op jit(solution)/shard_map/ppermute | solution.py:573
  107.7 25.1 %collective-permute-start.22 = (s16[336,128]{1,0:T(8,128)(2,1)S(1)}, s16[336,128]{1,0:T(8,128)(2,1)S(1)}, u32[]{:S(2)}, u32[]{:S(2)}) collective-permute-start(s16[336,128]{1,0:T(8,128)(2,1)S(1)} %get-tuple-element.102), channel_id=1, source_target_pairs={{0,7},{1,6},{2,5},{3,4},{4,3},{5,2},{6,1},{7,0},{8,15},{9,14},{10,... | collective-permute-start | bytes 258056 | tf_op jit(solution)/shard_map/ppermute | solution.py:492
  112.4 20.4 %collective-permute-start.23 = (s16[336,128]{1,0:T(8,128)(2,1)S(1)}, s16[336,128]{1,0:T(8,128)(2,1)S(1)}, u32[]{:S(2)}, u32[]{:S(2)}) collective-permute-start(s16[336,128]{1,0:T(8,128)(2,1)S(1)} %get-tuple-element.103), channel_id=1, source_target_pairs={{0,6},{1,7},{2,4},{3,5},{4,2},{5,3},{6,0},{7,1},{8,14},{9,15},{10,... | collective-permute-start | bytes 258056 | tf_op jit(solution)/shard_map/ppermute | solution.py:492
  116.3 17.4 %collective-permute-start.24 = (s16[336,128]{1,0:T(8,128)(2,1)S(1)}, s16[336,128]{1,0:T(8,128)(2,1)S(1)}, u32[]{:S(2)}, u32[]{:S(2)}) collective-permute-start(s16[336,128]{1,0:T(8,128)(2,1)S(1)} %get-tuple-element.104), channel_id=1, source_target_pairs={{0,5},{1,4},{2,7},{3,6},{4,1},{5,0},{6,3},{7,2},{8,13},{9,12},{10,... | collective-permute-start | bytes 258056 | tf_op jit(solution)/shard_map/ppermute | solution.py:492
  128.4 8.4 %collective-permute-start.25 = (s16[336,128]{1,0:T(8,128)(2,1)S(1)}, s16[336,128]{1,0:T(8,128)(2,1)S(1)}, u32[]{:S(2)}, u32[]{:S(2)}) collective-permute-start(s16[336,128]{1,0:T(8,128)(2,1)S(1)} %get-tuple-element.105), channel_id=1, source_target_pairs={{0,4},{1,5},{2,6},{3,7},{4,0},{5,1},{6,2},{7,3},{8,12},{9,13},{10,... | collective-permute-start | bytes 258056 | tf_op jit(solution)/shard_map/ppermute | solution.py:492
  128.4 8.4 %collective-permute-start.26 = (s16[336,128]{1,0:T(8,128)(2,1)S(1)}, s16[336,128]{1,0:T(8,128)(2,1)S(1)}, u32[]{:S(2)}, u32[]{:S(2)}) collective-permute-start(s16[336,128]{1,0:T(8,128)(2,1)S(1)} %get-tuple-element.106), channel_id=1, source_target_pairs={{0,3},{1,2},{2,1},{3,0},{4,7},{5,6},{6,5},{7,4},{8,11},{9,10},{10,... | collective-permute-start | bytes 258056 | tf_op jit(solution)/shard_map/ppermute | solution.py:492
  132.8 6.0 %collective-permute-start.27 = (s16[336,128]{1,0:T(8,128)(2,1)S(1)}, s16[336,128]{1,0:T(8,128)(2,1)S(1)}, u32[]{:S(2)}, u32[]{:S(2)}) collective-permute-start(s16[336,128]{1,0:T(8,128)(2,1)S(1)} %get-tuple-element.107), channel_id=1, source_target_pairs={{0,2},{1,3},{2,0},{3,1},{4,6},{5,7},{6,4},{7,5},{8,10},{9,11},{10,... | collective-permute-start | bytes 258056 | tf_op jit(solution)/shard_map/ppermute | solution.py:492
  132.8 6.0 %collective-permute-start.28 = (s16[336,128]{1,0:T(8,128)(2,1)S(1)}, s16[336,128]{1,0:T(8,128)(2,1)S(1)}, u32[]{:S(2)}, u32[]{:S(2)}) collective-permute-start(s16[336,128]{1,0:T(8,128)(2,1)S(1)} %get-tuple-element.108), channel_id=1, source_target_pairs={{0,1},{1,0},{2,3},{3,2},{4,5},{5,4},{6,7},{7,6},{8,9},{9,8},{10,11... | collective-permute-start | bytes 258056 | tf_op jit(solution)/shard_map/ppermute | solution.py:492
  139.7 2.3 %collective-permute-start.29 = (f32[1440,128]{1,0:T(8,128)S(1)}, f32[1440,128]{1,0:T(8,128)S(1)}, u32[]{:S(2)}, u32[]{:S(2)}) collective-permute-start(f32[1440,128]{1,0:T(8,128)S(1)} %get-tuple-element.110), channel_id=1, source_target_pairs={{0,8},{8,0},{16,24},{24,16},{32,40},{40,32},{48,56},{56,48},{64,72... | collective-permute-start | bytes 2211848 | tf_op jit(solution)/shard_map/ppermute | solution.py:606
  143.2 14.9 %collective-permute-start.30 = (s16[992,128]{1,0:T(8,128)(2,1)S(1)}, s16[992,128]{1,0:T(8,128)(2,1)S(1)}, u32[]{:S(2)}, u32[]{:S(2)}) collective-permute-start(s16[992,128]{1,0:T(8,128)(2,1)S(1)} %get-tuple-element.112), channel_id=1, source_target_pairs={{0,192},{8,200},{16,208},{24,216},{32,224},{40,232},{48,240},{56,2... | collective-permute-start | bytes 761864 | tf_op jit(solution)/shard_map/ppermute | solution.py:492
  143.8 14.4 %collective-permute-start.31 = (s16[992,128]{1,0:T(8,128)(2,1)S(1)}, s16[992,128]{1,0:T(8,128)(2,1)S(1)}, u32[]{:S(2)}, u32[]{:S(2)}) collective-permute-start(s16[992,128]{1,0:T(8,128)(2,1)S(1)} %get-tuple-element.113), channel_id=1, source_target_pairs={{0,128},{8,136},{16,144},{24,152},{32,160},{40,168},{48,176},{56,1... | collective-permute-start | bytes 761864 | tf_op jit(solution)/shard_map/ppermute | solution.py:492
  146.2 12.6 %collective-permute-start.32 = (s16[992,128]{1,0:T(8,128)(2,1)S(1)}, s16[992,128]{1,0:T(8,128)(2,1)S(1)}, u32[]{:S(2)}, u32[]{:S(2)}) collective-permute-start(s16[992,128]{1,0:T(8,128)(2,1)S(1)} %get-tuple-element.114), channel_id=1, source_target_pairs={{0,64},{8,72},{16,80},{24,88},{32,96},{40,104},{48,112},{56,120},{... | collective-permute-start | bytes 761864 | tf_op jit(solution)/shard_map/ppermute | solution.py:492
  159.1 20.5 %collective-permute-start.33 = (s16[256,128]{1,0:T(8,128)(2,1)S(1)}, s16[256,128]{1,0:T(8,128)(2,1)S(1)}, u32[]{:S(2)}, u32[]{:S(2)}) collective-permute-start(s16[256,128]{1,0:T(8,128)(2,1)S(1)} %get-tuple-element.116), channel_id=1, source_target_pairs={{0,48},{8,56},{16,32},{24,40},{32,16},{40,24},{48,0},{56,8},{64,11... | collective-permute-start | bytes 196616 | tf_op jit(solution)/shard_map/ppermute | solution.py:492
  161.0 22.1 %collective-permute-start.34 = (s16[256,128]{1,0:T(8,128)(2,1)S(1)}, s16[256,128]{1,0:T(8,128)(2,1)S(1)}, u32[]{:S(2)}, u32[]{:S(2)}) collective-permute-start(s16[256,128]{1,0:T(8,128)(2,1)S(1)} %get-tuple-element.117), channel_id=1, source_target_pairs={{0,32},{8,40},{16,48},{24,56},{32,0},{40,8},{48,16},{56,24},{64,96... | collective-permute-start | bytes 196616 | tf_op jit(solution)/shard_map/ppermute | solution.py:492
  179.6 4.3 %collective-permute-start.35 = (s16[256,128]{1,0:T(8,128)(2,1)S(1)}, s16[256,128]{1,0:T(8,128)(2,1)S(1)}, u32[]{:S(2)}, u32[]{:S(2)}) collective-permute-start(s16[256,128]{1,0:T(8,128)(2,1)S(1)} %get-tuple-element.118), channel_id=1, source_target_pairs={{0,16},{8,24},{16,0},{24,8},{32,48},{40,56},{48,32},{56,40},{64,80... | collective-permute-start | bytes 196616 | tf_op jit(solution)/shard_map/ppermute | solution.py:492
  (1 other events, 0.7 us)

commit v9 on v3

--- a/solution.py
+++ b/solution.py
@@ -106,6 +106,11 @@
     return lax.rem(lax.axis_index("dom"), 2)
 
 
+def at_border():
+    me, middle = lax.axis_index("dom"), lax.axis_size("dom") // HALVES
+    return (me == middle) | (me == middle - 1)
+
+
 def code_edges(fields, out_refs, level_ref):
     row_count, count_y, _ = fields[0].shape
     per = HALO * count_y // GROUP
@@ -204,8 +209,8 @@
 
 
 def first_kernel(halves, anchors, source, begin, wave, sum_f, sum_a, base_f, base_a, *rest):
-    next_f, next_a, courant, one, two, slab, level = rest[-7:]
-    pieces = rest[:-7]
+    next_f, next_a, courant, one, two, *parts, slab, level = rest[-7 - len(ROUTES) :]
+    pieces = rest[: -7 - len(ROUTES)]
     row_count, count_y, _ = sum_f.shape
     band = pieces[0].shape[0] // (row_count * halves)
     side = len(pieces)
@@ -230,6 +235,12 @@
     add_source(source, begin, wave, next_f, 0)
     code_edges((next_f, next_a), (one, two), level)
 
+    @pl.when(at_border())
+    def _():
+        for n, part in enumerate(parts):
+            size = part.shape[0]
+            part[...] = two[n * size : (n + 1) * size, :]
+
 
 def between_kernel(p1, q1, p0, q0, prev_f, courant, hit, part_f, part_a, bend, pad):
     row_count, count_y, count_z = p1.shape
@@ -264,21 +275,33 @@
     return [sum(COEFFS[r + j] * rows[j] for j in range(HALO - r)) for r in range(HALO)]
 
 
-def second_kernel(groups, anchors, source, begin, wave, p1, q1, p0, courant, part_f, part_a, bend, one, two, *rest):
+def second_kernel(groups, anchors, source, begin, wave, p1, q1, p0, courant, part_f, part_a, bend, *rest):
+    parts, (one, two), rest = rest[: len(ROUTES)], rest[len(ROUTES) :][:2], rest[len(ROUTES) + 2 :]
     next_f, next_a, own = rest[:3]
     sends = rest[3 : 2 + groups]
-    frame, scale_one, scale_two = rest[2 + groups :]
+    frame, held, scale_one, scale_two = rest[2 + groups :]
+
+    @pl.when(jnp.logical_not(at_border()))
+    def _():
+        held[...] = two[...]
+
+    @pl.when(at_border())
+    def _():
+        for n, part in enumerate(parts):
+            size = part.shape[0]
+            held[n * size : (n + 1) * size, :] = part[...]
+
     row_count, count_y, count_z = p1.shape
     band = own.shape[0] // row_count
     load_scales(one, scale_one)
-    load_scales(two, scale_two)
+    load_scales(held, scale_two)
     odd = odd_place()
     edge = (frame.shape[1] - count_y) // 2
     frame[:, 0:edge, :] = jnp.zeros((row_count, edge, count_z), F32)
     frame[:, edge + count_y :, :] = jnp.zeros((row_count, edge, count_z), F32)
     for y in range(0, count_y, GROUP):
         spot = pl.ds(y, GROUP)
-        for ref, scale, low in ((one, scale_one, odd), (two, scale_two, 1 - odd)):
+        for ref, scale, low in ((one, scale_one, odd), (held, scale_two, 1 - odd)):
             for f in range(2):
                 for r, term in enumerate(halo_terms(ref, scale, f, y, count_y, low)):
                     x = row_count - 1 - r + low * (2 * r + 1 - row_count)
@@ -340,6 +363,7 @@
 
 
 SIZE_X, SIZE_Z, SIZE_C = 4, 4, 2
+ROUTES = (0, 1, 3)
 HALVES = 2
 
 
@@ -552,15 +576,23 @@
         "v" * 7,
         (padded, scale, scale),
     )
-    p1, q1, courant, one, two = call(
+    part = struct((half // len(ROUTES), count_z), I16)
+    p1, q1, courant, one, two, *parts = call(
         functools.partial(first_kernel, HALVES),
-        (field, field, field, code, code),
+        (field, field, field, code, code, *[part] * len(ROUTES)),
         (*scalars, *sums, *pieces),
         "ssss" + "v" * (4 + side),
         (slab, levels),
     )
+    border = (side - 1, side)
+    moved = [lax.ppermute(part, "dom", [(a, a ^ k) for a in border]) for part, k in zip(parts[1:], ROUTES[1:])]
+    one, two, moved = lax.optimization_barrier((one, two, moved))
+    parts = [
+        lax.ppermute(part, "dom", [(a ^ k, b) for a, b in (border, border[::-1])])
+        for part, k in zip((parts[0], *moved), ROUTES)
+    ]
     from_one = lax.ppermute(one, "dom", one_pairs)
-    from_two = lax.ppermute(two, "dom", two_pairs)
+    from_two = lax.ppermute(two, "dom", [(a, b) for a, b in two_pairs if a not in border])
     part_f, part_a, bend = call(
         between_kernel,
         (field,) * 3,
@@ -575,9 +607,9 @@
     p2, q2, own, *sends = call(
         functools.partial(second_kernel, groups),
         (field, field, struct((piece, count_z), F32), *[coded] * (groups - 1)),
-        (*scalars, p1, q1, p0, courant, part_f, part_a, bend, from_one, from_two),
-        "ssss" + "v" * 9,
-        (frame, scale, scale),
+        (*scalars, p1, q1, p0, courant, part_f, part_a, bend, *parts, from_one, from_two),
+        "ssss" + "v" * (9 + len(ROUTES)),
+        (frame, pltpu.VMEM(code.shape, I16), scale, scale),
     )
     got = exchange(sends, "dom", between)[::-1]
 

time: 160 us -> 158 us (0.988)
  starting transfers between devices: 78.4 us -> 75.5 us
    ppermute x26, starting transfers between devices: 72.8 us -> 58.2 us  [exchange(): got[k] = lax.ppermute(parts[k - 1], axis, pairs(k))]
    ppermute x0 -> x6, starting transfers between devices: none -> 13.3 us  [the longest x3 10.7 us: body(): lax.ppermute(part, 'dom', [(a ^ k, b) for a, b in (border, border[::-1])])]
    ppermute x0 -> x6, waiting for transfers between devices: none -> 7.58 us  [the longest x2 7.57 us: body(): lax.ppermute(part, 'dom', [(a, a ^ k) for a in border])]
    ppermute x2, waiting for transfers between devices: 6.01 us -> 0.01 us  [body(): from_one = lax.ppermute(one, 'dom', one_pairs)]
  transfers between devices with their start and end apart: 36 -> 41, of which waited for: 20 -> 19; matrix products, arithmetic and copies ran while one was open for 0% -> 0% of each run, Pallas kernels for 10% -> 10%
where the time goes in v9:
time: 158 us; the launch traced here: 157 us
  starting transfers between devices  75.5 us (48%)
  waiting for transfers between devices  52.3 us (33%)
  Pallas kernels  24.9 us (16%)
  local copies, waits for them, and re-layouts  3.16 us (2%)
    ppermute x26, starting transfers between devices, exchange(): got[k] = lax.ppermute(parts[k - 1], axis, pairs(k))  58.2 us
    ppermute x26, waiting for transfers between devices, exchange(): got[k] = lax.ppermute(parts[k - 1], axis, pairs(k))  39.5 us
    pallas_call x12, Pallas kernels, call(): pl.pallas_call(kernel, out_shape=list(outs), in_specs=[smem() if s == 's'...  24.9 us
    ppermute x3, starting transfers between devices, body(): lax.ppermute(part, 'dom', [(a ^ k, b) for a, b in (border, border[::-1])])  10.7 us
    ppermute x2, waiting for transfers between devices, body(): lax.ppermute(part, 'dom', [(a, a ^ k) for a in border])  7.57 us
  transfers between devices with their start and end apart: 41, of which 19 were waited for; matrix products, arithmetic and copies ran while one was open for 0% of the time, Pallas kernels for 10%

profile of v9, /device:TPU:6, one launch (start us, length us, event | category | flops | bytes accessed | tf_op | source)
XLA Modules:
  0.0 157.4 jit_solution(7424404666502752785)
XLA Ops:
  0.6 5.9 %collective-permute-start.6 = (bf16[240,128]{1,0:T(8,128)(2,1)}, bf16[240,128]{1,0:T(8,128)(2,1)S(1)}, u32[]{:S(2)}, u32[]{:S(2)}) collective-permute-start(bf16[240,128]{1,0:T(8,128)(2,1)} %bitcast.23), channel_id=1, source_target_pairs={{0,52},{1,53},{2,54},{3,55},{4,48},{5,49},{6,50},{7,51},{8,60},{9,... | collective-permute-start | bytes 184328 | tf_op jit(solution)/shard_map/ppermute | solution.py:501
  7.1 4.0 %collective-permute-start.4 = (bf16[240,128]{1,0:T(8,128)(2,1)}, bf16[240,128]{1,0:T(8,128)(2,1)S(1)}, u32[]{:S(2)}, u32[]{:S(2)}) collective-permute-start(bf16[240,128]{1,0:T(8,128)(2,1)} %bitcast.25), channel_id=1, source_target_pairs={{0,20},{1,21},{2,22},{3,23},{4,16},{5,17},{6,18},{7,19},{8,28},{9,... | collective-permute-start | bytes 184328 | tf_op jit(solution)/shard_map/ppermute | solution.py:501
  11.1 1.8 %collective-permute-start.3 = (bf16[240,128]{1,0:T(8,128)(2,1)}, bf16[240,128]{1,0:T(8,128)(2,1)S(1)}, u32[]{:S(2)}, u32[]{:S(2)}) collective-permute-start(bf16[240,128]{1,0:T(8,128)(2,1)} %bitcast.26), channel_id=1, source_target_pairs={{0,4},{1,5},{2,6},{3,7},{4,0},{5,1},{6,2},{7,3},{8,12},{9,13},{10,... | collective-permute-start | bytes 184328 | tf_op jit(solution)/shard_map/ppermute | solution.py:501
  13.0 1.9 %collective-permute-start.2 = (bf16[240,128]{1,0:T(8,128)(2,1)}, bf16[240,128]{1,0:T(8,128)(2,1)S(1)}, u32[]{:S(2)}, u32[]{:S(2)}) collective-permute-start(bf16[240,128]{1,0:T(8,128)(2,1)} %bitcast.27), channel_id=1, source_target_pairs={{0,48},{1,49},{2,50},{3,51},{4,52},{5,53},{6,54},{7,55},{8,56},{9,... | collective-permute-start | bytes 184328 | tf_op jit(solution)/shard_map/ppermute | solution.py:501
  15.1 2.3 %collective-permute-start = (bf16[240,128]{1,0:T(8,128)(2,1)}, bf16[240,128]{1,0:T(8,128)(2,1)S(1)}, u32[]{:S(2)}, u32[]{:S(2)}) collective-permute-start(bf16[240,128]{1,0:T(8,128)(2,1)} %bitcast.29), channel_id=1, source_target_pairs={{0,16},{1,17},{2,18},{3,19},{4,20},{5,21},{6,22},{7,23},{8,24},{9,... | collective-permute-start | bytes 184328 | tf_op jit(solution)/shard_map/ppermute | solution.py:501
  17.4 1.2 copy-done
  18.6 1.2 copy-done.2
  20.4 0.8 collective-permute-start.16
  21.5 3.2 %collective-permute-done.1.refs_2_ = bf16[240,128]{1,0:T(8,128)(2,1)S(1)} collective-permute-done((bf16[240,128]{1,0:T(8,128)(2,1)}, bf16[240,128]{1,0:T(8,128)(2,1)S(1)}, u32[]{:S(2)}, u32[]{:S(2)}) %collective-permute-start.1) | collective-permute-done | bytes 61472 | tf_op jit(solution)/shard_map/ppermute | solution.py:501
  25.3 2.4 %collective-permute-start.9 = (bf16[1920,128]{1,0:T(8,128)(2,1)S(1)}, bf16[1920,128]{1,0:T(8,128)(2,1)S(1)}, u32[]{:S(2)}, u32[]{:S(2)}) collective-permute-start(bf16[1920,128]{1,0:T(8,128)(2,1)S(1)} %shard_map.130.refs_0_), channel_id=1, source_target_pairs={{0,128},{8,136},{16,144},{24,152},{32,160},{40,168},{48,176},{56,1... | collective-permute-start | bytes 1474568 | tf_op jit(solution)/shard_map/ppermute | solution.py:501
  27.7 1.2 collective-permute-start.8
  28.9 2.0 %collective-permute-start.15 = (s16[2112,128]{1,0:T(8,128)(2,1)S(1)}, s16[2112,128]{1,0:T(8,128)(2,1)S(1)}, u32[]{:S(2)}, u32[]{:S(2)}) collective-permute-start(s16[2112,128]{1,0:T(8,128)(2,1)S(1)} %get-tuple-element.66), channel_id=1, source_target_pairs={{0,1},{1,0},{2,3},{3,2},{4,5},{5,4},{6,7},{7,6},{8,9},{9,8},{10,11... | collective-permute-start | bytes 1622024 | tf_op jit(solution)/shard_map/ppermute | solution.py:540
  31.6 3.4 %shard_map.132 = (f32[8,256,128]{2,1,0:T(8,128)S(1)}, f32[8,256,128]{2,1,0:T(8,128)S(1)}) custom-call(s32[1]{0:T(128)S(6)} %copy.17.begin, s32[3,512]{1,0:T(4,128)S(1)} %bitcast.31, f32[64,512]{1,0:T(8,128)S(1)} %bitcast.22), custom_call_target="tpu_custom_call" | custom-call | tf_op jit(solution)/shard_map/pallas_call | solution.py:36
  35.0 13.7 %collective-permute-done.10.refs_3_ = bf16[1920,128]{1,0:T(8,128)(2,1)S(1)} collective-permute-done((bf16[1920,128]{1,0:T(8,128)(2,1)S(1)}, bf16[1920,128]{1,0:T(8,128)(2,1)S(1)}, u32[]{:S(2)}, u32[]{:S(2)}) %collective-permute-start.10) | collective-permute-done | bytes 491552 | tf_op jit(solution)/shard_map/ppermute | solution.py:501
  50.3 0.8 collective-permute-done.11.refs_4_
  51.2 0.7 collective-permute-done.12.refs_5_
  52.6 0.7 collective-permute-done.14.refs_7_
  53.3 1.1 shard_map.134
  54.4 9.2 %collective-permute-start.17 = (bf16[640,128]{1,0:T(8,128)(2,1)S(1)}, bf16[640,128]{1,0:T(8,128)(2,1)S(1)}, u32[]{:S(2)}, u32[]{:S(2)}) collective-permute-start(bf16[640,128]{1,0:T(8,128)(2,1)S(1)} %get-tuple-element.89), channel_id=1, source_target_pairs={{0,3},{1,2},{2,1},{3,0},{4,7},{5,6},{6,5},{7,4},{8,11},{9,10},{10,... | collective-permute-start | bytes 491528 | tf_op jit(solution)/shard_map/ppermute | solution.py:501
  63.6 1.1 collective-permute-start.19
  64.7 6.1 %shard_map.133 = (f32[8,256,128]{2,1,0:T(8,128)S(1)}, f32[8,256,128]{2,1,0:T(8,128)S(1)}, f32[8,256,128]{2,1,0:T(8,128)S(1)}, f32[8,256,128]{2,1,0:T(8,128)S(1)}) custom-call(f32[8,256,128]{2,1,0:T(8,128)S(1)} %bitcast.13, f32[8,256,128]{2,1,0:T(8,128)S(1)} %bitcast.17, f32[8,256,128]{2,1,0:T(8,128)S(1)} %bitcast.19, f32[8,256,128]{2,1,0:T(8,128)S(1)} %bitcast.21, ...), custom_call_target="tpu_custom_call" | custom-call | tf_op jit(solution)/shard_map/pallas_call | solution.py:36
  71.0 1.1 collective-permute-done.18.rest_2_
  73.2 1.5 shard_map.135
  75.4 1.3 collective-permute-start.22
  76.7 7.6 %collective-permute-done.22 = s16[704,128]{1,0:T(8,128)(2,1)S(1)} collective-permute-done((s16[704,128]{1,0:T(8,128)(2,1)S(1)}, s16[704,128]{1,0:T(8,128)(2,1)S(1)}, u32[]{:S(2)}, u32[]{:S(2)}) %collective-permute-start.22) | collective-permute-done | bytes 180256 | tf_op jit(solution)/shard_map/ppermute | solution.py:588
  86.3 9.3 %collective-permute-start.24 = (s16[704,128]{1,0:T(8,128)(2,1)S(1)}, s16[704,128]{1,0:T(8,128)(2,1)S(1)}, u32[]{:S(2)}, u32[]{:S(2)}) collective-permute-start(s16[704,128]{1,0:T(8,128)(2,1)S(1)} %collective-permute-done.22), channel_id=1, source_target_pairs={{0,4},{7,3},{8,12},{15,11},{16,20},{23,19},{24,28},{31,27},{32,36}... | collective-permute-start | bytes 540680 | tf_op jit(solution)/shard_map/ppermute | solution.py:591
  95.7 5.9 %shard_map.136 = (f32[8,256,128]{2,1,0:T(8,128)S(1)}, f32[8,256,128]{2,1,0:T(8,128)S(1)}, f32[8,256,128]{2,1,0:T(8,128)S(1)}) custom-call(f32[8,256,128]{2,1,0:T(8,128)S(1)} %get-tuple-element.92.p1, f32[8,256,128]{2,1,0:T(8,128)S(1)} %get-tuple-element.93.q1, f32[8,256,128]{2,1,0:T(8,128)S(1)} %bitcast.14, f32[8,256,128]{2,1,0:T(8,128)S(1)} %bitcast.18, ...), custom_call_target="tpu_custom_call" | custom-call | tf_op jit(solution)/shard_map/pallas_call | solution.py:36
  101.7 3.0 %shard_map.137 = (f32[8,256,128]{2,1,0:T(8,128)}, f32[8,256,128]{2,1,0:T(8,128)}, f32[320,128]{1,0:T(8,128)S(1)}, s16[336,128]{1,0:T(8,128)(2,1)S(1)}, s16[336,1...) custom-call(s32[1,2]{1,0:T(1,128)S(1)} %copy-done.8, ...), custom_call_target="tpu_custom_call" | custom-call | tf_op jit(solution)/shard_map/pallas_call | solution.py:36
  104.7 3.5 %collective-permute-start.27 = (s16[336,128]{1,0:T(8,128)(2,1)S(1)}, s16[336,128]{1,0:T(8,128)(2,1)S(1)}, u32[]{:S(2)}, u32[]{:S(2)}) collective-permute-start(s16[336,128]{1,0:T(8,128)(2,1)S(1)} %get-tuple-element.112), channel_id=1, source_target_pairs={{0,7},{1,6},{2,5},{3,4},{4,3},{5,2},{6,1},{7,0},{8,15},{9,14},{10,... | collective-permute-start | bytes 258056 | tf_op jit(solution)/shard_map/ppermute | solution.py:501
  108.2 2.2 %collective-permute-start.28 = (s16[336,128]{1,0:T(8,128)(2,1)S(1)}, s16[336,128]{1,0:T(8,128)(2,1)S(1)}, u32[]{:S(2)}, u32[]{:S(2)}) collective-permute-start(s16[336,128]{1,0:T(8,128)(2,1)S(1)} %get-tuple-element.113), channel_id=1, source_target_pairs={{0,6},{1,7},{2,4},{3,5},{4,2},{5,3},{6,0},{7,1},{8,14},{9,15},{10,... | collective-permute-start | bytes 258056 | tf_op jit(solution)/shard_map/ppermute | solution.py:501
  110.4 7.3 %collective-permute-start.29 = (s16[336,128]{1,0:T(8,128)(2,1)S(1)}, s16[336,128]{1,0:T(8,128)(2,1)S(1)}, u32[]{:S(2)}, u32[]{:S(2)}) collective-permute-start(s16[336,128]{1,0:T(8,128)(2,1)S(1)} %get-tuple-element.114), channel_id=1, source_target_pairs={{0,5},{1,4},{2,7},{3,6},{4,1},{5,0},{6,3},{7,2},{8,13},{9,12},{10,... | collective-permute-start | bytes 258056 | tf_op jit(solution)/shard_map/ppermute | solution.py:501
  117.7 1.3 collective-permute-start.30
  119.0 2.7 %collective-permute-start.31 = (s16[336,128]{1,0:T(8,128)(2,1)S(1)}, s16[336,128]{1,0:T(8,128)(2,1)S(1)}, u32[]{:S(2)}, u32[]{:S(2)}) collective-permute-start(s16[336,128]{1,0:T(8,128)(2,1)S(1)} %get-tuple-element.116), channel_id=1, source_target_pairs={{0,3},{1,2},{2,1},{3,0},{4,7},{5,6},{6,5},{7,4},{8,11},{9,10},{10,... | collective-permute-start | bytes 258056 | tf_op jit(solution)/shard_map/ppermute | solution.py:501
  121.7 1.4 collective-permute-start.33
  123.1 3.3 %collective-permute-done.30.refs_3_ = s16[336,128]{1,0:T(8,128)(2,1)S(1)} collective-permute-done((s16[336,128]{1,0:T(8,128)(2,1)S(1)}, s16[336,128]{1,0:T(8,128)(2,1)S(1)}, u32[]{:S(2)}, u32[]{:S(2)}) %collective-permute-start.30) | collective-permute-done | bytes 86048 | tf_op jit(solution)/shard_map/ppermute | solution.py:501
  126.4 1.2 collective-permute-done.32.refs_5_
  127.7 0.9 shard_map.138
  128.6 2.2 %collective-permute-done.34.got = f32[1440,128]{1,0:T(8,128)S(1)} collective-permute-done((f32[1440,128]{1,0:T(8,128)S(1)}, f32[1440,128]{1,0:T(8,128)S(1)}, u32[]{:S(2)}, u32[]{:S(2)}) %collective-permute-start.34) | collective-permute-done | bytes 737312 | tf_op jit(solution)/shard_map/ppermute | solution.py:624
  130.8 1.2 shard_map.139
  132.6 2.4 %collective-permute-start.36 = (s16[992,128]{1,0:T(8,128)(2,1)S(1)}, s16[992,128]{1,0:T(8,128)(2,1)S(1)}, u32[]{:S(2)}, u32[]{:S(2)}) collective-permute-start(s16[992,128]{1,0:T(8,128)(2,1)S(1)} %get-tuple-element.123), channel_id=1, source_target_pairs={{0,128},{8,136},{16,144},{24,152},{32,160},{40,168},{48,176},{56,1... | collective-permute-start | bytes 761864 | tf_op jit(solution)/shard_map/ppermute | solution.py:501
  135.1 1.2 collective-permute-start.37
  136.3 10.7 %collective-permute-done.35.refs_0_ = s16[992,128]{1,0:T(8,128)(2,1)S(1)} collective-permute-done((s16[992,128]{1,0:T(8,128)(2,1)S(1)}, s16[992,128]{1,0:T(8,128)(2,1)S(1)}, u32[]{:S(2)}, u32[]{:S(2)}) %collective-permute-start.35) | collective-permute-done | bytes 253984 | tf_op jit(solution)/shard_map/ppermute | solution.py:501
  148.0 2.0 %collective-permute-start.38 = (s16[256,128]{1,0:T(8,128)(2,1)S(1)}, s16[256,128]{1,0:T(8,128)(2,1)S(1)}, u32[]{:S(2)}, u32[]{:S(2)}) collective-permute-start(s16[256,128]{1,0:T(8,128)(2,1)S(1)} %get-tuple-element.126), channel_id=1, source_target_pairs={{0,48},{8,56},{16,32},{24,40},{32,16},{40,24},{48,0},{56,8},{64,11... | collective-permute-start | bytes 196616 | tf_op jit(solution)/shard_map/ppermute | solution.py:501
  150.0 1.6 collective-permute-start.39
  151.5 0.9 collective-permute-start.40
  152.5 2.3 %collective-permute-done.38.refs_0_ = s16[256,128]{1,0:T(8,128)(2,1)S(1)} collective-permute-done((s16[256,128]{1,0:T(8,128)(2,1)S(1)}, s16[256,128]{1,0:T(8,128)(2,1)S(1)}, u32[]{:S(2)}, u32[]{:S(2)}) %collective-permute-start.38) | collective-permute-done | bytes 65568 | tf_op jit(solution)/shard_map/ppermute | solution.py:501
  154.8 2.0 %collective-permute-done.39.refs_1_ = s16[256,128]{1,0:T(8,128)(2,1)S(1)} collective-permute-done((s16[256,128]{1,0:T(8,128)(2,1)S(1)}, s16[256,128]{1,0:T(8,128)(2,1)S(1)}, u32[]{:S(2)}, u32[]{:S(2)}) %collective-permute-start.39) | collective-permute-done | bytes 65568 | tf_op jit(solution)/shard_map/ppermute | solution.py:501
  156.7 0.7 shard_map.141
  (71 shorter events, 10.0 us)
Async XLA Ops:
  0.6 14.2 %collective-permute-start.6 = (bf16[240,128]{1,0:T(8,128)(2,1)}, bf16[240,128]{1,0:T(8,128)(2,1)S(1)}, u32[]{:S(2)}, u32[]{:S(2)}) collective-permute-start(bf16[240,128]{1,0:T(8,128)(2,1)} %bitcast.23), channel_id=1, source_target_pairs={{0,52},{1,53},{2,54},{3,55},{4,48},{5,49},{6,50},{7,51},{8,60},{9,... | collective-permute-start | bytes 184328 | tf_op jit(solution)/shard_map/ppermute | solution.py:501
  6.6 8.5 %collective-permute-start.5 = (bf16[240,128]{1,0:T(8,128)(2,1)}, bf16[240,128]{1,0:T(8,128)(2,1)S(1)}, u32[]{:S(2)}, u32[]{:S(2)}) collective-permute-start(bf16[240,128]{1,0:T(8,128)(2,1)} %bitcast.24), channel_id=1, source_target_pairs={{0,36},{1,37},{2,38},{3,39},{4,32},{5,33},{6,34},{7,35},{8,44},{9,... | collective-permute-start | bytes 184328 | tf_op jit(solution)/shard_map/ppermute | solution.py:501
  7.1 13.3 %collective-permute-start.4 = (bf16[240,128]{1,0:T(8,128)(2,1)}, bf16[240,128]{1,0:T(8,128)(2,1)S(1)}, u32[]{:S(2)}, u32[]{:S(2)}) collective-permute-start(bf16[240,128]{1,0:T(8,128)(2,1)} %bitcast.25), channel_id=1, source_target_pairs={{0,20},{1,21},{2,22},{3,23},{4,16},{5,17},{6,18},{7,19},{8,28},{9,... | collective-permute-start | bytes 184328 | tf_op jit(solution)/shard_map/ppermute | solution.py:501
  11.1 10.3 %collective-permute-start.3 = (bf16[240,128]{1,0:T(8,128)(2,1)}, bf16[240,128]{1,0:T(8,128)(2,1)S(1)}, u32[]{:S(2)}, u32[]{:S(2)}) collective-permute-start(bf16[240,128]{1,0:T(8,128)(2,1)} %bitcast.26), channel_id=1, source_target_pairs={{0,4},{1,5},{2,6},{3,7},{4,0},{5,1},{6,2},{7,3},{8,12},{9,13},{10,... | collective-permute-start | bytes 184328 | tf_op jit(solution)/shard_map/ppermute | solution.py:501
  13.0 8.5 %collective-permute-start.2 = (bf16[240,128]{1,0:T(8,128)(2,1)}, bf16[240,128]{1,0:T(8,128)(2,1)S(1)}, u32[]{:S(2)}, u32[]{:S(2)}) collective-permute-start(bf16[240,128]{1,0:T(8,128)(2,1)} %bitcast.27), channel_id=1, source_target_pairs={{0,48},{1,49},{2,50},{3,51},{4,52},{5,53},{6,54},{7,55},{8,56},{9,... | collective-permute-start | bytes 184328 | tf_op jit(solution)/shard_map/ppermute | solution.py:501
  14.9 9.8 %collective-permute-start.1 = (bf16[240,128]{1,0:T(8,128)(2,1)}, bf16[240,128]{1,0:T(8,128)(2,1)S(1)}, u32[]{:S(2)}, u32[]{:S(2)}) collective-permute-start(bf16[240,128]{1,0:T(8,128)(2,1)} %bitcast.28), channel_id=1, source_target_pairs={{0,32},{1,33},{2,34},{3,35},{4,36},{5,37},{6,38},{7,39},{8,40},{9,... | collective-permute-start | bytes 184328 | tf_op jit(solution)/shard_map/ppermute | solution.py:501
  15.1 9.5 %collective-permute-start = (bf16[240,128]{1,0:T(8,128)(2,1)}, bf16[240,128]{1,0:T(8,128)(2,1)S(1)}, u32[]{:S(2)}, u32[]{:S(2)}) collective-permute-start(bf16[240,128]{1,0:T(8,128)(2,1)} %bitcast.29), channel_id=1, source_target_pairs={{0,16},{1,17},{2,18},{3,19},{4,20},{5,21},{6,22},{7,23},{8,24},{9,... | collective-permute-start | bytes 184328 | tf_op jit(solution)/shard_map/ppermute | solution.py:501
  19.8 4.8 %copy-start.7 = (bf16[6,40,128]{2,1,0:T(8,128)(2,1)S(1)}, bf16[6,40,128]{2,1,0:T(8,128)(2,1)}, u32[]{:S(2)}) copy-start(bf16[6,40,128]{2,1,0:T(8,128)(2,1)} %param.11) | copy-start | bytes 184324
  20.4 11.2 %copy-start.6 = (f32[1,64,512]{2,1,0:T(8,128)S(1)}, f32[1,64,512]{2,1,0:T(8,128)}, u32[]{:S(2)}) copy-start(f32[1,64,512]{2,1,0:T(8,128)} %param.16) | copy-start | bytes 393220
  20.4 29.5 %collective-permute-start.16 = (s16[2112,128]{1,0:T(8,128)(2,1)S(1)}, s16[2112,128]{1,0:T(8,128)(2,1)S(1)}, u32[]{:S(2)}, u32[]{:S(2)}) collective-permute-start(s16[2112,128]{1,0:T(8,128)(2,1)S(1)} %get-tuple-element.73), channel_id=1, source_target_pairs={{1,2},{3,4},{5,6},{2,1},{4,3},{6,5},{9,10},{11,12},{13,14},{10,9},... | collective-permute-start | bytes 1622024 | tf_op jit(solution)/shard_map/ppermute | solution.py:541
  21.5 3.2 %collective-permute-start.7 = (s32[1,2]{1,0:T(1,128)S(1)}, s32[1,2]{1,0:T(1,128)S(1)}, u32[]{:S(2)}, u32[]{:S(2)}) collective-permute-start(s32[1,2]{1,0:T(1,128)S(1)} %copy-done.8), channel_id=1, source_target_pairs={{0,8},{8,0},{16,24},{24,16},{32,40},{40,32},{48,56},{56,48},{64,72... | collective-permute-start | bytes 32 | tf_op jit(solution)/shard_map/ppermute | solution.py:533
  24.6 6.9 %copy-start.11 = (s32[1,3,512]{2,0,1:T(1,128)S(1)}, s32[1,3,512]{2,0,1:T(1,128)}, u32[]{:S(2)}) copy-start(s32[1,3,512]{2,0,1:T(1,128)} %param.15) | copy-start | bytes 18436
  24.6 40.1 %copy-start.5 = (f32[1,8,256,128]{3,2,1,0:T(8,128)S(1)}, f32[1,8,256,128]{3,2,1,0:T(8,128)}, u32[]{:S(2)}) copy-start(f32[1,8,256,128]{3,2,1,0:T(8,128)} %param.20) | copy-start | bytes 3145732
  24.7 24.0 %collective-permute-start.10 = (bf16[1920,128]{1,0:T(8,128)(2,1)S(1)}, bf16[1920,128]{1,0:T(8,128)(2,1)S(1)}, u32[]{:S(2)}, u32[]{:S(2)}) collective-permute-start(bf16[1920,128]{1,0:T(8,128)(2,1)S(1)} %shard_map.130.refs_0_), channel_id=1, source_target_pairs={{0,192},{8,200},{16,208},{24,216},{32,224},{40,232},{48,240},{56,2... | collective-permute-start | bytes 1474568 | tf_op jit(solution)/shard_map/ppermute | solution.py:501
  25.3 23.4 %collective-permute-start.9 = (bf16[1920,128]{1,0:T(8,128)(2,1)S(1)}, bf16[1920,128]{1,0:T(8,128)(2,1)S(1)}, u32[]{:S(2)}, u32[]{:S(2)}) collective-permute-start(bf16[1920,128]{1,0:T(8,128)(2,1)S(1)} %shard_map.130.refs_0_), channel_id=1, source_target_pairs={{0,128},{8,136},{16,144},{24,152},{32,160},{40,168},{48,176},{56,1... | collective-permute-start | bytes 1474568 | tf_op jit(solution)/shard_map/ppermute | solution.py:501
  27.7 21.6 %collective-permute-start.8 = (bf16[1920,128]{1,0:T(8,128)(2,1)S(1)}, bf16[1920,128]{1,0:T(8,128)(2,1)S(1)}, u32[]{:S(2)}, u32[]{:S(2)}) collective-permute-start(bf16[1920,128]{1,0:T(8,128)(2,1)S(1)} %shard_map.130.refs_0_), channel_id=1, source_target_pairs={{0,64},{8,72},{16,80},{24,88},{32,96},{40,104},{48,112},{56,120},{... | collective-permute-start | bytes 1474568 | tf_op jit(solution)/shard_map/ppermute | solution.py:501
  28.9 21.4 %collective-permute-start.15 = (s16[2112,128]{1,0:T(8,128)(2,1)S(1)}, s16[2112,128]{1,0:T(8,128)(2,1)S(1)}, u32[]{:S(2)}, u32[]{:S(2)}) collective-permute-start(s16[2112,128]{1,0:T(8,128)(2,1)S(1)} %get-tuple-element.66), channel_id=1, source_target_pairs={{0,1},{1,0},{2,3},{3,2},{4,5},{5,4},{6,7},{7,6},{8,9},{9,8},{10,11... | collective-permute-start | bytes 1622024 | tf_op jit(solution)/shard_map/ppermute | solution.py:540
  49.3 15.4 %copy-start.1 = (f32[1,8,256,128]{3,2,1,0:T(8,128)S(1)}, f32[1,8,256,128]{3,2,1,0:T(8,128)}, u32[]{:S(2)}) copy-start(f32[1,8,256,128]{3,2,1,0:T(8,128)} %param.19) | copy-start | bytes 3145732
  49.3 15.4 %copy-start.3 = (f32[1,8,256,128]{3,2,1,0:T(8,128)S(1)}, f32[1,8,256,128]{3,2,1,0:T(8,128)}, u32[]{:S(2)}) copy-start(f32[1,8,256,128]{3,2,1,0:T(8,128)} %param.21) | copy-start | bytes 3145732
  49.3 15.5 %copy-start.4 = (f32[1,8,256,128]{3,2,1,0:T(8,128)S(1)}, f32[1,8,256,128]{3,2,1,0:T(8,128)}, u32[]{:S(2)}) copy-start(f32[1,8,256,128]{3,2,1,0:T(8,128)} %param.18) | copy-start | bytes 3145732
  49.3 1.9 %collective-permute-start.11 = (bf16[1920,128]{1,0:T(8,128)(2,1)S(1)}, bf16[1920,128]{1,0:T(8,128)(2,1)S(1)}, u32[]{:S(2)}, u32[]{:S(2)}) collective-permute-start(bf16[1920,128]{1,0:T(8,128)(2,1)S(1)} %shard_map.130.refs_0_), channel_id=1, source_target_pairs={{0,8},{8,0},{16,24},{24,16},{32,40},{40,32},{48,56},{56,48},{64,72... | collective-permute-start | bytes 1474568 | tf_op jit(solution)/shard_map/ppermute | solution.py:549
  49.3 2.6 %collective-permute-start.12 = (bf16[1920,128]{1,0:T(8,128)(2,1)S(1)}, bf16[1920,128]{1,0:T(8,128)(2,1)S(1)}, u32[]{:S(2)}, u32[]{:S(2)}) collective-permute-start(bf16[1920,128]{1,0:T(8,128)(2,1)S(1)} %collective-permute-done.8.refs_1_), channel_id=1, source_target_pairs={{0,8},{8,0},{16,24},{24,16},{32,40},{40,32},{48,56},{56,48},{64,72... | collective-permute-start | bytes 1474568 | tf_op jit(solution)/shard_map/ppermute | solution.py:549
  49.8 2.8 %collective-permute-start.13 = (bf16[1920,128]{1,0:T(8,128)(2,1)S(1)}, bf16[1920,128]{1,0:T(8,128)(2,1)S(1)}, u32[]{:S(2)}, u32[]{:S(2)}) collective-permute-start(bf16[1920,128]{1,0:T(8,128)(2,1)S(1)} %collective-permute-done.9.refs_2_), channel_id=1, source_target_pairs={{0,8},{8,0},{16,24},{24,16},{32,40},{40,32},{48,56},{56,48},{64,72... | collective-permute-start | bytes 1474568 | tf_op jit(solution)/shard_map/ppermute | solution.py:549
  49.9 3.4 %collective-permute-start.14 = (bf16[1920,128]{1,0:T(8,128)(2,1)S(1)}, bf16[1920,128]{1,0:T(8,128)(2,1)S(1)}, u32[]{:S(2)}, u32[]{:S(2)}) collective-permute-start(bf16[1920,128]{1,0:T(8,128)(2,1)S(1)} %collective-permute-done.10.refs_3_), channel_id=1, source_target_pairs={{0,8},{8,0},{16,24},{24,16},{32,40},{40,32},{48,56},{56,48},{64,72... | collective-permute-start | bytes 1474568 | tf_op jit(solution)/shard_map/ppermute | solution.py:549
  54.4 16.6 %collective-permute-start.17 = (bf16[640,128]{1,0:T(8,128)(2,1)S(1)}, bf16[640,128]{1,0:T(8,128)(2,1)S(1)}, u32[]{:S(2)}, u32[]{:S(2)}) collective-permute-start(bf16[640,128]{1,0:T(8,128)(2,1)S(1)} %get-tuple-element.89), channel_id=1, source_target_pairs={{0,3},{1,2},{2,1},{3,0},{4,7},{5,6},{6,5},{7,4},{8,11},{9,10},{10,... | collective-permute-start | bytes 491528 | tf_op jit(solution)/shard_map/ppermute | solution.py:501
  63.6 8.6 %collective-permute-start.18 = (bf16[640,128]{1,0:T(8,128)(2,1)S(1)}, bf16[640,128]{1,0:T(8,128)(2,1)S(1)}, u32[]{:S(2)}, u32[]{:S(2)}) collective-permute-start(bf16[640,128]{1,0:T(8,128)(2,1)S(1)} %get-tuple-element.90), channel_id=1, source_target_pairs={{0,2},{1,3},{2,0},{3,1},{4,6},{5,7},{6,4},{7,5},{8,10},{9,11},{10,... | collective-permute-start | bytes 491528 | tf_op jit(solution)/shard_map/ppermute | solution.py:501
  63.6 8.9 %collective-permute-start.19 = (bf16[640,128]{1,0:T(8,128)(2,1)S(1)}, bf16[640,128]{1,0:T(8,128)(2,1)S(1)}, u32[]{:S(2)}, u32[]{:S(2)}) collective-permute-start(bf16[640,128]{1,0:T(8,128)(2,1)S(1)} %get-tuple-element.91), channel_id=1, source_target_pairs={{0,1},{1,0},{2,3},{3,2},{4,5},{5,4},{6,7},{7,6},{8,9},{9,8},{10,11... | collective-permute-start | bytes 491528 | tf_op jit(solution)/shard_map/ppermute | solution.py:501
  74.7 2.0 %collective-permute-start.21 = (s16[704,128]{1,0:T(8,128)(2,1)S(1)}, s16[704,128]{1,0:T(8,128)(2,1)S(1)}, u32[]{:S(2)}, u32[]{:S(2)}) collective-permute-start(s16[704,128]{1,0:T(8,128)(2,1)S(1)} %get-tuple-element.102), channel_id=1, source_target_pairs={{3,2},{4,5},{11,10},{12,13},{19,18},{20,21},{27,26},{28,29},{35,34... | collective-permute-start | bytes 540680 | tf_op jit(solution)/shard_map/ppermute | solution.py:588
  75.4 8.9 %collective-permute-start.22 = (s16[704,128]{1,0:T(8,128)(2,1)S(1)}, s16[704,128]{1,0:T(8,128)(2,1)S(1)}, u32[]{:S(2)}, u32[]{:S(2)}) collective-permute-start(s16[704,128]{1,0:T(8,128)(2,1)S(1)} %get-tuple-element.103), channel_id=1, source_target_pairs={{3,0},{4,7},{11,8},{12,15},{19,16},{20,23},{27,24},{28,31},{35,32}... | collective-permute-start | bytes 540680 | tf_op jit(solution)/shard_map/ppermute | solution.py:588
  84.3 17.4 %collective-permute-start.25 = (s16[2112,128]{1,0:T(8,128)(2,1)S(1)}, s16[2112,128]{1,0:T(8,128)(2,1)S(1)}, u32[]{:S(2)}, u32[]{:S(2)}) collective-permute-start(s16[2112,128]{1,0:T(8,128)(2,1)S(1)} %get-tuple-element.106), channel_id=1, source_target_pairs={{0,1},{1,0},{2,3},{3,2},{4,5},{5,4},{6,7},{7,6},{8,9},{9,8},{10,11... | collective-permute-start | bytes 1622024 | tf_op jit(solution)/shard_map/ppermute | solution.py:594
  84.3 17.4 %collective-permute-start.26 = (s16[2112,128]{1,0:T(8,128)(2,1)S(1)}, s16[2112,128]{1,0:T(8,128)(2,1)S(1)}, u32[]{:S(2)}, u32[]{:S(2)}) collective-permute-start(s16[2112,128]{1,0:T(8,128)(2,1)S(1)} %get-tuple-element.107), channel_id=1, source_target_pairs={{1,2},{5,6},{2,1},{6,5},{9,10},{13,14},{10,9},{14,13},{17,18},{21,... | collective-permute-start | bytes 1622024 | tf_op jit(solution)/shard_map/ppermute | solution.py:595
  85.0 16.7 %collective-permute-start.20 = (s16[704,128]{1,0:T(8,128)(2,1)S(1)}, s16[704,128]{1,0:T(8,128)(2,1)S(1)}, u32[]{:S(2)}, u32[]{:S(2)}) collective-permute-start(s16[704,128]{1,0:T(8,128)(2,1)S(1)} %get-tuple-element.99), channel_id=1, source_target_pairs={{3,4},{4,3},{11,12},{12,11},{19,20},{20,19},{27,28},{28,27},{35,36... | collective-permute-start | bytes 540680 | tf_op jit(solution)/shard_map/ppermute | solution.py:591
  85.7 16.0 %collective-permute-start.23 = (s16[704,128]{1,0:T(8,128)(2,1)S(1)}, s16[704,128]{1,0:T(8,128)(2,1)S(1)}, u32[]{:S(2)}, u32[]{:S(2)}) collective-permute-start(s16[704,128]{1,0:T(8,128)(2,1)S(1)} %collective-permute-done.21), channel_id=1, source_target_pairs={{2,4},{5,3},{10,12},{13,11},{18,20},{21,19},{26,28},{29,27},{34,36... | collective-permute-start | bytes 540680 | tf_op jit(solution)/shard_map/ppermute | solution.py:591
  86.3 15.3 %collective-permute-start.24 = (s16[704,128]{1,0:T(8,128)(2,1)S(1)}, s16[704,128]{1,0:T(8,128)(2,1)S(1)}, u32[]{:S(2)}, u32[]{:S(2)}) collective-permute-start(s16[704,128]{1,0:T(8,128)(2,1)S(1)} %collective-permute-done.22), channel_id=1, source_target_pairs={{0,4},{7,3},{8,12},{15,11},{16,20},{23,19},{24,28},{31,27},{32,36}... | collective-permute-start | bytes 540680 | tf_op jit(solution)/shard_map/ppermute | solution.py:591
  104.7 17.0 %collective-permute-start.27 = (s16[336,128]{1,0:T(8,128)(2,1)S(1)}, s16[336,128]{1,0:T(8,128)(2,1)S(1)}, u32[]{:S(2)}, u32[]{:S(2)}) collective-permute-start(s16[336,128]{1,0:T(8,128)(2,1)S(1)} %get-tuple-element.112), channel_id=1, source_target_pairs={{0,7},{1,6},{2,5},{3,4},{4,3},{5,2},{6,1},{7,0},{8,15},{9,14},{10,... | collective-permute-start | bytes 258056 | tf_op jit(solution)/shard_map/ppermute | solution.py:501
  108.2 13.5 %collective-permute-start.28 = (s16[336,128]{1,0:T(8,128)(2,1)S(1)}, s16[336,128]{1,0:T(8,128)(2,1)S(1)}, u32[]{:S(2)}, u32[]{:S(2)}) collective-permute-start(s16[336,128]{1,0:T(8,128)(2,1)S(1)} %get-tuple-element.113), channel_id=1, source_target_pairs={{0,6},{1,7},{2,4},{3,5},{4,2},{5,3},{6,0},{7,1},{8,14},{9,15},{10,... | collective-permute-start | bytes 258056 | tf_op jit(solution)/shard_map/ppermute | solution.py:501
  110.4 12.7 %collective-permute-start.29 = (s16[336,128]{1,0:T(8,128)(2,1)S(1)}, s16[336,128]{1,0:T(8,128)(2,1)S(1)}, u32[]{:S(2)}, u32[]{:S(2)}) collective-permute-start(s16[336,128]{1,0:T(8,128)(2,1)S(1)} %get-tuple-element.114), channel_id=1, source_target_pairs={{0,5},{1,4},{2,7},{3,6},{4,1},{5,0},{6,3},{7,2},{8,13},{9,12},{10,... | collective-permute-start | bytes 258056 | tf_op jit(solution)/shard_map/ppermute | solution.py:501
  117.7 8.8 %collective-permute-start.30 = (s16[336,128]{1,0:T(8,128)(2,1)S(1)}, s16[336,128]{1,0:T(8,128)(2,1)S(1)}, u32[]{:S(2)}, u32[]{:S(2)}) collective-permute-start(s16[336,128]{1,0:T(8,128)(2,1)S(1)} %get-tuple-element.115), channel_id=1, source_target_pairs={{0,4},{1,5},{2,6},{3,7},{4,0},{5,1},{6,2},{7,3},{8,12},{9,13},{10,... | collective-permute-start | bytes 258056 | tf_op jit(solution)/shard_map/ppermute | solution.py:501
  119.0 7.4 %collective-permute-start.31 = (s16[336,128]{1,0:T(8,128)(2,1)S(1)}, s16[336,128]{1,0:T(8,128)(2,1)S(1)}, u32[]{:S(2)}, u32[]{:S(2)}) collective-permute-start(s16[336,128]{1,0:T(8,128)(2,1)S(1)} %get-tuple-element.116), channel_id=1, source_target_pairs={{0,3},{1,2},{2,1},{3,0},{4,7},{5,6},{6,5},{7,4},{8,11},{9,10},{10,... | collective-permute-start | bytes 258056 | tf_op jit(solution)/shard_map/ppermute | solution.py:501
  121.7 6.0 %collective-permute-start.32 = (s16[336,128]{1,0:T(8,128)(2,1)S(1)}, s16[336,128]{1,0:T(8,128)(2,1)S(1)}, u32[]{:S(2)}, u32[]{:S(2)}) collective-permute-start(s16[336,128]{1,0:T(8,128)(2,1)S(1)} %get-tuple-element.117), channel_id=1, source_target_pairs={{0,2},{1,3},{2,0},{3,1},{4,6},{5,7},{6,4},{7,5},{8,10},{9,11},{10,... | collective-permute-start | bytes 258056 | tf_op jit(solution)/shard_map/ppermute | solution.py:501
  121.7 6.0 %collective-permute-start.33 = (s16[336,128]{1,0:T(8,128)(2,1)S(1)}, s16[336,128]{1,0:T(8,128)(2,1)S(1)}, u32[]{:S(2)}, u32[]{:S(2)}) collective-permute-start(s16[336,128]{1,0:T(8,128)(2,1)S(1)} %get-tuple-element.118), channel_id=1, source_target_pairs={{0,1},{1,0},{2,3},{3,2},{4,5},{5,4},{6,7},{7,6},{8,9},{9,8},{10,11... | collective-permute-start | bytes 258056 | tf_op jit(solution)/shard_map/ppermute | solution.py:501
  128.5 2.3 %collective-permute-start.34 = (f32[1440,128]{1,0:T(8,128)S(1)}, f32[1440,128]{1,0:T(8,128)S(1)}, u32[]{:S(2)}, u32[]{:S(2)}) collective-permute-start(f32[1440,128]{1,0:T(8,128)S(1)} %get-tuple-element.120), channel_id=1, source_target_pairs={{0,8},{8,0},{16,24},{24,16},{32,40},{40,32},{48,56},{56,48},{64,72... | collective-permute-start | bytes 2211848 | tf_op jit(solution)/shard_map/ppermute | solution.py:624
  132.1 14.9 %collective-permute-start.35 = (s16[992,128]{1,0:T(8,128)(2,1)S(1)}, s16[992,128]{1,0:T(8,128)(2,1)S(1)}, u32[]{:S(2)}, u32[]{:S(2)}) collective-permute-start(s16[992,128]{1,0:T(8,128)(2,1)S(1)} %get-tuple-element.122), channel_id=1, source_target_pairs={{0,192},{8,200},{16,208},{24,216},{32,224},{40,232},{48,240},{56,2... | collective-permute-start | bytes 761864 | tf_op jit(solution)/shard_map/ppermute | solution.py:501
  132.6 14.4 %collective-permute-start.36 = (s16[992,128]{1,0:T(8,128)(2,1)S(1)}, s16[992,128]{1,0:T(8,128)(2,1)S(1)}, u32[]{:S(2)}, u32[]{:S(2)}) collective-permute-start(s16[992,128]{1,0:T(8,128)(2,1)S(1)} %get-tuple-element.123), channel_id=1, source_target_pairs={{0,128},{8,136},{16,144},{24,152},{32,160},{40,168},{48,176},{56,1... | collective-permute-start | bytes 761864 | tf_op jit(solution)/shard_map/ppermute | solution.py:501
  135.1 12.6 %collective-permute-start.37 = (s16[992,128]{1,0:T(8,128)(2,1)S(1)}, s16[992,128]{1,0:T(8,128)(2,1)S(1)}, u32[]{:S(2)}, u32[]{:S(2)}) collective-permute-start(s16[992,128]{1,0:T(8,128)(2,1)S(1)} %get-tuple-element.124), channel_id=1, source_target_pairs={{0,64},{8,72},{16,80},{24,88},{32,96},{40,104},{48,112},{56,120},{... | collective-permute-start | bytes 761864 | tf_op jit(solution)/shard_map/ppermute | solution.py:501
  148.0 6.8 %collective-permute-start.38 = (s16[256,128]{1,0:T(8,128)(2,1)S(1)}, s16[256,128]{1,0:T(8,128)(2,1)S(1)}, u32[]{:S(2)}, u32[]{:S(2)}) collective-permute-start(s16[256,128]{1,0:T(8,128)(2,1)S(1)} %get-tuple-element.126), channel_id=1, source_target_pairs={{0,48},{8,56},{16,32},{24,40},{32,16},{40,24},{48,0},{56,8},{64,11... | collective-permute-start | bytes 196616 | tf_op jit(solution)/shard_map/ppermute | solution.py:501
  150.0 6.8 %collective-permute-start.39 = (s16[256,128]{1,0:T(8,128)(2,1)S(1)}, s16[256,128]{1,0:T(8,128)(2,1)S(1)}, u32[]{:S(2)}, u32[]{:S(2)}) collective-permute-start(s16[256,128]{1,0:T(8,128)(2,1)S(1)} %get-tuple-element.127), channel_id=1, source_target_pairs={{0,32},{8,40},{16,48},{24,56},{32,0},{40,8},{48,16},{56,24},{64,96... | collective-permute-start | bytes 196616 | tf_op jit(solution)/shard_map/ppermute | solution.py:501
  151.5 5.2 %collective-permute-start.40 = (s16[256,128]{1,0:T(8,128)(2,1)S(1)}, s16[256,128]{1,0:T(8,128)(2,1)S(1)}, u32[]{:S(2)}, u32[]{:S(2)}) collective-permute-start(s16[256,128]{1,0:T(8,128)(2,1)S(1)} %get-tuple-element.128), channel_id=1, source_target_pairs={{0,16},{8,24},{16,0},{24,8},{32,48},{40,56},{48,32},{56,40},{64,80... | collective-permute-start | bytes 196616 | tf_op jit(solution)/shard_map/ppermute | solution.py:501
  (5 other events, 4.9 us)

commit v10 on v9

--- a/solution.py
+++ b/solution.py
@@ -586,20 +586,20 @@
     )
     border = (side - 1, side)
     moved = [lax.ppermute(part, "dom", [(a, a ^ k) for a in border]) for part, k in zip(parts[1:], ROUTES[1:])]
-    one, two, moved = lax.optimization_barrier((one, two, moved))
+    part_f, part_a, bend = call(
+        between_kernel,
+        (field,) * 3,
+        (p1, q1, p0, q0, p_prev, courant, hits[1]),
+        "v" * 7,
+        (padded,),
+    )
+    one, two, moved, part_f = lax.optimization_barrier((one, two, moved, part_f))
     parts = [
         lax.ppermute(part, "dom", [(a ^ k, b) for a, b in (border, border[::-1])])
         for part, k in zip((parts[0], *moved), ROUTES)
     ]
     from_one = lax.ppermute(one, "dom", one_pairs)
     from_two = lax.ppermute(two, "dom", [(a, b) for a, b in two_pairs if a not in border])
-    part_f, part_a, bend = call(
-        between_kernel,
-        (field,) * 3,
-        (p1, q1, p0, q0, p_prev, courant, hits[1]),
-        "v" * 7,
-        (padded,),
-    )
 
     edge = groups * band - count_y
     coded = struct((code_rows_of(row_count, band), count_z), I16)

time: 158 us -> 161 us (1.019)
  starting transfers between devices: 75.5 us -> 79.9 us
  waiting for transfers between devices: 52.3 us -> 50.5 us
    ppermute x2, waiting for transfers between devices: 7.57 us -> 1.61 us  [body(): lax.ppermute(part, 'dom', [(a, a ^ k) for a in border])]
    ppermute x3, waiting for transfers between devices: 0.01 us -> 3.34 us  [body(): lax.ppermute(part, 'dom', [(a ^ k, b) for a, b in (border, border[::-1])])]
    ppermute x26, starting transfers between devices: 58.2 us -> 60.5 us  [exchange(): got[k] = lax.ppermute(parts[k - 1], axis, pairs(k))]
    ppermute x3, starting transfers between devices: 10.7 us -> 12.9 us  [body(): lax.ppermute(part, 'dom', [(a ^ k, b) for a, b in (border, border[::-1])])]
  transfers between devices with their start and end apart: 41 -> 41, of which waited for: 19 -> 21; matrix products, arithmetic and copies ran while one was open for 0% -> 0% of each run, Pallas kernels for 10% -> 10%
where the time goes in v10:
time: 161 us; the launch traced here: 160 us
  starting transfers between devices  79.9 us (50%)
  waiting for transfers between devices  50.5 us (31%)
  Pallas kernels  24.9 us (15%)
  local copies, waits for them, and re-layouts  3.16 us (2%)
    ppermute x26, starting transfers between devices, exchange(): got[k] = lax.ppermute(parts[k - 1], axis, pairs(k))  60.5 us
    ppermute x26, waiting for transfers between devices, exchange(): got[k] = lax.ppermute(parts[k - 1], axis, pairs(k))  40.4 us
    pallas_call x12, Pallas kernels, call(): pl.pallas_call(kernel, out_shape=list(outs), in_specs=[smem() if s == 's'...  24.9 us
    ppermute x3, starting transfers between devices, body(): lax.ppermute(part, 'dom', [(a ^ k, b) for a, b in (border, border[::-1])])  12.9 us
    ppermute x3, waiting for transfers between devices, body(): lax.ppermute(part, 'dom', [(a ^ k, b) for a, b in (border, border[::-1])])  3.34 us
  transfers between devices with their start and end apart: 41, of which 21 were waited for; matrix products, arithmetic and copies ran while one was open for 0% of the time, Pallas kernels for 10%

profile of v10, /device:TPU:6, one launch (start us, length us, event | category | flops | bytes accessed | tf_op | source)
XLA Modules:
  0.0 160.1 jit_solution(14436661894897916005)
XLA Ops:
  0.6 5.9 %collective-permute-start.6 = (bf16[240,128]{1,0:T(8,128)(2,1)}, bf16[240,128]{1,0:T(8,128)(2,1)S(1)}, u32[]{:S(2)}, u32[]{:S(2)}) collective-permute-start(bf16[240,128]{1,0:T(8,128)(2,1)} %bitcast.23), channel_id=1, source_target_pairs={{0,52},{1,53},{2,54},{3,55},{4,48},{5,49},{6,50},{7,51},{8,60},{9,... | collective-permute-start | bytes 184328 | tf_op jit(solution)/shard_map/ppermute | solution.py:501
  7.1 4.0 %collective-permute-start.4 = (bf16[240,128]{1,0:T(8,128)(2,1)}, bf16[240,128]{1,0:T(8,128)(2,1)S(1)}, u32[]{:S(2)}, u32[]{:S(2)}) collective-permute-start(bf16[240,128]{1,0:T(8,128)(2,1)} %bitcast.25), channel_id=1, source_target_pairs={{0,20},{1,21},{2,22},{3,23},{4,16},{5,17},{6,18},{7,19},{8,28},{9,... | collective-permute-start | bytes 184328 | tf_op jit(solution)/shard_map/ppermute | solution.py:501
  11.1 1.8 %collective-permute-start.3 = (bf16[240,128]{1,0:T(8,128)(2,1)}, bf16[240,128]{1,0:T(8,128)(2,1)S(1)}, u32[]{:S(2)}, u32[]{:S(2)}) collective-permute-start(bf16[240,128]{1,0:T(8,128)(2,1)} %bitcast.26), channel_id=1, source_target_pairs={{0,4},{1,5},{2,6},{3,7},{4,0},{5,1},{6,2},{7,3},{8,12},{9,13},{10,... | collective-permute-start | bytes 184328 | tf_op jit(solution)/shard_map/ppermute | solution.py:501
  13.0 1.9 %collective-permute-start.2 = (bf16[240,128]{1,0:T(8,128)(2,1)}, bf16[240,128]{1,0:T(8,128)(2,1)S(1)}, u32[]{:S(2)}, u32[]{:S(2)}) collective-permute-start(bf16[240,128]{1,0:T(8,128)(2,1)} %bitcast.27), channel_id=1, source_target_pairs={{0,48},{1,49},{2,50},{3,51},{4,52},{5,53},{6,54},{7,55},{8,56},{9,... | collective-permute-start | bytes 184328 | tf_op jit(solution)/shard_map/ppermute | solution.py:501
  15.1 2.3 %collective-permute-start = (bf16[240,128]{1,0:T(8,128)(2,1)}, bf16[240,128]{1,0:T(8,128)(2,1)S(1)}, u32[]{:S(2)}, u32[]{:S(2)}) collective-permute-start(bf16[240,128]{1,0:T(8,128)(2,1)} %bitcast.29), channel_id=1, source_target_pairs={{0,16},{1,17},{2,18},{3,19},{4,20},{5,21},{6,22},{7,23},{8,24},{9,... | collective-permute-start | bytes 184328 | tf_op jit(solution)/shard_map/ppermute | solution.py:501
  17.4 1.2 copy-done
  18.6 1.2 copy-done.2
  20.4 0.8 collective-permute-start.16
  21.5 3.2 %collective-permute-done.1.refs_2_ = bf16[240,128]{1,0:T(8,128)(2,1)S(1)} collective-permute-done((bf16[240,128]{1,0:T(8,128)(2,1)}, bf16[240,128]{1,0:T(8,128)(2,1)S(1)}, u32[]{:S(2)}, u32[]{:S(2)}) %collective-permute-start.1) | collective-permute-done | bytes 61472 | tf_op jit(solution)/shard_map/ppermute | solution.py:501
  25.3 2.4 %collective-permute-start.9 = (bf16[1920,128]{1,0:T(8,128)(2,1)S(1)}, bf16[1920,128]{1,0:T(8,128)(2,1)S(1)}, u32[]{:S(2)}, u32[]{:S(2)}) collective-permute-start(bf16[1920,128]{1,0:T(8,128)(2,1)S(1)} %shard_map.130.refs_0_), channel_id=1, source_target_pairs={{0,128},{8,136},{16,144},{24,152},{32,160},{40,168},{48,176},{56,1... | collective-permute-start | bytes 1474568 | tf_op jit(solution)/shard_map/ppermute | solution.py:501
  27.7 1.2 collective-permute-start.8
  28.9 2.0 %collective-permute-start.15 = (s16[2112,128]{1,0:T(8,128)(2,1)S(1)}, s16[2112,128]{1,0:T(8,128)(2,1)S(1)}, u32[]{:S(2)}, u32[]{:S(2)}) collective-permute-start(s16[2112,128]{1,0:T(8,128)(2,1)S(1)} %get-tuple-element.67), channel_id=1, source_target_pairs={{0,1},{1,0},{2,3},{3,2},{4,5},{5,4},{6,7},{7,6},{8,9},{9,8},{10,11... | collective-permute-start | bytes 1622024 | tf_op jit(solution)/shard_map/ppermute | solution.py:540
  31.6 3.4 %shard_map.132 = (f32[8,256,128]{2,1,0:T(8,128)S(1)}, f32[8,256,128]{2,1,0:T(8,128)S(1)}) custom-call(s32[1]{0:T(128)S(6)} %copy.17.begin, s32[3,512]{1,0:T(4,128)S(1)} %bitcast.31, f32[64,512]{1,0:T(8,128)S(1)} %bitcast.22), custom_call_target="tpu_custom_call" | custom-call | tf_op jit(solution)/shard_map/pallas_call | solution.py:36
  35.0 13.7 %collective-permute-done.10.refs_3_ = bf16[1920,128]{1,0:T(8,128)(2,1)S(1)} collective-permute-done((bf16[1920,128]{1,0:T(8,128)(2,1)S(1)}, bf16[1920,128]{1,0:T(8,128)(2,1)S(1)}, u32[]{:S(2)}, u32[]{:S(2)}) %collective-permute-start.10) | collective-permute-done | bytes 491552 | tf_op jit(solution)/shard_map/ppermute | solution.py:501
  50.3 0.8 collective-permute-done.11.refs_4_
  51.2 0.7 collective-permute-done.12.refs_5_
  52.6 0.7 collective-permute-done.14.refs_7_
  53.3 1.1 shard_map.134
  54.4 9.2 %collective-permute-start.17 = (bf16[640,128]{1,0:T(8,128)(2,1)S(1)}, bf16[640,128]{1,0:T(8,128)(2,1)S(1)}, u32[]{:S(2)}, u32[]{:S(2)}) collective-permute-start(bf16[640,128]{1,0:T(8,128)(2,1)S(1)} %get-tuple-element.90), channel_id=1, source_target_pairs={{0,3},{1,2},{2,1},{3,0},{4,7},{5,6},{6,5},{7,4},{8,11},{9,10},{10,... | collective-permute-start | bytes 491528 | tf_op jit(solution)/shard_map/ppermute | solution.py:501
  63.6 1.1 collective-permute-start.19
  64.7 6.1 %shard_map.133 = (f32[8,256,128]{2,1,0:T(8,128)S(1)}, f32[8,256,128]{2,1,0:T(8,128)S(1)}, f32[8,256,128]{2,1,0:T(8,128)S(1)}, f32[8,256,128]{2,1,0:T(8,128)S(1)}) custom-call(f32[8,256,128]{2,1,0:T(8,128)S(1)} %bitcast.13, f32[8,256,128]{2,1,0:T(8,128)S(1)} %bitcast.17, f32[8,256,128]{2,1,0:T(8,128)S(1)} %bitcast.19, f32[8,256,128]{2,1,0:T(8,128)S(1)} %bitcast.21, ...), custom_call_target="tpu_custom_call" | custom-call | tf_op jit(solution)/shard_map/pallas_call | solution.py:36
  71.0 1.2 collective-permute-done.18.rest_2_
  73.2 1.5 shard_map.135
  75.4 1.3 collective-permute-start.21
  76.7 5.9 %shard_map.136 = (f32[8,256,128]{2,1,0:T(8,128)S(1)}, f32[8,256,128]{2,1,0:T(8,128)S(1)}, f32[8,256,128]{2,1,0:T(8,128)S(1)}) custom-call(f32[8,256,128]{2,1,0:T(8,128)S(1)} %get-tuple-element.93.p1, f32[8,256,128]{2,1,0:T(8,128)S(1)} %get-tuple-element.94.q1, f32[8,256,128]{2,1,0:T(8,128)S(1)} %bitcast.14, f32[8,256,128]{2,1,0:T(8,128)S(1)} %bitcast.18, ...), custom_call_target="tpu_custom_call" | custom-call | tf_op jit(solution)/shard_map/pallas_call | solution.py:36
  82.7 1.6 %collective-permute-done.21 = s16[704,128]{1,0:T(8,128)(2,1)S(1)} collective-permute-done((s16[704,128]{1,0:T(8,128)(2,1)S(1)}, s16[704,128]{1,0:T(8,128)(2,1)S(1)}, u32[]{:S(2)}, u32[]{:S(2)}) %collective-permute-start.21) | collective-permute-done | bytes 180256 | tf_op jit(solution)/shard_map/ppermute | solution.py:588
  86.3 11.5 %collective-permute-start.24 = (s16[704,128]{1,0:T(8,128)(2,1)S(1)}, s16[704,128]{1,0:T(8,128)(2,1)S(1)}, u32[]{:S(2)}, u32[]{:S(2)}) collective-permute-start(s16[704,128]{1,0:T(8,128)(2,1)S(1)} %collective-permute-done.21), channel_id=1, source_target_pairs={{0,4},{7,3},{8,12},{15,11},{16,20},{23,19},{24,28},{31,27},{32,36}... | collective-permute-start | bytes 540680 | tf_op jit(solution)/shard_map/ppermute | solution.py:598
  97.9 3.3 %collective-permute-done.24.rest_2_ = s16[704,128]{1,0:T(8,128)(2,1)S(1)} collective-permute-done((s16[704,128]{1,0:T(8,128)(2,1)S(1)}, s16[704,128]{1,0:T(8,128)(2,1)S(1)}, u32[]{:S(2)}, u32[]{:S(2)}) %collective-permute-start.24) | collective-permute-done | bytes 180256 | tf_op jit(solution)/shard_map/ppermute | solution.py:598
  101.2 3.0 %shard_map.137 = (f32[8,256,128]{2,1,0:T(8,128)}, f32[8,256,128]{2,1,0:T(8,128)}, f32[320,128]{1,0:T(8,128)S(1)}, s16[336,128]{1,0:T(8,128)(2,1)S(1)}, s16[336,1...) custom-call(s32[1,2]{1,0:T(1,128)S(1)} %copy-done.8, ...), custom_call_target="tpu_custom_call" | custom-call | tf_op jit(solution)/shard_map/pallas_call | solution.py:36
  104.2 4.4 %collective-permute-start.27 = (s16[336,128]{1,0:T(8,128)(2,1)S(1)}, s16[336,128]{1,0:T(8,128)(2,1)S(1)}, u32[]{:S(2)}, u32[]{:S(2)}) collective-permute-start(s16[336,128]{1,0:T(8,128)(2,1)S(1)} %get-tuple-element.114), channel_id=1, source_target_pairs={{0,7},{1,6},{2,5},{3,4},{4,3},{5,2},{6,1},{7,0},{8,15},{9,14},{10,... | collective-permute-start | bytes 258056 | tf_op jit(solution)/shard_map/ppermute | solution.py:501
  108.6 2.4 %collective-permute-start.28 = (s16[336,128]{1,0:T(8,128)(2,1)S(1)}, s16[336,128]{1,0:T(8,128)(2,1)S(1)}, u32[]{:S(2)}, u32[]{:S(2)}) collective-permute-start(s16[336,128]{1,0:T(8,128)(2,1)S(1)} %get-tuple-element.115), channel_id=1, source_target_pairs={{0,6},{1,7},{2,4},{3,5},{4,2},{5,3},{6,0},{7,1},{8,14},{9,15},{10,... | collective-permute-start | bytes 258056 | tf_op jit(solution)/shard_map/ppermute | solution.py:501
  111.0 8.7 %collective-permute-start.29 = (s16[336,128]{1,0:T(8,128)(2,1)S(1)}, s16[336,128]{1,0:T(8,128)(2,1)S(1)}, u32[]{:S(2)}, u32[]{:S(2)}) collective-permute-start(s16[336,128]{1,0:T(8,128)(2,1)S(1)} %get-tuple-element.116), channel_id=1, source_target_pairs={{0,5},{1,4},{2,7},{3,6},{4,1},{5,0},{6,3},{7,2},{8,13},{9,12},{10,... | collective-permute-start | bytes 258056 | tf_op jit(solution)/shard_map/ppermute | solution.py:501
  119.7 4.3 %collective-permute-start.31 = (s16[336,128]{1,0:T(8,128)(2,1)S(1)}, s16[336,128]{1,0:T(8,128)(2,1)S(1)}, u32[]{:S(2)}, u32[]{:S(2)}) collective-permute-start(s16[336,128]{1,0:T(8,128)(2,1)S(1)} %get-tuple-element.118), channel_id=1, source_target_pairs={{0,3},{1,2},{2,1},{3,0},{4,7},{5,6},{6,5},{7,4},{8,11},{9,10},{10,... | collective-permute-start | bytes 258056 | tf_op jit(solution)/shard_map/ppermute | solution.py:501
  124.0 0.9 collective-permute-start.33
  124.8 1.9 %collective-permute-done.29.refs_2_ = s16[336,128]{1,0:T(8,128)(2,1)S(1)} collective-permute-done((s16[336,128]{1,0:T(8,128)(2,1)S(1)}, s16[336,128]{1,0:T(8,128)(2,1)S(1)}, u32[]{:S(2)}, u32[]{:S(2)}) %collective-permute-start.29) | collective-permute-done | bytes 86048 | tf_op jit(solution)/shard_map/ppermute | solution.py:501
  126.7 2.3 %collective-permute-done.30.refs_3_ = s16[336,128]{1,0:T(8,128)(2,1)S(1)} collective-permute-done((s16[336,128]{1,0:T(8,128)(2,1)S(1)}, s16[336,128]{1,0:T(8,128)(2,1)S(1)}, u32[]{:S(2)}, u32[]{:S(2)}) %collective-permute-start.30) | collective-permute-done | bytes 86048 | tf_op jit(solution)/shard_map/ppermute | solution.py:501
  129.0 0.9 collective-permute-done.32.refs_5_
  130.0 0.9 shard_map.138
  130.9 2.2 %collective-permute-done.34.got = f32[1440,128]{1,0:T(8,128)S(1)} collective-permute-done((f32[1440,128]{1,0:T(8,128)S(1)}, f32[1440,128]{1,0:T(8,128)S(1)}, u32[]{:S(2)}, u32[]{:S(2)}) %collective-permute-start.34) | collective-permute-done | bytes 737312 | tf_op jit(solution)/shard_map/ppermute | solution.py:624
  133.1 1.2 shard_map.139
  134.9 2.4 %collective-permute-start.36 = (s16[992,128]{1,0:T(8,128)(2,1)S(1)}, s16[992,128]{1,0:T(8,128)(2,1)S(1)}, u32[]{:S(2)}, u32[]{:S(2)}) collective-permute-start(s16[992,128]{1,0:T(8,128)(2,1)S(1)} %get-tuple-element.125), channel_id=1, source_target_pairs={{0,128},{8,136},{16,144},{24,152},{32,160},{40,168},{48,176},{56,1... | collective-permute-start | bytes 761864 | tf_op jit(solution)/shard_map/ppermute | solution.py:501
  137.4 1.2 collective-permute-start.37
  138.6 10.7 %collective-permute-done.35.refs_0_ = s16[992,128]{1,0:T(8,128)(2,1)S(1)} collective-permute-done((s16[992,128]{1,0:T(8,128)(2,1)S(1)}, s16[992,128]{1,0:T(8,128)(2,1)S(1)}, u32[]{:S(2)}, u32[]{:S(2)}) %collective-permute-start.35) | collective-permute-done | bytes 253984 | tf_op jit(solution)/shard_map/ppermute | solution.py:501
  150.2 2.2 %collective-permute-start.38 = (s16[256,128]{1,0:T(8,128)(2,1)S(1)}, s16[256,128]{1,0:T(8,128)(2,1)S(1)}, u32[]{:S(2)}, u32[]{:S(2)}) collective-permute-start(s16[256,128]{1,0:T(8,128)(2,1)S(1)} %get-tuple-element.128), channel_id=1, source_target_pairs={{0,48},{8,56},{16,32},{24,40},{32,16},{40,24},{48,0},{56,8},{64,11... | collective-permute-start | bytes 196616 | tf_op jit(solution)/shard_map/ppermute | solution.py:501
  152.5 2.2 %collective-permute-start.39 = (s16[256,128]{1,0:T(8,128)(2,1)S(1)}, s16[256,128]{1,0:T(8,128)(2,1)S(1)}, u32[]{:S(2)}, u32[]{:S(2)}) collective-permute-start(s16[256,128]{1,0:T(8,128)(2,1)S(1)} %get-tuple-element.129), channel_id=1, source_target_pairs={{0,32},{8,40},{16,48},{24,56},{32,0},{40,8},{48,16},{56,24},{64,96... | collective-permute-start | bytes 196616 | tf_op jit(solution)/shard_map/ppermute | solution.py:501
  154.7 2.1 %collective-permute-done.38.refs_0_ = s16[256,128]{1,0:T(8,128)(2,1)S(1)} collective-permute-done((s16[256,128]{1,0:T(8,128)(2,1)S(1)}, s16[256,128]{1,0:T(8,128)(2,1)S(1)}, u32[]{:S(2)}, u32[]{:S(2)}) %collective-permute-start.38) | collective-permute-done | bytes 65568 | tf_op jit(solution)/shard_map/ppermute | solution.py:501
  156.9 2.5 %collective-permute-done.39.refs_1_ = s16[256,128]{1,0:T(8,128)(2,1)S(1)} collective-permute-done((s16[256,128]{1,0:T(8,128)(2,1)S(1)}, s16[256,128]{1,0:T(8,128)(2,1)S(1)}, u32[]{:S(2)}, u32[]{:S(2)}) %collective-permute-start.39) | collective-permute-done | bytes 65568 | tf_op jit(solution)/shard_map/ppermute | solution.py:501
  159.4 0.7 shard_map.141
  (71 shorter events, 10.0 us)
Async XLA Ops:
  0.6 14.2 %collective-permute-start.6 = (bf16[240,128]{1,0:T(8,128)(2,1)}, bf16[240,128]{1,0:T(8,128)(2,1)S(1)}, u32[]{:S(2)}, u32[]{:S(2)}) collective-permute-start(bf16[240,128]{1,0:T(8,128)(2,1)} %bitcast.23), channel_id=1, source_target_pairs={{0,52},{1,53},{2,54},{3,55},{4,48},{5,49},{6,50},{7,51},{8,60},{9,... | collective-permute-start | bytes 184328 | tf_op jit(solution)/shard_map/ppermute | solution.py:501
  6.6 8.5 %collective-permute-start.5 = (bf16[240,128]{1,0:T(8,128)(2,1)}, bf16[240,128]{1,0:T(8,128)(2,1)S(1)}, u32[]{:S(2)}, u32[]{:S(2)}) collective-permute-start(bf16[240,128]{1,0:T(8,128)(2,1)} %bitcast.24), channel_id=1, source_target_pairs={{0,36},{1,37},{2,38},{3,39},{4,32},{5,33},{6,34},{7,35},{8,44},{9,... | collective-permute-start | bytes 184328 | tf_op jit(solution)/shard_map/ppermute | solution.py:501
  7.1 13.3 %collective-permute-start.4 = (bf16[240,128]{1,0:T(8,128)(2,1)}, bf16[240,128]{1,0:T(8,128)(2,1)S(1)}, u32[]{:S(2)}, u32[]{:S(2)}) collective-permute-start(bf16[240,128]{1,0:T(8,128)(2,1)} %bitcast.25), channel_id=1, source_target_pairs={{0,20},{1,21},{2,22},{3,23},{4,16},{5,17},{6,18},{7,19},{8,28},{9,... | collective-permute-start | bytes 184328 | tf_op jit(solution)/shard_map/ppermute | solution.py:501
  11.1 10.3 %collective-permute-start.3 = (bf16[240,128]{1,0:T(8,128)(2,1)}, bf16[240,128]{1,0:T(8,128)(2,1)S(1)}, u32[]{:S(2)}, u32[]{:S(2)}) collective-permute-start(bf16[240,128]{1,0:T(8,128)(2,1)} %bitcast.26), channel_id=1, source_target_pairs={{0,4},{1,5},{2,6},{3,7},{4,0},{5,1},{6,2},{7,3},{8,12},{9,13},{10,... | collective-permute-start | bytes 184328 | tf_op jit(solution)/shard_map/ppermute | solution.py:501
  13.0 8.5 %collective-permute-start.2 = (bf16[240,128]{1,0:T(8,128)(2,1)}, bf16[240,128]{1,0:T(8,128)(2,1)S(1)}, u32[]{:S(2)}, u32[]{:S(2)}) collective-permute-start(bf16[240,128]{1,0:T(8,128)(2,1)} %bitcast.27), channel_id=1, source_target_pairs={{0,48},{1,49},{2,50},{3,51},{4,52},{5,53},{6,54},{7,55},{8,56},{9,... | collective-permute-start | bytes 184328 | tf_op jit(solution)/shard_map/ppermute | solution.py:501
  14.9 9.8 %collective-permute-start.1 = (bf16[240,128]{1,0:T(8,128)(2,1)}, bf16[240,128]{1,0:T(8,128)(2,1)S(1)}, u32[]{:S(2)}, u32[]{:S(2)}) collective-permute-start(bf16[240,128]{1,0:T(8,128)(2,1)} %bitcast.28), channel_id=1, source_target_pairs={{0,32},{1,33},{2,34},{3,35},{4,36},{5,37},{6,38},{7,39},{8,40},{9,... | collective-permute-start | bytes 184328 | tf_op jit(solution)/shard_map/ppermute | solution.py:501
  15.1 9.5 %collective-permute-start = (bf16[240,128]{1,0:T(8,128)(2,1)}, bf16[240,128]{1,0:T(8,128)(2,1)S(1)}, u32[]{:S(2)}, u32[]{:S(2)}) collective-permute-start(bf16[240,128]{1,0:T(8,128)(2,1)} %bitcast.29), channel_id=1, source_target_pairs={{0,16},{1,17},{2,18},{3,19},{4,20},{5,21},{6,22},{7,23},{8,24},{9,... | collective-permute-start | bytes 184328 | tf_op jit(solution)/shard_map/ppermute | solution.py:501
  19.8 4.8 %copy-start.7 = (bf16[6,40,128]{2,1,0:T(8,128)(2,1)S(1)}, bf16[6,40,128]{2,1,0:T(8,128)(2,1)}, u32[]{:S(2)}) copy-start(bf16[6,40,128]{2,1,0:T(8,128)(2,1)} %param.11) | copy-start | bytes 184324
  20.4 11.2 %copy-start.6 = (f32[1,64,512]{2,1,0:T(8,128)S(1)}, f32[1,64,512]{2,1,0:T(8,128)}, u32[]{:S(2)}) copy-start(f32[1,64,512]{2,1,0:T(8,128)} %param.16) | copy-start | bytes 393220
  20.4 29.5 %collective-permute-start.16 = (s16[2112,128]{1,0:T(8,128)(2,1)S(1)}, s16[2112,128]{1,0:T(8,128)(2,1)S(1)}, u32[]{:S(2)}, u32[]{:S(2)}) collective-permute-start(s16[2112,128]{1,0:T(8,128)(2,1)S(1)} %get-tuple-element.74), channel_id=1, source_target_pairs={{1,2},{3,4},{5,6},{2,1},{4,3},{6,5},{9,10},{11,12},{13,14},{10,9},... | collective-permute-start | bytes 1622024 | tf_op jit(solution)/shard_map/ppermute | solution.py:541
  21.5 3.2 %collective-permute-start.7 = (s32[1,2]{1,0:T(1,128)S(1)}, s32[1,2]{1,0:T(1,128)S(1)}, u32[]{:S(2)}, u32[]{:S(2)}) collective-permute-start(s32[1,2]{1,0:T(1,128)S(1)} %copy-done.8), channel_id=1, source_target_pairs={{0,8},{8,0},{16,24},{24,16},{32,40},{40,32},{48,56},{56,48},{64,72... | collective-permute-start | bytes 32 | tf_op jit(solution)/shard_map/ppermute | solution.py:533
  24.6 6.9 %copy-start.11 = (s32[1,3,512]{2,0,1:T(1,128)S(1)}, s32[1,3,512]{2,0,1:T(1,128)}, u32[]{:S(2)}) copy-start(s32[1,3,512]{2,0,1:T(1,128)} %param.15) | copy-start | bytes 18436
  24.6 40.1 %copy-start.5 = (f32[1,8,256,128]{3,2,1,0:T(8,128)S(1)}, f32[1,8,256,128]{3,2,1,0:T(8,128)}, u32[]{:S(2)}) copy-start(f32[1,8,256,128]{3,2,1,0:T(8,128)} %param.20) | copy-start | bytes 3145732
  24.7 24.0 %collective-permute-start.10 = (bf16[1920,128]{1,0:T(8,128)(2,1)S(1)}, bf16[1920,128]{1,0:T(8,128)(2,1)S(1)}, u32[]{:S(2)}, u32[]{:S(2)}) collective-permute-start(bf16[1920,128]{1,0:T(8,128)(2,1)S(1)} %shard_map.130.refs_0_), channel_id=1, source_target_pairs={{0,192},{8,200},{16,208},{24,216},{32,224},{40,232},{48,240},{56,2... | collective-permute-start | bytes 1474568 | tf_op jit(solution)/shard_map/ppermute | solution.py:501
  25.3 23.4 %collective-permute-start.9 = (bf16[1920,128]{1,0:T(8,128)(2,1)S(1)}, bf16[1920,128]{1,0:T(8,128)(2,1)S(1)}, u32[]{:S(2)}, u32[]{:S(2)}) collective-permute-start(bf16[1920,128]{1,0:T(8,128)(2,1)S(1)} %shard_map.130.refs_0_), channel_id=1, source_target_pairs={{0,128},{8,136},{16,144},{24,152},{32,160},{40,168},{48,176},{56,1... | collective-permute-start | bytes 1474568 | tf_op jit(solution)/shard_map/ppermute | solution.py:501
  27.7 21.6 %collective-permute-start.8 = (bf16[1920,128]{1,0:T(8,128)(2,1)S(1)}, bf16[1920,128]{1,0:T(8,128)(2,1)S(1)}, u32[]{:S(2)}, u32[]{:S(2)}) collective-permute-start(bf16[1920,128]{1,0:T(8,128)(2,1)S(1)} %shard_map.130.refs_0_), channel_id=1, source_target_pairs={{0,64},{8,72},{16,80},{24,88},{32,96},{40,104},{48,112},{56,120},{... | collective-permute-start | bytes 1474568 | tf_op jit(solution)/shard_map/ppermute | solution.py:501
  28.9 21.4 %collective-permute-start.15 = (s16[2112,128]{1,0:T(8,128)(2,1)S(1)}, s16[2112,128]{1,0:T(8,128)(2,1)S(1)}, u32[]{:S(2)}, u32[]{:S(2)}) collective-permute-start(s16[2112,128]{1,0:T(8,128)(2,1)S(1)} %get-tuple-element.67), channel_id=1, source_target_pairs={{0,1},{1,0},{2,3},{3,2},{4,5},{5,4},{6,7},{7,6},{8,9},{9,8},{10,11... | collective-permute-start | bytes 1622024 | tf_op jit(solution)/shard_map/ppermute | solution.py:540
  49.3 15.4 %copy-start.1 = (f32[1,8,256,128]{3,2,1,0:T(8,128)S(1)}, f32[1,8,256,128]{3,2,1,0:T(8,128)}, u32[]{:S(2)}) copy-start(f32[1,8,256,128]{3,2,1,0:T(8,128)} %param.19) | copy-start | bytes 3145732
  49.3 15.4 %copy-start.3 = (f32[1,8,256,128]{3,2,1,0:T(8,128)S(1)}, f32[1,8,256,128]{3,2,1,0:T(8,128)}, u32[]{:S(2)}) copy-start(f32[1,8,256,128]{3,2,1,0:T(8,128)} %param.21) | copy-start | bytes 3145732
  49.3 15.5 %copy-start.4 = (f32[1,8,256,128]{3,2,1,0:T(8,128)S(1)}, f32[1,8,256,128]{3,2,1,0:T(8,128)}, u32[]{:S(2)}) copy-start(f32[1,8,256,128]{3,2,1,0:T(8,128)} %param.18) | copy-start | bytes 3145732
  49.3 1.9 %collective-permute-start.11 = (bf16[1920,128]{1,0:T(8,128)(2,1)S(1)}, bf16[1920,128]{1,0:T(8,128)(2,1)S(1)}, u32[]{:S(2)}, u32[]{:S(2)}) collective-permute-start(bf16[1920,128]{1,0:T(8,128)(2,1)S(1)} %shard_map.130.refs_0_), channel_id=1, source_target_pairs={{0,8},{8,0},{16,24},{24,16},{32,40},{40,32},{48,56},{56,48},{64,72... | collective-permute-start | bytes 1474568 | tf_op jit(solution)/shard_map/ppermute | solution.py:549
  49.3 2.6 %collective-permute-start.12 = (bf16[1920,128]{1,0:T(8,128)(2,1)S(1)}, bf16[1920,128]{1,0:T(8,128)(2,1)S(1)}, u32[]{:S(2)}, u32[]{:S(2)}) collective-permute-start(bf16[1920,128]{1,0:T(8,128)(2,1)S(1)} %collective-permute-done.8.refs_1_), channel_id=1, source_target_pairs={{0,8},{8,0},{16,24},{24,16},{32,40},{40,32},{48,56},{56,48},{64,72... | collective-permute-start | bytes 1474568 | tf_op jit(solution)/shard_map/ppermute | solution.py:549
  49.8 2.8 %collective-permute-start.13 = (bf16[1920,128]{1,0:T(8,128)(2,1)S(1)}, bf16[1920,128]{1,0:T(8,128)(2,1)S(1)}, u32[]{:S(2)}, u32[]{:S(2)}) collective-permute-start(bf16[1920,128]{1,0:T(8,128)(2,1)S(1)} %collective-permute-done.9.refs_2_), channel_id=1, source_target_pairs={{0,8},{8,0},{16,24},{24,16},{32,40},{40,32},{48,56},{56,48},{64,72... | collective-permute-start | bytes 1474568 | tf_op jit(solution)/shard_map/ppermute | solution.py:549
  49.9 3.4 %collective-permute-start.14 = (bf16[1920,128]{1,0:T(8,128)(2,1)S(1)}, bf16[1920,128]{1,0:T(8,128)(2,1)S(1)}, u32[]{:S(2)}, u32[]{:S(2)}) collective-permute-start(bf16[1920,128]{1,0:T(8,128)(2,1)S(1)} %collective-permute-done.10.refs_3_), channel_id=1, source_target_pairs={{0,8},{8,0},{16,24},{24,16},{32,40},{40,32},{48,56},{56,48},{64,72... | collective-permute-start | bytes 1474568 | tf_op jit(solution)/shard_map/ppermute | solution.py:549
  54.4 16.6 %collective-permute-start.17 = (bf16[640,128]{1,0:T(8,128)(2,1)S(1)}, bf16[640,128]{1,0:T(8,128)(2,1)S(1)}, u32[]{:S(2)}, u32[]{:S(2)}) collective-permute-start(bf16[640,128]{1,0:T(8,128)(2,1)S(1)} %get-tuple-element.90), channel_id=1, source_target_pairs={{0,3},{1,2},{2,1},{3,0},{4,7},{5,6},{6,5},{7,4},{8,11},{9,10},{10,... | collective-permute-start | bytes 491528 | tf_op jit(solution)/shard_map/ppermute | solution.py:501
  63.6 8.6 %collective-permute-start.18 = (bf16[640,128]{1,0:T(8,128)(2,1)S(1)}, bf16[640,128]{1,0:T(8,128)(2,1)S(1)}, u32[]{:S(2)}, u32[]{:S(2)}) collective-permute-start(bf16[640,128]{1,0:T(8,128)(2,1)S(1)} %get-tuple-element.91), channel_id=1, source_target_pairs={{0,2},{1,3},{2,0},{3,1},{4,6},{5,7},{6,4},{7,5},{8,10},{9,11},{10,... | collective-permute-start | bytes 491528 | tf_op jit(solution)/shard_map/ppermute | solution.py:501
  63.6 8.9 %collective-permute-start.19 = (bf16[640,128]{1,0:T(8,128)(2,1)S(1)}, bf16[640,128]{1,0:T(8,128)(2,1)S(1)}, u32[]{:S(2)}, u32[]{:S(2)}) collective-permute-start(bf16[640,128]{1,0:T(8,128)(2,1)S(1)} %get-tuple-element.92), channel_id=1, source_target_pairs={{0,1},{1,0},{2,3},{3,2},{4,5},{5,4},{6,7},{7,6},{8,9},{9,8},{10,11... | collective-permute-start | bytes 491528 | tf_op jit(solution)/shard_map/ppermute | solution.py:501
  74.7 7.9 %collective-permute-start.20 = (s16[704,128]{1,0:T(8,128)(2,1)S(1)}, s16[704,128]{1,0:T(8,128)(2,1)S(1)}, u32[]{:S(2)}, u32[]{:S(2)}) collective-permute-start(s16[704,128]{1,0:T(8,128)(2,1)S(1)} %get-tuple-element.98), channel_id=1, source_target_pairs={{3,2},{4,5},{11,10},{12,13},{19,18},{20,21},{27,26},{28,29},{35,34... | collective-permute-start | bytes 540680 | tf_op jit(solution)/shard_map/ppermute | solution.py:588
  75.4 8.9 %collective-permute-start.21 = (s16[704,128]{1,0:T(8,128)(2,1)S(1)}, s16[704,128]{1,0:T(8,128)(2,1)S(1)}, u32[]{:S(2)}, u32[]{:S(2)}) collective-permute-start(s16[704,128]{1,0:T(8,128)(2,1)S(1)} %get-tuple-element.99), channel_id=1, source_target_pairs={{3,0},{4,7},{11,8},{12,15},{19,16},{20,23},{27,24},{28,31},{35,32}... | collective-permute-start | bytes 540680 | tf_op jit(solution)/shard_map/ppermute | solution.py:588
  84.3 16.9 %collective-permute-start.25 = (s16[2112,128]{1,0:T(8,128)(2,1)S(1)}, s16[2112,128]{1,0:T(8,128)(2,1)S(1)}, u32[]{:S(2)}, u32[]{:S(2)}) collective-permute-start(s16[2112,128]{1,0:T(8,128)(2,1)S(1)} %get-tuple-element.108), channel_id=1, source_target_pairs={{0,1},{1,0},{2,3},{3,2},{4,5},{5,4},{6,7},{7,6},{8,9},{9,8},{10,11... | collective-permute-start | bytes 1622024 | tf_op jit(solution)/shard_map/ppermute | solution.py:601
  84.3 16.9 %collective-permute-start.26 = (s16[2112,128]{1,0:T(8,128)(2,1)S(1)}, s16[2112,128]{1,0:T(8,128)(2,1)S(1)}, u32[]{:S(2)}, u32[]{:S(2)}) collective-permute-start(s16[2112,128]{1,0:T(8,128)(2,1)S(1)} %get-tuple-element.109), channel_id=1, source_target_pairs={{1,2},{5,6},{2,1},{6,5},{9,10},{13,14},{10,9},{14,13},{17,18},{21,... | collective-permute-start | bytes 1622024 | tf_op jit(solution)/shard_map/ppermute | solution.py:602
  85.0 12.9 %collective-permute-start.22 = (s16[704,128]{1,0:T(8,128)(2,1)S(1)}, s16[704,128]{1,0:T(8,128)(2,1)S(1)}, u32[]{:S(2)}, u32[]{:S(2)}) collective-permute-start(s16[704,128]{1,0:T(8,128)(2,1)S(1)} %get-tuple-element.105), channel_id=1, source_target_pairs={{3,4},{4,3},{11,12},{12,11},{19,20},{20,19},{27,28},{28,27},{35,36... | collective-permute-start | bytes 540680 | tf_op jit(solution)/shard_map/ppermute | solution.py:598
  85.6 12.2 %collective-permute-start.23 = (s16[704,128]{1,0:T(8,128)(2,1)S(1)}, s16[704,128]{1,0:T(8,128)(2,1)S(1)}, u32[]{:S(2)}, u32[]{:S(2)}) collective-permute-start(s16[704,128]{1,0:T(8,128)(2,1)S(1)} %collective-permute-done.20), channel_id=1, source_target_pairs={{2,4},{5,3},{10,12},{13,11},{18,20},{21,19},{26,28},{29,27},{34,36... | collective-permute-start | bytes 540680 | tf_op jit(solution)/shard_map/ppermute | solution.py:598
  86.3 14.9 %collective-permute-start.24 = (s16[704,128]{1,0:T(8,128)(2,1)S(1)}, s16[704,128]{1,0:T(8,128)(2,1)S(1)}, u32[]{:S(2)}, u32[]{:S(2)}) collective-permute-start(s16[704,128]{1,0:T(8,128)(2,1)S(1)} %collective-permute-done.21), channel_id=1, source_target_pairs={{0,4},{7,3},{8,12},{15,11},{16,20},{23,19},{24,28},{31,27},{32,36}... | collective-permute-start | bytes 540680 | tf_op jit(solution)/shard_map/ppermute | solution.py:598
  104.2 19.8 %collective-permute-start.27 = (s16[336,128]{1,0:T(8,128)(2,1)S(1)}, s16[336,128]{1,0:T(8,128)(2,1)S(1)}, u32[]{:S(2)}, u32[]{:S(2)}) collective-permute-start(s16[336,128]{1,0:T(8,128)(2,1)S(1)} %get-tuple-element.114), channel_id=1, source_target_pairs={{0,7},{1,6},{2,5},{3,4},{4,3},{5,2},{6,1},{7,0},{8,15},{9,14},{10,... | collective-permute-start | bytes 258056 | tf_op jit(solution)/shard_map/ppermute | solution.py:501
  108.6 15.4 %collective-permute-start.28 = (s16[336,128]{1,0:T(8,128)(2,1)S(1)}, s16[336,128]{1,0:T(8,128)(2,1)S(1)}, u32[]{:S(2)}, u32[]{:S(2)}) collective-permute-start(s16[336,128]{1,0:T(8,128)(2,1)S(1)} %get-tuple-element.115), channel_id=1, source_target_pairs={{0,6},{1,7},{2,4},{3,5},{4,2},{5,3},{6,0},{7,1},{8,14},{9,15},{10,... | collective-permute-start | bytes 258056 | tf_op jit(solution)/shard_map/ppermute | solution.py:501
  111.0 15.8 %collective-permute-start.29 = (s16[336,128]{1,0:T(8,128)(2,1)S(1)}, s16[336,128]{1,0:T(8,128)(2,1)S(1)}, u32[]{:S(2)}, u32[]{:S(2)}) collective-permute-start(s16[336,128]{1,0:T(8,128)(2,1)S(1)} %get-tuple-element.116), channel_id=1, source_target_pairs={{0,5},{1,4},{2,7},{3,6},{4,1},{5,0},{6,3},{7,2},{8,13},{9,12},{10,... | collective-permute-start | bytes 258056 | tf_op jit(solution)/shard_map/ppermute | solution.py:501
  119.7 9.3 %collective-permute-start.30 = (s16[336,128]{1,0:T(8,128)(2,1)S(1)}, s16[336,128]{1,0:T(8,128)(2,1)S(1)}, u32[]{:S(2)}, u32[]{:S(2)}) collective-permute-start(s16[336,128]{1,0:T(8,128)(2,1)S(1)} %get-tuple-element.117), channel_id=1, source_target_pairs={{0,4},{1,5},{2,6},{3,7},{4,0},{5,1},{6,2},{7,3},{8,12},{9,13},{10,... | collective-permute-start | bytes 258056 | tf_op jit(solution)/shard_map/ppermute | solution.py:501
  119.7 9.3 %collective-permute-start.31 = (s16[336,128]{1,0:T(8,128)(2,1)S(1)}, s16[336,128]{1,0:T(8,128)(2,1)S(1)}, u32[]{:S(2)}, u32[]{:S(2)}) collective-permute-start(s16[336,128]{1,0:T(8,128)(2,1)S(1)} %get-tuple-element.118), channel_id=1, source_target_pairs={{0,3},{1,2},{2,1},{3,0},{4,7},{5,6},{6,5},{7,4},{8,11},{9,10},{10,... | collective-permute-start | bytes 258056 | tf_op jit(solution)/shard_map/ppermute | solution.py:501
  124.0 6.0 %collective-permute-start.32 = (s16[336,128]{1,0:T(8,128)(2,1)S(1)}, s16[336,128]{1,0:T(8,128)(2,1)S(1)}, u32[]{:S(2)}, u32[]{:S(2)}) collective-permute-start(s16[336,128]{1,0:T(8,128)(2,1)S(1)} %get-tuple-element.119), channel_id=1, source_target_pairs={{0,2},{1,3},{2,0},{3,1},{4,6},{5,7},{6,4},{7,5},{8,10},{9,11},{10,... | collective-permute-start | bytes 258056 | tf_op jit(solution)/shard_map/ppermute | solution.py:501
  124.0 6.0 %collective-permute-start.33 = (s16[336,128]{1,0:T(8,128)(2,1)S(1)}, s16[336,128]{1,0:T(8,128)(2,1)S(1)}, u32[]{:S(2)}, u32[]{:S(2)}) collective-permute-start(s16[336,128]{1,0:T(8,128)(2,1)S(1)} %get-tuple-element.120), channel_id=1, source_target_pairs={{0,1},{1,0},{2,3},{3,2},{4,5},{5,4},{6,7},{7,6},{8,9},{9,8},{10,11... | collective-permute-start | bytes 258056 | tf_op jit(solution)/shard_map/ppermute | solution.py:501
  130.8 2.3 %collective-permute-start.34 = (f32[1440,128]{1,0:T(8,128)S(1)}, f32[1440,128]{1,0:T(8,128)S(1)}, u32[]{:S(2)}, u32[]{:S(2)}) collective-permute-start(f32[1440,128]{1,0:T(8,128)S(1)} %get-tuple-element.122), channel_id=1, source_target_pairs={{0,8},{8,0},{16,24},{24,16},{32,40},{40,32},{48,56},{56,48},{64,72... | collective-permute-start | bytes 2211848 | tf_op jit(solution)/shard_map/ppermute | solution.py:624
  134.4 14.9 %collective-permute-start.35 = (s16[992,128]{1,0:T(8,128)(2,1)S(1)}, s16[992,128]{1,0:T(8,128)(2,1)S(1)}, u32[]{:S(2)}, u32[]{:S(2)}) collective-permute-start(s16[992,128]{1,0:T(8,128)(2,1)S(1)} %get-tuple-element.124), channel_id=1, source_target_pairs={{0,192},{8,200},{16,208},{24,216},{32,224},{40,232},{48,240},{56,2... | collective-permute-start | bytes 761864 | tf_op jit(solution)/shard_map/ppermute | solution.py:501
  134.9 14.3 %collective-permute-start.36 = (s16[992,128]{1,0:T(8,128)(2,1)S(1)}, s16[992,128]{1,0:T(8,128)(2,1)S(1)}, u32[]{:S(2)}, u32[]{:S(2)}) collective-permute-start(s16[992,128]{1,0:T(8,128)(2,1)S(1)} %get-tuple-element.125), channel_id=1, source_target_pairs={{0,128},{8,136},{16,144},{24,152},{32,160},{40,168},{48,176},{56,1... | collective-permute-start | bytes 761864 | tf_op jit(solution)/shard_map/ppermute | solution.py:501
  137.4 12.5 %collective-permute-start.37 = (s16[992,128]{1,0:T(8,128)(2,1)S(1)}, s16[992,128]{1,0:T(8,128)(2,1)S(1)}, u32[]{:S(2)}, u32[]{:S(2)}) collective-permute-start(s16[992,128]{1,0:T(8,128)(2,1)S(1)} %get-tuple-element.126), channel_id=1, source_target_pairs={{0,64},{8,72},{16,80},{24,88},{32,96},{40,104},{48,112},{56,120},{... | collective-permute-start | bytes 761864 | tf_op jit(solution)/shard_map/ppermute | solution.py:501
  150.2 6.6 %collective-permute-start.38 = (s16[256,128]{1,0:T(8,128)(2,1)S(1)}, s16[256,128]{1,0:T(8,128)(2,1)S(1)}, u32[]{:S(2)}, u32[]{:S(2)}) collective-permute-start(s16[256,128]{1,0:T(8,128)(2,1)S(1)} %get-tuple-element.128), channel_id=1, source_target_pairs={{0,48},{8,56},{16,32},{24,40},{32,16},{40,24},{48,0},{56,8},{64,11... | collective-permute-start | bytes 196616 | tf_op jit(solution)/shard_map/ppermute | solution.py:501
  152.5 6.9 %collective-permute-start.39 = (s16[256,128]{1,0:T(8,128)(2,1)S(1)}, s16[256,128]{1,0:T(8,128)(2,1)S(1)}, u32[]{:S(2)}, u32[]{:S(2)}) collective-permute-start(s16[256,128]{1,0:T(8,128)(2,1)S(1)} %get-tuple-element.129), channel_id=1, source_target_pairs={{0,32},{8,40},{16,48},{24,56},{32,0},{40,8},{48,16},{56,24},{64,96... | collective-permute-start | bytes 196616 | tf_op jit(solution)/shard_map/ppermute | solution.py:501
  154.7 4.7 %collective-permute-start.40 = (s16[256,128]{1,0:T(8,128)(2,1)S(1)}, s16[256,128]{1,0:T(8,128)(2,1)S(1)}, u32[]{:S(2)}, u32[]{:S(2)}) collective-permute-start(s16[256,128]{1,0:T(8,128)(2,1)S(1)} %get-tuple-element.130), channel_id=1, source_target_pairs={{0,16},{8,24},{16,0},{24,8},{32,48},{40,56},{48,32},{56,40},{64,80... | collective-permute-start | bytes 196616 | tf_op jit(solution)/shard_map/ppermute | solution.py:501
  (5 other events, 4.9 us)

commit v11 on v9

--- a/solution.py
+++ b/solution.py
@@ -530,7 +530,6 @@
     between = functools.partial(across, groups)
 
     local = velocity.reshape(block, count_z)
-    other = lax.ppermute(anchors, "shot", swap("c", 1))
     near = [local] + exchange([local] * (HALVES * SIZE_Z - 1), ("shot", "dom"), functools.partial(swap_z, groups))
 
     half = halo_rows(2 * HALO, count_y)
@@ -541,7 +540,7 @@
     from_two = lax.ppermute(two, "dom", two_pairs)
 
     (line,) = call(join_kernel, (struct((len(near) * block, count_z), BF16),), near, "v" * len(near))
-    line, other, one = lax.optimization_barrier((line, other, one))
+    line, one = lax.optimization_barrier((line, one))
     field = struct((row_count, count_y, count_z), F32)
     hits = call(hit_kernel, (field, field), (start_step, receivers[0], traces[0]), "svv")
     plane = [line] + exchange([line] * (SIZE_X - 1), "shot", along["x"])
@@ -564,6 +563,8 @@
         "s" + "v" * len(plane),
         (pltpu.VMEM((HALVES, -(-(row_count * side + own_rows - 1) // own_rows) * block, count_z), F32),),
     )
+    *pieces, late_anchors = lax.optimization_barrier((*pieces, anchors))
+    other = lax.ppermute(late_anchors, "shot", swap("c", 1))
     pieces = [pieces[0]] + exchange(pieces[1:], "dom", between)[::-1]
 
     padded = pltpu.VMEM((row_count + 2 * HALO, count_y + 2 * PAD, count_z), F32)
@@ -633,7 +634,8 @@
         "ssvv",
         (total,),
     )
-    got = exchange(sends, "shot", along["x"])[::-1]
+    one_x, two_x, three_x = exchange(sends, "shot", along["x"])
+    got = (two_x, three_x, one_x)
 
     coded = struct((code_rows_of(own_rows, band), count_z), I16)
     own, *sends = call(

time: 158 us -> 157 us (level)
    ppermute x1, waiting for transfers between devices: 2.2 us -> 0.01 us  [body(): got = lax.ppermute(send, 'shot', swap('c', 1))]
    ppermute x1, waiting for transfers between devices: 0.01 us -> 1.7 us  [body(): other = lax.ppermute(late_anchors, 'shot', swap('c', 1))]
where the time goes in v11:
time: 157 us; the launch traced here: 156 us
  starting transfers between devices  74.7 us (48%)
  waiting for transfers between devices  51.9 us (33%)
  Pallas kernels  24.9 us (16%)
  local copies, waits for them, and re-layouts  3.16 us (2%)
    ppermute x26, starting transfers between devices, exchange(): got[k] = lax.ppermute(parts[k - 1], axis, pairs(k))  56.9 us
    ppermute x26, waiting for transfers between devices, exchange(): got[k] = lax.ppermute(parts[k - 1], axis, pairs(k))  38.9 us
    pallas_call x12, Pallas kernels, call(): pl.pallas_call(kernel, out_shape=list(outs), in_specs=[smem() if s == 's'...  24.9 us
    ppermute x3, starting transfers between devices, body(): lax.ppermute(part, 'dom', [(a ^ k, b) for a, b in (border, border[::-1])])  11.2 us
    ppermute x2, waiting for transfers between devices, body(): lax.ppermute(part, 'dom', [(a, a ^ k) for a in border])  8.28 us
    unnamed x25, local copies, waits for them, and re-layouts  3.16 us
  transfers between devices with their start and end apart: 41, of which 19 were waited for; matrix products, arithmetic and copies ran while one was open for 0% of the time, Pallas kernels for 10%

profile of v11, /device:TPU:6, one launch (start us, length us, event | category | flops | bytes accessed | tf_op | source)
XLA Modules:
  0.0 156.3 jit_solution(7126703850237392816)
XLA Ops:
  0.6 2.0 %collective-permute-start = (bf16[240,128]{1,0:T(8,128)(2,1)}, bf16[240,128]{1,0:T(8,128)(2,1)S(1)}, u32[]{:S(2)}, u32[]{:S(2)}) collective-permute-start(bf16[240,128]{1,0:T(8,128)(2,1)} %bitcast.23), channel_id=1, source_target_pairs={{0,16},{1,17},{2,18},{3,19},{4,20},{5,21},{6,22},{7,23},{8,24},{9,... | collective-permute-start | bytes 184328 | tf_op jit(solution)/shard_map/ppermute | solution.py:501
  2.6 3.3 %collective-permute-start.1 = (bf16[240,128]{1,0:T(8,128)(2,1)}, bf16[240,128]{1,0:T(8,128)(2,1)S(1)}, u32[]{:S(2)}, u32[]{:S(2)}) collective-permute-start(bf16[240,128]{1,0:T(8,128)(2,1)} %bitcast.24), channel_id=1, source_target_pairs={{0,32},{1,33},{2,34},{3,35},{4,36},{5,37},{6,38},{7,39},{8,40},{9,... | collective-permute-start | bytes 184328 | tf_op jit(solution)/shard_map/ppermute | solution.py:501
  5.9 6.4 %collective-permute-start.3 = (bf16[240,128]{1,0:T(8,128)(2,1)}, bf16[240,128]{1,0:T(8,128)(2,1)S(1)}, u32[]{:S(2)}, u32[]{:S(2)}) collective-permute-start(bf16[240,128]{1,0:T(8,128)(2,1)} %bitcast.26), channel_id=1, source_target_pairs={{0,4},{1,5},{2,6},{3,7},{4,0},{5,1},{6,2},{7,3},{8,12},{9,13},{10,... | collective-permute-start | bytes 184328 | tf_op jit(solution)/shard_map/ppermute | solution.py:501
  12.3 4.6 %collective-permute-start.5 = (bf16[240,128]{1,0:T(8,128)(2,1)}, bf16[240,128]{1,0:T(8,128)(2,1)S(1)}, u32[]{:S(2)}, u32[]{:S(2)}) collective-permute-start(bf16[240,128]{1,0:T(8,128)(2,1)} %bitcast.28), channel_id=1, source_target_pairs={{0,36},{1,37},{2,38},{3,39},{4,32},{5,33},{6,34},{7,35},{8,44},{9,... | collective-permute-start | bytes 184328 | tf_op jit(solution)/shard_map/ppermute | solution.py:501
  16.9 1.5 collective-permute-start.6
  18.4 1.2 copy-done
  19.6 1.2 copy-done.2
  21.4 1.7 %collective-permute-start.14 = (s16[2112,128]{1,0:T(8,128)(2,1)S(1)}, s16[2112,128]{1,0:T(8,128)(2,1)S(1)}, u32[]{:S(2)}, u32[]{:S(2)}) collective-permute-start(s16[2112,128]{1,0:T(8,128)(2,1)S(1)} %get-tuple-element.70), channel_id=1, source_target_pairs={{0,1},{1,0},{2,3},{3,2},{4,5},{5,4},{6,7},{7,6},{8,9},{9,8},{10,11... | collective-permute-start | bytes 1622024 | tf_op jit(solution)/shard_map/ppermute | solution.py:539
  23.8 0.9 collective-permute-start.7
  24.7 1.1 collective-permute-start.8
  25.8 2.8 %collective-permute-start.9 = (bf16[1920,128]{1,0:T(8,128)(2,1)S(1)}, bf16[1920,128]{1,0:T(8,128)(2,1)S(1)}, u32[]{:S(2)}, u32[]{:S(2)}) collective-permute-start(bf16[1920,128]{1,0:T(8,128)(2,1)S(1)} %shard_map.130.refs_0_), channel_id=1, source_target_pairs={{0,192},{8,200},{16,208},{24,216},{32,224},{40,232},{48,240},{56,2... | collective-permute-start | bytes 1474568 | tf_op jit(solution)/shard_map/ppermute | solution.py:501
  30.0 3.4 %shard_map.132 = (f32[8,256,128]{2,1,0:T(8,128)S(1)}, f32[8,256,128]{2,1,0:T(8,128)S(1)}) custom-call(s32[1]{0:T(128)S(6)} %copy.17.begin, s32[3,512]{1,0:T(4,128)S(1)} %bitcast.31, f32[64,512]{1,0:T(8,128)S(1)} %bitcast.22), custom_call_target="tpu_custom_call" | custom-call | tf_op jit(solution)/shard_map/pallas_call | solution.py:36
  33.3 4.7 %collective-permute-done.7.refs_1_ = bf16[1920,128]{1,0:T(8,128)(2,1)S(1)} collective-permute-done((bf16[1920,128]{1,0:T(8,128)(2,1)S(1)}, bf16[1920,128]{1,0:T(8,128)(2,1)S(1)}, u32[]{:S(2)}, u32[]{:S(2)}) %collective-permute-start.7) | collective-permute-done | bytes 491552 | tf_op jit(solution)/shard_map/ppermute | solution.py:501
  38.1 7.8 %collective-permute-done.8.refs_2_ = bf16[1920,128]{1,0:T(8,128)(2,1)S(1)} collective-permute-done((bf16[1920,128]{1,0:T(8,128)(2,1)S(1)}, bf16[1920,128]{1,0:T(8,128)(2,1)S(1)}, u32[]{:S(2)}, u32[]{:S(2)}) %collective-permute-start.8) | collective-permute-done | bytes 491552 | tf_op jit(solution)/shard_map/ppermute | solution.py:501
  45.8 2.6 %collective-permute-done.9.refs_3_ = bf16[1920,128]{1,0:T(8,128)(2,1)S(1)} collective-permute-done((bf16[1920,128]{1,0:T(8,128)(2,1)S(1)}, bf16[1920,128]{1,0:T(8,128)(2,1)S(1)}, u32[]{:S(2)}, u32[]{:S(2)}) %collective-permute-start.9) | collective-permute-done | bytes 491552 | tf_op jit(solution)/shard_map/ppermute | solution.py:501
  49.4 0.8 collective-permute-done.10.refs_4_
  50.2 0.7 collective-permute-done.11.refs_5_
  51.0 0.7 collective-permute-done.12.refs_6_
  51.7 0.7 collective-permute-done.13.refs_7_
  52.4 1.2 shard_map.134
  53.5 3.1 %collective-permute-start.16 = (bf16[640,128]{1,0:T(8,128)(2,1)S(1)}, bf16[640,128]{1,0:T(8,128)(2,1)S(1)}, u32[]{:S(2)}, u32[]{:S(2)}) collective-permute-start(bf16[640,128]{1,0:T(8,128)(2,1)S(1)} %get-tuple-element.97), channel_id=1, source_target_pairs={{0,3},{1,2},{2,1},{3,0},{4,7},{5,6},{6,5},{7,4},{8,11},{9,10},{10,... | collective-permute-start | bytes 491528 | tf_op jit(solution)/shard_map/ppermute | solution.py:501
  57.7 6.1 %shard_map.133 = (f32[8,256,128]{2,1,0:T(8,128)S(1)}, f32[8,256,128]{2,1,0:T(8,128)S(1)}, f32[8,256,128]{2,1,0:T(8,128)S(1)}, f32[8,256,128]{2,1,0:T(8,128)S(1)}) custom-call(f32[8,256,128]{2,1,0:T(8,128)S(1)} %bitcast.13, f32[8,256,128]{2,1,0:T(8,128)S(1)} %bitcast.17, f32[8,256,128]{2,1,0:T(8,128)S(1)} %bitcast.19, f32[8,256,128]{2,1,0:T(8,128)S(1)} %bitcast.21, ...), custom_call_target="tpu_custom_call" | custom-call | tf_op jit(solution)/shard_map/pallas_call | solution.py:36
  64.0 1.2 collective-permute-done.17.rest_2_
  66.0 1.5 shard_map.135
  68.2 1.3 collective-permute-start.21
  69.6 8.3 %collective-permute-done.21 = s16[704,128]{1,0:T(8,128)(2,1)S(1)} collective-permute-done((s16[704,128]{1,0:T(8,128)(2,1)S(1)}, s16[704,128]{1,0:T(8,128)(2,1)S(1)}, u32[]{:S(2)}, u32[]{:S(2)}) %collective-permute-start.21) | collective-permute-done | bytes 180256 | tf_op jit(solution)/shard_map/ppermute | solution.py:589
  77.8 0.7 collective-permute-start.25
  79.9 9.9 %collective-permute-start.23 = (s16[704,128]{1,0:T(8,128)(2,1)S(1)}, s16[704,128]{1,0:T(8,128)(2,1)S(1)}, u32[]{:S(2)}, u32[]{:S(2)}) collective-permute-start(s16[704,128]{1,0:T(8,128)(2,1)S(1)} %collective-permute-done.21), channel_id=1, source_target_pairs={{0,4},{7,3},{8,12},{15,11},{16,20},{23,19},{24,28},{31,27},{32,36}... | collective-permute-start | bytes 540680 | tf_op jit(solution)/shard_map/ppermute | solution.py:592
  89.8 5.9 %shard_map.136 = (f32[8,256,128]{2,1,0:T(8,128)S(1)}, f32[8,256,128]{2,1,0:T(8,128)S(1)}, f32[8,256,128]{2,1,0:T(8,128)S(1)}) custom-call(f32[8,256,128]{2,1,0:T(8,128)S(1)} %get-tuple-element.100.p1, f32[8,256,128]{2,1,0:T(8,128)S(1)} %get-tuple-element.101.q1, f32[8,256,128]{2,1,0:T(8,128)S(1)} %bitcast.14, f32[8,256,128]{2,1,0:T(8,128)S(1)} %bitcast.18, ...), custom_call_target="tpu_custom_call" | custom-call | tf_op jit(solution)/shard_map/pallas_call | solution.py:36
  95.8 3.0 %shard_map.137 = (f32[8,256,128]{2,1,0:T(8,128)}, f32[8,256,128]{2,1,0:T(8,128)}, f32[320,128]{1,0:T(8,128)S(1)}, s16[336,128]{1,0:T(8,128)(2,1)S(1)}, s16[336,1...) custom-call(s32[1,2]{1,0:T(1,128)S(1)} %copy-done.8, ...), custom_call_target="tpu_custom_call" | custom-call | tf_op jit(solution)/shard_map/pallas_call | solution.py:36
  98.8 4.8 %collective-permute-start.27 = (s16[336,128]{1,0:T(8,128)(2,1)S(1)}, s16[336,128]{1,0:T(8,128)(2,1)S(1)}, u32[]{:S(2)}, u32[]{:S(2)}) collective-permute-start(s16[336,128]{1,0:T(8,128)(2,1)S(1)} %get-tuple-element.120), channel_id=1, source_target_pairs={{0,7},{1,6},{2,5},{3,4},{4,3},{5,2},{6,1},{7,0},{8,15},{9,14},{10,... | collective-permute-start | bytes 258056 | tf_op jit(solution)/shard_map/ppermute | solution.py:501
  103.6 8.8 %collective-permute-start.29 = (s16[336,128]{1,0:T(8,128)(2,1)S(1)}, s16[336,128]{1,0:T(8,128)(2,1)S(1)}, u32[]{:S(2)}, u32[]{:S(2)}) collective-permute-start(s16[336,128]{1,0:T(8,128)(2,1)S(1)} %get-tuple-element.122), channel_id=1, source_target_pairs={{0,5},{1,4},{2,7},{3,6},{4,1},{5,0},{6,3},{7,2},{8,13},{9,12},{10,... | collective-permute-start | bytes 258056 | tf_op jit(solution)/shard_map/ppermute | solution.py:501
  113.1 4.5 %collective-permute-start.31 = (s16[336,128]{1,0:T(8,128)(2,1)S(1)}, s16[336,128]{1,0:T(8,128)(2,1)S(1)}, u32[]{:S(2)}, u32[]{:S(2)}) collective-permute-start(s16[336,128]{1,0:T(8,128)(2,1)S(1)} %get-tuple-element.124), channel_id=1, source_target_pairs={{0,3},{1,2},{2,1},{3,0},{4,7},{5,6},{6,5},{7,4},{8,11},{9,10},{10,... | collective-permute-start | bytes 258056 | tf_op jit(solution)/shard_map/ppermute | solution.py:501
  117.6 0.9 collective-permute-start.33
  118.4 2.8 %collective-permute-done.30.refs_3_ = s16[336,128]{1,0:T(8,128)(2,1)S(1)} collective-permute-done((s16[336,128]{1,0:T(8,128)(2,1)S(1)}, s16[336,128]{1,0:T(8,128)(2,1)S(1)}, u32[]{:S(2)}, u32[]{:S(2)}) %collective-permute-start.30) | collective-permute-done | bytes 86048 | tf_op jit(solution)/shard_map/ppermute | solution.py:501
  121.3 2.3 %collective-permute-done.32.refs_5_ = s16[336,128]{1,0:T(8,128)(2,1)S(1)} collective-permute-done((s16[336,128]{1,0:T(8,128)(2,1)S(1)}, s16[336,128]{1,0:T(8,128)(2,1)S(1)}, u32[]{:S(2)}, u32[]{:S(2)}) %collective-permute-start.32) | collective-permute-done | bytes 86048 | tf_op jit(solution)/shard_map/ppermute | solution.py:501
  123.6 0.9 shard_map.138
  125.0 1.7 %collective-permute-done.26.other = s32[1,2]{1,0:T(1,128)S(1)} collective-permute-done((s32[1,2]{1,0:T(1,128)S(1)}, s32[1,2]{1,0:T(1,128)S(1)}, u32[]{:S(2)}, u32[]{:S(2)}) %collective-permute-start.26) | collective-permute-done | bytes 40 | tf_op jit(solution)/shard_map/ppermute | solution.py:567
  126.8 1.2 shard_map.139
  128.0 0.8 collective-permute-start.35
  128.7 1.7 %collective-permute-start.36 = (s16[992,128]{1,0:T(8,128)(2,1)S(1)}, s16[992,128]{1,0:T(8,128)(2,1)S(1)}, u32[]{:S(2)}, u32[]{:S(2)}) collective-permute-start(s16[992,128]{1,0:T(8,128)(2,1)S(1)} %get-tuple-element.131), channel_id=1, source_target_pairs={{0,192},{8,200},{16,208},{24,216},{32,224},{40,232},{48,240},{56,2... | collective-permute-start | bytes 761864 | tf_op jit(solution)/shard_map/ppermute | solution.py:501
  130.5 1.1 collective-permute-start.37
  131.6 7.0 %collective-permute-done.35.refs_0_ = s16[992,128]{1,0:T(8,128)(2,1)S(1)} collective-permute-done((s16[992,128]{1,0:T(8,128)(2,1)S(1)}, s16[992,128]{1,0:T(8,128)(2,1)S(1)}, u32[]{:S(2)}, u32[]{:S(2)}) %collective-permute-start.35) | collective-permute-done | bytes 253984 | tf_op jit(solution)/shard_map/ppermute | solution.py:501
  138.6 4.6 %collective-permute-done.36.refs_1_ = s16[992,128]{1,0:T(8,128)(2,1)S(1)} collective-permute-done((s16[992,128]{1,0:T(8,128)(2,1)S(1)}, s16[992,128]{1,0:T(8,128)(2,1)S(1)}, u32[]{:S(2)}, u32[]{:S(2)}) %collective-permute-start.36) | collective-permute-done | bytes 253984 | tf_op jit(solution)/shard_map/ppermute | solution.py:501
  143.6 3.3 %collective-permute-start.38 = (s16[256,128]{1,0:T(8,128)(2,1)S(1)}, s16[256,128]{1,0:T(8,128)(2,1)S(1)}, u32[]{:S(2)}, u32[]{:S(2)}) collective-permute-start(s16[256,128]{1,0:T(8,128)(2,1)S(1)} %get-tuple-element.134), channel_id=1, source_target_pairs={{0,48},{8,56},{16,32},{24,40},{32,16},{40,24},{48,0},{56,8},{64,11... | collective-permute-start | bytes 196616 | tf_op jit(solution)/shard_map/ppermute | solution.py:501
  146.9 3.7 %collective-permute-start.39 = (s16[256,128]{1,0:T(8,128)(2,1)S(1)}, s16[256,128]{1,0:T(8,128)(2,1)S(1)}, u32[]{:S(2)}, u32[]{:S(2)}) collective-permute-start(s16[256,128]{1,0:T(8,128)(2,1)S(1)} %get-tuple-element.135), channel_id=1, source_target_pairs={{0,32},{8,40},{16,48},{24,56},{32,0},{40,8},{48,16},{56,24},{64,96... | collective-permute-start | bytes 196616 | tf_op jit(solution)/shard_map/ppermute | solution.py:501
  150.6 4.7 %collective-permute-done.39.refs_1_ = s16[256,128]{1,0:T(8,128)(2,1)S(1)} collective-permute-done((s16[256,128]{1,0:T(8,128)(2,1)S(1)}, s16[256,128]{1,0:T(8,128)(2,1)S(1)}, u32[]{:S(2)}, u32[]{:S(2)}) %collective-permute-start.39) | collective-permute-done | bytes 65568 | tf_op jit(solution)/shard_map/ppermute | solution.py:501
  155.6 0.7 shard_map.141
  (71 shorter events, 9.0 us)
Async XLA Ops:
  0.6 11.7 %collective-permute-start = (bf16[240,128]{1,0:T(8,128)(2,1)}, bf16[240,128]{1,0:T(8,128)(2,1)S(1)}, u32[]{:S(2)}, u32[]{:S(2)}) collective-permute-start(bf16[240,128]{1,0:T(8,128)(2,1)} %bitcast.23), channel_id=1, source_target_pairs={{0,16},{1,17},{2,18},{3,19},{4,20},{5,21},{6,22},{7,23},{8,24},{9,... | collective-permute-start | bytes 184328 | tf_op jit(solution)/shard_map/ppermute | solution.py:501
  2.6 14.3 %collective-permute-start.1 = (bf16[240,128]{1,0:T(8,128)(2,1)}, bf16[240,128]{1,0:T(8,128)(2,1)S(1)}, u32[]{:S(2)}, u32[]{:S(2)}) collective-permute-start(bf16[240,128]{1,0:T(8,128)(2,1)} %bitcast.24), channel_id=1, source_target_pairs={{0,32},{1,33},{2,34},{3,35},{4,36},{5,37},{6,38},{7,39},{8,40},{9,... | collective-permute-start | bytes 184328 | tf_op jit(solution)/shard_map/ppermute | solution.py:501
  5.9 15.5 %collective-permute-start.2 = (bf16[240,128]{1,0:T(8,128)(2,1)}, bf16[240,128]{1,0:T(8,128)(2,1)S(1)}, u32[]{:S(2)}, u32[]{:S(2)}) collective-permute-start(bf16[240,128]{1,0:T(8,128)(2,1)} %bitcast.25), channel_id=1, source_target_pairs={{0,48},{1,49},{2,50},{3,51},{4,52},{5,53},{6,54},{7,55},{8,56},{9,... | collective-permute-start | bytes 184328 | tf_op jit(solution)/shard_map/ppermute | solution.py:501
  5.9 17.2 %collective-permute-start.3 = (bf16[240,128]{1,0:T(8,128)(2,1)}, bf16[240,128]{1,0:T(8,128)(2,1)S(1)}, u32[]{:S(2)}, u32[]{:S(2)}) collective-permute-start(bf16[240,128]{1,0:T(8,128)(2,1)} %bitcast.26), channel_id=1, source_target_pairs={{0,4},{1,5},{2,6},{3,7},{4,0},{5,1},{6,2},{7,3},{8,12},{9,13},{10,... | collective-permute-start | bytes 184328 | tf_op jit(solution)/shard_map/ppermute | solution.py:501
  12.3 10.8 %collective-permute-start.4 = (bf16[240,128]{1,0:T(8,128)(2,1)}, bf16[240,128]{1,0:T(8,128)(2,1)S(1)}, u32[]{:S(2)}, u32[]{:S(2)}) collective-permute-start(bf16[240,128]{1,0:T(8,128)(2,1)} %bitcast.27), channel_id=1, source_target_pairs={{0,20},{1,21},{2,22},{3,23},{4,16},{5,17},{6,18},{7,19},{8,28},{9,... | collective-permute-start | bytes 184328 | tf_op jit(solution)/shard_map/ppermute | solution.py:501
  12.3 10.8 %collective-permute-start.5 = (bf16[240,128]{1,0:T(8,128)(2,1)}, bf16[240,128]{1,0:T(8,128)(2,1)S(1)}, u32[]{:S(2)}, u32[]{:S(2)}) collective-permute-start(bf16[240,128]{1,0:T(8,128)(2,1)} %bitcast.28), channel_id=1, source_target_pairs={{0,36},{1,37},{2,38},{3,39},{4,32},{5,33},{6,34},{7,35},{8,44},{9,... | collective-permute-start | bytes 184328 | tf_op jit(solution)/shard_map/ppermute | solution.py:501
  16.9 6.9 %collective-permute-start.6 = (bf16[240,128]{1,0:T(8,128)(2,1)}, bf16[240,128]{1,0:T(8,128)(2,1)S(1)}, u32[]{:S(2)}, u32[]{:S(2)}) collective-permute-start(bf16[240,128]{1,0:T(8,128)(2,1)} %bitcast.29), channel_id=1, source_target_pairs={{0,52},{1,53},{2,54},{3,55},{4,48},{5,49},{6,50},{7,51},{8,60},{9,... | collective-permute-start | bytes 184328 | tf_op jit(solution)/shard_map/ppermute | solution.py:501
  20.8 31.5 %copy-start.8 = (s32[1,2]{1,0:T(1,128)S(1)}, s32[1,2]{1,0:T(1,128)}, u32[]{:S(2)}) copy-start(s32[1,2]{1,0:T(1,128)} %anchors.9) | copy-start | bytes 28
  21.4 8.6 %copy-start.6 = (f32[1,64,512]{2,1,0:T(8,128)S(1)}, f32[1,64,512]{2,1,0:T(8,128)}, u32[]{:S(2)}) copy-start(f32[1,64,512]{2,1,0:T(8,128)} %param.16) | copy-start | bytes 393220
  21.4 27.6 %collective-permute-start.14 = (s16[2112,128]{1,0:T(8,128)(2,1)S(1)}, s16[2112,128]{1,0:T(8,128)(2,1)S(1)}, u32[]{:S(2)}, u32[]{:S(2)}) collective-permute-start(s16[2112,128]{1,0:T(8,128)(2,1)S(1)} %get-tuple-element.70), channel_id=1, source_target_pairs={{0,1},{1,0},{2,3},{3,2},{4,5},{5,4},{6,7},{7,6},{8,9},{9,8},{10,11... | collective-permute-start | bytes 1622024 | tf_op jit(solution)/shard_map/ppermute | solution.py:539
  23.1 6.9 %copy-start.11 = (s32[1,3,512]{2,0,1:T(1,128)S(1)}, s32[1,3,512]{2,0,1:T(1,128)}, u32[]{:S(2)}) copy-start(s32[1,3,512]{2,0,1:T(1,128)} %param.15) | copy-start | bytes 18436
  23.8 33.9 %copy-start.5 = (f32[1,8,256,128]{3,2,1,0:T(8,128)S(1)}, f32[1,8,256,128]{3,2,1,0:T(8,128)}, u32[]{:S(2)}) copy-start(f32[1,8,256,128]{3,2,1,0:T(8,128)} %param.20) | copy-start | bytes 3145732
  23.8 14.2 %collective-permute-start.7 = (bf16[1920,128]{1,0:T(8,128)(2,1)S(1)}, bf16[1920,128]{1,0:T(8,128)(2,1)S(1)}, u32[]{:S(2)}, u32[]{:S(2)}) collective-permute-start(bf16[1920,128]{1,0:T(8,128)(2,1)S(1)} %shard_map.130.refs_0_), channel_id=1, source_target_pairs={{0,64},{8,72},{16,80},{24,88},{32,96},{40,104},{48,112},{56,120},{... | collective-permute-start | bytes 1474568 | tf_op jit(solution)/shard_map/ppermute | solution.py:501
  24.7 21.1 %collective-permute-start.8 = (bf16[1920,128]{1,0:T(8,128)(2,1)S(1)}, bf16[1920,128]{1,0:T(8,128)(2,1)S(1)}, u32[]{:S(2)}, u32[]{:S(2)}) collective-permute-start(bf16[1920,128]{1,0:T(8,128)(2,1)S(1)} %shard_map.130.refs_0_), channel_id=1, source_target_pairs={{0,128},{8,136},{16,144},{24,152},{32,160},{40,168},{48,176},{56,1... | collective-permute-start | bytes 1474568 | tf_op jit(solution)/shard_map/ppermute | solution.py:501
  25.8 22.5 %collective-permute-start.9 = (bf16[1920,128]{1,0:T(8,128)(2,1)S(1)}, bf16[1920,128]{1,0:T(8,128)(2,1)S(1)}, u32[]{:S(2)}, u32[]{:S(2)}) collective-permute-start(bf16[1920,128]{1,0:T(8,128)(2,1)S(1)} %shard_map.130.refs_0_), channel_id=1, source_target_pairs={{0,192},{8,200},{16,208},{24,216},{32,224},{40,232},{48,240},{56,2... | collective-permute-start | bytes 1474568 | tf_op jit(solution)/shard_map/ppermute | solution.py:501
  28.6 20.8 %collective-permute-start.15 = (s16[2112,128]{1,0:T(8,128)(2,1)S(1)}, s16[2112,128]{1,0:T(8,128)(2,1)S(1)}, u32[]{:S(2)}, u32[]{:S(2)}) collective-permute-start(s16[2112,128]{1,0:T(8,128)(2,1)S(1)} %get-tuple-element.77), channel_id=1, source_target_pairs={{1,2},{3,4},{5,6},{2,1},{4,3},{6,5},{9,10},{11,12},{13,14},{10,9},... | collective-permute-start | bytes 1622024 | tf_op jit(solution)/shard_map/ppermute | solution.py:540
  48.4 9.3 %copy-start.1 = (f32[1,8,256,128]{3,2,1,0:T(8,128)S(1)}, f32[1,8,256,128]{3,2,1,0:T(8,128)}, u32[]{:S(2)}) copy-start(f32[1,8,256,128]{3,2,1,0:T(8,128)} %param.19) | copy-start | bytes 3145732
  48.4 9.3 %copy-start.3 = (f32[1,8,256,128]{3,2,1,0:T(8,128)S(1)}, f32[1,8,256,128]{3,2,1,0:T(8,128)}, u32[]{:S(2)}) copy-start(f32[1,8,256,128]{3,2,1,0:T(8,128)} %param.21) | copy-start | bytes 3145732
  48.4 9.3 %copy-start.4 = (f32[1,8,256,128]{3,2,1,0:T(8,128)S(1)}, f32[1,8,256,128]{3,2,1,0:T(8,128)}, u32[]{:S(2)}) copy-start(f32[1,8,256,128]{3,2,1,0:T(8,128)} %param.18) | copy-start | bytes 3145732
  48.4 1.9 %collective-permute-start.10 = (bf16[1920,128]{1,0:T(8,128)(2,1)S(1)}, bf16[1920,128]{1,0:T(8,128)(2,1)S(1)}, u32[]{:S(2)}, u32[]{:S(2)}) collective-permute-start(bf16[1920,128]{1,0:T(8,128)(2,1)S(1)} %shard_map.130.refs_0_), channel_id=1, source_target_pairs={{0,8},{8,0},{16,24},{24,16},{32,40},{40,32},{48,56},{56,48},{64,72... | collective-permute-start | bytes 1474568 | tf_op jit(solution)/shard_map/ppermute | solution.py:548
  48.4 2.6 %collective-permute-start.11 = (bf16[1920,128]{1,0:T(8,128)(2,1)S(1)}, bf16[1920,128]{1,0:T(8,128)(2,1)S(1)}, u32[]{:S(2)}, u32[]{:S(2)}) collective-permute-start(bf16[1920,128]{1,0:T(8,128)(2,1)S(1)} %collective-permute-done.7.refs_1_), channel_id=1, source_target_pairs={{0,8},{8,0},{16,24},{24,16},{32,40},{40,32},{48,56},{56,48},{64,72... | collective-permute-start | bytes 1474568 | tf_op jit(solution)/shard_map/ppermute | solution.py:548
  48.9 2.8 %collective-permute-start.12 = (bf16[1920,128]{1,0:T(8,128)(2,1)S(1)}, bf16[1920,128]{1,0:T(8,128)(2,1)S(1)}, u32[]{:S(2)}, u32[]{:S(2)}) collective-permute-start(bf16[1920,128]{1,0:T(8,128)(2,1)S(1)} %collective-permute-done.8.refs_2_), channel_id=1, source_target_pairs={{0,8},{8,0},{16,24},{24,16},{32,40},{40,32},{48,56},{56,48},{64,72... | collective-permute-start | bytes 1474568 | tf_op jit(solution)/shard_map/ppermute | solution.py:548
  49.0 3.4 %collective-permute-start.13 = (bf16[1920,128]{1,0:T(8,128)(2,1)S(1)}, bf16[1920,128]{1,0:T(8,128)(2,1)S(1)}, u32[]{:S(2)}, u32[]{:S(2)}) collective-permute-start(bf16[1920,128]{1,0:T(8,128)(2,1)S(1)} %collective-permute-done.9.refs_3_), channel_id=1, source_target_pairs={{0,8},{8,0},{16,24},{24,16},{32,40},{40,32},{48,56},{56,48},{64,72... | collective-permute-start | bytes 1474568 | tf_op jit(solution)/shard_map/ppermute | solution.py:548
  53.5 10.5 %collective-permute-start.16 = (bf16[640,128]{1,0:T(8,128)(2,1)S(1)}, bf16[640,128]{1,0:T(8,128)(2,1)S(1)}, u32[]{:S(2)}, u32[]{:S(2)}) collective-permute-start(bf16[640,128]{1,0:T(8,128)(2,1)S(1)} %get-tuple-element.97), channel_id=1, source_target_pairs={{0,3},{1,2},{2,1},{3,0},{4,7},{5,6},{6,5},{7,4},{8,11},{9,10},{10,... | collective-permute-start | bytes 491528 | tf_op jit(solution)/shard_map/ppermute | solution.py:501
  56.6 8.6 %collective-permute-start.17 = (bf16[640,128]{1,0:T(8,128)(2,1)S(1)}, bf16[640,128]{1,0:T(8,128)(2,1)S(1)}, u32[]{:S(2)}, u32[]{:S(2)}) collective-permute-start(bf16[640,128]{1,0:T(8,128)(2,1)S(1)} %get-tuple-element.98), channel_id=1, source_target_pairs={{0,2},{1,3},{2,0},{3,1},{4,6},{5,7},{6,4},{7,5},{8,10},{9,11},{10,... | collective-permute-start | bytes 491528 | tf_op jit(solution)/shard_map/ppermute | solution.py:501
  57.3 8.1 %collective-permute-start.18 = (bf16[640,128]{1,0:T(8,128)(2,1)S(1)}, bf16[640,128]{1,0:T(8,128)(2,1)S(1)}, u32[]{:S(2)}, u32[]{:S(2)}) collective-permute-start(bf16[640,128]{1,0:T(8,128)(2,1)S(1)} %get-tuple-element.99), channel_id=1, source_target_pairs={{0,1},{1,0},{2,3},{3,2},{4,5},{5,4},{6,7},{7,6},{8,9},{9,8},{10,11... | collective-permute-start | bytes 491528 | tf_op jit(solution)/shard_map/ppermute | solution.py:501
  67.6 2.0 %collective-permute-start.20 = (s16[704,128]{1,0:T(8,128)(2,1)S(1)}, s16[704,128]{1,0:T(8,128)(2,1)S(1)}, u32[]{:S(2)}, u32[]{:S(2)}) collective-permute-start(s16[704,128]{1,0:T(8,128)(2,1)S(1)} %get-tuple-element.110), channel_id=1, source_target_pairs={{3,2},{4,5},{11,10},{12,13},{19,18},{20,21},{27,26},{28,29},{35,34... | collective-permute-start | bytes 540680 | tf_op jit(solution)/shard_map/ppermute | solution.py:589
  68.2 9.6 %collective-permute-start.21 = (s16[704,128]{1,0:T(8,128)(2,1)S(1)}, s16[704,128]{1,0:T(8,128)(2,1)S(1)}, u32[]{:S(2)}, u32[]{:S(2)}) collective-permute-start(s16[704,128]{1,0:T(8,128)(2,1)S(1)} %get-tuple-element.111), channel_id=1, source_target_pairs={{3,0},{4,7},{11,8},{12,15},{19,16},{20,23},{27,24},{28,31},{35,32}... | collective-permute-start | bytes 540680 | tf_op jit(solution)/shard_map/ppermute | solution.py:589
  77.8 17.9 %collective-permute-start.24 = (s16[2112,128]{1,0:T(8,128)(2,1)S(1)}, s16[2112,128]{1,0:T(8,128)(2,1)S(1)}, u32[]{:S(2)}, u32[]{:S(2)}) collective-permute-start(s16[2112,128]{1,0:T(8,128)(2,1)S(1)} %get-tuple-element.114), channel_id=1, source_target_pairs={{0,1},{1,0},{2,3},{3,2},{4,5},{5,4},{6,7},{7,6},{8,9},{9,8},{10,11... | collective-permute-start | bytes 1622024 | tf_op jit(solution)/shard_map/ppermute | solution.py:595
  77.8 17.9 %collective-permute-start.25 = (s16[2112,128]{1,0:T(8,128)(2,1)S(1)}, s16[2112,128]{1,0:T(8,128)(2,1)S(1)}, u32[]{:S(2)}, u32[]{:S(2)}) collective-permute-start(s16[2112,128]{1,0:T(8,128)(2,1)S(1)} %get-tuple-element.115), channel_id=1, source_target_pairs={{1,2},{5,6},{2,1},{6,5},{9,10},{13,14},{10,9},{14,13},{17,18},{21,... | collective-permute-start | bytes 1622024 | tf_op jit(solution)/shard_map/ppermute | solution.py:596
  78.5 17.2 %collective-permute-start.19 = (s16[704,128]{1,0:T(8,128)(2,1)S(1)}, s16[704,128]{1,0:T(8,128)(2,1)S(1)}, u32[]{:S(2)}, u32[]{:S(2)}) collective-permute-start(s16[704,128]{1,0:T(8,128)(2,1)S(1)} %get-tuple-element.107), channel_id=1, source_target_pairs={{3,4},{4,3},{11,12},{12,11},{19,20},{20,19},{27,28},{28,27},{35,36... | collective-permute-start | bytes 540680 | tf_op jit(solution)/shard_map/ppermute | solution.py:592
  79.2 16.5 %collective-permute-start.22 = (s16[704,128]{1,0:T(8,128)(2,1)S(1)}, s16[704,128]{1,0:T(8,128)(2,1)S(1)}, u32[]{:S(2)}, u32[]{:S(2)}) collective-permute-start(s16[704,128]{1,0:T(8,128)(2,1)S(1)} %collective-permute-done.20), channel_id=1, source_target_pairs={{2,4},{5,3},{10,12},{13,11},{18,20},{21,19},{26,28},{29,27},{34,36... | collective-permute-start | bytes 540680 | tf_op jit(solution)/shard_map/ppermute | solution.py:592
  79.9 15.8 %collective-permute-start.23 = (s16[704,128]{1,0:T(8,128)(2,1)S(1)}, s16[704,128]{1,0:T(8,128)(2,1)S(1)}, u32[]{:S(2)}, u32[]{:S(2)}) collective-permute-start(s16[704,128]{1,0:T(8,128)(2,1)S(1)} %collective-permute-done.21), channel_id=1, source_target_pairs={{0,4},{7,3},{8,12},{15,11},{16,20},{23,19},{24,28},{31,27},{32,36}... | collective-permute-start | bytes 540680 | tf_op jit(solution)/shard_map/ppermute | solution.py:592
  98.8 18.8 %collective-permute-start.27 = (s16[336,128]{1,0:T(8,128)(2,1)S(1)}, s16[336,128]{1,0:T(8,128)(2,1)S(1)}, u32[]{:S(2)}, u32[]{:S(2)}) collective-permute-start(s16[336,128]{1,0:T(8,128)(2,1)S(1)} %get-tuple-element.120), channel_id=1, source_target_pairs={{0,7},{1,6},{2,5},{3,4},{4,3},{5,2},{6,1},{7,0},{8,15},{9,14},{10,... | collective-permute-start | bytes 258056 | tf_op jit(solution)/shard_map/ppermute | solution.py:501
  103.6 14.0 %collective-permute-start.28 = (s16[336,128]{1,0:T(8,128)(2,1)S(1)}, s16[336,128]{1,0:T(8,128)(2,1)S(1)}, u32[]{:S(2)}, u32[]{:S(2)}) collective-permute-start(s16[336,128]{1,0:T(8,128)(2,1)S(1)} %get-tuple-element.121), channel_id=1, source_target_pairs={{0,6},{1,7},{2,4},{3,5},{4,2},{5,3},{6,0},{7,1},{8,14},{9,15},{10,... | collective-permute-start | bytes 258056 | tf_op jit(solution)/shard_map/ppermute | solution.py:501
  103.6 14.8 %collective-permute-start.29 = (s16[336,128]{1,0:T(8,128)(2,1)S(1)}, s16[336,128]{1,0:T(8,128)(2,1)S(1)}, u32[]{:S(2)}, u32[]{:S(2)}) collective-permute-start(s16[336,128]{1,0:T(8,128)(2,1)S(1)} %get-tuple-element.122), channel_id=1, source_target_pairs={{0,5},{1,4},{2,7},{3,6},{4,1},{5,0},{6,3},{7,2},{8,13},{9,12},{10,... | collective-permute-start | bytes 258056 | tf_op jit(solution)/shard_map/ppermute | solution.py:501
  112.4 8.9 %collective-permute-start.30 = (s16[336,128]{1,0:T(8,128)(2,1)S(1)}, s16[336,128]{1,0:T(8,128)(2,1)S(1)}, u32[]{:S(2)}, u32[]{:S(2)}) collective-permute-start(s16[336,128]{1,0:T(8,128)(2,1)S(1)} %get-tuple-element.123), channel_id=1, source_target_pairs={{0,4},{1,5},{2,6},{3,7},{4,0},{5,1},{6,2},{7,3},{8,12},{9,13},{10,... | collective-permute-start | bytes 258056 | tf_op jit(solution)/shard_map/ppermute | solution.py:501
  113.1 8.2 %collective-permute-start.31 = (s16[336,128]{1,0:T(8,128)(2,1)S(1)}, s16[336,128]{1,0:T(8,128)(2,1)S(1)}, u32[]{:S(2)}, u32[]{:S(2)}) collective-permute-start(s16[336,128]{1,0:T(8,128)(2,1)S(1)} %get-tuple-element.124), channel_id=1, source_target_pairs={{0,3},{1,2},{2,1},{3,0},{4,7},{5,6},{6,5},{7,4},{8,11},{9,10},{10,... | collective-permute-start | bytes 258056 | tf_op jit(solution)/shard_map/ppermute | solution.py:501
  117.6 6.0 %collective-permute-start.32 = (s16[336,128]{1,0:T(8,128)(2,1)S(1)}, s16[336,128]{1,0:T(8,128)(2,1)S(1)}, u32[]{:S(2)}, u32[]{:S(2)}) collective-permute-start(s16[336,128]{1,0:T(8,128)(2,1)S(1)} %get-tuple-element.125), channel_id=1, source_target_pairs={{0,2},{1,3},{2,0},{3,1},{4,6},{5,7},{6,4},{7,5},{8,10},{9,11},{10,... | collective-permute-start | bytes 258056 | tf_op jit(solution)/shard_map/ppermute | solution.py:501
  117.6 6.0 %collective-permute-start.33 = (s16[336,128]{1,0:T(8,128)(2,1)S(1)}, s16[336,128]{1,0:T(8,128)(2,1)S(1)}, u32[]{:S(2)}, u32[]{:S(2)}) collective-permute-start(s16[336,128]{1,0:T(8,128)(2,1)S(1)} %get-tuple-element.126), channel_id=1, source_target_pairs={{0,1},{1,0},{2,3},{3,2},{4,5},{5,4},{6,7},{7,6},{8,9},{9,8},{10,11... | collective-permute-start | bytes 258056 | tf_op jit(solution)/shard_map/ppermute | solution.py:501
  124.4 2.3 %collective-permute-start.34 = (f32[1440,128]{1,0:T(8,128)S(1)}, f32[1440,128]{1,0:T(8,128)S(1)}, u32[]{:S(2)}, u32[]{:S(2)}) collective-permute-start(f32[1440,128]{1,0:T(8,128)S(1)} %get-tuple-element.128), channel_id=1, source_target_pairs={{0,8},{8,0},{16,24},{24,16},{32,40},{40,32},{48,56},{56,48},{64,72... | collective-permute-start | bytes 2211848 | tf_op jit(solution)/shard_map/ppermute | solution.py:625
  124.5 2.2 %collective-permute-start.26 = (s32[1,2]{1,0:T(1,128)S(1)}, s32[1,2]{1,0:T(1,128)S(1)}, u32[]{:S(2)}, u32[]{:S(2)}) collective-permute-start(s32[1,2]{1,0:T(1,128)S(1)} %copy-done.8), channel_id=1, source_target_pairs={{0,8},{8,0},{16,24},{24,16},{32,40},{40,32},{48,56},{56,48},{64,72... | collective-permute-start | bytes 32 | tf_op jit(solution)/shard_map/ppermute | solution.py:567
  128.0 10.6 %collective-permute-start.35 = (s16[992,128]{1,0:T(8,128)(2,1)S(1)}, s16[992,128]{1,0:T(8,128)(2,1)S(1)}, u32[]{:S(2)}, u32[]{:S(2)}) collective-permute-start(s16[992,128]{1,0:T(8,128)(2,1)S(1)} %get-tuple-element.130), channel_id=1, source_target_pairs={{0,128},{8,136},{16,144},{24,152},{32,160},{40,168},{48,176},{56,1... | collective-permute-start | bytes 761864 | tf_op jit(solution)/shard_map/ppermute | solution.py:501
  128.7 14.5 %collective-permute-start.36 = (s16[992,128]{1,0:T(8,128)(2,1)S(1)}, s16[992,128]{1,0:T(8,128)(2,1)S(1)}, u32[]{:S(2)}, u32[]{:S(2)}) collective-permute-start(s16[992,128]{1,0:T(8,128)(2,1)S(1)} %get-tuple-element.131), channel_id=1, source_target_pairs={{0,192},{8,200},{16,208},{24,216},{32,224},{40,232},{48,240},{56,2... | collective-permute-start | bytes 761864 | tf_op jit(solution)/shard_map/ppermute | solution.py:501
  130.5 12.7 %collective-permute-start.37 = (s16[992,128]{1,0:T(8,128)(2,1)S(1)}, s16[992,128]{1,0:T(8,128)(2,1)S(1)}, u32[]{:S(2)}, u32[]{:S(2)}) collective-permute-start(s16[992,128]{1,0:T(8,128)(2,1)S(1)} %get-tuple-element.132), channel_id=1, source_target_pairs={{0,64},{8,72},{16,80},{24,88},{32,96},{40,104},{48,112},{56,120},{... | collective-permute-start | bytes 761864 | tf_op jit(solution)/shard_map/ppermute | solution.py:501
  143.6 7.0 %collective-permute-start.38 = (s16[256,128]{1,0:T(8,128)(2,1)S(1)}, s16[256,128]{1,0:T(8,128)(2,1)S(1)}, u32[]{:S(2)}, u32[]{:S(2)}) collective-permute-start(s16[256,128]{1,0:T(8,128)(2,1)S(1)} %get-tuple-element.134), channel_id=1, source_target_pairs={{0,48},{8,56},{16,32},{24,40},{32,16},{40,24},{48,0},{56,8},{64,11... | collective-permute-start | bytes 196616 | tf_op jit(solution)/shard_map/ppermute | solution.py:501
  146.9 8.4 %collective-permute-start.39 = (s16[256,128]{1,0:T(8,128)(2,1)S(1)}, s16[256,128]{1,0:T(8,128)(2,1)S(1)}, u32[]{:S(2)}, u32[]{:S(2)}) collective-permute-start(s16[256,128]{1,0:T(8,128)(2,1)S(1)} %get-tuple-element.135), channel_id=1, source_target_pairs={{0,32},{8,40},{16,48},{24,56},{32,0},{40,8},{48,16},{56,24},{64,96... | collective-permute-start | bytes 196616 | tf_op jit(solution)/shard_map/ppermute | solution.py:501
  150.6 5.0 %collective-permute-start.40 = (s16[256,128]{1,0:T(8,128)(2,1)S(1)}, s16[256,128]{1,0:T(8,128)(2,1)S(1)}, u32[]{:S(2)}, u32[]{:S(2)}) collective-permute-start(s16[256,128]{1,0:T(8,128)(2,1)S(1)} %get-tuple-element.136), channel_id=1, source_target_pairs={{0,16},{8,24},{16,0},{24,8},{32,48},{40,56},{48,32},{56,40},{64,80... | collective-permute-start | bytes 196616 | tf_op jit(solution)/shard_map/ppermute | solution.py:501
  (5 other events, 6.7 us)

commit v12 on v11

--- a/solution.py
+++ b/solution.py
@@ -237,9 +237,10 @@
 
     @pl.when(at_border())
     def _():
-        for n, part in enumerate(parts):
-            size = part.shape[0]
-            part[...] = two[n * size : (n + 1) * size, :]
+        base = 0
+        for part in parts:
+            part[...] = two[base : base + part.shape[0], :]
+            base += part.shape[0]
 
 
 def between_kernel(p1, q1, p0, q0, prev_f, courant, hit, part_f, part_a, bend, pad):
@@ -287,9 +288,10 @@
 
     @pl.when(at_border())
     def _():
-        for n, part in enumerate(parts):
-            size = part.shape[0]
-            held[n * size : (n + 1) * size, :] = part[...]
+        base = 0
+        for part in parts:
+            held[base : base + part.shape[0], :] = part[...]
+            base += part.shape[0]
 
     row_count, count_y, count_z = p1.shape
     band = own.shape[0] // row_count
@@ -363,7 +365,7 @@
 
 
 SIZE_X, SIZE_Z, SIZE_C = 4, 4, 2
-ROUTES = (0, 1, 3)
+ROUTES = (1, 3, 0)
 HALVES = 2
 
 
@@ -577,20 +579,21 @@
         "v" * 7,
         (padded, scale, scale),
     )
-    part = struct((half // len(ROUTES), count_z), I16)
+    most = (-(-half // (16 * len(ROUTES))) + 1) * 16
+    shares = [most] * (len(ROUTES) - 1) + [half - (len(ROUTES) - 1) * most]
     p1, q1, courant, one, two, *parts = call(
         functools.partial(first_kernel, HALVES),
-        (field, field, field, code, code, *[part] * len(ROUTES)),
+        (field, field, field, code, code, *[struct((share, count_z), I16) for share in shares]),
         (*scalars, *sums, *pieces),
         "ssss" + "v" * (4 + side),
         (slab, levels),
     )
     border = (side - 1, side)
-    moved = [lax.ppermute(part, "dom", [(a, a ^ k) for a in border]) for part, k in zip(parts[1:], ROUTES[1:])]
+    moved = [lax.ppermute(part, "dom", [(a, a ^ k) for a in border]) for part, k in zip(parts[:-1], ROUTES[:-1])]
     one, two, moved = lax.optimization_barrier((one, two, moved))
     parts = [
         lax.ppermute(part, "dom", [(a ^ k, b) for a, b in (border, border[::-1])])
-        for part, k in zip((parts[0], *moved), ROUTES)
+        for part, k in zip((*moved, parts[-1]), ROUTES)
     ]
     from_one = lax.ppermute(one, "dom", one_pairs)
     from_two = lax.ppermute(two, "dom", [(a, b) for a, b in two_pairs if a not in border])

time: 157 us -> 154 us (0.981)
  starting transfers between devices: 74.7 us -> 68.4 us
  waiting for transfers between devices: 51.9 us -> 54.3 us
    ppermute x3, starting transfers between devices: 11.2 us -> 6.75 us  [body(): lax.ppermute(part, 'dom', [(a ^ k, b) for a, b in (border, border[::-1])])]
    ppermute x2, waiting for transfers between devices: 0.01 us -> 2.53 us  [body(): from_one = lax.ppermute(one, 'dom', one_pairs)]
    ppermute x26, starting transfers between devices: 56.9 us -> 55 us  [exchange(): got[k] = lax.ppermute(parts[k - 1], axis, pairs(k))]
  transfers between devices with their start and end apart: 41 -> 41, of which waited for: 19 -> 21; matrix products, arithmetic and copies ran while one was open for 0% -> 0% of each run, Pallas kernels for 10% -> 11%
where the time goes in v12:
time: 154 us; the launch traced here: 152 us
  starting transfers between devices  68.4 us (44%)
  waiting for transfers between devices  54.3 us (35%)
  Pallas kernels  24.9 us (16%)
  local copies, waits for them, and re-layouts  3.16 us (2%)
    ppermute x26, starting transfers between devices, exchange(): got[k] = lax.ppermute(parts[k - 1], axis, pairs(k))  55 us
    ppermute x26, waiting for transfers between devices, exchange(): got[k] = lax.ppermute(parts[k - 1], axis, pairs(k))  38.8 us
    pallas_call x12, Pallas kernels, call(): pl.pallas_call(kernel, out_shape=list(outs), in_specs=[smem() if s == 's'...  24.9 us
    ppermute x2, waiting for transfers between devices, body(): lax.ppermute(part, 'dom', [(a, a ^ k) for a in border])  8.33 us
    ppermute x3, starting transfers between devices, body(): lax.ppermute(part, 'dom', [(a ^ k, b) for a, b in (border, border[::-1])])  6.75 us
    unnamed x25, local copies, waits for them, and re-layouts  3.16 us
  transfers between devices with their start and end apart: 41, of which 21 were waited for; matrix products, arithmetic and copies ran while one was open for 0% of the time, Pallas kernels for 11%

profile of v12, /device:TPU:6, one launch (start us, length us, event | category | flops | bytes accessed | tf_op | source)
XLA Modules:
  0.0 152.3 jit_solution(17207570379082976690)
XLA Ops:
  0.6 2.0 %collective-permute-start = (bf16[240,128]{1,0:T(8,128)(2,1)}, bf16[240,128]{1,0:T(8,128)(2,1)S(1)}, u32[]{:S(2)}, u32[]{:S(2)}) collective-permute-start(bf16[240,128]{1,0:T(8,128)(2,1)} %bitcast.23), channel_id=1, source_target_pairs={{0,16},{1,17},{2,18},{3,19},{4,20},{5,21},{6,22},{7,23},{8,24},{9,... | collective-permute-start | bytes 184328 | tf_op jit(solution)/shard_map/ppermute | solution.py:503
  2.6 3.3 %collective-permute-start.1 = (bf16[240,128]{1,0:T(8,128)(2,1)}, bf16[240,128]{1,0:T(8,128)(2,1)S(1)}, u32[]{:S(2)}, u32[]{:S(2)}) collective-permute-start(bf16[240,128]{1,0:T(8,128)(2,1)} %bitcast.24), channel_id=1, source_target_pairs={{0,32},{1,33},{2,34},{3,35},{4,36},{5,37},{6,38},{7,39},{8,40},{9,... | collective-permute-start | bytes 184328 | tf_op jit(solution)/shard_map/ppermute | solution.py:503
  5.9 6.4 %collective-permute-start.3 = (bf16[240,128]{1,0:T(8,128)(2,1)}, bf16[240,128]{1,0:T(8,128)(2,1)S(1)}, u32[]{:S(2)}, u32[]{:S(2)}) collective-permute-start(bf16[240,128]{1,0:T(8,128)(2,1)} %bitcast.26), channel_id=1, source_target_pairs={{0,4},{1,5},{2,6},{3,7},{4,0},{5,1},{6,2},{7,3},{8,12},{9,13},{10,... | collective-permute-start | bytes 184328 | tf_op jit(solution)/shard_map/ppermute | solution.py:503
  12.3 4.6 %collective-permute-start.5 = (bf16[240,128]{1,0:T(8,128)(2,1)}, bf16[240,128]{1,0:T(8,128)(2,1)S(1)}, u32[]{:S(2)}, u32[]{:S(2)}) collective-permute-start(bf16[240,128]{1,0:T(8,128)(2,1)} %bitcast.28), channel_id=1, source_target_pairs={{0,36},{1,37},{2,38},{3,39},{4,32},{5,33},{6,34},{7,35},{8,44},{9,... | collective-permute-start | bytes 184328 | tf_op jit(solution)/shard_map/ppermute | solution.py:503
  16.9 1.5 collective-permute-start.6
  18.4 1.2 copy-done
  19.6 1.2 copy-done.2
  21.4 1.7 %collective-permute-start.14 = (s16[2112,128]{1,0:T(8,128)(2,1)S(1)}, s16[2112,128]{1,0:T(8,128)(2,1)S(1)}, u32[]{:S(2)}, u32[]{:S(2)}) collective-permute-start(s16[2112,128]{1,0:T(8,128)(2,1)S(1)} %get-tuple-element.70), channel_id=1, source_target_pairs={{0,1},{1,0},{2,3},{3,2},{4,5},{5,4},{6,7},{7,6},{8,9},{9,8},{10,11... | collective-permute-start | bytes 1622024 | tf_op jit(solution)/shard_map/ppermute | solution.py:541
  23.8 0.9 collective-permute-start.7
  24.7 1.1 collective-permute-start.8
  25.8 2.8 %collective-permute-start.9 = (bf16[1920,128]{1,0:T(8,128)(2,1)S(1)}, bf16[1920,128]{1,0:T(8,128)(2,1)S(1)}, u32[]{:S(2)}, u32[]{:S(2)}) collective-permute-start(bf16[1920,128]{1,0:T(8,128)(2,1)S(1)} %shard_map.130.refs_0_), channel_id=1, source_target_pairs={{0,192},{8,200},{16,208},{24,216},{32,224},{40,232},{48,240},{56,2... | collective-permute-start | bytes 1474568 | tf_op jit(solution)/shard_map/ppermute | solution.py:503
  30.0 3.4 %shard_map.132 = (f32[8,256,128]{2,1,0:T(8,128)S(1)}, f32[8,256,128]{2,1,0:T(8,128)S(1)}) custom-call(s32[1]{0:T(128)S(6)} %copy.17.begin, s32[3,512]{1,0:T(4,128)S(1)} %bitcast.31, f32[64,512]{1,0:T(8,128)S(1)} %bitcast.22), custom_call_target="tpu_custom_call" | custom-call | tf_op jit(solution)/shard_map/pallas_call | solution.py:36
  33.3 4.7 %collective-permute-done.7.refs_1_ = bf16[1920,128]{1,0:T(8,128)(2,1)S(1)} collective-permute-done((bf16[1920,128]{1,0:T(8,128)(2,1)S(1)}, bf16[1920,128]{1,0:T(8,128)(2,1)S(1)}, u32[]{:S(2)}, u32[]{:S(2)}) %collective-permute-start.7) | collective-permute-done | bytes 491552 | tf_op jit(solution)/shard_map/ppermute | solution.py:503
  38.1 7.8 %collective-permute-done.8.refs_2_ = bf16[1920,128]{1,0:T(8,128)(2,1)S(1)} collective-permute-done((bf16[1920,128]{1,0:T(8,128)(2,1)S(1)}, bf16[1920,128]{1,0:T(8,128)(2,1)S(1)}, u32[]{:S(2)}, u32[]{:S(2)}) %collective-permute-start.8) | collective-permute-done | bytes 491552 | tf_op jit(solution)/shard_map/ppermute | solution.py:503
  45.8 2.6 %collective-permute-done.9.refs_3_ = bf16[1920,128]{1,0:T(8,128)(2,1)S(1)} collective-permute-done((bf16[1920,128]{1,0:T(8,128)(2,1)S(1)}, bf16[1920,128]{1,0:T(8,128)(2,1)S(1)}, u32[]{:S(2)}, u32[]{:S(2)}) %collective-permute-start.9) | collective-permute-done | bytes 491552 | tf_op jit(solution)/shard_map/ppermute | solution.py:503
  49.4 0.8 collective-permute-done.10.refs_4_
  50.2 0.7 collective-permute-done.11.refs_5_
  51.7 0.7 collective-permute-done.13.refs_7_
  52.4 1.2 shard_map.134
  53.5 3.1 %collective-permute-start.16 = (bf16[640,128]{1,0:T(8,128)(2,1)S(1)}, bf16[640,128]{1,0:T(8,128)(2,1)S(1)}, u32[]{:S(2)}, u32[]{:S(2)}) collective-permute-start(bf16[640,128]{1,0:T(8,128)(2,1)S(1)} %get-tuple-element.97), channel_id=1, source_target_pairs={{0,3},{1,2},{2,1},{3,0},{4,7},{5,6},{6,5},{7,4},{8,11},{9,10},{10,... | collective-permute-start | bytes 491528 | tf_op jit(solution)/shard_map/ppermute | solution.py:503
  57.7 6.1 %shard_map.133 = (f32[8,256,128]{2,1,0:T(8,128)S(1)}, f32[8,256,128]{2,1,0:T(8,128)S(1)}, f32[8,256,128]{2,1,0:T(8,128)S(1)}, f32[8,256,128]{2,1,0:T(8,128)S(1)}) custom-call(f32[8,256,128]{2,1,0:T(8,128)S(1)} %bitcast.13, f32[8,256,128]{2,1,0:T(8,128)S(1)} %bitcast.17, f32[8,256,128]{2,1,0:T(8,128)S(1)} %bitcast.19, f32[8,256,128]{2,1,0:T(8,128)S(1)} %bitcast.21, ...), custom_call_target="tpu_custom_call" | custom-call | tf_op jit(solution)/shard_map/pallas_call | solution.py:36
  64.0 1.2 collective-permute-done.17.rest_2_
  66.0 1.6 %shard_map.135 = (f32[8,256,128]{2,1,0:T(8,128)S(1)}, f32[8,256,128]{2,1,0:T(8,128)S(1)}, f32[8,256,128]{2,1,0:T(8,128)S(1)}, s16[2112,128]{1,0:T(8,128)(2,1)S(1...) custom-call(s32[1,2]{1,0:T(1,128)S(1)} %copy-done.8, ...), custom_call_target="tpu_custom_call" | custom-call | tf_op jit(solution)/shard_map/pallas_call | solution.py:36
  68.3 1.3 collective-permute-start.20
  69.6 8.3 %collective-permute-done.20 = s16[720,128]{1,0:T(8,128)(2,1)S(1)} collective-permute-done((s16[720,128]{1,0:T(8,128)(2,1)S(1)}, s16[720,128]{1,0:T(8,128)(2,1)S(1)}, u32[]{:S(2)}, u32[]{:S(2)}) %collective-permute-start.20) | collective-permute-done | bytes 184352 | tf_op jit(solution)/shard_map/ppermute | solution.py:592
  79.3 5.4 %collective-permute-start.22 = (s16[720,128]{1,0:T(8,128)(2,1)S(1)}, s16[720,128]{1,0:T(8,128)(2,1)S(1)}, u32[]{:S(2)}, u32[]{:S(2)}) collective-permute-start(s16[720,128]{1,0:T(8,128)(2,1)S(1)} %collective-permute-done.20), channel_id=1, source_target_pairs={{0,4},{7,3},{8,12},{15,11},{16,20},{23,19},{24,28},{31,27},{32,36}... | collective-permute-start | bytes 552968 | tf_op jit(solution)/shard_map/ppermute | solution.py:595
  85.4 5.9 %shard_map.136 = (f32[8,256,128]{2,1,0:T(8,128)S(1)}, f32[8,256,128]{2,1,0:T(8,128)S(1)}, f32[8,256,128]{2,1,0:T(8,128)S(1)}) custom-call(f32[8,256,128]{2,1,0:T(8,128)S(1)} %get-tuple-element.100.p1, f32[8,256,128]{2,1,0:T(8,128)S(1)} %get-tuple-element.101.q1, f32[8,256,128]{2,1,0:T(8,128)S(1)} %bitcast.14, f32[8,256,128]{2,1,0:T(8,128)S(1)} %bitcast.18, ...), custom_call_target="tpu_custom_call" | custom-call | tf_op jit(solution)/shard_map/pallas_call | solution.py:36
  91.3 2.5 %collective-permute-done.24.rest_3_ = s16[2112,128]{1,0:T(8,128)(2,1)S(1)} collective-permute-done((s16[2112,128]{1,0:T(8,128)(2,1)S(1)}, s16[2112,128]{1,0:T(8,128)(2,1)S(1)}, u32[]{:S(2)}, u32[]{:S(2)}) %collective-permute-start.24) | collective-permute-done | bytes 540704 | tf_op jit(solution)/shard_map/ppermute | solution.py:598
  93.9 3.0 %shard_map.137 = (f32[8,256,128]{2,1,0:T(8,128)}, f32[8,256,128]{2,1,0:T(8,128)}, f32[320,128]{1,0:T(8,128)S(1)}, s16[336,128]{1,0:T(8,128)(2,1)S(1)}, s16[336,1...) custom-call(s32[1,2]{1,0:T(1,128)S(1)} %copy-done.8, ...), custom_call_target="tpu_custom_call" | custom-call | tf_op jit(solution)/shard_map/pallas_call | solution.py:36
  96.9 5.6 %collective-permute-start.27 = (s16[336,128]{1,0:T(8,128)(2,1)S(1)}, s16[336,128]{1,0:T(8,128)(2,1)S(1)}, u32[]{:S(2)}, u32[]{:S(2)}) collective-permute-start(s16[336,128]{1,0:T(8,128)(2,1)S(1)} %get-tuple-element.120), channel_id=1, source_target_pairs={{0,7},{1,6},{2,5},{3,4},{4,3},{5,2},{6,1},{7,0},{8,15},{9,14},{10,... | collective-permute-start | bytes 258056 | tf_op jit(solution)/shard_map/ppermute | solution.py:503
  102.5 0.9 collective-permute-start.28
  103.4 7.0 %collective-permute-start.29 = (s16[336,128]{1,0:T(8,128)(2,1)S(1)}, s16[336,128]{1,0:T(8,128)(2,1)S(1)}, u32[]{:S(2)}, u32[]{:S(2)}) collective-permute-start(s16[336,128]{1,0:T(8,128)(2,1)S(1)} %get-tuple-element.122), channel_id=1, source_target_pairs={{0,5},{1,4},{2,7},{3,6},{4,1},{5,0},{6,3},{7,2},{8,13},{9,12},{10,... | collective-permute-start | bytes 258056 | tf_op jit(solution)/shard_map/ppermute | solution.py:503
  110.4 0.7 collective-permute-start.30
  111.1 2.9 %collective-permute-start.31 = (s16[336,128]{1,0:T(8,128)(2,1)S(1)}, s16[336,128]{1,0:T(8,128)(2,1)S(1)}, u32[]{:S(2)}, u32[]{:S(2)}) collective-permute-start(s16[336,128]{1,0:T(8,128)(2,1)S(1)} %get-tuple-element.124), channel_id=1, source_target_pairs={{0,3},{1,2},{2,1},{3,0},{4,7},{5,6},{6,5},{7,4},{8,11},{9,10},{10,... | collective-permute-start | bytes 258056 | tf_op jit(solution)/shard_map/ppermute | solution.py:503
  114.3 0.9 collective-permute-start.33
  115.2 4.1 %collective-permute-done.30.refs_3_ = s16[336,128]{1,0:T(8,128)(2,1)S(1)} collective-permute-done((s16[336,128]{1,0:T(8,128)(2,1)S(1)}, s16[336,128]{1,0:T(8,128)(2,1)S(1)}, u32[]{:S(2)}, u32[]{:S(2)}) %collective-permute-start.30) | collective-permute-done | bytes 86048 | tf_op jit(solution)/shard_map/ppermute | solution.py:503
  120.0 0.9 shard_map.138
  121.5 1.7 %collective-permute-done.26.other = s32[1,2]{1,0:T(1,128)S(1)} collective-permute-done((s32[1,2]{1,0:T(1,128)S(1)}, s32[1,2]{1,0:T(1,128)S(1)}, u32[]{:S(2)}, u32[]{:S(2)}) %collective-permute-start.26) | collective-permute-done | bytes 40 | tf_op jit(solution)/shard_map/ppermute | solution.py:569
  123.2 1.2 shard_map.139
  124.4 1.3 collective-permute-start.35
  125.7 1.7 %collective-permute-start.36 = (s16[992,128]{1,0:T(8,128)(2,1)S(1)}, s16[992,128]{1,0:T(8,128)(2,1)S(1)}, u32[]{:S(2)}, u32[]{:S(2)}) collective-permute-start(s16[992,128]{1,0:T(8,128)(2,1)S(1)} %get-tuple-element.131), channel_id=1, source_target_pairs={{0,192},{8,200},{16,208},{24,216},{32,224},{40,232},{48,240},{56,2... | collective-permute-start | bytes 761864 | tf_op jit(solution)/shard_map/ppermute | solution.py:503
  127.4 0.8 collective-permute-start.37
  128.2 6.8 %collective-permute-done.35.refs_0_ = s16[992,128]{1,0:T(8,128)(2,1)S(1)} collective-permute-done((s16[992,128]{1,0:T(8,128)(2,1)S(1)}, s16[992,128]{1,0:T(8,128)(2,1)S(1)}, u32[]{:S(2)}, u32[]{:S(2)}) %collective-permute-start.35) | collective-permute-done | bytes 253984 | tf_op jit(solution)/shard_map/ppermute | solution.py:503
  135.0 4.6 %collective-permute-done.36.refs_1_ = s16[992,128]{1,0:T(8,128)(2,1)S(1)} collective-permute-done((s16[992,128]{1,0:T(8,128)(2,1)S(1)}, s16[992,128]{1,0:T(8,128)(2,1)S(1)}, u32[]{:S(2)}, u32[]{:S(2)}) %collective-permute-start.36) | collective-permute-done | bytes 253984 | tf_op jit(solution)/shard_map/ppermute | solution.py:503
  140.1 2.5 %collective-permute-start.38 = (s16[256,128]{1,0:T(8,128)(2,1)S(1)}, s16[256,128]{1,0:T(8,128)(2,1)S(1)}, u32[]{:S(2)}, u32[]{:S(2)}) collective-permute-start(s16[256,128]{1,0:T(8,128)(2,1)S(1)} %get-tuple-element.134), channel_id=1, source_target_pairs={{0,48},{8,56},{16,32},{24,40},{32,16},{40,24},{48,0},{56,8},{64,11... | collective-permute-start | bytes 196616 | tf_op jit(solution)/shard_map/ppermute | solution.py:503
  142.7 3.9 %collective-permute-start.39 = (s16[256,128]{1,0:T(8,128)(2,1)S(1)}, s16[256,128]{1,0:T(8,128)(2,1)S(1)}, u32[]{:S(2)}, u32[]{:S(2)}) collective-permute-start(s16[256,128]{1,0:T(8,128)(2,1)S(1)} %get-tuple-element.135), channel_id=1, source_target_pairs={{0,32},{8,40},{16,48},{24,56},{32,0},{40,8},{48,16},{56,24},{64,96... | collective-permute-start | bytes 196616 | tf_op jit(solution)/shard_map/ppermute | solution.py:503
  146.6 4.9 %collective-permute-done.39.refs_1_ = s16[256,128]{1,0:T(8,128)(2,1)S(1)} collective-permute-done((s16[256,128]{1,0:T(8,128)(2,1)S(1)}, s16[256,128]{1,0:T(8,128)(2,1)S(1)}, u32[]{:S(2)}, u32[]{:S(2)}) %collective-permute-start.39) | collective-permute-done | bytes 65568 | tf_op jit(solution)/shard_map/ppermute | solution.py:503
  151.6 0.7 shard_map.141
  (71 shorter events, 10.6 us)
Async XLA Ops:
  0.6 11.7 %collective-permute-start = (bf16[240,128]{1,0:T(8,128)(2,1)}, bf16[240,128]{1,0:T(8,128)(2,1)S(1)}, u32[]{:S(2)}, u32[]{:S(2)}) collective-permute-start(bf16[240,128]{1,0:T(8,128)(2,1)} %bitcast.23), channel_id=1, source_target_pairs={{0,16},{1,17},{2,18},{3,19},{4,20},{5,21},{6,22},{7,23},{8,24},{9,... | collective-permute-start | bytes 184328 | tf_op jit(solution)/shard_map/ppermute | solution.py:503
  2.6 14.3 %collective-permute-start.1 = (bf16[240,128]{1,0:T(8,128)(2,1)}, bf16[240,128]{1,0:T(8,128)(2,1)S(1)}, u32[]{:S(2)}, u32[]{:S(2)}) collective-permute-start(bf16[240,128]{1,0:T(8,128)(2,1)} %bitcast.24), channel_id=1, source_target_pairs={{0,32},{1,33},{2,34},{3,35},{4,36},{5,37},{6,38},{7,39},{8,40},{9,... | collective-permute-start | bytes 184328 | tf_op jit(solution)/shard_map/ppermute | solution.py:503
  5.9 15.5 %collective-permute-start.2 = (bf16[240,128]{1,0:T(8,128)(2,1)}, bf16[240,128]{1,0:T(8,128)(2,1)S(1)}, u32[]{:S(2)}, u32[]{:S(2)}) collective-permute-start(bf16[240,128]{1,0:T(8,128)(2,1)} %bitcast.25), channel_id=1, source_target_pairs={{0,48},{1,49},{2,50},{3,51},{4,52},{5,53},{6,54},{7,55},{8,56},{9,... | collective-permute-start | bytes 184328 | tf_op jit(solution)/shard_map/ppermute | solution.py:503
  5.9 17.2 %collective-permute-start.3 = (bf16[240,128]{1,0:T(8,128)(2,1)}, bf16[240,128]{1,0:T(8,128)(2,1)S(1)}, u32[]{:S(2)}, u32[]{:S(2)}) collective-permute-start(bf16[240,128]{1,0:T(8,128)(2,1)} %bitcast.26), channel_id=1, source_target_pairs={{0,4},{1,5},{2,6},{3,7},{4,0},{5,1},{6,2},{7,3},{8,12},{9,13},{10,... | collective-permute-start | bytes 184328 | tf_op jit(solution)/shard_map/ppermute | solution.py:503
  12.3 10.8 %collective-permute-start.4 = (bf16[240,128]{1,0:T(8,128)(2,1)}, bf16[240,128]{1,0:T(8,128)(2,1)S(1)}, u32[]{:S(2)}, u32[]{:S(2)}) collective-permute-start(bf16[240,128]{1,0:T(8,128)(2,1)} %bitcast.27), channel_id=1, source_target_pairs={{0,20},{1,21},{2,22},{3,23},{4,16},{5,17},{6,18},{7,19},{8,28},{9,... | collective-permute-start | bytes 184328 | tf_op jit(solution)/shard_map/ppermute | solution.py:503
  12.3 10.8 %collective-permute-start.5 = (bf16[240,128]{1,0:T(8,128)(2,1)}, bf16[240,128]{1,0:T(8,128)(2,1)S(1)}, u32[]{:S(2)}, u32[]{:S(2)}) collective-permute-start(bf16[240,128]{1,0:T(8,128)(2,1)} %bitcast.28), channel_id=1, source_target_pairs={{0,36},{1,37},{2,38},{3,39},{4,32},{5,33},{6,34},{7,35},{8,44},{9,... | collective-permute-start | bytes 184328 | tf_op jit(solution)/shard_map/ppermute | solution.py:503
  16.9 6.9 %collective-permute-start.6 = (bf16[240,128]{1,0:T(8,128)(2,1)}, bf16[240,128]{1,0:T(8,128)(2,1)S(1)}, u32[]{:S(2)}, u32[]{:S(2)}) collective-permute-start(bf16[240,128]{1,0:T(8,128)(2,1)} %bitcast.29), channel_id=1, source_target_pairs={{0,52},{1,53},{2,54},{3,55},{4,48},{5,49},{6,50},{7,51},{8,60},{9,... | collective-permute-start | bytes 184328 | tf_op jit(solution)/shard_map/ppermute | solution.py:503
  20.8 31.5 %copy-start.8 = (s32[1,2]{1,0:T(1,128)S(1)}, s32[1,2]{1,0:T(1,128)}, u32[]{:S(2)}) copy-start(s32[1,2]{1,0:T(1,128)} %anchors.9) | copy-start | bytes 28
  21.4 8.6 %copy-start.6 = (f32[1,64,512]{2,1,0:T(8,128)S(1)}, f32[1,64,512]{2,1,0:T(8,128)}, u32[]{:S(2)}) copy-start(f32[1,64,512]{2,1,0:T(8,128)} %param.16) | copy-start | bytes 393220
  21.4 27.6 %collective-permute-start.14 = (s16[2112,128]{1,0:T(8,128)(2,1)S(1)}, s16[2112,128]{1,0:T(8,128)(2,1)S(1)}, u32[]{:S(2)}, u32[]{:S(2)}) collective-permute-start(s16[2112,128]{1,0:T(8,128)(2,1)S(1)} %get-tuple-element.70), channel_id=1, source_target_pairs={{0,1},{1,0},{2,3},{3,2},{4,5},{5,4},{6,7},{7,6},{8,9},{9,8},{10,11... | collective-permute-start | bytes 1622024 | tf_op jit(solution)/shard_map/ppermute | solution.py:541
  23.1 6.9 %copy-start.11 = (s32[1,3,512]{2,0,1:T(1,128)S(1)}, s32[1,3,512]{2,0,1:T(1,128)}, u32[]{:S(2)}) copy-start(s32[1,3,512]{2,0,1:T(1,128)} %param.15) | copy-start | bytes 18436
  23.8 33.9 %copy-start.5 = (f32[1,8,256,128]{3,2,1,0:T(8,128)S(1)}, f32[1,8,256,128]{3,2,1,0:T(8,128)}, u32[]{:S(2)}) copy-start(f32[1,8,256,128]{3,2,1,0:T(8,128)} %param.20) | copy-start | bytes 3145732
  23.8 14.2 %collective-permute-start.7 = (bf16[1920,128]{1,0:T(8,128)(2,1)S(1)}, bf16[1920,128]{1,0:T(8,128)(2,1)S(1)}, u32[]{:S(2)}, u32[]{:S(2)}) collective-permute-start(bf16[1920,128]{1,0:T(8,128)(2,1)S(1)} %shard_map.130.refs_0_), channel_id=1, source_target_pairs={{0,64},{8,72},{16,80},{24,88},{32,96},{40,104},{48,112},{56,120},{... | collective-permute-start | bytes 1474568 | tf_op jit(solution)/shard_map/ppermute | solution.py:503
  24.7 21.1 %collective-permute-start.8 = (bf16[1920,128]{1,0:T(8,128)(2,1)S(1)}, bf16[1920,128]{1,0:T(8,128)(2,1)S(1)}, u32[]{:S(2)}, u32[]{:S(2)}) collective-permute-start(bf16[1920,128]{1,0:T(8,128)(2,1)S(1)} %shard_map.130.refs_0_), channel_id=1, source_target_pairs={{0,128},{8,136},{16,144},{24,152},{32,160},{40,168},{48,176},{56,1... | collective-permute-start | bytes 1474568 | tf_op jit(solution)/shard_map/ppermute | solution.py:503
  25.8 22.5 %collective-permute-start.9 = (bf16[1920,128]{1,0:T(8,128)(2,1)S(1)}, bf16[1920,128]{1,0:T(8,128)(2,1)S(1)}, u32[]{:S(2)}, u32[]{:S(2)}) collective-permute-start(bf16[1920,128]{1,0:T(8,128)(2,1)S(1)} %shard_map.130.refs_0_), channel_id=1, source_target_pairs={{0,192},{8,200},{16,208},{24,216},{32,224},{40,232},{48,240},{56,2... | collective-permute-start | bytes 1474568 | tf_op jit(solution)/shard_map/ppermute | solution.py:503
  28.6 20.8 %collective-permute-start.15 = (s16[2112,128]{1,0:T(8,128)(2,1)S(1)}, s16[2112,128]{1,0:T(8,128)(2,1)S(1)}, u32[]{:S(2)}, u32[]{:S(2)}) collective-permute-start(s16[2112,128]{1,0:T(8,128)(2,1)S(1)} %get-tuple-element.77), channel_id=1, source_target_pairs={{1,2},{3,4},{5,6},{2,1},{4,3},{6,5},{9,10},{11,12},{13,14},{10,9},... | collective-permute-start | bytes 1622024 | tf_op jit(solution)/shard_map/ppermute | solution.py:542
  48.4 9.3 %copy-start.1 = (f32[1,8,256,128]{3,2,1,0:T(8,128)S(1)}, f32[1,8,256,128]{3,2,1,0:T(8,128)}, u32[]{:S(2)}) copy-start(f32[1,8,256,128]{3,2,1,0:T(8,128)} %param.19) | copy-start | bytes 3145732
  48.4 9.3 %copy-start.3 = (f32[1,8,256,128]{3,2,1,0:T(8,128)S(1)}, f32[1,8,256,128]{3,2,1,0:T(8,128)}, u32[]{:S(2)}) copy-start(f32[1,8,256,128]{3,2,1,0:T(8,128)} %param.21) | copy-start | bytes 3145732
  48.4 9.3 %copy-start.4 = (f32[1,8,256,128]{3,2,1,0:T(8,128)S(1)}, f32[1,8,256,128]{3,2,1,0:T(8,128)}, u32[]{:S(2)}) copy-start(f32[1,8,256,128]{3,2,1,0:T(8,128)} %param.18) | copy-start | bytes 3145732
  48.4 1.9 %collective-permute-start.10 = (bf16[1920,128]{1,0:T(8,128)(2,1)S(1)}, bf16[1920,128]{1,0:T(8,128)(2,1)S(1)}, u32[]{:S(2)}, u32[]{:S(2)}) collective-permute-start(bf16[1920,128]{1,0:T(8,128)(2,1)S(1)} %shard_map.130.refs_0_), channel_id=1, source_target_pairs={{0,8},{8,0},{16,24},{24,16},{32,40},{40,32},{48,56},{56,48},{64,72... | collective-permute-start | bytes 1474568 | tf_op jit(solution)/shard_map/ppermute | solution.py:550
  48.4 2.6 %collective-permute-start.11 = (bf16[1920,128]{1,0:T(8,128)(2,1)S(1)}, bf16[1920,128]{1,0:T(8,128)(2,1)S(1)}, u32[]{:S(2)}, u32[]{:S(2)}) collective-permute-start(bf16[1920,128]{1,0:T(8,128)(2,1)S(1)} %collective-permute-done.7.refs_1_), channel_id=1, source_target_pairs={{0,8},{8,0},{16,24},{24,16},{32,40},{40,32},{48,56},{56,48},{64,72... | collective-permute-start | bytes 1474568 | tf_op jit(solution)/shard_map/ppermute | solution.py:550
  48.9 2.8 %collective-permute-start.12 = (bf16[1920,128]{1,0:T(8,128)(2,1)S(1)}, bf16[1920,128]{1,0:T(8,128)(2,1)S(1)}, u32[]{:S(2)}, u32[]{:S(2)}) collective-permute-start(bf16[1920,128]{1,0:T(8,128)(2,1)S(1)} %collective-permute-done.8.refs_2_), channel_id=1, source_target_pairs={{0,8},{8,0},{16,24},{24,16},{32,40},{40,32},{48,56},{56,48},{64,72... | collective-permute-start | bytes 1474568 | tf_op jit(solution)/shard_map/ppermute | solution.py:550
  49.0 3.4 %collective-permute-start.13 = (bf16[1920,128]{1,0:T(8,128)(2,1)S(1)}, bf16[1920,128]{1,0:T(8,128)(2,1)S(1)}, u32[]{:S(2)}, u32[]{:S(2)}) collective-permute-start(bf16[1920,128]{1,0:T(8,128)(2,1)S(1)} %collective-permute-done.9.refs_3_), channel_id=1, source_target_pairs={{0,8},{8,0},{16,24},{24,16},{32,40},{40,32},{48,56},{56,48},{64,72... | collective-permute-start | bytes 1474568 | tf_op jit(solution)/shard_map/ppermute | solution.py:550
  53.5 10.5 %collective-permute-start.16 = (bf16[640,128]{1,0:T(8,128)(2,1)S(1)}, bf16[640,128]{1,0:T(8,128)(2,1)S(1)}, u32[]{:S(2)}, u32[]{:S(2)}) collective-permute-start(bf16[640,128]{1,0:T(8,128)(2,1)S(1)} %get-tuple-element.97), channel_id=1, source_target_pairs={{0,3},{1,2},{2,1},{3,0},{4,7},{5,6},{6,5},{7,4},{8,11},{9,10},{10,... | collective-permute-start | bytes 491528 | tf_op jit(solution)/shard_map/ppermute | solution.py:503
  56.6 8.6 %collective-permute-start.17 = (bf16[640,128]{1,0:T(8,128)(2,1)S(1)}, bf16[640,128]{1,0:T(8,128)(2,1)S(1)}, u32[]{:S(2)}, u32[]{:S(2)}) collective-permute-start(bf16[640,128]{1,0:T(8,128)(2,1)S(1)} %get-tuple-element.98), channel_id=1, source_target_pairs={{0,2},{1,3},{2,0},{3,1},{4,6},{5,7},{6,4},{7,5},{8,10},{9,11},{10,... | collective-permute-start | bytes 491528 | tf_op jit(solution)/shard_map/ppermute | solution.py:503
  57.3 8.1 %collective-permute-start.18 = (bf16[640,128]{1,0:T(8,128)(2,1)S(1)}, bf16[640,128]{1,0:T(8,128)(2,1)S(1)}, u32[]{:S(2)}, u32[]{:S(2)}) collective-permute-start(bf16[640,128]{1,0:T(8,128)(2,1)S(1)} %get-tuple-element.99), channel_id=1, source_target_pairs={{0,1},{1,0},{2,3},{3,2},{4,5},{5,4},{6,7},{7,6},{8,9},{9,8},{10,11... | collective-permute-start | bytes 491528 | tf_op jit(solution)/shard_map/ppermute | solution.py:503
  67.6 2.0 %collective-permute-start.19 = (s16[720,128]{1,0:T(8,128)(2,1)S(1)}, s16[720,128]{1,0:T(8,128)(2,1)S(1)}, u32[]{:S(2)}, u32[]{:S(2)}) collective-permute-start(s16[720,128]{1,0:T(8,128)(2,1)S(1)} %get-tuple-element.109), channel_id=1, source_target_pairs={{3,2},{4,5},{11,10},{12,13},{19,18},{20,21},{27,26},{28,29},{35,34... | collective-permute-start | bytes 552968 | tf_op jit(solution)/shard_map/ppermute | solution.py:592
  68.3 9.6 %collective-permute-start.20 = (s16[720,128]{1,0:T(8,128)(2,1)S(1)}, s16[720,128]{1,0:T(8,128)(2,1)S(1)}, u32[]{:S(2)}, u32[]{:S(2)}) collective-permute-start(s16[720,128]{1,0:T(8,128)(2,1)S(1)} %get-tuple-element.110), channel_id=1, source_target_pairs={{3,0},{4,7},{11,8},{12,15},{19,16},{20,23},{27,24},{28,31},{35,32}... | collective-permute-start | bytes 552968 | tf_op jit(solution)/shard_map/ppermute | solution.py:592
  77.9 16.0 %collective-permute-start.24 = (s16[2112,128]{1,0:T(8,128)(2,1)S(1)}, s16[2112,128]{1,0:T(8,128)(2,1)S(1)}, u32[]{:S(2)}, u32[]{:S(2)}) collective-permute-start(s16[2112,128]{1,0:T(8,128)(2,1)S(1)} %get-tuple-element.114), channel_id=1, source_target_pairs={{0,1},{1,0},{2,3},{3,2},{4,5},{5,4},{6,7},{7,6},{8,9},{9,8},{10,11... | collective-permute-start | bytes 1622024 | tf_op jit(solution)/shard_map/ppermute | solution.py:598
  77.9 16.0 %collective-permute-start.25 = (s16[2112,128]{1,0:T(8,128)(2,1)S(1)}, s16[2112,128]{1,0:T(8,128)(2,1)S(1)}, u32[]{:S(2)}, u32[]{:S(2)}) collective-permute-start(s16[2112,128]{1,0:T(8,128)(2,1)S(1)} %get-tuple-element.115), channel_id=1, source_target_pairs={{1,2},{5,6},{2,1},{6,5},{9,10},{13,14},{10,9},{14,13},{17,18},{21,... | collective-permute-start | bytes 1622024 | tf_op jit(solution)/shard_map/ppermute | solution.py:599
  78.6 12.7 %collective-permute-start.21 = (s16[720,128]{1,0:T(8,128)(2,1)S(1)}, s16[720,128]{1,0:T(8,128)(2,1)S(1)}, u32[]{:S(2)}, u32[]{:S(2)}) collective-permute-start(s16[720,128]{1,0:T(8,128)(2,1)S(1)} %collective-permute-done.19), channel_id=1, source_target_pairs={{2,4},{5,3},{10,12},{13,11},{18,20},{21,19},{26,28},{29,27},{34,36... | collective-permute-start | bytes 552968 | tf_op jit(solution)/shard_map/ppermute | solution.py:595
  79.3 12.1 %collective-permute-start.22 = (s16[720,128]{1,0:T(8,128)(2,1)S(1)}, s16[720,128]{1,0:T(8,128)(2,1)S(1)}, u32[]{:S(2)}, u32[]{:S(2)}) collective-permute-start(s16[720,128]{1,0:T(8,128)(2,1)S(1)} %collective-permute-done.20), channel_id=1, source_target_pairs={{0,4},{7,3},{8,12},{15,11},{16,20},{23,19},{24,28},{31,27},{32,36}... | collective-permute-start | bytes 552968 | tf_op jit(solution)/shard_map/ppermute | solution.py:595
  84.7 6.6 %collective-permute-start.23 = (s16[672,128]{1,0:T(8,128)(2,1)S(1)}, s16[672,128]{1,0:T(8,128)(2,1)S(1)}, u32[]{:S(2)}, u32[]{:S(2)}) collective-permute-start(s16[672,128]{1,0:T(8,128)(2,1)S(1)} %get-tuple-element.113), channel_id=1, source_target_pairs={{3,4},{4,3},{11,12},{12,11},{19,20},{20,19},{27,28},{28,27},{35,36... | collective-permute-start | bytes 516104 | tf_op jit(solution)/shard_map/ppermute | solution.py:595
  96.9 17.1 %collective-permute-start.27 = (s16[336,128]{1,0:T(8,128)(2,1)S(1)}, s16[336,128]{1,0:T(8,128)(2,1)S(1)}, u32[]{:S(2)}, u32[]{:S(2)}) collective-permute-start(s16[336,128]{1,0:T(8,128)(2,1)S(1)} %get-tuple-element.120), channel_id=1, source_target_pairs={{0,7},{1,6},{2,5},{3,4},{4,3},{5,2},{6,1},{7,0},{8,15},{9,14},{10,... | collective-permute-start | bytes 258056 | tf_op jit(solution)/shard_map/ppermute | solution.py:503
  102.5 11.8 %collective-permute-start.28 = (s16[336,128]{1,0:T(8,128)(2,1)S(1)}, s16[336,128]{1,0:T(8,128)(2,1)S(1)}, u32[]{:S(2)}, u32[]{:S(2)}) collective-permute-start(s16[336,128]{1,0:T(8,128)(2,1)S(1)} %get-tuple-element.121), channel_id=1, source_target_pairs={{0,6},{1,7},{2,4},{3,5},{4,2},{5,3},{6,0},{7,1},{8,14},{9,15},{10,... | collective-permute-start | bytes 258056 | tf_op jit(solution)/shard_map/ppermute | solution.py:503
  103.4 11.8 %collective-permute-start.29 = (s16[336,128]{1,0:T(8,128)(2,1)S(1)}, s16[336,128]{1,0:T(8,128)(2,1)S(1)}, u32[]{:S(2)}, u32[]{:S(2)}) collective-permute-start(s16[336,128]{1,0:T(8,128)(2,1)S(1)} %get-tuple-element.122), channel_id=1, source_target_pairs={{0,5},{1,4},{2,7},{3,6},{4,1},{5,0},{6,3},{7,2},{8,13},{9,12},{10,... | collective-permute-start | bytes 258056 | tf_op jit(solution)/shard_map/ppermute | solution.py:503
  110.4 8.9 %collective-permute-start.30 = (s16[336,128]{1,0:T(8,128)(2,1)S(1)}, s16[336,128]{1,0:T(8,128)(2,1)S(1)}, u32[]{:S(2)}, u32[]{:S(2)}) collective-permute-start(s16[336,128]{1,0:T(8,128)(2,1)S(1)} %get-tuple-element.123), channel_id=1, source_target_pairs={{0,4},{1,5},{2,6},{3,7},{4,0},{5,1},{6,2},{7,3},{8,12},{9,13},{10,... | collective-permute-start | bytes 258056 | tf_op jit(solution)/shard_map/ppermute | solution.py:503
  111.1 8.2 %collective-permute-start.31 = (s16[336,128]{1,0:T(8,128)(2,1)S(1)}, s16[336,128]{1,0:T(8,128)(2,1)S(1)}, u32[]{:S(2)}, u32[]{:S(2)}) collective-permute-start(s16[336,128]{1,0:T(8,128)(2,1)S(1)} %get-tuple-element.124), channel_id=1, source_target_pairs={{0,3},{1,2},{2,1},{3,0},{4,7},{5,6},{6,5},{7,4},{8,11},{9,10},{10,... | collective-permute-start | bytes 258056 | tf_op jit(solution)/shard_map/ppermute | solution.py:503
  114.0 6.0 %collective-permute-start.32 = (s16[336,128]{1,0:T(8,128)(2,1)S(1)}, s16[336,128]{1,0:T(8,128)(2,1)S(1)}, u32[]{:S(2)}, u32[]{:S(2)}) collective-permute-start(s16[336,128]{1,0:T(8,128)(2,1)S(1)} %get-tuple-element.125), channel_id=1, source_target_pairs={{0,2},{1,3},{2,0},{3,1},{4,6},{5,7},{6,4},{7,5},{8,10},{9,11},{10,... | collective-permute-start | bytes 258056 | tf_op jit(solution)/shard_map/ppermute | solution.py:503
  114.3 5.7 %collective-permute-start.33 = (s16[336,128]{1,0:T(8,128)(2,1)S(1)}, s16[336,128]{1,0:T(8,128)(2,1)S(1)}, u32[]{:S(2)}, u32[]{:S(2)}) collective-permute-start(s16[336,128]{1,0:T(8,128)(2,1)S(1)} %get-tuple-element.126), channel_id=1, source_target_pairs={{0,1},{1,0},{2,3},{3,2},{4,5},{5,4},{6,7},{7,6},{8,9},{9,8},{10,11... | collective-permute-start | bytes 258056 | tf_op jit(solution)/shard_map/ppermute | solution.py:503
  120.9 2.3 %collective-permute-start.34 = (f32[1440,128]{1,0:T(8,128)S(1)}, f32[1440,128]{1,0:T(8,128)S(1)}, u32[]{:S(2)}, u32[]{:S(2)}) collective-permute-start(f32[1440,128]{1,0:T(8,128)S(1)} %get-tuple-element.128), channel_id=1, source_target_pairs={{0,8},{8,0},{16,24},{24,16},{32,40},{40,32},{48,56},{56,48},{64,72... | collective-permute-start | bytes 2211848 | tf_op jit(solution)/shard_map/ppermute | solution.py:628
  121.0 2.2 %collective-permute-start.26 = (s32[1,2]{1,0:T(1,128)S(1)}, s32[1,2]{1,0:T(1,128)S(1)}, u32[]{:S(2)}, u32[]{:S(2)}) collective-permute-start(s32[1,2]{1,0:T(1,128)S(1)} %copy-done.8), channel_id=1, source_target_pairs={{0,8},{8,0},{16,24},{24,16},{32,40},{40,32},{48,56},{56,48},{64,72... | collective-permute-start | bytes 32 | tf_op jit(solution)/shard_map/ppermute | solution.py:569
  124.4 10.6 %collective-permute-start.35 = (s16[992,128]{1,0:T(8,128)(2,1)S(1)}, s16[992,128]{1,0:T(8,128)(2,1)S(1)}, u32[]{:S(2)}, u32[]{:S(2)}) collective-permute-start(s16[992,128]{1,0:T(8,128)(2,1)S(1)} %get-tuple-element.130), channel_id=1, source_target_pairs={{0,128},{8,136},{16,144},{24,152},{32,160},{40,168},{48,176},{56,1... | collective-permute-start | bytes 761864 | tf_op jit(solution)/shard_map/ppermute | solution.py:503
  125.7 13.9 %collective-permute-start.36 = (s16[992,128]{1,0:T(8,128)(2,1)S(1)}, s16[992,128]{1,0:T(8,128)(2,1)S(1)}, u32[]{:S(2)}, u32[]{:S(2)}) collective-permute-start(s16[992,128]{1,0:T(8,128)(2,1)S(1)} %get-tuple-element.131), channel_id=1, source_target_pairs={{0,192},{8,200},{16,208},{24,216},{32,224},{40,232},{48,240},{56,2... | collective-permute-start | bytes 761864 | tf_op jit(solution)/shard_map/ppermute | solution.py:503
  127.4 12.4 %collective-permute-start.37 = (s16[992,128]{1,0:T(8,128)(2,1)S(1)}, s16[992,128]{1,0:T(8,128)(2,1)S(1)}, u32[]{:S(2)}, u32[]{:S(2)}) collective-permute-start(s16[992,128]{1,0:T(8,128)(2,1)S(1)} %get-tuple-element.132), channel_id=1, source_target_pairs={{0,64},{8,72},{16,80},{24,88},{32,96},{40,104},{48,112},{56,120},{... | collective-permute-start | bytes 761864 | tf_op jit(solution)/shard_map/ppermute | solution.py:503
  140.1 6.5 %collective-permute-start.38 = (s16[256,128]{1,0:T(8,128)(2,1)S(1)}, s16[256,128]{1,0:T(8,128)(2,1)S(1)}, u32[]{:S(2)}, u32[]{:S(2)}) collective-permute-start(s16[256,128]{1,0:T(8,128)(2,1)S(1)} %get-tuple-element.134), channel_id=1, source_target_pairs={{0,48},{8,56},{16,32},{24,40},{32,16},{40,24},{48,0},{56,8},{64,11... | collective-permute-start | bytes 196616 | tf_op jit(solution)/shard_map/ppermute | solution.py:503
  142.7 8.8 %collective-permute-start.39 = (s16[256,128]{1,0:T(8,128)(2,1)S(1)}, s16[256,128]{1,0:T(8,128)(2,1)S(1)}, u32[]{:S(2)}, u32[]{:S(2)}) collective-permute-start(s16[256,128]{1,0:T(8,128)(2,1)S(1)} %get-tuple-element.135), channel_id=1, source_target_pairs={{0,32},{8,40},{16,48},{24,56},{32,0},{40,8},{48,16},{56,24},{64,96... | collective-permute-start | bytes 196616 | tf_op jit(solution)/shard_map/ppermute | solution.py:503
  146.6 5.0 %collective-permute-start.40 = (s16[256,128]{1,0:T(8,128)(2,1)S(1)}, s16[256,128]{1,0:T(8,128)(2,1)S(1)}, u32[]{:S(2)}, u32[]{:S(2)}) collective-permute-start(s16[256,128]{1,0:T(8,128)(2,1)S(1)} %get-tuple-element.136), channel_id=1, source_target_pairs={{0,16},{8,24},{16,0},{24,8},{32,48},{40,56},{48,32},{56,40},{64,80... | collective-permute-start | bytes 196616 | tf_op jit(solution)/shard_map/ppermute | solution.py:503
  (5 other events, 6.7 us)
